TPU v7x, 128 devices: a whole 4x4x4 slice. The times are simulated.
128 devices in a mesh: dp: 8 (over z, core), cent: 16 (over y, x).
Axes of the slice: x: 4, y: 4, z: 4, core: 2. Of those that a mesh axis runs over, the one named last changes fastest.
Arguments:
- vectors: bfloat16 [131072, 768], P(('dp', 'cent')), may hold values from -110 to 110
- centroids: bfloat16 [32768, 768], P('cent'), may hold values from -0.29882812 to 0.29882812
- candidates: int32 [131072, 4], P(('dp', 'cent')), may hold values from 0 to 63, all different within a row; in each aligned block of 1024 rows (0 to 1023, 1024 to 2047, ...) at most 96 rows name the same one
Outputs:
- updated: bfloat16 [32768, 768], P('cent')
Inputs may be any that keep to these rules, and one draw needn't show every extreme that they name: `candidates`: each row names four different blocks; among the 1024 rows of one device no block is named more than 96 times, and some block exactly 96 times.
All inputs are finite; a program needn't handle non-finite values.
Results may differ from a plain program's by a relative error of at most 0.02.
Values may be sent and summed in bfloat16 or wider, within the bound.
No kernel may reach another device: no remote copies, remote signals or barrier semaphores. Data moves between devices by JAX's collectives and lax.ppermute only.
A program may use at most 128 MiB of HBM per device.

v0:
```python
import math

import jax
import jax.numpy as jnp
from jax import lax
from jax.sharding import PartitionSpec as P

BS = 512


def pair_ranks(flat_blocks, nblocks):
    pair_count = flat_blocks.shape[0]
    span = math.gcd(pair_count, 512)
    pieces = pair_count // span
    onehot = flat_blocks[:, None] == jnp.arange(nblocks, dtype=jnp.int32)[None, :]
    hits = onehot.astype(jnp.bfloat16).reshape(pieces, span, nblocks)
    lower = (
        jnp.arange(span, dtype=jnp.int32)[None, :] < jnp.arange(span, dtype=jnp.int32)[:, None]
    ).astype(jnp.bfloat16)
    within = jnp.einsum("ij,rjb->rib", lower, hits, preferred_element_type=jnp.float32)
    piece_sums = jnp.sum(hits.astype(jnp.float32), axis=1)
    earlier = (
        jnp.arange(pieces, dtype=jnp.int32)[None, :] < jnp.arange(pieces, dtype=jnp.int32)[:, None]
    ).astype(jnp.float32)
    prefix = jnp.dot(
        earlier, piece_sums, precision=lax.Precision.HIGHEST, preferred_element_type=jnp.float32
    )
    before = (within + prefix[:, None, :]).reshape(pair_count, nblocks)
    return jnp.sum(jnp.where(onehot, before, 0.0), axis=1).astype(jnp.int32)


def fetch_pairs(values, slot_pairs, slot_range):
    columns = []
    for pick in range(4):
        hit = slot_range[None, :] == slot_pairs[:, pick : pick + 1]
        columns.append(jnp.sum(jnp.where(hit, values[None, :], 0.0), axis=1))
    return jnp.stack(columns, axis=1)


def body(vectors, centroids, candidates):
    tok_rows = vectors.shape[0]
    width = vectors.shape[1]
    groups = lax.axis_size("cent")
    kdev = centroids.shape[0]
    blk_here = kdev // BS
    nblocks = blk_here * groups
    most_rows = 6 * tok_rows // nblocks
    slot_total = nblocks * most_rows
    flat_blocks = candidates.reshape(-1)
    rank = pair_ranks(flat_blocks, nblocks)
    slot_pairs = (flat_blocks * most_rows + rank).reshape(tok_rows, 4)
    slot_range = jnp.arange(slot_total, dtype=jnp.int32)
    routed = slot_range[:, None] == slot_pairs[None, :, 0]
    for pick in range(1, 4):
        routed = routed | (slot_range[:, None] == slot_pairs[None, :, pick])
    dispatch = routed.astype(jnp.bfloat16)
    sendbuf = jnp.dot(dispatch, vectors, preferred_element_type=jnp.float32).astype(jnp.bfloat16)
    outgoing = sendbuf.reshape(groups, blk_here * most_rows, width)
    received_rows = lax.all_to_all(outgoing, "cent", split_axis=0, concat_axis=0, tiled=True)
    received_rows = received_rows.reshape(groups, blk_here, most_rows, width)
    candidate_blocks = centroids.reshape(blk_here, BS, width)
    squares = jnp.sum(centroids.astype(jnp.float32) ** 2, axis=1).reshape(blk_here, BS)
    unscaled_scores = jnp.einsum(
        "erlp,ryp->erly", received_rows, candidate_blocks, preferred_element_type=jnp.float32
    )
    scores = unscaled_scores - 0.5 * squares[None, :, None, :]
    peak = jnp.max(scores, axis=3)
    total = jnp.sum(jnp.exp(scores - peak[..., None]), axis=3)
    back_peak, back_total = (
        lax.all_to_all(
            peak.reshape(groups, blk_here * most_rows),
            "cent",
            split_axis=0,
            concat_axis=0,
            tiled=True,
        ),
        lax.all_to_all(
            total.reshape(groups, blk_here * most_rows),
            "cent",
            split_axis=0,
            concat_axis=0,
            tiled=True,
        ),
    )
    pair_peak = fetch_pairs(back_peak.reshape(-1), slot_pairs, slot_range)
    pair_total = fetch_pairs(back_total.reshape(-1), slot_pairs, slot_range)
    top = jnp.max(pair_peak, axis=1)
    lse = top + jnp.log(jnp.sum(pair_total * jnp.exp(pair_peak - top[:, None]), axis=1))
    filled = jnp.sum(jnp.where(routed, lse[None, :], 0.0), axis=1)
    norm_buf = jnp.where(jnp.any(routed, axis=1), filled, 1e30)
    norm_in = lax.all_to_all(
        norm_buf.reshape(groups, blk_here * most_rows),
        "cent",
        split_axis=0,
        concat_axis=0,
        tiled=True,
    )
    norm_in = norm_in.reshape(groups, blk_here, most_rows)
    weight = jnp.exp(scores - norm_in[..., None])
    weight_sum = jnp.sum(weight, axis=(0, 2)).reshape(kdev)
    block_weight = weight.astype(jnp.bfloat16)
    sums = jnp.einsum(
        "yhzc,yhzu->hcu", block_weight, received_rows, preferred_element_type=jnp.float32
    ).reshape(kdev, width)
    totals, counts = (
        lax.psum(sums.astype(jnp.bfloat16), "dp").astype(jnp.float32),
        lax.psum(weight_sum.astype(jnp.bfloat16), "dp").astype(jnp.float32),
    )
    fresh = (totals + centroids.astype(jnp.float32)) / (counts + 1.0)[:, None]
    return fresh.astype(jnp.bfloat16)


def solution(mesh):
    return jax.shard_map(
        body,
        mesh=mesh,
        in_specs=(P(("dp", "cent"), None), P("cent", None), P(("dp", "cent"), None)),
        out_specs=P("cent", None),
        check_vma=False,
    )
```

profile of v0, /device:TPU:1, one launch (start us, length us, event | category | flops | bytes accessed | tf_op | source)
XLA Modules:
  0.0 370.0 jit_solution(18268139172502421644)
XLA Ops:
  6.5 1.1 copy.46
  7.6 0.3 eq.68
  7.9 0.2 convert_reduce_fusion
  8.1 0.1 fusion.31
  8.2 0.6 fusion.24
  8.7 0.5 convert_element_type.51
  9.3 0.2 copy.47
  9.5 0.7 multiply_add_fusion
  10.2 18.8 %convolution_convert_fusion = bf16[6144,768]{1,0:T(8,128)(2,1)} fusion(bf16[1024,768]{1,0:T(8,128)(2,1)S(1)} %copy-done, s32[1024]{0:T(1024)S(1)} %bitcast.79, s32[1024]{0:T(1024)S(1)} %bitcast.83, s32[1024]{0:T(1024)S(1)} %bitcast.87, s32[1024]{0:T(1024)S(1)} %bitcast.75), kind=kOutput, calls=%fused_computation.28 | convolution fusion | flops 9712435200 | bytes 11026432 | tf_op jit(solution)/shard_map/dot_general | solution.py:57
  29.0 7.6 %all-to-all-start = ((bf16[16,384,768]{2,1,0:T(8,128)(2,1)}), bf16[16,384,768]{2,1,0:T(8,128)(2,1)}, u32[]{:S(2)}, u32[]{:S(2)}) async-start(bf16[16,384,768]{2,1,0:T(8,128)(2,1)} %bitcast.60), calls=%async_computation | async-start | bytes 18874368 | tf_op jit(solution)/shard_map/all_to_all | solution.py:59
  36.7 2.6 fusion.12
  39.3 136.1 %all-to-all-done = bf16[16,384,768]{2,1,0:T(8,128)(2,1)} async-done(((bf16[16,384,768]{2,1,0:T(8,128)(2,1)}), bf16[16,384,768]{2,1,0:T(8,128)(2,1)}, u32[]{:S(2)}, u32[]{:S(2)}) %all-to-all-start) | async-done | bytes 9437216 | tf_op jit(solution)/shard_map/all_to_all | solution.py:59
  175.3 8.8 %bitcast_reduce_fusion = (f32[16,4,96]{2,0,1:T(8,128)S(1)}, f32[4,16,96,512]{3,2,1,0:T(8,128)S(1)}) fusion(f32[4,512]{1,0:T(4,128)S(1)} %mul.28, bf16[4,512,768,1]{2,1,3,0:T(8,128)(2,1)} %bitcast.59, bf16[16,4,96,768]{3,2,1,0:T(8,128)(2,1)} %bitcast.7), kind=kOutput, calls=%fused_computation.22 | convolution fusion | flops 4838123520 | bytes 25198592 | tf_op jit(solution)/shard_map/erlp,ryp->erly/dot_general | solution.py:63
  184.1 4.6 %copy-done.1 = f32[4,16,96,512]{3,2,1,0:T(8,128)} copy-done((f32[4,16,96,512]{3,2,1,0:T(8,128)}, f32[4,16,96,512]{3,2,1,0:T(8,128)S(1)}, u32[]{:S(2)}) %copy-start.1) | copy-done | bytes 12582936
  188.7 3.3 fusion.4
  192.1 0.7 all_to_all.26
  192.8 5.3 %all-to-all-start.2 = ((f32[16,1,384]{2,1,0:T(1,128)}), f32[16,1,384]{2,1,0:T(1,128)S(1)}, u32[]{:S(2)}, u32[]{:S(2)}) async-start(f32[16,1,384]{2,1,0:T(1,128)} %all_to_all.26), calls=%async_computation.2 | async-start | bytes 49152 | tf_op jit(solution)/shard_map/all_to_all | solution.py:77
  198.1 0.7 all_to_all.25
  198.8 5.7 %all-to-all-done.2 = f32[16,1,384]{2,1,0:T(1,128)S(1)} async-done(((f32[16,1,384]{2,1,0:T(1,128)}), f32[16,1,384]{2,1,0:T(1,128)S(1)}, u32[]{:S(2)}, u32[]{:S(2)}) %all-to-all-start.2) | async-done | bytes 24608 | tf_op jit(solution)/shard_map/all_to_all | solution.py:77
  204.5 3.5 all-to-all-start.1
  208.0 0.2 all-reduce.2.cloned.1.call-start
  208.3 12.7 %fusion.32 = pred[6144]{0:T(1024)(128)(4,1)S(1)} fusion(s32[1024]{0:T(1024)S(1)} %bitcast.80, s32[1024]{0:T(1024)S(1)} %bitcast.84, s32[1024]{0:T(1024)S(1)} %bitcast.88, s32[1024]{0:T(1024)S(1)} %bitcast.76), kind=kLoop, calls=%fused_computation.64 | loop fusion | flops 50325504 | bytes 22528 | tf_op jit(solution)/shard_map/reduce_or | solution.py:90
  220.9 32.2 %select_reduce_fusion.7 = (f32[1024]{0:T(1024)S(1)}, f32[1024]{0:T(1024)S(1)}, f32[1024]{0:T(1024)S(1)}, f32[1024]{0:T(1024)S(1)}, f32[1024]{0:T(1024)S(1)}, /*i...) fusion(s32[1024]{0:T(1024)S(1)} %bitcast.89, f32[6144]{0:T(1024)S(1)} %bitcast.64, s32[1024]{0:T(1024)S(1)} %bitcast.85, ...), kind=kLoop, calls=%fused_computation.9 | loop fusion | flops 125820928 | bytes 98304 | tf_op jit(solution)/shard_map/reduce_sum | solution.py:36
  253.2 0.1 fusion.29
  253.3 10.2 %select_reduce_fusion = f32[6144]{0:T(1024)S(1)} fusion(f32[1024]{0:T(1024)S(1)} %log_add_fusion, s32[1024]{0:T(1024)S(1)} %bitcast.82, s32[1024]{0:T(1024)S(1)} %bitcast.86, s32[1024]{0:T(1024)S(1)} %bitcast.90, s32[1024]{0:T(1024)S(1)} %bitcast.78), kind=kLoop, calls=%fused_computation | loop fusion | flops 56616960 | bytes 45056 | tf_op jit(solution)/shard_map/reduce_sum | solution.py:89
  263.5 12.8 %all_to_all.31 = f32[16,1,384]{2,1,0:T(1,128)S(1)} all-to-all(f32[16,1,384]{2,1,0:T(1,128)S(1)} %bitcast.62), channel_id=1, replica_groups=mesh['dp'=8,'cent'=16] {'cent'}, dimensions={0} | all-to-all | bytes 49152 | tf_op jit(solution)/shard_map/all_to_all | solution.py:91
  276.4 0.1 sub.44
  276.5 11.6 %bitcast_convert_fusion = bf16[4,512,768]{2,1,0:T(8,128)(2,1)} fusion(bf16[16,4,96,768]{3,2,1,0:T(8,128)(2,1)} %bitcast.7, f32[4,16,96,512]{3,2,1,0:T(8,128)} %copy-done.1, f32[16,4,96]{2,0,1:T(8,128)S(1)} %copy.53, f32[4,512]{1,0:T(4,128)S(1)} %mul.28), kind=kOutput, calls=%fused_computation.38 | convolution fusion | flops 4842848256 | bytes 25198592 | tf_op jit(solution)/shard_map/yhzc,yhzu->hcu/dot_general | solution.py:102
  288.1 6.1 %fusion.6 = bf16[4,512]{1,0:T(4,128)(2,1)S(1)} fusion(f32[4,16,96,512]{3,2,1,0:T(8,128)} %copy-done.1, f32[16,4,96]{2,0,1:T(8,128)S(1)} %copy.53, f32[4,512]{1,0:T(4,128)S(1)} %mul.28), kind=kLoop, calls=%fused_computation.26 | loop fusion | flops 9435136 | bytes 12619776 | tf_op jit(solution)/shard_map/reduce_sum | solution.py:100
  294.2 18.1 %psum.15 = bf16[2048]{0:T(1024)(128)(2,1)S(1)} all-reduce(bf16[2048]{0:T(1024)(128)(2,1)S(1)} %bitcast.70), channel_id=1, replica_groups=mesh['dp'=8,'cent'=16] {'dp'}, use_global_device_ids=true, to_apply=%region_18.19 | all-reduce | flops 2048 | bytes 8192 | tf_op jit(solution)/shard_map/psum | solution.py:107
  312.4 46.3 %all-reduce.2.cloned.1.call-done = bf16[2048,768]{1,0:T(8,128)(2,1)} async-done(((bf16[2048,768]{1,0:T(8,128)(2,1)}), bf16[2048,768]{1,0:T(8,128)(2,1)}) %all-reduce.2.cloned.1.call-update) | async-done | bytes 3145744 | tf_op jit(solution)/shard_map/psum | solution.py:106
  358.6 4.5 %fusion.14 = bf16[2048,768]{1,0:T(8,128)(2,1)} fusion(bf16[2048,768]{1,0:T(8,128)(2,1)} %param.4, bf16[2048,768]{1,0:T(8,128)(2,1)} %all-reduce.2.cloned.1.call-done, f32[2048]{0:T(1024)S(1)} %convert_add_fusion.1), kind=kLoop, calls=%fused_computation.37 | loop fusion | flops 7864320 | bytes 9445376 | tf_op jit(solution)/shard_map/convert_element_type | solution.py:110
  (18 shorter events, 0.2 us)
Async XLA Ops:
  6.5 3.7 copy-start
  29.0 146.3 %all-to-all-start = ((bf16[16,384,768]{2,1,0:T(8,128)(2,1)}), bf16[16,384,768]{2,1,0:T(8,128)(2,1)}, u32[]{:S(2)}, u32[]{:S(2)}) async-start(bf16[16,384,768]{2,1,0:T(8,128)(2,1)} %bitcast.60), calls=%async_computation | async-start | bytes 18874368 | tf_op jit(solution)/shard_map/all_to_all | solution.py:59
  184.1 4.6 %copy-start.1 = (f32[4,16,96,512]{3,2,1,0:T(8,128)}, f32[4,16,96,512]{3,2,1,0:T(8,128)S(1)}, u32[]{:S(2)}) copy-start(f32[4,16,96,512]{3,2,1,0:T(8,128)S(1)} %get-tuple-element.22) | copy-start | bytes 37748740
  192.8 11.8 %all-to-all-start.2 = ((f32[16,1,384]{2,1,0:T(1,128)}), f32[16,1,384]{2,1,0:T(1,128)S(1)}, u32[]{:S(2)}, u32[]{:S(2)}) async-start(f32[16,1,384]{2,1,0:T(1,128)} %all_to_all.26), calls=%async_computation.2 | async-start | bytes 49152 | tf_op jit(solution)/shard_map/all_to_all | solution.py:77
  204.5 16.4 %all-to-all-start.1 = ((f32[16,1,384]{2,1,0:T(1,128)}), f32[16,1,384]{2,1,0:T(1,128)S(1)}, u32[]{:S(2)}, u32[]{:S(2)}) async-start(f32[16,1,384]{2,1,0:T(1,128)} %all_to_all.25), calls=%async_computation.1 | async-start | bytes 49152 | tf_op jit(solution)/shard_map/all_to_all | solution.py:70
  208.0 150.6 %all-reduce.2.cloned.1.call-start = ((), (), s32[]{:S(2)}) async-start(), calls=%async_computation.4 | async-start | bytes 6291456 | tf_op jit(solution)/shard_map/psum | solution.py:106
Sparse Core Ops, SparseCore 0:
  288.2 70.3 all-reduce.1
where the time goes:
time: 372 us; the launch traced here: 370 us
  waiting for transfers between devices  188 us (51%)
  other arithmetic  72.7 us (20%)
  matrix products  39.8 us (11%)
  blocking collectives  31 us (8%)
  starting transfers between devices  16.6 us (4%)
  between operations  13.6 us (4%)
  local copies, waits for them, and re-layouts  8.18 us (2%)
    all_to_all x1, waiting for transfers between devices, body(): lax.all_to_all(outgoing, 'cent', split_axis=0, concat_axis=0, tiled=True)  136 us
    psum x1, waiting for transfers between devices, body(): lax.psum(sums.astype(jnp.bfloat16), 'dp').astype(jnp.float32)  46.3 us
    reduce_sum x1, other arithmetic, fetch_pairs(): columns.append(jnp.sum(jnp.where(hit, values[None, :], 0.0), axis=1))  32.2 us
    dot_general x1, matrix products, body(): jnp.dot(dispatch, vectors, preferred_element_type=jnp.float32)  18.8 us
    psum x1, blocking collectives, body(): lax.psum(weight_sum.astype(jnp.bfloat16), 'dp').astype(jnp.float32)  18.1 us
    all_to_all x1, blocking collectives, body(): lax.all_to_all(norm_buf.reshape(groups, blk_here * most_rows), 'cent', sp...  12.8 us
    reduce_or x1, other arithmetic, body(): norm_buf = jnp.where(jnp.any(routed, axis=1), filled, 1e+30)  12.7 us
    dot_general x1, matrix products, body(): jnp.einsum('yhzc,yhzu->hcu', block_weight, received_rows, preferred_eleme...  11.6 us
  transfers between devices with their start and end apart: 4, of which 3 were waited for; matrix products, arithmetic and copies ran while one was open for 6% of the time, Pallas kernels for 0%

commit v1 on v0

v1 whole, which is shorter than its diff:
```python
import jax
import jax.numpy as jnp
import numpy as np
from jax import lax
from jax.experimental import pallas as pl
from jax.experimental.pallas import tpu as pltpu
from jax.sharding import Mesh, PartitionSpec as P

BS = 512
MOST = 96
TOK = 1024
D = 768
NSRC = 8
NBLK = 8
SLOTS = NSRC * MOST
LOW = -1e30
F32 = jnp.float32
BF16 = jnp.bfloat16
VMEM = 56 * 1024 * 1024

FROM_D = (4, 3, 0, 7, 6, 1, 2, 5)
FROM_E = (2, 5, 6, 1, 0, 7, 4, 3)
FROM_F = (6, 7, 4, 5, 2, 3, 0, 1)


def turn(a, axis, sign):
    axes = ("z", "core") if axis == "z" else ("core", axis)
    at = (lambda core, i: i * 2 + core) if axis == "z" else (lambda core, i: core * 4 + i)
    pairs = []
    for core in range(2):
        for i in range(4):
            pairs.append((at(core, i), at(core, (i + (sign if core == 0 else -sign)) % 4)))
    return lax.ppermute(a, axes, pairs)


def far(a, axis):
    return lax.ppermute(a, axis, [(i, (i + 2) % 4) for i in range(4)])


def swap(a):
    return lax.ppermute(a, "core", [(0, 1), (1, 0)])


def params(**kw):
    return pltpu.CompilerParams(vmem_limit_bytes=VMEM, **kw)


def cost(flops, nbytes, trans=0):
    return pl.CostEstimate(flops=int(flops), bytes_accessed=int(nbytes), transcendentals=int(trans))


def prep_kernel(cand_ref, blk_ref, rank_ref, idx_ref):
    up = lax.broadcasted_iota(jnp.int32, (TOK, TOK), 0) < lax.broadcasted_iota(jnp.int32, (TOK, TOK), 1)
    up = jnp.where(up, 1.0, 0.0).astype(BF16)
    blk = blk_ref[:, 0:1]
    hits = []
    for s in range(NSRC):
        c = cand_ref[s]
        m = c[0:1] == blk
        for pick in range(1, 4):
            m = m | (c[pick : pick + 1] == blk)
        hits.append(jnp.where(m, 1.0, 0.0))
    hits = jnp.concatenate(hits, axis=0)
    before = jnp.dot(hits.astype(BF16), up, preferred_element_type=F32)
    rank = jnp.where(hits > 0, before, -1.0)
    for s in range(NSRC):
        rank_ref[s] = rank[s * NBLK : (s + 1) * NBLK]
    row = lax.broadcasted_iota(jnp.int32, (8, TOK), 0)
    v = lax.broadcasted_iota(jnp.int32, (8, TOK), 1)
    place = jnp.where(row == 0, v >> 3, jnp.where(row == 1, v & 7, jnp.where(row == 2, 1, 0)))
    place = place.astype(F32).astype(BF16)
    lane = lax.broadcasted_iota(jnp.int32, (1, SLOTS), 1)
    base = jnp.zeros((1, SLOTS), F32)
    for s in range(1, NSRC):
        base = base + jnp.where(lane >= s * MOST, float(TOK), 0.0)
    slot = lax.broadcasted_iota(jnp.int32, (MOST, TOK), 0).astype(F32)
    for b in range(NBLK):
        hot = [
            jnp.where(slot == rank[s * NBLK + b : s * NBLK + b + 1], 1.0, 0.0).astype(BF16)
            for s in range(NSRC)
        ]
        hot = jnp.concatenate(hot, axis=0)
        found = lax.dot_general(place, hot, (((1,), (1,)), ((), ())), preferred_element_type=F32)
        where = found[0:1] * 8.0 + found[1:2] + base
        idx_ref[b : b + 1, :] = jnp.where(found[2:3] > 0, where, -1.0).astype(jnp.int32)


def prep(cand, blk):
    return pl.pallas_call(
        prep_kernel,
        out_shape=(
            jax.ShapeDtypeStruct((NSRC, NBLK, TOK), F32),
            jax.ShapeDtypeStruct((NBLK, SLOTS), jnp.int32),
        ),
        compiler_params=params(),
        cost_estimate=cost(8e9, 1e6),
        name="prep",
    )(cand, blk)


def dispatch_kernel(v_ref, rank_ref, *refs):
    out_ref = refs[-1]
    half = pl.program_id(0)
    slot = lax.broadcasted_iota(jnp.int32, (MOST, TOK), 0).astype(F32)
    hot = []
    for k in range(4):
        r = rank_ref[0, pl.ds(half * 4 + k, 1), :]
        hot.append(jnp.where(slot == r, 1.0, 0.0).astype(BF16))
    hot = jnp.concatenate(hot, axis=0)
    rows = jnp.dot(hot, v_ref[...], preferred_element_type=F32).astype(BF16)
    out_ref[...] = rows.reshape(4, 1, MOST, D)


def dispatch(s, v, rank, rows):
    in_specs = [
        pl.BlockSpec((TOK, D), lambda i: (0, 0)),
        pl.BlockSpec((1, NBLK, TOK), lambda i: (s, 0, 0)),
    ]
    args = [v, rank]
    alias = {}
    if rows is not None:
        in_specs.append(pl.BlockSpec(memory_space=pl.ANY))
        args.append(rows)
        alias = {2: 0}
    return pl.pallas_call(
        dispatch_kernel,
        grid=(2,),
        in_specs=in_specs,
        out_specs=pl.BlockSpec((4, 1, MOST, D), lambda i: (i, s, 0, 0)),
        out_shape=jax.ShapeDtypeStruct((NBLK, NSRC, MOST, D), BF16),
        input_output_aliases=alias,
        compiler_params=params(),
        cost_estimate=cost(2 * NBLK * MOST * TOK * D, 3e6),
        name=f"dispatch{s}",
    )(*args)


def score_kernel(rows_ref, c0, c1, c2, c3, rank_ref, e_ref, peak_ref, stat_ref, cbuf, tot_scr):
    b = pl.program_id(0)
    for q, c in enumerate((c0, c1, c2, c3)):
        @pl.when(b // 2 == q)
        def _(c=c):
            cbuf[...] = c[...]

    cent = cbuf[...]
    rows = rows_ref[...].reshape(SLOTS, D)
    raw = lax.dot_general(cent, rows, (((1,), (1,)), ((), ())), preferred_element_type=F32)
    wide = cent.astype(F32)
    score = raw - 0.5 * jnp.sum(wide * wide, axis=1, keepdims=True)
    peak = jnp.max(score, axis=0, keepdims=True)
    e = jnp.exp(score - peak)
    e_ref[0] = e.astype(BF16)
    peak_ref[pl.ds(b, 1), :] = peak
    tot_scr[pl.ds(b, 1), :] = jnp.sum(e, axis=0, keepdims=True)

    @pl.when(b == NBLK - 1)
    def _():
        for s in range(NSRC):
            k0, k1 = s * MOST // 128, (s * MOST + MOST - 1) // 128
            for j in range(TOK // 128):
                r = rank_ref[s, :, j * 128 : (j + 1) * 128].astype(jnp.int32)
                at = r + s * MOST
                low = at & 127
                near = (at >> 7) == k0

                def fetch(ref):
                    first = jnp.take_along_axis(ref[:, k0 * 128 : (k0 + 1) * 128], low, axis=1, mode="promise_in_bounds")
                    if k1 == k0:
                        return first
                    second = jnp.take_along_axis(ref[:, k1 * 128 : (k1 + 1) * 128], low, axis=1, mode="promise_in_bounds")
                    return jnp.where(near, first, second)

                here = r >= 0
                pv = jnp.where(here, fetch(peak_ref), LOW)
                tv = jnp.where(here, fetch(tot_scr), 0.0)
                m = jnp.max(pv, axis=0, keepdims=True)
                t = jnp.sum(tv * jnp.exp(pv - m), axis=0, keepdims=True)
                stat_ref[0, s : s + 1, j * 128 : (j + 1) * 128] = m
                stat_ref[1, s : s + 1, j * 128 : (j + 1) * 128] = t


def score(rows, cents, rank):
    def cspec(q):
        return pl.BlockSpec((BS, D), lambda b: (jnp.clip(b - 2 * q, 0, 1), 0))

    return pl.pallas_call(
        score_kernel,
        grid=(NBLK,),
        in_specs=[pl.BlockSpec((1, NSRC, MOST, D), lambda b: (b, 0, 0, 0))]
        + [cspec(q) for q in range(4)]
        + [pl.BlockSpec((NSRC, NBLK, TOK), lambda b: (0, 0, 0))],
        out_specs=(
            pl.BlockSpec((1, BS, SLOTS), lambda b: (b, 0, 0)),
            pl.BlockSpec((NBLK, SLOTS), lambda b: (0, 0)),
            pl.BlockSpec((2, NSRC, TOK), lambda b: (0, 0, 0)),
        ),
        out_shape=(
            jax.ShapeDtypeStruct((NBLK, BS, SLOTS), BF16),
            jax.ShapeDtypeStruct((NBLK, SLOTS), F32),
            jax.ShapeDtypeStruct((2, NSRC, TOK), F32),
        ),
        scratch_shapes=[pltpu.VMEM((BS, D), BF16), pltpu.VMEM((NBLK, SLOTS), F32)],
        compiler_params=params(),
        cost_estimate=cost(2 * NBLK * BS * SLOTS * D, 23e6, NBLK * BS * SLOTS),
        name="score",
    )(rows, *cents, rank)


def factor_kernel(stat_refs, idx_ref, peak_ref, f_scr):
    own, from_d, from_e, from_f = stat_refs
    tables = []
    for s in range(NSRC):
        ms = [own[0, s : s + 1, :]]
        ts = [own[1, s : s + 1, :]]
        for ref, order in ((from_d, FROM_D), (from_e, FROM_E), (from_f, FROM_F)):
            o = order[s]
            ms.append(ref[0, o : o + 1, :])
            ts.append(ref[1, o : o + 1, :])
        m = jnp.maximum(jnp.maximum(ms[0], ms[1]), jnp.maximum(ms[2], ms[3]))
        t = ts[0] * jnp.exp(ms[0] - m)
        for k in range(1, 4):
            t = t + ts[k] * jnp.exp(ms[k] - m)
        tables.append(m + jnp.log(t))
    for k in range(SLOTS // 128):
        at = idx_ref[:, k * 128 : (k + 1) * 128]
        low = at & 127
        high = at >> 7
        lse = jnp.zeros((NBLK, 128), F32)
        for s in range(k * 128 // MOST, (k * 128 + 127) // MOST + 1):
            for j in range(TOK // 128):
                table = jnp.broadcast_to(tables[s][:, j * 128 : (j + 1) * 128], (NBLK, 128))
                got = jnp.take_along_axis(table, low, axis=1, mode="promise_in_bounds")
                lse = jnp.where(high == s * (TOK // 128) + j, got, lse)
        f = jnp.exp(peak_ref[:, k * 128 : (k + 1) * 128] - lse)
        f_scr[:, k * 128 : (k + 1) * 128] = jnp.where(at >= 0, f, 0.0)


def sums_kernel(part, where_ref, s0, s1, s2, s3, idx_ref, peak_ref, e_ref, rows_ref, o0, o1, o2, o3, cnt_ref, f_scr, acc):
    q = pl.program_id(0)

    @pl.when(q == 0)
    def _():
        factor_kernel((s0, s1, s2, s3), idx_ref, peak_ref, f_scr)

    f = f_scr[pl.ds(2 * q + part, 1), :]
    w = e_ref[0].astype(F32) * f
    count = jnp.sum(w, axis=1, keepdims=True)
    count = jnp.transpose(jnp.broadcast_to(count, (BS, 128)))[0:1]
    cnt_ref[pl.ds(where_ref[q], 1), :] = count
    rows = rows_ref[...].reshape(SLOTS, D)
    total = jnp.dot(w.astype(BF16), rows, preferred_element_type=F32)
    outs = (o0, o1, o2, o3)
    if part == 0:
        for k in range(4):
            @pl.when(q == k)
            def _(k=k):
                outs[k][...] = total.astype(BF16)
    else:
        acc[...] = total
        for k in range(4):
            start = pl.multiple_of(where_ref[4 + k] * 128, 128)
            outs[k][pl.ds(q, 1)] = acc[pl.ds(start, 128), :].astype(BF16)[None]


def sums(part, where, stats, idx, peak, e, rows):
    full = lambda *shape: pl.BlockSpec(shape, lambda q: (0,) * len(shape))
    shape = (BS, D) if part == 0 else (4, 128, D)

    def kern(*refs):
        sums_kernel(part, *refs)

    return pl.pallas_call(
        kern,
        grid=(4,),
        in_specs=[pl.BlockSpec(memory_space=pltpu.SMEM)]
        + [full(2, NSRC, TOK)] * 4
        + [
            full(NBLK, SLOTS),
            full(NBLK, SLOTS),
            pl.BlockSpec((1, BS, SLOTS), lambda q: (2 * q + part, 0, 0)),
            pl.BlockSpec((1, NSRC, MOST, D), lambda q: (2 * q + part, 0, 0, 0)),
        ],
        out_specs=tuple([full(*shape)] * 4 + [full(4, BS)]),
        out_shape=tuple([jax.ShapeDtypeStruct(shape, BF16)] * 4 + [jax.ShapeDtypeStruct((4, BS), F32)]),
        scratch_shapes=[pltpu.VMEM((NBLK, SLOTS), F32), pltpu.VMEM((BS, D), F32)],
        compiler_params=params(),
        cost_estimate=cost(2 * 4 * BS * SLOTS * D, 12e6),
        name=f"sums{part}",
    )(where, *stats, idx, peak, e, rows)


def place_kernel(where_ref, *refs):
    parts, out_ref, sems = refs[:8], refs[8], refs[9]
    copies = []
    for side in range(2):
        for k in range(4):
            for i in range(2):
                block = where_ref[8 + side] * 2 + i
                quarter = where_ref[4 * (side + 1) - 4 + k]
                copies.append(
                    pltpu.make_async_copy(
                        parts[side * 4 + k].at[i], out_ref.at[block, quarter], sems.at[len(copies)]
                    )
                )
    for copy in copies:
        copy.start()
    for copy in copies:
        copy.wait()


def place(where, parts):
    return pl.pallas_call(
        place_kernel,
        in_specs=[pl.BlockSpec(memory_space=pltpu.SMEM)] + [pl.BlockSpec(memory_space=pl.ANY)] * 8,
        out_specs=pl.BlockSpec(memory_space=pl.ANY),
        out_shape=jax.ShapeDtypeStruct((4, 4, 128, D), BF16),
        scratch_shapes=[pltpu.SemaphoreType.DMA((16,))],
        cost_estimate=cost(0, 6e6),
        name="place",
    )(where, *parts)


def add(*terms):
    total = terms[0].astype(F32)
    for t in terms[1:]:
        total = total + t.astype(F32)
    return total


def ring_sum(own, d, e, f, axis):
    r1 = turn(f, axis, 1)
    r2 = turn(d, axis, -1)
    r3 = turn(add(e, r1).astype(BF16), axis, 1)
    return add(own, r2, r3)


def body(vectors, centroids, candidates):
    core, x, y, z = (lax.axis_index(a) for a in ("core", "x", "y", "z"))
    step = 1 - 2 * core

    def around(i):
        return jnp.stack([i, (i - step) % 4, (i + step) % 4, (i + 2) % 4]).astype(jnp.int32)

    xs, zs = around(x), around(z)
    other_zs = jnp.stack([zs[0], zs[2], zs[1], zs[3]])

    cand = candidates.T.astype(F32)
    pair = jnp.stack([cand, swap(cand)])
    cd, ce, cf = turn(pair, "y", 1), turn(pair, "y", -1), far(pair, "y")
    cands = jnp.stack([pair[0], pair[1], cd[0], ce[1], ce[0], cd[1], cf[0], cf[1]])

    c0 = lax.dynamic_slice_in_dim(centroids, core * 1024, 1024, 0)
    a, b = turn(vectors, "y", 1), turn(vectors, "y", -1)
    c1, c2 = turn(c0, "x", 1), turn(c0, "x", -1)
    c = turn(a, "y", 1)
    c3 = turn(c1, "x", 1)
    sources = [vectors, swap(vectors), a, swap(a), b, swap(b), c, swap(c)]

    blk = ((y * 4 + xs) * 4 + 2 * core)[:, None] + jnp.arange(2, dtype=jnp.int32)[None, :]
    blk = jnp.broadcast_to(blk.reshape(NBLK, 1), (NBLK, 128)).astype(F32)
    rank, idx = prep(cands, blk)
    rows = None
    for s, v in enumerate(sources):
        rows = dispatch(s, v, rank, rows)
    e, peak, stat = score(rows, (c0, c1, c2, c3), rank)

    theirs = swap(stat)
    theirs = jnp.flip(theirs.reshape(2, 4, 2, TOK), axis=2).reshape(2, NSRC, TOK)
    m = jnp.maximum(stat[0], theirs[0])
    t = stat[1] * jnp.exp(stat[0] - m) + theirs[1] * jnp.exp(theirs[0] - m)
    merged = jnp.stack([m, t])
    stats = (merged, turn(merged, "y", 1), turn(merged, "y", -1), far(merged, "y"))

    where = jnp.concatenate([xs, zs])
    *h, cnt0 = sums(0, where, stats, idx, peak, e, rows)
    *g, cnt1 = sums(1, where, stats, idx, peak, e, rows)
    counts = lax.psum(jnp.stack([cnt0, cnt1]), ("x", "z"))
    counts = lax.dynamic_index_in_dim(counts, x, 1, keepdims=False)
    counts = lax.dynamic_slice_in_dim(counts, z * 128, 128, 1)

    h = ring_sum(*h, "x").astype(BF16)
    h = ring_sum(*(lax.dynamic_slice_in_dim(h, zs[k] * 128, 128, 0) for k in range(4)), "z")
    g = ring_sum(*g, "z").astype(BF16)
    g = ring_sum(*(g[k] for k in range(4)), "x")
    mine = lax.dynamic_slice_in_dim(c0.reshape(2, BS, D), z * 128, 128, 1).astype(F32)
    fresh = ((jnp.stack([h, g]) + mine) / (counts + 1.0)[:, :, None]).astype(BF16)

    fa, fb = turn(fresh, "z", 1), turn(fresh, "z", -1)
    fc = turn(fa, "z", 1)
    parts = [fresh, fa, fb, fc] + [swap(p) for p in (fresh, fa, fb, fc)]
    places = jnp.concatenate([zs, other_zs, jnp.stack([core, 1 - core])]).astype(jnp.int32)
    return place(places, parts).reshape(2048, D)


def solution(mesh):
    fine = Mesh(np.asarray(mesh.devices).reshape(4, 2, 4, 4), ("z", "core", "y", "x"))
    return jax.shard_map(
        body,
        mesh=fine,
        in_specs=(P(("z", "core", "y", "x"), None), P(("y", "x"), None), P(("z", "core", "y", "x"), None)),
        out_specs=P(("y", "x"), None),
        check_vma=False,
    )
```

time: 372 us -> 397 us (1.067)
  Pallas kernels: 0 us -> 164 us
  waiting for transfers between devices: 188 us -> 77.2 us
  other arithmetic: 72.7 us -> 8.94 us
  starting transfers between devices: 16.6 us -> 77.7 us
  matrix products: 39.8 us -> 0 us
  blocking collectives: 31 us -> 59.5 us
  between operations: 13.6 us -> 0.44 us
    pallas_call x0 -> x13, Pallas kernels: none -> 164 us  [the longest x1 97.2 us: place(): pl.pallas_call(place_kernel, in_specs=[pl.BlockSpec(memory_space=pltpu.SM...]
    all_to_all x3 -> x0, waiting for transfers between devices: 142 us -> none  [the longest x1 136 us: body(): lax.all_to_all(outgoing, 'cent', split_axis=0, concat_axis=0, tiled=True)]
    ppermute x0 -> x37, starting transfers between devices: none -> 77.7 us  [the longest x10 37.9 us: swap(): return lax.ppermute(a, 'core', [(0, 1), (1, 0)])]
    ppermute x0 -> x37, waiting for transfers between devices: none -> 77.2 us  [the longest x25 71.5 us: turn(): return lax.ppermute(a, axes, pairs)]
    reduce_sum x7 -> x0, other arithmetic: 54.7 us -> none  [the longest x1 32.2 us: fetch_pairs(): columns.append(jnp.sum(jnp.where(hit, values[None, :], 0.0), axis=1))]
    psum x1 -> x0, waiting for transfers between devices: 46.3 us -> none  [body(): lax.psum(sums.astype(jnp.bfloat16), 'dp').astype(jnp.float32)]
    psum x1, blocking collectives: 18.1 us -> 59.5 us  [body(): counts = lax.psum(jnp.stack([cnt0, cnt1]), ('x', 'z'))]
    dot_general x5 -> x0, matrix products: 39.8 us -> none  [the longest x1 18.8 us: body(): jnp.dot(dispatch, vectors, preferred_element_type=jnp.float32)]
  transfers between devices with their start and end apart: 4 -> 37, of which waited for: 3 -> 13; matrix products, arithmetic and copies ran while one was open for 6% -> 3% of each run, Pallas kernels for 0% -> 11%
where the time goes in v1:
time: 397 us; the launch traced here: 396 us
  Pallas kernels  164 us (41%)
  starting transfers between devices  77.7 us (20%)
  waiting for transfers between devices  77.2 us (19%)
  blocking collectives  59.5 us (15%)
  other arithmetic  8.94 us (2%)
  local copies, waits for them, and re-layouts  8.24 us (2%)
    pallas_call x1, Pallas kernels, place(): pl.pallas_call(place_kernel, in_specs=[pl.BlockSpec(memory_space=pltpu.SM...  97.2 us
    ppermute x25, waiting for transfers between devices, turn(): return lax.ppermute(a, axes, pairs)  71.5 us
    psum x1, blocking collectives, body(): counts = lax.psum(jnp.stack([cnt0, cnt1]), ('x', 'z'))  59.5 us
    ppermute x10, starting transfers between devices, swap(): return lax.ppermute(a, 'core', [(0, 1), (1, 0)])  37.9 us
    ppermute x25, starting transfers between devices, turn(): return lax.ppermute(a, axes, pairs)  37.6 us
    pallas_call x8, Pallas kernels, dispatch(): pl.pallas_call(dispatch_kernel, grid=(2,), in_specs=in_specs, out_specs=p...  30.7 us
    pallas_call x2, Pallas kernels, sums(): pl.pallas_call(kern, grid=(4,), in_specs=[pl.BlockSpec(memory_space=pltpu...  15.4 us
    pallas_call x1, Pallas kernels, score(): pl.pallas_call(score_kernel, grid=(NBLK,), in_specs=[pl.BlockSpec((1, NSR...  15.3 us
  transfers between devices with their start and end apart: 37, of which 13 were waited for; matrix products, arithmetic and copies ran while one was open for 3% of the time, Pallas kernels for 11%

profile of v1, /device:TPU:1, one launch (start us, length us, event | category | flops | bytes accessed | tf_op | source)
XLA Modules:
  0.0 396.0 jit_solution(16373101508230838105)
XLA Ops:
  0.0 3.6 collective-permute-start
  9.3 27.3 %collective-permute-done.v_ref = bf16[1024,768]{1,0:T(8,128)(2,1)} collective-permute-done((bf16[1024,768]{1,0:T(8,128)(2,1)}, bf16[1024,768]{1,0:T(8,128)(2,1)}, u32[]{:S(2)}, u32[]{:S(2)}) %collective-permute-start) | collective-permute-done | bytes 1572896 | tf_op jit(solution)/shard_map/ppermute | solution.py:33
  36.6 3.4 collective-permute-start.1
  40.4 17.6 %collective-permute-done.4 = f32[2,4,1024]{2,1,0:T(4,128)S(1)} collective-permute-done((f32[2,4,1024]{2,1,0:T(4,128)S(1)}, f32[2,4,1024]{2,1,0:T(4,128)S(1)}, u32[]{:S(2)}, u32[]{:S(2)}) %collective-permute-start.4) | collective-permute-done | bytes 32800 | tf_op jit(solution)/shard_map/ppermute | solution.py:33
  57.9 4.4 %collective-permute-done.5 = f32[2,4,1024]{2,1,0:T(4,128)S(1)} collective-permute-done((f32[2,4,1024]{2,1,0:T(4,128)S(1)}, f32[2,4,1024]{2,1,0:T(4,128)S(1)}, u32[]{:S(2)}, u32[]{:S(2)}) %collective-permute-start.5) | collective-permute-done | bytes 32800 | tf_op jit(solution)/shard_map/ppermute | solution.py:33
  63.3 3.4 collective-permute-done.6
  66.6 3.6 collective-permute-start.9
  74.3 5.2 %prep.1 = (f32[8,8,1024]{2,1,0:T(8,128)}, s32[8,768]{1,0:T(8,128)}) custom-call(f32[8,4,1024]{2,1,0:T(4,128)} %copy-done.15, f32[8,128]{1,0:T(8,128)} %broadcast_in_dim.2.blk_ref), custom_call_target="tpu_custom_call" | custom-call | flops 8000000000 | bytes 1000000 | tf_op jit(solution)/shard_map/prep/pallas_call | solution.py:89
  79.5 3.8 dispatch0.1.refs_0_
  83.3 3.8 dispatch1.1.refs_0_
  87.2 3.9 dispatch2.1.refs_0_
  92.2 3.8 dispatch3.1.refs_0_
  96.0 3.8 dispatch4.1.refs_0_
  101.0 3.9 dispatch5.1.refs_0_
  104.9 3.8 dispatch6.1.refs_0_
  109.8 3.8 dispatch7.1.rows_ref.refs_8_
  113.7 15.3 %score.1 = (bf16[8,512,768]{2,1,0:T(8,128)(2,1)}, f32[8,768]{1,0:T(8,128)}, f32[2,8,1024]{2,1,0:T(8,128)}) custom-call(bf16[8,8,96,768]{3,2,1,0:T(8,128)(2,1)} %dispatch7.1.rows_ref.refs_8_, bf16[1024,768]{1,0:T(8,128)(2,1)} %constant_dynamic-slice_fusion.3.c0, bf16[1024,768]{1,0:T(8,128)(2,1)} %collective-permute-done.11.c1, ...), custom_call_target="tpu_custom_call" | custom-call | flops 4831838208 | bytes 23000000 | tf_op jit(solution)/shard_map/score/pallas_call | solution.py:186
  132.0 3.0 collective-permute-start.15
  137.0 3.9 collective-permute-done.16.refs_3_
  141.6 7.7 %sums0.1 = (bf16[512,768]{1,0:T(8,128)(2,1)}, bf16[512,768]{1,0:T(8,128)(2,1)}, bf16[512,768]{1,0:T(8,128)(2,1)}, bf16[512,768]{1,0:T(8,128)(2,1)}, f32[4,512]{1,0:T(4,128)}) custom-call(s32[8]{0:T(128)} %concatenate.13.refs_0_, f32[2,8,1024]{2,1,0:T(8,128)} %copy-done.8, f32[2,8,1024]{2,1,0:T(8,128)} %copy-done.9, f32[2,8,1024]{2,1,0:T(8,128)} %copy-done.10, ...), custom_call_target="tpu_custom_call" | custom-call | flops 2415919104 | bytes 12000000 | tf_op jit(solution)/shard_map/sums0/pallas_call | solution.py:272
  151.3 7.7 %sums1.1 = (bf16[4,128,768]{2,1,0:T(8,128)(2,1)}, bf16[4,128,768]{2,1,0:T(8,128)(2,1)}, bf16[4,128,768]{2,1,0:T(8,128)(2,1)}, bf16[4,128,768]{2,1,0:T(8,128)(2,1)}, f32[4,512]{1,0:T(4,128)}) custom-call(s32[8]{0:T(128)} %concatenate.13.refs_0_, f32[2,8,1024]{2,1,0:T(8,128)} %copy-done.8, f32[2,8,1024]{2,1,0:T(8,128)} %copy-done.9, f32[2,8,1024]{2,1,0:T(8,128)} %copy-done.10, ...), custom_call_target="tpu_custom_call" | custom-call | flops 2415919104 | bytes 12000000 | tf_op jit(solution)/shard_map/sums1/pallas_call | solution.py:272
  159.0 3.8 collective-permute-start.25
  163.9 2.7 collective-permute-start.20
  166.6 8.0 %collective-permute-done.25 = bf16[4,128,768]{2,1,0:T(8,128)(2,1)S(1)} collective-permute-done((bf16[4,128,768]{2,1,0:T(8,128)(2,1)}, bf16[4,128,768]{2,1,0:T(8,128)(2,1)S(1)}, u32[]{:S(2)}, u32[]{:S(2)}) %collective-permute-start.25) | collective-permute-done | bytes 786464 | tf_op jit(solution)/shard_map/ppermute | solution.py:33
  175.6 3.4 collective-permute-start.26
  179.1 59.5 %psum.7 = f32[2,4,512]{2,1,0:T(4,128)S(1)} all-reduce(f32[2,4,512]{2,1,0:T(4,128)S(1)} %pad_maximum_fusion.2), channel_id=1, replica_groups=mesh['z'=4,'core'=2,'y'=4,'x'=4] {'x','z'}, use_global_device_ids=true, to_apply=%region_0.1 | all-reduce | flops 4096 | bytes 32768 | tf_op jit(solution)/shard_map/psum | solution.py:377
  250.4 2.8 collective-permute-done.29
  255.9 5.3 %collective-permute-done.30.refs_1_ = bf16[2,128,768]{2,1,0:T(8,128)(2,1)} collective-permute-done((bf16[2,128,768]{2,1,0:T(8,128)(2,1)S(1)}, bf16[2,128,768]{2,1,0:T(8,128)(2,1)}, u32[]{:S(2)}, u32[]{:S(2)}) %collective-permute-start.30) | collective-permute-done | bytes 393248 | tf_op jit(solution)/shard_map/ppermute | solution.py:33
  261.2 2.5 collective-permute-start.32
  263.7 23.9 %collective-permute-start.33 = (bf16[2,128,768]{2,1,0:T(8,128)(2,1)S(1)}, bf16[2,128,768]{2,1,0:T(8,128)(2,1)}, u32[]{:S(2)}, u32[]{:S(2)}) collective-permute-start(bf16[2,128,768]{2,1,0:T(8,128)(2,1)S(1)} %fusion.1.refs_0_), channel_id=1, source_target_pairs={{0,16},{16,0},{1,17},{17,1},{2,18},{18,2},{3,19},{19,3},{4,20},{20... | collective-permute-start | bytes 1179656 | tf_op jit(solution)/shard_map/ppermute | solution.py:41
  288.1 8.8 %collective-permute-start.36 = (bf16[2,128,768]{2,1,0:T(8,128)(2,1)}, bf16[2,128,768]{2,1,0:T(8,128)(2,1)}, u32[]{:S(2)}, u32[]{:S(2)}) collective-permute-start(bf16[2,128,768]{2,1,0:T(8,128)(2,1)} %collective-permute-done.32.refs_3_), channel_id=1, source_target_pairs={{0,16},{16,0},{1,17},{17,1},{2,18},{18,2},{3,19},{19,3},{4,20},{20... | collective-permute-start | bytes 1179656 | tf_op jit(solution)/shard_map/ppermute | solution.py:41
  298.6 97.2 %place.1 = bf16[4,4,128,768]{3,2,1,0:T(8,128)(2,1)} custom-call(s32[10]{0:T(128)} %concatenate.12.where_ref, bf16[2,128,768]{2,1,0:T(8,128)(2,1)} %copy-done.4, bf16[2,128,768]{2,1,0:T(8,128)(2,1)} %collective-permute-done.30.refs_1_, bf16[2,128,768]{2,1,0:T(8,128)(2,1)} %collective-permute-done.31.refs_2_, ...), custom_call_target="tpu_custom_call" | custom-call | bytes 6000000 | tf_op jit(solution)/shard_map/place/pallas_call | solution.py:312
  (126 shorter events, 40.9 us)
Async XLA Ops:
  0.0 36.6 %collective-permute-start = (bf16[1024,768]{1,0:T(8,128)(2,1)}, bf16[1024,768]{1,0:T(8,128)(2,1)}, u32[]{:S(2)}, u32[]{:S(2)}) collective-permute-start(bf16[1024,768]{1,0:T(8,128)(2,1)} %v_ref.1), channel_id=1, source_target_pairs={{0,4},{4,8},{8,12},{12,0},{16,28},{20,16},{24,20},{28,24},{1,5},{5... | collective-permute-start | bytes 4718600 | tf_op jit(solution)/shard_map/ppermute | solution.py:33
  3.6 67.2 %collective-permute-start.10 = (bf16[1024,768]{1,0:T(8,128)(2,1)}, bf16[1024,768]{1,0:T(8,128)(2,1)}, u32[]{:S(2)}, u32[]{:S(2)}) collective-permute-start(bf16[1024,768]{1,0:T(8,128)(2,1)} %v_ref.1), channel_id=1, source_target_pairs={{0,16},{16,0},{1,17},{17,1},{2,18},{18,2},{3,19},{19,3},{4,20},{20... | collective-permute-start | bytes 4718600 | tf_op jit(solution)/shard_map/ppermute | solution.py:41
  3.6 66.7 %collective-permute-start.7 = (bf16[1024,768]{1,0:T(8,128)(2,1)}, bf16[1024,768]{1,0:T(8,128)(2,1)}, u32[]{:S(2)}, u32[]{:S(2)}) collective-permute-start(bf16[1024,768]{1,0:T(8,128)(2,1)} %v_ref.1), channel_id=1, source_target_pairs={{0,12},{4,0},{8,4},{12,8},{16,20},{20,24},{24,28},{28,16},{1,13},{... | collective-permute-start | bytes 4718600 | tf_op jit(solution)/shard_map/ppermute | solution.py:33
  5.1 35.1 %collective-permute-start.3 = (f32[4,1024]{1,0:T(4,128)S(1)}, f32[4,1024]{1,0:T(4,128)S(1)}, u32[]{:S(2)}, u32[]{:S(2)}) collective-permute-start(f32[4,1024]{1,0:T(4,128)S(1)} %get-tuple-element.44), channel_id=1, source_target_pairs={{0,16},{16,0},{1,17},{17,1},{2,18},{18,2},{3,19},{19,3},{4,20},{20... | collective-permute-start | bytes 49160 | tf_op jit(solution)/shard_map/ppermute | solution.py:41
  6.8 65.2 %collective-permute-start.11 = (bf16[1024,768]{1,0:T(8,128)(2,1)}, bf16[1024,768]{1,0:T(8,128)(2,1)}, u32[]{:S(2)}, u32[]{:S(2)}) collective-permute-start(bf16[1024,768]{1,0:T(8,128)(2,1)} %constant_dynamic-slice_fusion.3.c0), channel_id=1, source_target_pairs={{0,1},{1,2},{2,3},{3,0},{16,19},{17,16},{18,17},{19,18},{4,5},{5,6... | collective-permute-start | bytes 4718600 | tf_op jit(solution)/shard_map/ppermute | solution.py:33
  36.6 33.7 %collective-permute-start.1 = (bf16[1024,768]{1,0:T(8,128)(2,1)}, bf16[1024,768]{1,0:T(8,128)(2,1)}, u32[]{:S(2)}, u32[]{:S(2)}) collective-permute-start(bf16[1024,768]{1,0:T(8,128)(2,1)} %collective-permute-done.v_ref), channel_id=1, source_target_pairs={{0,4},{4,8},{8,12},{12,0},{16,28},{20,16},{24,20},{28,24},{1,5},{5... | collective-permute-start | bytes 4718600 | tf_op jit(solution)/shard_map/ppermute | solution.py:33
  40.3 17.7 %collective-permute-start.4 = (f32[2,4,1024]{2,1,0:T(4,128)S(1)}, f32[2,4,1024]{2,1,0:T(4,128)S(1)}, u32[]{:S(2)}, u32[]{:S(2)}) collective-permute-start(f32[2,4,1024]{2,1,0:T(4,128)S(1)} %pad_maximum_fusion.1), channel_id=1, source_target_pairs={{0,4},{4,8},{8,12},{12,0},{16,28},{20,16},{24,20},{28,24},{1,5},{5... | collective-permute-start | bytes 98312 | tf_op jit(solution)/shard_map/ppermute | solution.py:33
  66.6 24.4 %collective-permute-start.9 = (bf16[1024,768]{1,0:T(8,128)(2,1)}, bf16[1024,768]{1,0:T(8,128)(2,1)S(1)}, u32[]{:S(2)}, u32[]{:S(2)}) collective-permute-start(bf16[1024,768]{1,0:T(8,128)(2,1)} %collective-permute-done.v_ref), channel_id=1, source_target_pairs={{0,16},{16,0},{1,17},{17,1},{2,18},{18,2},{3,19},{19,3},{4,20},{20... | collective-permute-start | bytes 4718600 | tf_op jit(solution)/shard_map/ppermute | solution.py:41
  70.2 29.6 %collective-permute-start.8 = (bf16[1024,768]{1,0:T(8,128)(2,1)}, bf16[1024,768]{1,0:T(8,128)(2,1)S(1)}, u32[]{:S(2)}, u32[]{:S(2)}) collective-permute-start(bf16[1024,768]{1,0:T(8,128)(2,1)} %collective-permute-done.7.v_ref), channel_id=1, source_target_pairs={{0,16},{16,0},{1,17},{17,1},{2,18},{18,2},{3,19},{19,3},{4,20},{20... | collective-permute-start | bytes 4718600 | tf_op jit(solution)/shard_map/ppermute | solution.py:41
  70.3 38.4 %collective-permute-start.2 = (bf16[1024,768]{1,0:T(8,128)(2,1)}, bf16[1024,768]{1,0:T(8,128)(2,1)S(1)}, u32[]{:S(2)}, u32[]{:S(2)}) collective-permute-start(bf16[1024,768]{1,0:T(8,128)(2,1)} %collective-permute-done.1.v_ref), channel_id=1, source_target_pairs={{0,16},{16,0},{1,17},{17,1},{2,18},{18,2},{3,19},{19,3},{4,20},{20... | collective-permute-start | bytes 4718600 | tf_op jit(solution)/shard_map/ppermute | solution.py:41
  70.8 42.9 %collective-permute-start.12 = (bf16[1024,768]{1,0:T(8,128)(2,1)}, bf16[1024,768]{1,0:T(8,128)(2,1)}, u32[]{:S(2)}, u32[]{:S(2)}) collective-permute-start(bf16[1024,768]{1,0:T(8,128)(2,1)} %constant_dynamic-slice_fusion.3.c0), channel_id=1, source_target_pairs={{0,3},{1,0},{2,1},{3,2},{16,17},{17,18},{18,19},{19,16},{4,7},{5,4... | collective-permute-start | bytes 4718600 | tf_op jit(solution)/shard_map/ppermute | solution.py:33
  72.1 41.6 %collective-permute-start.13 = (bf16[1024,768]{1,0:T(8,128)(2,1)}, bf16[1024,768]{1,0:T(8,128)(2,1)}, u32[]{:S(2)}, u32[]{:S(2)}) collective-permute-start(bf16[1024,768]{1,0:T(8,128)(2,1)} %collective-permute-done.11.c1), channel_id=1, source_target_pairs={{0,1},{1,2},{2,3},{3,0},{16,19},{17,16},{18,17},{19,18},{4,5},{5,6... | collective-permute-start | bytes 4718600 | tf_op jit(solution)/shard_map/ppermute | solution.py:33
  132.0 5.0 %collective-permute-start.15 = (f32[2,8,1024]{2,1,0:T(8,128)S(1)}, f32[2,8,1024]{2,1,0:T(8,128)S(1)}, u32[]{:S(2)}, u32[]{:S(2)}) collective-permute-start(f32[2,8,1024]{2,1,0:T(8,128)S(1)} %pad_maximum_fusion.refs_1_), channel_id=1, source_target_pairs={{0,4},{4,8},{8,12},{12,0},{16,28},{20,16},{24,20},{28,24},{1,5},{5... | collective-permute-start | bytes 196616 | tf_op jit(solution)/shard_map/ppermute | solution.py:33
  135.1 5.9 %collective-permute-start.16 = (f32[2,8,1024]{2,1,0:T(8,128)S(1)}, f32[2,8,1024]{2,1,0:T(8,128)S(1)}, u32[]{:S(2)}, u32[]{:S(2)}) collective-permute-start(f32[2,8,1024]{2,1,0:T(8,128)S(1)} %pad_maximum_fusion.refs_1_), channel_id=1, source_target_pairs={{0,12},{4,0},{8,4},{12,8},{16,20},{20,24},{24,28},{28,16},{1,13},{... | collective-permute-start | bytes 196616 | tf_op jit(solution)/shard_map/ppermute | solution.py:33
  135.1 5.9 %collective-permute-start.17 = (f32[2,8,1024]{2,1,0:T(8,128)S(1)}, f32[2,8,1024]{2,1,0:T(8,128)S(1)}, u32[]{:S(2)}, u32[]{:S(2)}) collective-permute-start(f32[2,8,1024]{2,1,0:T(8,128)S(1)} %pad_maximum_fusion.refs_1_), channel_id=1, source_target_pairs={{0,8},{4,12},{8,0},{12,4},{1,9},{5,13},{9,1},{13,5},{2,10},{6,14},... | collective-permute-start | bytes 196616 | tf_op jit(solution)/shard_map/ppermute | solution.py:37
  149.3 13.5 %collective-permute-start.19 = (bf16[512,768]{1,0:T(8,128)(2,1)}, bf16[512,768]{1,0:T(8,128)(2,1)S(1)}, u32[]{:S(2)}, u32[]{:S(2)}) collective-permute-start(bf16[512,768]{1,0:T(8,128)(2,1)} %get-tuple-element.28), channel_id=1, source_target_pairs={{0,1},{1,2},{2,3},{3,0},{16,19},{17,16},{18,17},{19,18},{4,5},{5,6... | collective-permute-start | bytes 2359304 | tf_op jit(solution)/shard_map/ppermute | solution.py:33
  159.0 15.6 %collective-permute-start.25 = (bf16[4,128,768]{2,1,0:T(8,128)(2,1)}, bf16[4,128,768]{2,1,0:T(8,128)(2,1)S(1)}, u32[]{:S(2)}, u32[]{:S(2)}) collective-permute-start(bf16[4,128,768]{2,1,0:T(8,128)(2,1)} %get-tuple-element.32), channel_id=1, source_target_pairs={{0,32},{32,64},{64,96},{96,0},{16,112},{48,16},{80,48},{112,80},{1... | collective-permute-start | bytes 2359304 | tf_op jit(solution)/shard_map/ppermute | solution.py:33
  162.8 75.9 %collective-permute-start.18 = (bf16[512,768]{1,0:T(8,128)(2,1)}, bf16[512,768]{1,0:T(8,128)(2,1)}, u32[]{:S(2)}, u32[]{:S(2)}) collective-permute-start(bf16[512,768]{1,0:T(8,128)(2,1)} %get-tuple-element.26), channel_id=1, source_target_pairs={{0,3},{1,0},{2,1},{3,2},{16,17},{17,18},{18,19},{19,16},{4,7},{5,4... | collective-permute-start | bytes 2359304 | tf_op jit(solution)/shard_map/ppermute | solution.py:33
  163.9 74.8 %collective-permute-start.20 = (bf16[512,768]{1,0:T(8,128)(2,1)}, bf16[512,768]{1,0:T(8,128)(2,1)}, u32[]{:S(2)}, u32[]{:S(2)}) collective-permute-start(bf16[512,768]{1,0:T(8,128)(2,1)} %add_convert_fusion.3), channel_id=1, source_target_pairs={{0,1},{1,2},{2,3},{3,0},{16,19},{17,16},{18,17},{19,18},{4,5},{5,6... | collective-permute-start | bytes 2359304 | tf_op jit(solution)/shard_map/ppermute | solution.py:33
  166.6 75.7 %collective-permute-start.24 = (bf16[4,128,768]{2,1,0:T(8,128)(2,1)}, bf16[4,128,768]{2,1,0:T(8,128)(2,1)}, u32[]{:S(2)}, u32[]{:S(2)}) collective-permute-start(bf16[4,128,768]{2,1,0:T(8,128)(2,1)} %get-tuple-element.30), channel_id=1, source_target_pairs={{0,96},{32,0},{64,32},{96,64},{16,48},{48,80},{80,112},{112,16},{1... | collective-permute-start | bytes 2359304 | tf_op jit(solution)/shard_map/ppermute | solution.py:33
  175.6 66.6 %collective-permute-start.26 = (bf16[4,128,768]{2,1,0:T(8,128)(2,1)}, bf16[4,128,768]{2,1,0:T(8,128)(2,1)}, u32[]{:S(2)}, u32[]{:S(2)}) collective-permute-start(bf16[4,128,768]{2,1,0:T(8,128)(2,1)} %add_convert_fusion.1), channel_id=1, source_target_pairs={{0,32},{32,64},{64,96},{96,0},{16,112},{48,16},{80,48},{112,80},{1... | collective-permute-start | bytes 2359304 | tf_op jit(solution)/shard_map/ppermute | solution.py:33
  240.7 5.0 %collective-permute-start.22 = (bf16[128,768]{1,0:T(8,128)(2,1)S(1)}, bf16[128,768]{1,0:T(8,128)(2,1)S(1)}, u32[]{:S(2)}, u32[]{:S(2)}) collective-permute-start(bf16[128,768]{1,0:T(8,128)(2,1)S(1)} %get-tuple-element.36), channel_id=1, source_target_pairs={{0,32},{32,64},{64,96},{96,0},{16,112},{48,16},{80,48},{112,80},{1... | collective-permute-start | bytes 589832 | tf_op jit(solution)/shard_map/ppermute | solution.py:33
  240.8 9.1 %collective-permute-start.21 = (bf16[128,768]{1,0:T(8,128)(2,1)S(1)}, bf16[128,768]{1,0:T(8,128)(2,1)S(1)}, u32[]{:S(2)}, u32[]{:S(2)}) collective-permute-start(bf16[128,768]{1,0:T(8,128)(2,1)S(1)} %get-tuple-element.35), channel_id=1, source_target_pairs={{0,96},{32,0},{64,32},{96,64},{16,48},{48,80},{80,112},{112,16},{1... | collective-permute-start | bytes 589832 | tf_op jit(solution)/shard_map/ppermute | solution.py:33
  244.0 6.4 %collective-permute-start.27 = (bf16[128,768]{1,0:T(8,128)(2,1)S(1)}, bf16[128,768]{1,0:T(8,128)(2,1)S(1)}, u32[]{:S(2)}, u32[]{:S(2)}) collective-permute-start(bf16[128,768]{1,0:T(8,128)(2,1)S(1)} %get-tuple-element.37), channel_id=1, source_target_pairs={{0,3},{1,0},{2,1},{3,2},{16,17},{17,18},{18,19},{19,16},{4,7},{5,4... | collective-permute-start | bytes 589832 | tf_op jit(solution)/shard_map/ppermute | solution.py:33
  245.7 4.6 %collective-permute-start.23 = (bf16[128,768]{1,0:T(8,128)(2,1)S(1)}, bf16[128,768]{1,0:T(8,128)(2,1)S(1)}, u32[]{:S(2)}, u32[]{:S(2)}) collective-permute-start(bf16[128,768]{1,0:T(8,128)(2,1)S(1)} %add_convert_fusion.4), channel_id=1, source_target_pairs={{0,32},{32,64},{64,96},{96,0},{16,112},{48,16},{80,48},{112,80},{1... | collective-permute-start | bytes 589832 | tf_op jit(solution)/shard_map/ppermute | solution.py:33
  254.4 6.8 %collective-permute-start.30 = (bf16[2,128,768]{2,1,0:T(8,128)(2,1)S(1)}, bf16[2,128,768]{2,1,0:T(8,128)(2,1)}, u32[]{:S(2)}, u32[]{:S(2)}) collective-permute-start(bf16[2,128,768]{2,1,0:T(8,128)(2,1)S(1)} %fusion.1.refs_0_), channel_id=1, source_target_pairs={{0,32},{32,64},{64,96},{96,0},{16,112},{48,16},{80,48},{112,80},{1... | collective-permute-start | bytes 1179656 | tf_op jit(solution)/shard_map/ppermute | solution.py:33
  255.8 31.8 %collective-permute-start.31 = (bf16[2,128,768]{2,1,0:T(8,128)(2,1)S(1)}, bf16[2,128,768]{2,1,0:T(8,128)(2,1)}, u32[]{:S(2)}, u32[]{:S(2)}) collective-permute-start(bf16[2,128,768]{2,1,0:T(8,128)(2,1)S(1)} %fusion.1.refs_0_), channel_id=1, source_target_pairs={{0,96},{32,0},{64,32},{96,64},{16,48},{48,80},{80,112},{112,16},{1... | collective-permute-start | bytes 1179656 | tf_op jit(solution)/shard_map/ppermute | solution.py:33
  261.2 26.9 %collective-permute-start.32 = (bf16[2,128,768]{2,1,0:T(8,128)(2,1)}, bf16[2,128,768]{2,1,0:T(8,128)(2,1)}, u32[]{:S(2)}, u32[]{:S(2)}) collective-permute-start(bf16[2,128,768]{2,1,0:T(8,128)(2,1)} %collective-permute-done.30.refs_1_), channel_id=1, source_target_pairs={{0,32},{32,64},{64,96},{96,0},{16,112},{48,16},{80,48},{112,80},{1... | collective-permute-start | bytes 1179656 | tf_op jit(solution)/shard_map/ppermute | solution.py:33
  263.7 33.8 %collective-permute-start.33 = (bf16[2,128,768]{2,1,0:T(8,128)(2,1)S(1)}, bf16[2,128,768]{2,1,0:T(8,128)(2,1)}, u32[]{:S(2)}, u32[]{:S(2)}) collective-permute-start(bf16[2,128,768]{2,1,0:T(8,128)(2,1)S(1)} %fusion.1.refs_0_), channel_id=1, source_target_pairs={{0,16},{16,0},{1,17},{17,1},{2,18},{18,2},{3,19},{19,3},{4,20},{20... | collective-permute-start | bytes 1179656 | tf_op jit(solution)/shard_map/ppermute | solution.py:41
  287.6 9.9 %collective-permute-start.34 = (bf16[2,128,768]{2,1,0:T(8,128)(2,1)}, bf16[2,128,768]{2,1,0:T(8,128)(2,1)}, u32[]{:S(2)}, u32[]{:S(2)}) collective-permute-start(bf16[2,128,768]{2,1,0:T(8,128)(2,1)} %collective-permute-done.30.refs_1_), channel_id=1, source_target_pairs={{0,16},{16,0},{1,17},{17,1},{2,18},{18,2},{3,19},{19,3},{4,20},{20... | collective-permute-start | bytes 1179656 | tf_op jit(solution)/shard_map/ppermute | solution.py:41
  287.6 9.9 %collective-permute-start.35 = (bf16[2,128,768]{2,1,0:T(8,128)(2,1)}, bf16[2,128,768]{2,1,0:T(8,128)(2,1)}, u32[]{:S(2)}, u32[]{:S(2)}) collective-permute-start(bf16[2,128,768]{2,1,0:T(8,128)(2,1)} %collective-permute-done.31.refs_2_), channel_id=1, source_target_pairs={{0,16},{16,0},{1,17},{17,1},{2,18},{18,2},{3,19},{19,3},{4,20},{20... | collective-permute-start | bytes 1179656 | tf_op jit(solution)/shard_map/ppermute | solution.py:41
  288.1 10.5 %collective-permute-start.36 = (bf16[2,128,768]{2,1,0:T(8,128)(2,1)}, bf16[2,128,768]{2,1,0:T(8,128)(2,1)}, u32[]{:S(2)}, u32[]{:S(2)}) collective-permute-start(bf16[2,128,768]{2,1,0:T(8,128)(2,1)} %collective-permute-done.32.refs_3_), channel_id=1, source_target_pairs={{0,16},{16,0},{1,17},{17,1},{2,18},{18,2},{3,19},{19,3},{4,20},{20... | collective-permute-start | bytes 1179656 | tf_op jit(solution)/shard_map/ppermute | solution.py:41
  (21 other events, 156.9 us)

commit v2 on v1

v2 whole, which is shorter than its diff:
```python
import jax
import jax.numpy as jnp
import numpy as np
from jax import lax
from jax.experimental import pallas as pl
from jax.experimental.pallas import tpu as pltpu
from jax.sharding import Mesh, PartitionSpec as P

BS = 512
MOST = 96
TOK = 1024
D = 768
NSRC = 8
NBLK = 8
SLOTS = NSRC * MOST
EXTRA = 16
EXT = TOK + EXTRA
LOW = -1e30
F32 = jnp.float32
BF16 = jnp.bfloat16
VMEM = 56 * 1024 * 1024

NAMES = ("v", "v'", "a", "b", "a'", "b'", "c", "c'")


def order(**came):
    return tuple(NAMES.index(came[n.replace("'", "_")]) for n in NAMES)


SWAPPED = order(v="v'", v_="v", a="a'", a_="a", b="b'", b_="b", c="c'", c_="c")
FROM_D = order(a="v", b_="v'", c="a", v_="a'", v="b", c_="b'", b="c", a_="c'")
FROM_E = order(b="v", a_="v'", v="a", c_="a'", c="b", v_="b'", a="c", b_="c'")
FROM_F = order(c="v", c_="v'", b="a", b_="a'", a="b", a_="b'", v="c", v_="c'")


def turn(a, axis, sign):
    axes = ("z", "core") if axis == "z" else ("core", axis)
    at = (lambda core, i: i * 2 + core) if axis == "z" else (lambda core, i: core * 4 + i)
    pairs = []
    for core in range(2):
        for i in range(4):
            pairs.append((at(core, i), at(core, (i + (sign if core == 0 else -sign)) % 4)))
    return lax.ppermute(a, axes, pairs)


def far(a, axis):
    return lax.ppermute(a, axis, [(i, (i + 2) % 4) for i in range(4)])


def swap(a):
    return lax.ppermute(a, "core", [(0, 1), (1, 0)])


def params(**kw):
    return pltpu.CompilerParams(vmem_limit_bytes=VMEM, **kw)


def cost(flops, nbytes, trans=0):
    return pl.CostEstimate(flops=int(flops), bytes_accessed=int(nbytes), transcendentals=int(trans))


def earlier():
    up = lax.broadcasted_iota(jnp.int32, (TOK, TOK), 0) < lax.broadcasted_iota(jnp.int32, (TOK, TOK), 1)
    return jnp.where(up, 1.0, 0.0).astype(BF16)


def ranks(tail, blk, up):
    tail = tail.astype(F32)
    hit = None
    for pick in range(4):
        named = jnp.concatenate([tail[2 * pick : 2 * pick + 1, 0:512], tail[2 * pick + 1 : 2 * pick + 2, 0:512]], axis=1)
        m = named == blk
        hit = m if hit is None else hit | m
    hit = jnp.where(hit, 1.0, 0.0)
    hits = jnp.concatenate([hit, jnp.zeros((8, TOK), F32)], axis=0).astype(BF16)
    before = jnp.dot(hits, up, preferred_element_type=F32)[0:NBLK]
    return jnp.where(hit > 0, before, -1.0)


def gathered(rank, vectors):
    slot = lax.broadcasted_iota(jnp.int32, (MOST, TOK), 0).astype(F32)
    hot = [jnp.where(slot == rank[b : b + 1, :], 1.0, 0.0).astype(BF16) for b in range(NBLK)]
    hot = jnp.concatenate(hot, axis=0)
    rows = jnp.dot(hot, vectors, preferred_element_type=F32).astype(BF16)
    return rows.reshape(NBLK, MOST, D)


def index_kernel(*refs):
    rank_refs, idx_ref = refs[:-1], refs[-1]
    sources = [(ref, k) for ref in rank_refs for k in range(ref.shape[0])]
    row = lax.broadcasted_iota(jnp.int32, (8, TOK), 0)
    v = lax.broadcasted_iota(jnp.int32, (8, TOK), 1)
    place = jnp.where(row == 0, v >> 3, jnp.where(row == 1, v & 7, jnp.where(row == 2, 1, 0)))
    place = place.astype(F32).astype(BF16)
    lane = lax.broadcasted_iota(jnp.int32, (1, SLOTS), 1)
    base = jnp.zeros((1, SLOTS), F32)
    for s in range(1, NSRC):
        base = base + jnp.where(lane >= s * MOST, float(TOK), 0.0)
    slot = lax.broadcasted_iota(jnp.int32, (MOST, TOK), 0).astype(F32)
    for b in range(NBLK):
        hot = [jnp.where(slot == ref[k, b : b + 1, :], 1.0, 0.0).astype(BF16) for ref, k in sources]
        hot = jnp.concatenate(hot, axis=0)
        found = lax.dot_general(place, hot, (((1,), (1,)), ((), ())), preferred_element_type=F32)
        where = found[0:1] * 8.0 + found[1:2] + base
        idx_ref[b : b + 1, :] = jnp.where(found[2:3] > 0, where, -1.0).astype(jnp.int32)


def indices(*rank):
    return pl.pallas_call(
        index_kernel,
        out_shape=jax.ShapeDtypeStruct((NBLK, SLOTS), jnp.int32),
        compiler_params=params(),
        cost_estimate=cost(4e9, 1e6),
        name="indices",
    )(*rank)


def dispatch_kernel(n, *refs):
    sources, blk_ref, (rank_ref, out_ref, buf, sems, up) = refs[:n], refs[n], refs[-5:]
    i = pl.program_id(0)

    def copy(k):
        return pltpu.make_async_copy(sources[k], buf.at[k % 2], sems.at[k % 2])

    @pl.when(i == 0)
    def _():
        copy(0).start()
        up[...] = earlier()

    for k in range(n):
        @pl.when(i == k)
        def _(k=k):
            if k + 1 < n:
                copy(k + 1).start()
            copy(k).wait()

    rank = ranks(buf[i % 2, TOK:EXT, :], blk_ref[:, 0:1], up[...])
    rank_ref[0] = rank
    out_ref[...] = gathered(rank, buf[i % 2, 0:TOK, :])


def dispatch(first, sources, blk, rows):
    n = len(sources)
    anywhere = pl.BlockSpec(memory_space=pltpu.HBM)
    in_specs = [anywhere] * n + [pl.BlockSpec((NBLK, 128), lambda i: (0, 0))]
    args = [*sources, blk]
    alias = {}
    if rows is not None:
        in_specs.append(anywhere)
        args.append(rows)
        alias = {n + 1: 1}

    def kern(*refs):
        dispatch_kernel(n, *refs)

    return pl.pallas_call(
        kern,
        grid=(n,),
        in_specs=in_specs,
        out_specs=(
            pl.BlockSpec((1, NBLK, TOK), lambda i: (i, 0, 0)),
            pl.BlockSpec((NBLK, MOST, D), lambda i: (0, first + i, 0)),
        ),
        out_shape=(
            jax.ShapeDtypeStruct((n, NBLK, TOK), F32),
            jax.ShapeDtypeStruct((NBLK, SLOTS, D), BF16),
        ),
        scratch_shapes=[
            pltpu.VMEM((2, EXT, D), BF16),
            pltpu.SemaphoreType.DMA((2,)),
            pltpu.VMEM((TOK, TOK), BF16),
        ],
        input_output_aliases=alias,
        compiler_params=params(),
        cost_estimate=cost(2 * n * NBLK * MOST * TOK * D, n * 3e6),
        name=f"dispatch{first}",
    )(*args)


def score_block(b, rows, cent_refs, cbuf):
    for q, c in enumerate(cent_refs):
        @pl.when(b // 2 == q)
        def _(c=c):
            cbuf[...] = c[...]

    cent = cbuf[...]
    raw = lax.dot_general(cent, rows, (((1,), (1,)), ((), ())), preferred_element_type=F32)
    wide = cent.astype(F32)
    score = raw - 0.5 * jnp.sum(wide * wide, axis=1, keepdims=True)
    peak = jnp.max(score, axis=0, keepdims=True)
    e = jnp.exp(score - peak)
    return e, peak, jnp.sum(e, axis=0, keepdims=True)


def early_kernel(rows_ref, c0, c1, c2, *refs):
    e_ref, peak_ref, lse_ref, cbuf = refs[-4:]
    b = pl.program_id(0)
    e, peak, total = score_block(b, rows_ref[0], (c0, c1, c2), cbuf)
    e_ref[0] = e.astype(BF16)
    peak_ref[pl.ds(b, 1), :] = peak
    lse_ref[pl.ds(b, 1), :] = peak + jnp.log(total)


def cent_spec(q, block):
    return pl.BlockSpec((BS, D), lambda i: (jnp.clip(block(i) - 2 * q, 0, 1), 0))


def early_scores(rows, cents, part, width, e):
    in_specs = [pl.BlockSpec((1, width, D), lambda b: (b, part, 0))] + [cent_spec(q, lambda i: i) for q in range(3)]
    args = [rows, *cents]
    alias = {}
    if e is not None:
        in_specs.append(pl.BlockSpec(memory_space=pltpu.HBM))
        args.append(e)
        alias = {4: 0}
    return pl.pallas_call(
        early_kernel,
        grid=(6,),
        in_specs=in_specs,
        out_specs=(
            pl.BlockSpec((1, BS, width), lambda b: (b, 0, part)),
            pl.BlockSpec((NBLK, width), lambda b: (0, 0)),
            pl.BlockSpec((NBLK, width), lambda b: (0, 0)),
        ),
        out_shape=(
            jax.ShapeDtypeStruct((NBLK, BS, SLOTS), BF16),
            jax.ShapeDtypeStruct((NBLK, width), F32),
            jax.ShapeDtypeStruct((NBLK, width), F32),
        ),
        scratch_shapes=[pltpu.VMEM((BS, D), BF16)],
        input_output_aliases=alias,
        compiler_params=params(),
        cost_estimate=cost(2 * 6 * BS * width * D, 12e6, 6 * BS * width),
        name=f"early_scores{part}",
    )(*args)


def late_block(i):
    return jnp.where(i < 6, i, 6 + (i - 6) // 3)


def late_chunk(i):
    return jnp.where(i < 6, 2, (i - 6) % 3)


def late_kernel(
    source_ref, blk_ref, rows_ref, c0, c1, c2, c3, rank0, rank1, rank2, rank3, peak0, lse0, _,
    e_ref, out_ref, rank_ref, peak_ref, stat_ref, cbuf, lse_scr, buf, sem,
):
    i = pl.program_id(0)
    b, chunk = late_block(i), late_chunk(i)
    lanes = pl.ds(pl.multiple_of(chunk * 256, 256), 256)

    @pl.when(i == 0)
    def _():
        copy = pltpu.make_async_copy(source_ref, buf, sem)
        copy.start()
        peak_ref[:, 0:512] = peak0[...]
        lse_scr[:, 0:512] = lse0[...]
        up = earlier()
        copy.wait()
        rank = ranks(buf[TOK:EXT, :], blk_ref[:, 0:1], up)
        rank_ref[0] = rank
        out_ref[...] = gathered(rank, buf[0:TOK, :])

    head = rows_ref[0, 0:160, :]
    last = jnp.where(chunk == 2, out_ref[pl.ds(b, 1)][0], rows_ref[0, 160:256, :])
    e, peak, total = score_block(b, jnp.concatenate([head, last], axis=0), (c0, c1, c2, c3), cbuf)
    e_ref[0] = e.astype(BF16)
    peak_ref[pl.ds(b, 1), lanes] = peak
    lse_scr[pl.ds(b, 1), lanes] = peak + jnp.log(total)

    @pl.when(i == 11)
    def _():
        sources = [(ref, k) for ref in (rank0, rank1, rank2, rank3, rank_ref) for k in range(ref.shape[0])]
        for s, (ref, k) in enumerate(sources):
            k0, k1 = s * MOST // 128, (s * MOST + MOST - 1) // 128
            for j in range(TOK // 128):
                r = ref[k, :, j * 128 : (j + 1) * 128].astype(jnp.int32)
                at = r + s * MOST
                low = at & 127
                got = jnp.take_along_axis(lse_scr[:, k0 * 128 : (k0 + 1) * 128], low, axis=1, mode="promise_in_bounds")
                if k1 > k0:
                    other = jnp.take_along_axis(
                        lse_scr[:, k1 * 128 : (k1 + 1) * 128], low, axis=1, mode="promise_in_bounds"
                    )
                    got = jnp.where((at >> 7) == k0, got, other)
                got = jnp.where(r >= 0, got, LOW)
                m = jnp.max(got, axis=0, keepdims=True)
                t = jnp.sum(jnp.exp(got - m), axis=0, keepdims=True)
                stat_ref[s : s + 1, j * 128 : (j + 1) * 128] = m + jnp.log(t)


def late_scores(source, blk, rows, cents, ranked, before, e):
    full = lambda *shape: pl.BlockSpec(shape, lambda i: (0,) * len(shape))
    hbm = pl.BlockSpec(memory_space=pltpu.HBM)
    return pl.pallas_call(
        late_kernel,
        grid=(12,),
        in_specs=[hbm, full(NBLK, 128), pl.BlockSpec((1, 256, D), lambda i: (late_block(i), late_chunk(i), 0))]
        + [cent_spec(q, late_block) for q in range(4)]
        + [full(*r.shape) for r in ranked]
        + [full(*p.shape) for p in before]
        + [hbm],
        out_specs=(
            pl.BlockSpec((1, BS, 256), lambda i: (late_block(i), 0, late_chunk(i))),
            pl.BlockSpec((NBLK, MOST, D), lambda i: (0, NSRC - 1, 0)),
            full(1, NBLK, TOK),
            full(NBLK, SLOTS),
            full(NSRC, TOK),
        ),
        out_shape=(
            jax.ShapeDtypeStruct((NBLK, BS, SLOTS), BF16),
            jax.ShapeDtypeStruct((NBLK, SLOTS, D), BF16),
            jax.ShapeDtypeStruct((1, NBLK, TOK), F32),
            jax.ShapeDtypeStruct((NBLK, SLOTS), F32),
            jax.ShapeDtypeStruct((NSRC, TOK), F32),
        ),
        scratch_shapes=[
            pltpu.VMEM((BS, D), BF16),
            pltpu.VMEM((NBLK, SLOTS), F32),
            pltpu.VMEM((EXT, D), BF16),
            pltpu.SemaphoreType.DMA,
        ],
        input_output_aliases={13: 0, 2: 1},
        compiler_params=params(),
        cost_estimate=cost(2 * 4 * BS * SLOTS * D, 20e6, 4 * BS * SLOTS),
        name="late_scores",
    )(source, blk, rows, *cents, *ranked, *before, e)


def factor_kernel(stat_refs, idx_ref, peak_ref, f_scr):
    own, from_d, from_e, from_f = stat_refs
    tables = []
    for s in range(NSRC):
        parts = [own[s : s + 1, :]]
        for ref, order in ((from_d, FROM_D), (from_e, FROM_E), (from_f, FROM_F)):
            parts.append(ref[order[s] : order[s] + 1, :])
        m = jnp.maximum(jnp.maximum(parts[0], parts[1]), jnp.maximum(parts[2], parts[3]))
        t = jnp.exp(parts[0] - m)
        for k in range(1, 4):
            t = t + jnp.exp(parts[k] - m)
        tables.append(m + jnp.log(t))
    for k in range(SLOTS // 128):
        at = idx_ref[:, k * 128 : (k + 1) * 128]
        low = at & 127
        high = at >> 7
        lse = jnp.zeros((NBLK, 128), F32)
        for s in range(k * 128 // MOST, (k * 128 + 127) // MOST + 1):
            for j in range(TOK // 128):
                table = jnp.broadcast_to(tables[s][:, j * 128 : (j + 1) * 128], (NBLK, 128))
                got = jnp.take_along_axis(table, low, axis=1, mode="promise_in_bounds")
                lse = jnp.where(high == s * (TOK // 128) + j, got, lse)
        f = jnp.exp(peak_ref[:, k * 128 : (k + 1) * 128] - lse)
        f_scr[:, k * 128 : (k + 1) * 128] = jnp.where(at >= 0, f, 0.0)


def sums_owner(i):
    t = i % 4
    return jnp.where(t == 0, 3, jnp.where(t == 3, 0, t))


def sums_kernel(where_ref, s0, s1, s2, s3, idx_ref, peak_ref, e_ref, rows_ref, *refs):
    outs, (f_scr, acc, hbuf, gbuf, hsem, gsem) = refs[:8], refs[8:]
    i = pl.program_id(0)
    q, slot = sums_owner(i), i % 2

    def send_h(k):
        return pltpu.make_async_copy(hbuf.at[slot], outs[k], hsem.at[slot])

    def send_g(k):
        return pltpu.make_async_copy(gbuf.at[slot, k], outs[4 + k].at[q], gsem.at[slot, k])

    @pl.when(i == 0)
    def _():
        factor_kernel((s0, s1, s2, s3), idx_ref, peak_ref, f_scr)

    f = f_scr[pl.ds(2 * q + i // 4, 1), :]
    w = e_ref[0].astype(F32) * f
    count = jnp.sum(w, axis=1, keepdims=True)
    count = jnp.transpose(jnp.broadcast_to(count, (BS, 128)))[0:EXTRA]
    count = jnp.concatenate([count, jnp.zeros((EXTRA, D - BS), F32)], axis=1).astype(BF16)
    acc[...] = jnp.dot(w.astype(BF16), rows_ref[0], preferred_element_type=F32)

    @pl.when((i == 2) | (i == 3) | (i == 6) | (i == 7))
    def _():
        @pl.when(i < 4)
        def _():
            send_h(0).wait()

        @pl.when(i >= 4)
        def _():
            for k in range(4):
                send_g(k).wait()

    @pl.when(i < 4)
    def _():
        hbuf[slot, 0:BS, :] = acc[...].astype(BF16)
        hbuf[slot, BS : BS + EXTRA, :] = count
        for k in range(4):
            @pl.when(q == k)
            def _(k=k):
                send_h(k).start()

    @pl.when(i >= 4)
    def _():
        for k in range(4):
            start = pl.multiple_of(where_ref[4 + k] * 128, 128)
            gbuf[slot, k, 0:128, :] = acc[pl.ds(start, 128), :].astype(BF16)
            gbuf[slot, k, 128 : 128 + EXTRA, :] = count
            send_g(k).start()

    @pl.when(i == 7)
    def _():
        for other in range(2):
            pltpu.make_async_copy(hbuf.at[other], outs[0], hsem.at[other]).wait()
            for k in range(4):
                pltpu.make_async_copy(gbuf.at[other, k], outs[4 + k].at[0], gsem.at[other, k]).wait()


def sums(where, stats, idx, peak, e, rows):
    full = lambda *shape: pl.BlockSpec(shape, lambda i: (0,) * len(shape))
    h, g = (BS + EXTRA, D), (4, 128 + EXTRA, D)
    out = pl.pallas_call(
        sums_kernel,
        grid=(8,),
        in_specs=[pl.BlockSpec(memory_space=pltpu.SMEM)]
        + [full(NSRC, TOK)] * 4
        + [
            full(NBLK, SLOTS),
            full(NBLK, SLOTS),
            pl.BlockSpec((1, BS, SLOTS), lambda i: (2 * sums_owner(i) + i // 4, 0, 0)),
            pl.BlockSpec((1, SLOTS, D), lambda i: (2 * sums_owner(i) + i // 4, 0, 0)),
        ],
        out_specs=tuple([pl.BlockSpec(memory_space=pltpu.HBM)] * 8),
        out_shape=tuple([jax.ShapeDtypeStruct(h, BF16)] * 4 + [jax.ShapeDtypeStruct(g, BF16)] * 4),
        scratch_shapes=[
            pltpu.VMEM((NBLK, SLOTS), F32),
            pltpu.VMEM((BS, D), F32),
            pltpu.VMEM((2, *h), BF16),
            pltpu.VMEM((2, *g), BF16),
            pltpu.SemaphoreType.DMA((2,)),
            pltpu.SemaphoreType.DMA((2, 4)),
        ],
        compiler_params=params(),
        cost_estimate=cost(2 * 8 * BS * SLOTS * D, 24e6),
        name="sums",
    )(where, *stats, idx, peak, e, rows)
    return out[:4], out[4:]


def parted_kernel(where_ref, h0, h1, h2, g0, g1, g2, *refs):
    outs, acc = refs[:8], refs[8]
    acc[...] = h0[...].astype(F32) + h1[...].astype(F32) + h2[...].astype(F32)
    for k in range(4):
        start = pl.multiple_of(where_ref[4 + k] * 128, 128)
        outs[k][0:128, :] = acc[pl.ds(start, 128), :].astype(BF16)
        outs[k][128:, :] = acc[BS:, :].astype(BF16)
        total = g0[k].astype(F32) + g1[k].astype(F32) + g2[k].astype(F32)
        outs[4 + k][...] = total.astype(BF16)


def parted(where, h, g):
    vmem = pl.BlockSpec(memory_space=pltpu.VMEM)
    out = pl.pallas_call(
        parted_kernel,
        in_specs=[pl.BlockSpec(memory_space=pltpu.SMEM)] + [vmem] * 6,
        out_specs=(vmem,) * 8,
        out_shape=(jax.ShapeDtypeStruct((128 + EXTRA, D), BF16),) * 8,
        scratch_shapes=[pltpu.VMEM((BS + EXTRA, D), F32)],
        compiler_params=params(),
        cost_estimate=cost(1e6, 8e6),
        name="parted",
    )(where, *h, *g)
    return out[:4], out[4:]


def final_kernel(where_ref, h0, h1, h2, h3, g0, g1, g2, g3, mine_ref, out_ref):
    for i, refs in enumerate(((h0, h1, h2, h3), (g0, g1, g2, g3))):
        total = (refs[0][...].astype(F32) + refs[1][...].astype(F32)) + (refs[2][...].astype(F32) + refs[3][...].astype(F32))
        counts = total[128:136, 0:BS]
        picked = jnp.zeros((8, 128), F32)
        for k in range(4):
            picked = jnp.where(where_ref[4] == k, counts[:, k * 128 : (k + 1) * 128], picked)
        column = jnp.transpose(jnp.broadcast_to(picked[0:1], (128, 128)))[:, 0:1]
        fresh = (total[0:128] + mine_ref[i].astype(F32)) / (column + 1.0)
        out_ref[i] = fresh.astype(BF16)


def final(where, h, g, mine):
    return pl.pallas_call(
        final_kernel,
        in_specs=[pl.BlockSpec(memory_space=pltpu.SMEM)] + [pl.BlockSpec(memory_space=pltpu.VMEM)] * 9,
        out_specs=pl.BlockSpec(memory_space=pltpu.VMEM),
        out_shape=jax.ShapeDtypeStruct((2, 128, D), BF16),
        compiler_params=params(),
        cost_estimate=cost(1e6, 2e6),
        name="final",
    )(where, *h, *g, mine)


def place_kernel(where_ref, *refs):
    parts, out_ref = refs[:8], refs[8]
    for side in range(2):
        for k in range(4):
            for i in range(2):
                block = where_ref[8 + side] * 2 + i
                quarter = where_ref[4 * side + k]
                out_ref[pl.ds(block, 1), pl.ds(quarter, 1)] = parts[side * 4 + k][i][None, None]


def place(where, parts):
    return pl.pallas_call(
        place_kernel,
        in_specs=[pl.BlockSpec(memory_space=pltpu.SMEM)] + [pl.BlockSpec(memory_space=pltpu.VMEM)] * 8,
        out_specs=pl.BlockSpec(memory_space=pltpu.VMEM),
        out_shape=jax.ShapeDtypeStruct((4, 4, 128, D), BF16),
        compiler_params=params(),
        cost_estimate=cost(0, 6e6),
        name="place",
    )(where, *parts)


def tie(a, *after):
    return pl.pallas_call(
        lambda *refs: None,
        in_specs=[pl.BlockSpec(memory_space=pltpu.HBM)] * (1 + len(after)),
        out_specs=pl.BlockSpec(memory_space=pltpu.HBM),
        out_shape=jax.ShapeDtypeStruct(a.shape, a.dtype),
        input_output_aliases={0: 0},
        cost_estimate=cost(0, 0),
        name="tie",
    )(a, *after)


def add(*terms):
    total = terms[0].astype(F32)
    for t in terms[1:]:
        total = total + t.astype(F32)
    return total


def ring_terms(own, d, e, f, axis):
    r1 = turn(f, axis, 1)
    r2 = turn(d, axis, -1)
    r3 = turn(add(e, r1).astype(BF16), axis, 1)
    return own, r2, r3


def direct_terms(own, d, e, f, axis):
    return own, turn(d, axis, -1), turn(e, axis, 1), far(f, axis)


def body(vectors, centroids, candidates):
    core, x, y, z = (lax.axis_index(a) for a in ("core", "x", "y", "z"))
    step = 1 - 2 * core

    def around(i):
        return jnp.stack([i, (i - step) % 4, (i + step) % 4, (i + 2) % 4]).astype(jnp.int32)

    xs, zs = around(x), around(z)
    other_zs = jnp.stack([zs[0], zs[2], zs[1], zs[3]])

    where = jnp.concatenate([xs, zs])
    tail = jnp.pad(candidates.T.reshape(8, 512).astype(BF16), ((0, EXTRA - 8), (0, D - 512)))
    v = jnp.concatenate([vectors, tail])
    a, b = turn(v, "y", 1), turn(v, "y", -1)
    c0 = lax.dynamic_slice_in_dim(centroids, core * 1024, 1024, 0)
    c1, c2 = turn(c0, "x", 1), turn(c0, "x", -1)
    mine = lax.dynamic_slice_in_dim(c0.reshape(2, BS, D), z * 128, 128, 1)
    blk = ((y * 4 + xs) * 4 + 2 * core)[:, None] + jnp.arange(2, dtype=jnp.int32)[None, :]
    blk = jnp.broadcast_to(blk.reshape(NBLK, 1), (NBLK, 128)).astype(F32)

    rank0, rows = dispatch(0, (v, swap(v)), blk, None)
    a = tie(a, rows, b, c1, c2)
    c = turn(a, "y", 1)
    c3 = turn(c1, "x", 1)
    rank1, rows = dispatch(2, (a, b), blk, rows)
    rank2, rows = dispatch(4, (swap(a), swap(b)), blk, rows)
    e, peak0, lse0 = early_scores(rows, (c0, c1, c2), 0, 512, None)
    c = tie(c, e, c3)
    rank3, rows = dispatch(6, (c,), blk, rows)
    ranked = (rank0, rank1, rank2, rank3)
    e, rows, rank4, peak, stat = late_scores(swap(c), blk, rows, (c0, c1, c2, c3), ranked, (peak0, lse0), e)
    idx = indices(*ranked, rank4)

    theirs = swap(stat)
    theirs = jnp.concatenate([theirs[s : s + 1] for s in SWAPPED])
    m = jnp.maximum(stat, theirs)
    merged = m + jnp.log(jnp.exp(stat - m) + jnp.exp(theirs - m))
    stats = (merged, turn(merged, "y", 1), turn(merged, "y", -1), far(merged, "y"))

    h, g = sums(where, stats, idx, peak, e, rows)
    h, g = ring_terms(*h, "x"), ring_terms(*g, "z")
    h, g = parted(where, h, g)
    h, g = direct_terms(*h, "z"), direct_terms(*g, "x")
    fresh = final(where, h, g, mine)

    others = [turn(fresh, "z", 1), turn(fresh, "z", -1), far(fresh, "z")]
    parts = [fresh, *others] + [swap(p) for p in (fresh, *others)]
    places = jnp.concatenate([zs, other_zs, jnp.stack([core, 1 - core])]).astype(jnp.int32)
    return place(places, parts).reshape(2048, D)


def solution(mesh):
    fine = Mesh(np.asarray(mesh.devices).reshape(4, 2, 4, 4), ("z", "core", "y", "x"))
    return jax.shard_map(
        body,
        mesh=fine,
        in_specs=(P(("z", "core", "y", "x"), None), P(("y", "x"), None), P(("z", "core", "y", "x"), None)),
        out_specs=P(("y", "x"), None),
        check_vma=False,
    )
```

time: 397 us -> 214 us (0.54)
  Pallas kernels: 164 us -> 81 us
  blocking collectives: 59.5 us -> 0 us
  waiting for transfers between devices: 77.2 us -> 53.6 us
  starting transfers between devices: 77.7 us -> 60.1 us
    pallas_call x1, Pallas kernels: 97.2 us -> 3.71 us  [place(): pl.pallas_call(place_kernel, in_specs=[pl.BlockSpec(memory_space=pltpu.SM...]
    psum x1 -> x0, blocking collectives: 59.5 us -> none  [body(): counts = lax.psum(jnp.stack([cnt0, cnt1]), ('x', 'z'))]
    ppermute x25 -> x20, waiting for transfers between devices: 71.5 us -> 50.3 us  [turn(): return lax.ppermute(a, axes, pairs)]
    ppermute x10 -> x9, starting transfers between devices: 37.9 us -> 22.8 us  [swap(): return lax.ppermute(a, 'core', [(0, 1), (1, 0)])]
    pallas_call x12, Pallas kernels: 66.6 us -> 77.3 us  [the longest x4 24.8 us: dispatch(): pl.pallas_call(kern, grid=(n,), in_specs=in_specs, out_specs=(pl.BlockSpe...]
    ppermute x25 -> x20, starting transfers between devices: 37.6 us -> 30.9 us  [turn(): return lax.ppermute(a, axes, pairs)]
    convert_element_type x7 -> x3, other arithmetic: 7.02 us -> 2.5 us  [the longest x2 1.63 us: ring_terms(): r3 = turn(add(e, r1).astype(BF16), axis, 1)]
    ppermute x2 -> x4, starting transfers between devices: 2.17 us -> 6.41 us  [far(): return lax.ppermute(a, axis, [(i, (i + 2) % 4) for i in range(4)])]
  transfers between devices with their start and end apart: 37 -> 33, of which waited for: 13 -> 10; matrix products, arithmetic and copies ran while one was open for 3% -> 3% of each run, Pallas kernels for 11% -> 19%
where the time goes in v2:
time: 214 us; the launch traced here: 211 us
  Pallas kernels  81 us (38%)
  starting transfers between devices  60.1 us (28%)
  waiting for transfers between devices  53.6 us (25%)
  local copies, waits for them, and re-layouts  9.83 us (5%)
  other arithmetic  6.17 us (3%)
    ppermute x20, waiting for transfers between devices, turn(): return lax.ppermute(a, axes, pairs)  50.3 us
    ppermute x20, starting transfers between devices, turn(): return lax.ppermute(a, axes, pairs)  30.9 us
    pallas_call x4, Pallas kernels, dispatch(): pl.pallas_call(kern, grid=(n,), in_specs=in_specs, out_specs=(pl.BlockSpe...  24.8 us
    ppermute x9, starting transfers between devices, swap(): return lax.ppermute(a, 'core', [(0, 1), (1, 0)])  22.8 us
    pallas_call x1, Pallas kernels, late_scores(): pl.pallas_call(late_kernel, grid=(12,), in_specs=[hbm, full(NBLK, 128), p...  17.9 us
    pallas_call x1, Pallas kernels, sums(): pl.pallas_call(sums_kernel, grid=(8,), in_specs=[pl.BlockSpec(memory_spac...  13 us
    pallas_call x1, Pallas kernels, early_scores(): pl.pallas_call(early_kernel, grid=(6,), in_specs=in_specs, out_specs=(pl....  9.58 us
    ppermute x4, starting transfers between devices, far(): return lax.ppermute(a, axis, [(i, (i + 2) % 4) for i in range(4)])  6.41 us
  transfers between devices with their start and end apart: 33, of which 10 were waited for; matrix products, arithmetic and copies ran while one was open for 3% of the time, Pallas kernels for 19%

profile of v2, /device:TPU:1, one launch (start us, length us, event | category | flops | bytes accessed | tf_op | source)
XLA Modules:
  0.0 211.0 jit_solution(3218209882079692585)
XLA Ops:
  0.9 2.7 %fusion.1.refs_0_ = bf16[1040,768]{1,0:T(8,128)(2,1)} fusion(bf16[8,512]{1,0:T(8,128)(2,1)S(1)} %convert_element_type.36, bf16[1024,768]{1,0:T(8,128)(2,1)} %param.3), kind=kLoop, calls=%fused_computation.4 | loop fusion | flops 4792320 | bytes 3178496 | tf_op jit(solution)/shard_map/concatenate | solution.py:566
  5.0 2.8 %collective-permute-start = (bf16[1040,768]{1,0:T(8,128)(2,1)}, bf16[1040,768]{1,0:T(8,128)(2,1)}, u32[]{:S(2)}, u32[]{:S(2)}) collective-permute-start(bf16[1040,768]{1,0:T(8,128)(2,1)} %fusion.1.refs_0_), channel_id=1, source_target_pairs={{0,4},{4,8},{8,12},{12,0},{16,28},{20,16},{24,20},{28,24},{1,5},{5... | collective-permute-start | bytes 4792328 | tf_op jit(solution)/shard_map/ppermute | solution.py:43
  9.1 2.5 %collective-permute-start.3 = (bf16[1024,768]{1,0:T(8,128)(2,1)}, bf16[1024,768]{1,0:T(8,128)(2,1)}, u32[]{:S(2)}, u32[]{:S(2)}) collective-permute-start(bf16[1024,768]{1,0:T(8,128)(2,1)} %constant_dynamic-slice_fusion.1.c0), channel_id=1, source_target_pairs={{0,1},{1,2},{2,3},{3,0},{16,19},{17,16},{18,17},{19,18},{4,5},{5,6... | collective-permute-start | bytes 4718600 | tf_op jit(solution)/shard_map/ppermute | solution.py:43
  12.5 6.7 %dispatch0.1 = (f32[2,8,1024]{2,1,0:T(8,128)}, bf16[8,768,768]{2,1,0:T(8,128)(2,1)}) custom-call(bf16[1040,768]{1,0:T(8,128)(2,1)} %fusion.1.refs_0_, bf16[1040,768]{1,0:T(8,128)(2,1)} %collective-permute-done.1.refs_1_, f32[8,128]{1,0:T(8,128)} %broadcast_in_dim.2.refs_2_.refs_1_.blk_ref), custom_call_target="tpu_custom_call" | custom-call | flops 2415919104 | bytes 6000000 | tf_op jit(solution)/shard_map/dispatch0/pallas_call | solution.py:156
  19.2 25.5 %collective-permute-done.3.refs_3_.c1 = bf16[1024,768]{1,0:T(8,128)(2,1)} collective-permute-done((bf16[1024,768]{1,0:T(8,128)(2,1)}, bf16[1024,768]{1,0:T(8,128)(2,1)}, u32[]{:S(2)}, u32[]{:S(2)}) %collective-permute-start.3) | collective-permute-done | bytes 1572896 | tf_op jit(solution)/shard_map/ppermute | solution.py:43
  44.7 3.0 %collective-permute-done.4.refs_4_.c2 = bf16[1024,768]{1,0:T(8,128)(2,1)} collective-permute-done((bf16[1024,768]{1,0:T(8,128)(2,1)}, bf16[1024,768]{1,0:T(8,128)(2,1)}, u32[]{:S(2)}, u32[]{:S(2)}) %collective-permute-start.4) | collective-permute-done | bytes 1572896 | tf_op jit(solution)/shard_map/ppermute | solution.py:43
  49.8 2.9 %collective-permute-start.8 = (bf16[1024,768]{1,0:T(8,128)(2,1)}, bf16[1024,768]{1,0:T(8,128)(2,1)}, u32[]{:S(2)}, u32[]{:S(2)}) collective-permute-start(bf16[1024,768]{1,0:T(8,128)(2,1)} %collective-permute-done.3.refs_3_.c1), channel_id=1, source_target_pairs={{0,1},{1,2},{2,3},{3,0},{16,19},{17,16},{18,17},{19,18},{4,5},{5,6... | collective-permute-start | bytes 4718600 | tf_op jit(solution)/shard_map/ppermute | solution.py:43
  52.8 6.7 %dispatch2.1 = (f32[2,8,1024]{2,1,0:T(8,128)}, bf16[8,768,768]{2,1,0:T(8,128)(2,1)}) custom-call(bf16[1040,768]{1,0:T(8,128)(2,1)} %tie.2.refs_0_, bf16[1040,768]{1,0:T(8,128)(2,1)} %collective-permute-done.2.refs_2_.refs_1_, f32[8,128]{1,0:T(8,128)} %broadcast_in_dim.2.refs_2_.refs_1_.blk_ref, ...), custom_call_target="tpu_custom_call", output_to_operand_aliasing={{1}: (3, {})} | custom-call | flops 2415919104 | bytes 6000000 | tf_op jit(solution)/shard_map/dispatch2/pallas_call | solution.py:156
  61.2 6.7 %dispatch4.1 = (f32[2,8,1024]{2,1,0:T(8,128)}, bf16[8,768,768]{2,1,0:T(8,128)(2,1)}) custom-call(bf16[1040,768]{1,0:T(8,128)(2,1)} %copy-done.1, bf16[1040,768]{1,0:T(8,128)(2,1)} %copy-done.2, f32[8,128]{1,0:T(8,128)} %broadcast_in_dim.2.refs_2_.refs_1_.blk_ref, bf16[8,768,768]{2,1,0:T(8,128)(2,1)} %get-tuple-element.38.refs_3_), custom_call_target="tpu_custom_call", output_to_operand_aliasing={{1}: (3, {})} | custom-call | flops 2415919104 | bytes 6000000 | tf_op jit(solution)/shard_map/dispatch4/pallas_call | solution.py:156
  67.9 9.6 %early_scores0.1 = (bf16[8,512,768]{2,1,0:T(8,128)(2,1)}, f32[8,512]{1,0:T(8,128)}, f32[8,512]{1,0:T(8,128)}) custom-call(bf16[8,768,768]{2,1,0:T(8,128)(2,1)} %get-tuple-element.39.rows_ref.refs_2_, bf16[1024,768]{1,0:T(8,128)(2,1)} %constant_dynamic-slice_fusion.1.c0, bf16[1024,768]{1,0:T(8,128)(2,1)} %collective-permute-done.3.refs_3_.c1, ...), custom_call_target="tpu_custom_call" | custom-call | flops 2415919104 | bytes 12000000 | tf_op jit(solution)/shard_map/early_scores0/pallas_call | solution.py:216
  77.8 4.8 %dispatch6.1 = (f32[1,8,1024]{2,1,0:T(8,128)}, bf16[8,768,768]{2,1,0:T(8,128)(2,1)}) custom-call(bf16[1040,768]{1,0:T(8,128)(2,1)} %tie.3.refs_0_, f32[8,128]{1,0:T(8,128)} %broadcast_in_dim.2.refs_2_.refs_1_.blk_ref, bf16[8,768,768]{2,1,0:T(8,128)(2,1)} %get-tuple-element.39.rows_ref.refs_2_), custom_call_target="tpu_custom_call", output_to_operand_aliasing={{1}: (2, {})} | custom-call | flops 1207959552 | bytes 3000000 | tf_op jit(solution)/shard_map/dispatch6/pallas_call | solution.py:156
  83.7 17.9 %late_scores.1 = (bf16[8,512,768]{2,1,0:T(8,128)(2,1)}, bf16[8,768,768]{2,1,0:T(8,128)(2,1)}, f32[1,8,1024]{2,1,0:T(8,128)}, f32[8,768]{1,0:T(8,128)}, f32[8,1024]{1,0:T(8,128)}) custom-call(bf16[1040,768]{1,0:T(8,128)(2,1)} %copy-done.3, f32[8,128]{1,0:T(8,128)} %broadcast_in_dim.2.refs_2_.refs_1_.blk_ref, ...), custom_call_target="tpu_custom_call", output_to_operand_aliasing={{0}: (13, {}), {1}: (2, {})} | custom-call | flops 2415919104 | bytes 20000000 | tf_op jit(solution)/shard_map/late_scores/pallas_call | solution.py:297
  105.6 4.9 %indices.1.idx_ref = s32[8,768]{1,0:T(8,128)} custom-call(f32[2,8,1024]{2,1,0:T(8,128)} %get-tuple-element.42.rank0.refs_0_, f32[2,8,1024]{2,1,0:T(8,128)} %get-tuple-element.43.rank1.refs_1_, f32[2,8,1024]{2,1,0:T(8,128)} %get-tuple-element.44.rank2.refs_2_, f32[1,8,1024]{2,1,0:T(8,128)} %get-tuple-element.45.rank3.refs_3_, ...), custom_call_target="tpu_custom_call" | custom-call | flops 4000000000 | bytes 1000000 | tf_op jit(solution)/shard_map/indices/pallas_call | solution.py:109
  111.2 13.0 %sums.1 = (bf16[528,768]{1,0:T(8,128)(2,1)}, bf16[528,768]{1,0:T(8,128)(2,1)}, bf16[528,768]{1,0:T(8,128)(2,1)}, bf16[528,768]{1,0:T(8,128)(2,1)}, bf16[4,144,76...) custom-call(s32[8]{0:T(128)} %concatenate.20.where_ref, ...), custom_call_target="tpu_custom_call" | custom-call | flops 4831838208 | bytes 24000000 | tf_op jit(solution)/shard_map/sums/pallas_call | solution.py:424
  124.2 3.8 %collective-permute-start.18 = (bf16[4,144,768]{2,1,0:T(8,128)(2,1)}, bf16[4,144,768]{2,1,0:T(8,128)(2,1)S(1)}, u32[]{:S(2)}, u32[]{:S(2)}) collective-permute-start(bf16[4,144,768]{2,1,0:T(8,128)(2,1)} %get-tuple-element.60), channel_id=1, source_target_pairs={{0,32},{32,64},{64,96},{96,0},{16,112},{48,16},{80,48},{112,80},{1... | collective-permute-start | bytes 2654216 | tf_op jit(solution)/shard_map/ppermute | solution.py:43
  129.8 11.6 %collective-permute-done.18 = bf16[4,144,768]{2,1,0:T(8,128)(2,1)S(1)} collective-permute-done((bf16[4,144,768]{2,1,0:T(8,128)(2,1)}, bf16[4,144,768]{2,1,0:T(8,128)(2,1)S(1)}, u32[]{:S(2)}, u32[]{:S(2)}) %collective-permute-start.18) | collective-permute-done | bytes 884768 | tf_op jit(solution)/shard_map/ppermute | solution.py:43
  142.8 3.4 %collective-permute-start.19 = (bf16[4,144,768]{2,1,0:T(8,128)(2,1)S(1)}, bf16[4,144,768]{2,1,0:T(8,128)(2,1)S(1)}, u32[]{:S(2)}, u32[]{:S(2)}) collective-permute-start(bf16[4,144,768]{2,1,0:T(8,128)(2,1)S(1)} %add_convert_fusion), channel_id=1, source_target_pairs={{0,32},{32,64},{64,96},{96,0},{16,112},{48,16},{80,48},{112,80},{1... | collective-permute-start | bytes 2654216 | tf_op jit(solution)/shard_map/ppermute | solution.py:43
  147.3 3.1 %collective-permute-start.16 = (bf16[528,768]{1,0:T(8,128)(2,1)S(1)}, bf16[528,768]{1,0:T(8,128)(2,1)S(1)}, u32[]{:S(2)}, u32[]{:S(2)}) collective-permute-start(bf16[528,768]{1,0:T(8,128)(2,1)S(1)} %add_convert_fusion.1), channel_id=1, source_target_pairs={{0,1},{1,2},{2,3},{3,0},{16,19},{17,16},{18,17},{19,18},{4,5},{5,6... | collective-permute-start | bytes 2433032 | tf_op jit(solution)/shard_map/ppermute | solution.py:43
  150.9 8.7 %collective-permute-done.16.h2 = bf16[528,768]{1,0:T(8,128)(2,1)S(1)} collective-permute-done((bf16[528,768]{1,0:T(8,128)(2,1)S(1)}, bf16[528,768]{1,0:T(8,128)(2,1)S(1)}, u32[]{:S(2)}, u32[]{:S(2)}) %collective-permute-start.16) | collective-permute-done | bytes 811040 | tf_op jit(solution)/shard_map/ppermute | solution.py:43
  160.9 4.3 %parted.1 = (bf16[144,768]{1,0:T(8,128)(2,1)}, bf16[144,768]{1,0:T(8,128)(2,1)}, bf16[144,768]{1,0:T(8,128)(2,1)}, bf16[144,768]{1,0:T(8,128)(2,1)}, bf16[144,76...) custom-call(s32[8]{0:T(128)} %concatenate.20.where_ref, ...), custom_call_target="tpu_custom_call" | custom-call | flops 1000000 | bytes 8000000 | tf_op jit(solution)/shard_map/parted/pallas_call | solution.py:465
  165.1 2.7 %collective-permute-start.21 = (bf16[144,768]{1,0:T(8,128)(2,1)}, bf16[144,768]{1,0:T(8,128)(2,1)}, u32[]{:S(2)}, u32[]{:S(2)}) collective-permute-start(bf16[144,768]{1,0:T(8,128)(2,1)} %get-tuple-element.63), channel_id=1, source_target_pairs={{0,32},{32,64},{64,96},{96,0},{16,112},{48,16},{80,48},{112,80},{1... | collective-permute-start | bytes 663560 | tf_op jit(solution)/shard_map/ppermute | solution.py:43
  167.8 2.7 %collective-permute-start.23 = (bf16[144,768]{1,0:T(8,128)(2,1)}, bf16[144,768]{1,0:T(8,128)(2,1)}, u32[]{:S(2)}, u32[]{:S(2)}) collective-permute-start(bf16[144,768]{1,0:T(8,128)(2,1)} %get-tuple-element.66), channel_id=1, source_target_pairs={{0,3},{1,0},{2,1},{3,2},{16,17},{17,18},{18,19},{19,16},{4,7},{5,4... | collective-permute-start | bytes 663560 | tf_op jit(solution)/shard_map/ppermute | solution.py:43
  171.3 4.4 %collective-permute-start.25 = (bf16[144,768]{1,0:T(8,128)(2,1)}, bf16[144,768]{1,0:T(8,128)(2,1)}, u32[]{:S(2)}, u32[]{:S(2)}) collective-permute-start(bf16[144,768]{1,0:T(8,128)(2,1)} %get-tuple-element.68), channel_id=1, source_target_pairs={{0,2},{1,3},{2,0},{3,1},{4,6},{5,7},{6,4},{7,5},{8,10},{9,11},{10,... | collective-permute-start | bytes 663560 | tf_op jit(solution)/shard_map/ppermute | solution.py:47
  175.8 1.8 constant_dynamic-slice_fusion.mine_ref
  177.6 1.8 collective-permute-done.25.g3
  179.4 2.8 %final.1.refs_0_ = bf16[2,128,768]{2,1,0:T(8,128)(2,1)} custom-call(s32[8]{0:T(128)} %concatenate.20.where_ref, bf16[144,768]{1,0:T(8,128)(2,1)} %get-tuple-element.61.h0, bf16[144,768]{1,0:T(8,128)(2,1)} %copy-done.10, bf16[144,768]{1,0:T(8,128)(2,1)} %collective-permute-done.21.h2, bf16[144,768]{1,0:T(8,128)(2,1)} %collective-permute-done.22.h3, ...), custom_call_target="tpu_custom_call" | custom-call | flops 1000000 | bytes 2000000 | tf_op jit(solution)/shard_map/final/pallas_call | solution.py:491
  183.7 2.0 collective-permute-start.28
  185.6 9.7 %collective-permute-start.29 = (bf16[2,128,768]{2,1,0:T(8,128)(2,1)}, bf16[2,128,768]{2,1,0:T(8,128)(2,1)}, u32[]{:S(2)}, u32[]{:S(2)}) collective-permute-start(bf16[2,128,768]{2,1,0:T(8,128)(2,1)} %final.1.refs_0_), channel_id=1, source_target_pairs={{0,16},{16,0},{1,17},{17,1},{2,18},{18,2},{3,19},{19,3},{4,20},{20... | collective-permute-start | bytes 1179656 | tf_op jit(solution)/shard_map/ppermute | solution.py:51
  195.3 4.8 %collective-permute-start.30 = (bf16[2,128,768]{2,1,0:T(8,128)(2,1)S(1)}, bf16[2,128,768]{2,1,0:T(8,128)(2,1)}, u32[]{:S(2)}, u32[]{:S(2)}) collective-permute-start(bf16[2,128,768]{2,1,0:T(8,128)(2,1)S(1)} %collective-permute-done.26.refs_1_), channel_id=1, source_target_pairs={{0,16},{16,0},{1,17},{17,1},{2,18},{18,2},{3,19},{19,3},{4,20},{20... | collective-permute-start | bytes 1179656 | tf_op jit(solution)/shard_map/ppermute | solution.py:51
  200.1 3.5 %collective-permute-start.31 = (bf16[2,128,768]{2,1,0:T(8,128)(2,1)}, bf16[2,128,768]{2,1,0:T(8,128)(2,1)}, u32[]{:S(2)}, u32[]{:S(2)}) collective-permute-start(bf16[2,128,768]{2,1,0:T(8,128)(2,1)} %collective-permute-done.27.refs_2_), channel_id=1, source_target_pairs={{0,16},{16,0},{1,17},{17,1},{2,18},{18,2},{3,19},{19,3},{4,20},{20... | collective-permute-start | bytes 1179656 | tf_op jit(solution)/shard_map/ppermute | solution.py:51
  203.7 1.9 collective-permute-start.32
  207.3 3.7 %place.1 = bf16[4,4,128,768]{3,2,1,0:T(8,128)(2,1)} custom-call(s32[10]{0:T(128)} %concatenate.19.where_ref, bf16[2,128,768]{2,1,0:T(8,128)(2,1)} %final.1.refs_0_, bf16[2,128,768]{2,1,0:T(8,128)(2,1)} %copy-done.9, bf16[2,128,768]{2,1,0:T(8,128)(2,1)} %collective-permute-done.27.refs_2_, bf16[2,128,768]{2,1,0:T(8,128)(2,1)} %collective-permute-done.28.refs_3_, ...), custom_call_target="tpu_custom_call" | custom-call | bytes 6000000 | tf_op jit(solution)/shard_map/place/pallas_call | solution.py:513
  (94 shorter events, 24.4 us)
Async XLA Ops:
  3.6 8.2 %collective-permute-start.1 = (bf16[1040,768]{1,0:T(8,128)(2,1)}, bf16[1040,768]{1,0:T(8,128)(2,1)}, u32[]{:S(2)}, u32[]{:S(2)}) collective-permute-start(bf16[1040,768]{1,0:T(8,128)(2,1)} %fusion.1.refs_0_), channel_id=1, source_target_pairs={{0,16},{16,0},{1,17},{17,1},{2,18},{18,2},{3,19},{19,3},{4,20},{20... | collective-permute-start | bytes 4792328 | tf_op jit(solution)/shard_map/ppermute | solution.py:51
  5.0 42.6 %collective-permute-start = (bf16[1040,768]{1,0:T(8,128)(2,1)}, bf16[1040,768]{1,0:T(8,128)(2,1)}, u32[]{:S(2)}, u32[]{:S(2)}) collective-permute-start(bf16[1040,768]{1,0:T(8,128)(2,1)} %fusion.1.refs_0_), channel_id=1, source_target_pairs={{0,4},{4,8},{8,12},{12,0},{16,28},{20,16},{24,20},{28,24},{1,5},{5... | collective-permute-start | bytes 4792328 | tf_op jit(solution)/shard_map/ppermute | solution.py:43
  7.9 39.8 %collective-permute-start.2 = (bf16[1040,768]{1,0:T(8,128)(2,1)}, bf16[1040,768]{1,0:T(8,128)(2,1)}, u32[]{:S(2)}, u32[]{:S(2)}) collective-permute-start(bf16[1040,768]{1,0:T(8,128)(2,1)} %fusion.1.refs_0_), channel_id=1, source_target_pairs={{0,12},{4,0},{8,4},{12,8},{16,20},{20,24},{24,28},{28,16},{1,13},{... | collective-permute-start | bytes 4792328 | tf_op jit(solution)/shard_map/ppermute | solution.py:43
  9.1 35.6 %collective-permute-start.3 = (bf16[1024,768]{1,0:T(8,128)(2,1)}, bf16[1024,768]{1,0:T(8,128)(2,1)}, u32[]{:S(2)}, u32[]{:S(2)}) collective-permute-start(bf16[1024,768]{1,0:T(8,128)(2,1)} %constant_dynamic-slice_fusion.1.c0), channel_id=1, source_target_pairs={{0,1},{1,2},{2,3},{3,0},{16,19},{17,16},{18,17},{19,18},{4,5},{5,6... | collective-permute-start | bytes 4718600 | tf_op jit(solution)/shard_map/ppermute | solution.py:43
  11.6 36.1 %collective-permute-start.4 = (bf16[1024,768]{1,0:T(8,128)(2,1)}, bf16[1024,768]{1,0:T(8,128)(2,1)}, u32[]{:S(2)}, u32[]{:S(2)}) collective-permute-start(bf16[1024,768]{1,0:T(8,128)(2,1)} %constant_dynamic-slice_fusion.1.c0), channel_id=1, source_target_pairs={{0,3},{1,0},{2,1},{3,2},{16,17},{17,18},{18,19},{19,16},{4,7},{5,4... | collective-permute-start | bytes 4718600 | tf_op jit(solution)/shard_map/ppermute | solution.py:43
  47.7 11.8 %collective-permute-start.6 = (bf16[1040,768]{1,0:T(8,128)(2,1)}, bf16[1040,768]{1,0:T(8,128)(2,1)S(1)}, u32[]{:S(2)}, u32[]{:S(2)}) collective-permute-start(bf16[1040,768]{1,0:T(8,128)(2,1)} %tie.2.refs_0_), channel_id=1, source_target_pairs={{0,16},{16,0},{1,17},{17,1},{2,18},{18,2},{3,19},{19,3},{4,20},{20... | collective-permute-start | bytes 4792328 | tf_op jit(solution)/shard_map/ppermute | solution.py:51
  47.8 11.8 %collective-permute-start.7 = (bf16[1040,768]{1,0:T(8,128)(2,1)}, bf16[1040,768]{1,0:T(8,128)(2,1)S(1)}, u32[]{:S(2)}, u32[]{:S(2)}) collective-permute-start(bf16[1040,768]{1,0:T(8,128)(2,1)} %collective-permute-done.2.refs_2_.refs_1_), channel_id=1, source_target_pairs={{0,16},{16,0},{1,17},{17,1},{2,18},{18,2},{3,19},{19,3},{4,20},{20... | collective-permute-start | bytes 4792328 | tf_op jit(solution)/shard_map/ppermute | solution.py:51
  48.2 29.2 %collective-permute-start.5 = (bf16[1040,768]{1,0:T(8,128)(2,1)}, bf16[1040,768]{1,0:T(8,128)(2,1)}, u32[]{:S(2)}, u32[]{:S(2)}) collective-permute-start(bf16[1040,768]{1,0:T(8,128)(2,1)} %tie.2.refs_0_), channel_id=1, source_target_pairs={{0,4},{4,8},{8,12},{12,0},{16,28},{20,16},{24,20},{28,24},{1,5},{5... | collective-permute-start | bytes 4792328 | tf_op jit(solution)/shard_map/ppermute | solution.py:43
  49.8 27.6 %collective-permute-start.8 = (bf16[1024,768]{1,0:T(8,128)(2,1)}, bf16[1024,768]{1,0:T(8,128)(2,1)}, u32[]{:S(2)}, u32[]{:S(2)}) collective-permute-start(bf16[1024,768]{1,0:T(8,128)(2,1)} %collective-permute-done.3.refs_3_.c1), channel_id=1, source_target_pairs={{0,1},{1,2},{2,3},{3,0},{16,19},{17,16},{18,17},{19,18},{4,5},{5,6... | collective-permute-start | bytes 4718600 | tf_op jit(solution)/shard_map/ppermute | solution.py:43
  77.5 5.1 %collective-permute-start.9 = (bf16[1040,768]{1,0:T(8,128)(2,1)}, bf16[1040,768]{1,0:T(8,128)(2,1)S(1)}, u32[]{:S(2)}, u32[]{:S(2)}) collective-permute-start(bf16[1040,768]{1,0:T(8,128)(2,1)} %tie.3.refs_0_), channel_id=1, source_target_pairs={{0,16},{16,0},{1,17},{17,1},{2,18},{18,2},{3,19},{19,3},{4,20},{20... | collective-permute-start | bytes 4792328 | tf_op jit(solution)/shard_map/ppermute | solution.py:51
  104.1 6.5 %collective-permute-start.11 = (f32[8,1024]{1,0:T(8,128)S(1)}, f32[8,1024]{1,0:T(8,128)S(1)}, u32[]{:S(2)}, u32[]{:S(2)}) collective-permute-start(f32[8,1024]{1,0:T(8,128)S(1)} %log_add_fusion.s0), channel_id=1, source_target_pairs={{0,4},{4,8},{8,12},{12,0},{16,28},{20,16},{24,20},{28,24},{1,5},{5... | collective-permute-start | bytes 98312 | tf_op jit(solution)/shard_map/ppermute | solution.py:43
  104.2 6.4 %collective-permute-start.12 = (f32[8,1024]{1,0:T(8,128)S(1)}, f32[8,1024]{1,0:T(8,128)S(1)}, u32[]{:S(2)}, u32[]{:S(2)}) collective-permute-start(f32[8,1024]{1,0:T(8,128)S(1)} %log_add_fusion.s0), channel_id=1, source_target_pairs={{0,12},{4,0},{8,4},{12,8},{16,20},{20,24},{24,28},{28,16},{1,13},{... | collective-permute-start | bytes 98312 | tf_op jit(solution)/shard_map/ppermute | solution.py:43
  105.6 5.0 %collective-permute-start.13 = (f32[8,1024]{1,0:T(8,128)S(1)}, f32[8,1024]{1,0:T(8,128)S(1)}, u32[]{:S(2)}, u32[]{:S(2)}) collective-permute-start(f32[8,1024]{1,0:T(8,128)S(1)} %log_add_fusion.s0), channel_id=1, source_target_pairs={{0,8},{4,12},{8,0},{12,4},{1,9},{5,13},{9,1},{13,5},{2,10},{6,14},... | collective-permute-start | bytes 98312 | tf_op jit(solution)/shard_map/ppermute | solution.py:47
  124.2 17.2 %collective-permute-start.18 = (bf16[4,144,768]{2,1,0:T(8,128)(2,1)}, bf16[4,144,768]{2,1,0:T(8,128)(2,1)S(1)}, u32[]{:S(2)}, u32[]{:S(2)}) collective-permute-start(bf16[4,144,768]{2,1,0:T(8,128)(2,1)} %get-tuple-element.60), channel_id=1, source_target_pairs={{0,32},{32,64},{64,96},{96,0},{16,112},{48,16},{80,48},{112,80},{1... | collective-permute-start | bytes 2654216 | tf_op jit(solution)/shard_map/ppermute | solution.py:43
  128.0 19.1 %collective-permute-start.15 = (bf16[528,768]{1,0:T(8,128)(2,1)}, bf16[528,768]{1,0:T(8,128)(2,1)S(1)}, u32[]{:S(2)}, u32[]{:S(2)}) collective-permute-start(bf16[528,768]{1,0:T(8,128)(2,1)} %get-tuple-element.56), channel_id=1, source_target_pairs={{0,1},{1,2},{2,3},{3,0},{16,19},{17,16},{18,17},{19,18},{4,5},{5,6... | collective-permute-start | bytes 2433032 | tf_op jit(solution)/shard_map/ppermute | solution.py:43
  129.8 20.7 %collective-permute-start.14 = (bf16[528,768]{1,0:T(8,128)(2,1)}, bf16[528,768]{1,0:T(8,128)(2,1)S(1)}, u32[]{:S(2)}, u32[]{:S(2)}) collective-permute-start(bf16[528,768]{1,0:T(8,128)(2,1)} %get-tuple-element.54), channel_id=1, source_target_pairs={{0,3},{1,0},{2,1},{3,2},{16,17},{17,18},{18,19},{19,16},{4,7},{5,4... | collective-permute-start | bytes 2433032 | tf_op jit(solution)/shard_map/ppermute | solution.py:43
  129.8 21.1 %collective-permute-start.17 = (bf16[4,144,768]{2,1,0:T(8,128)(2,1)}, bf16[4,144,768]{2,1,0:T(8,128)(2,1)S(1)}, u32[]{:S(2)}, u32[]{:S(2)}) collective-permute-start(bf16[4,144,768]{2,1,0:T(8,128)(2,1)} %get-tuple-element.58), channel_id=1, source_target_pairs={{0,96},{32,0},{64,32},{96,64},{16,48},{48,80},{80,112},{112,16},{1... | collective-permute-start | bytes 2654216 | tf_op jit(solution)/shard_map/ppermute | solution.py:43
  142.8 16.8 %collective-permute-start.19 = (bf16[4,144,768]{2,1,0:T(8,128)(2,1)S(1)}, bf16[4,144,768]{2,1,0:T(8,128)(2,1)S(1)}, u32[]{:S(2)}, u32[]{:S(2)}) collective-permute-start(bf16[4,144,768]{2,1,0:T(8,128)(2,1)S(1)} %add_convert_fusion), channel_id=1, source_target_pairs={{0,32},{32,64},{64,96},{96,0},{16,112},{48,16},{80,48},{112,80},{1... | collective-permute-start | bytes 2654216 | tf_op jit(solution)/shard_map/ppermute | solution.py:43
  147.3 12.3 %collective-permute-start.16 = (bf16[528,768]{1,0:T(8,128)(2,1)S(1)}, bf16[528,768]{1,0:T(8,128)(2,1)S(1)}, u32[]{:S(2)}, u32[]{:S(2)}) collective-permute-start(bf16[528,768]{1,0:T(8,128)(2,1)S(1)} %add_convert_fusion.1), channel_id=1, source_target_pairs={{0,1},{1,2},{2,3},{3,0},{16,19},{17,16},{18,17},{19,18},{4,5},{5,6... | collective-permute-start | bytes 2433032 | tf_op jit(solution)/shard_map/ppermute | solution.py:43
  165.1 6.2 %collective-permute-start.20 = (bf16[144,768]{1,0:T(8,128)(2,1)}, bf16[144,768]{1,0:T(8,128)(2,1)S(1)}, u32[]{:S(2)}, u32[]{:S(2)}) collective-permute-start(bf16[144,768]{1,0:T(8,128)(2,1)} %get-tuple-element.62), channel_id=1, source_target_pairs={{0,96},{32,0},{64,32},{96,64},{16,48},{48,80},{80,112},{112,16},{1... | collective-permute-start | bytes 663560 | tf_op jit(solution)/shard_map/ppermute | solution.py:43
  165.1 12.4 %collective-permute-start.21 = (bf16[144,768]{1,0:T(8,128)(2,1)}, bf16[144,768]{1,0:T(8,128)(2,1)}, u32[]{:S(2)}, u32[]{:S(2)}) collective-permute-start(bf16[144,768]{1,0:T(8,128)(2,1)} %get-tuple-element.63), channel_id=1, source_target_pairs={{0,32},{32,64},{64,96},{96,0},{16,112},{48,16},{80,48},{112,80},{1... | collective-permute-start | bytes 663560 | tf_op jit(solution)/shard_map/ppermute | solution.py:43
  167.8 9.7 %collective-permute-start.22 = (bf16[144,768]{1,0:T(8,128)(2,1)}, bf16[144,768]{1,0:T(8,128)(2,1)}, u32[]{:S(2)}, u32[]{:S(2)}) collective-permute-start(bf16[144,768]{1,0:T(8,128)(2,1)} %get-tuple-element.64), channel_id=1, source_target_pairs={{0,64},{32,96},{64,0},{96,32},{1,65},{33,97},{65,1},{97,33},{2,66}... | collective-permute-start | bytes 663560 | tf_op jit(solution)/shard_map/ppermute | solution.py:47
  167.8 9.7 %collective-permute-start.23 = (bf16[144,768]{1,0:T(8,128)(2,1)}, bf16[144,768]{1,0:T(8,128)(2,1)}, u32[]{:S(2)}, u32[]{:S(2)}) collective-permute-start(bf16[144,768]{1,0:T(8,128)(2,1)} %get-tuple-element.66), channel_id=1, source_target_pairs={{0,3},{1,0},{2,1},{3,2},{16,17},{17,18},{18,19},{19,16},{4,7},{5,4... | collective-permute-start | bytes 663560 | tf_op jit(solution)/shard_map/ppermute | solution.py:43
  170.5 7.1 %collective-permute-start.24 = (bf16[144,768]{1,0:T(8,128)(2,1)}, bf16[144,768]{1,0:T(8,128)(2,1)}, u32[]{:S(2)}, u32[]{:S(2)}) collective-permute-start(bf16[144,768]{1,0:T(8,128)(2,1)} %get-tuple-element.67), channel_id=1, source_target_pairs={{0,1},{1,2},{2,3},{3,0},{16,19},{17,16},{18,17},{19,18},{4,5},{5,6... | collective-permute-start | bytes 663560 | tf_op jit(solution)/shard_map/ppermute | solution.py:43
  171.3 8.1 %collective-permute-start.25 = (bf16[144,768]{1,0:T(8,128)(2,1)}, bf16[144,768]{1,0:T(8,128)(2,1)}, u32[]{:S(2)}, u32[]{:S(2)}) collective-permute-start(bf16[144,768]{1,0:T(8,128)(2,1)} %get-tuple-element.68), channel_id=1, source_target_pairs={{0,2},{1,3},{2,0},{3,1},{4,6},{5,7},{6,4},{7,5},{8,10},{9,11},{10,... | collective-permute-start | bytes 663560 | tf_op jit(solution)/shard_map/ppermute | solution.py:47
  182.2 13.1 %collective-permute-start.26 = (bf16[2,128,768]{2,1,0:T(8,128)(2,1)}, bf16[2,128,768]{2,1,0:T(8,128)(2,1)S(1)}, u32[]{:S(2)}, u32[]{:S(2)}) collective-permute-start(bf16[2,128,768]{2,1,0:T(8,128)(2,1)} %final.1.refs_0_), channel_id=1, source_target_pairs={{0,32},{32,64},{64,96},{96,0},{16,112},{48,16},{80,48},{112,80},{1... | collective-permute-start | bytes 1179656 | tf_op jit(solution)/shard_map/ppermute | solution.py:43
  182.4 17.7 %collective-permute-start.27 = (bf16[2,128,768]{2,1,0:T(8,128)(2,1)}, bf16[2,128,768]{2,1,0:T(8,128)(2,1)}, u32[]{:S(2)}, u32[]{:S(2)}) collective-permute-start(bf16[2,128,768]{2,1,0:T(8,128)(2,1)} %final.1.refs_0_), channel_id=1, source_target_pairs={{0,96},{32,0},{64,32},{96,64},{16,48},{48,80},{80,112},{112,16},{1... | collective-permute-start | bytes 1179656 | tf_op jit(solution)/shard_map/ppermute | solution.py:43
  183.7 20.0 %collective-permute-start.28 = (bf16[2,128,768]{2,1,0:T(8,128)(2,1)}, bf16[2,128,768]{2,1,0:T(8,128)(2,1)}, u32[]{:S(2)}, u32[]{:S(2)}) collective-permute-start(bf16[2,128,768]{2,1,0:T(8,128)(2,1)} %final.1.refs_0_), channel_id=1, source_target_pairs={{0,64},{32,96},{64,0},{96,32},{1,65},{33,97},{65,1},{97,33},{2,66}... | collective-permute-start | bytes 1179656 | tf_op jit(solution)/shard_map/ppermute | solution.py:47
  185.6 20.6 %collective-permute-start.29 = (bf16[2,128,768]{2,1,0:T(8,128)(2,1)}, bf16[2,128,768]{2,1,0:T(8,128)(2,1)}, u32[]{:S(2)}, u32[]{:S(2)}) collective-permute-start(bf16[2,128,768]{2,1,0:T(8,128)(2,1)} %final.1.refs_0_), channel_id=1, source_target_pairs={{0,16},{16,0},{1,17},{17,1},{2,18},{18,2},{3,19},{19,3},{4,20},{20... | collective-permute-start | bytes 1179656 | tf_op jit(solution)/shard_map/ppermute | solution.py:51
  195.3 11.0 %collective-permute-start.30 = (bf16[2,128,768]{2,1,0:T(8,128)(2,1)S(1)}, bf16[2,128,768]{2,1,0:T(8,128)(2,1)}, u32[]{:S(2)}, u32[]{:S(2)}) collective-permute-start(bf16[2,128,768]{2,1,0:T(8,128)(2,1)S(1)} %collective-permute-done.26.refs_1_), channel_id=1, source_target_pairs={{0,16},{16,0},{1,17},{17,1},{2,18},{18,2},{3,19},{19,3},{4,20},{20... | collective-permute-start | bytes 1179656 | tf_op jit(solution)/shard_map/ppermute | solution.py:51
  200.1 6.1 %collective-permute-start.31 = (bf16[2,128,768]{2,1,0:T(8,128)(2,1)}, bf16[2,128,768]{2,1,0:T(8,128)(2,1)}, u32[]{:S(2)}, u32[]{:S(2)}) collective-permute-start(bf16[2,128,768]{2,1,0:T(8,128)(2,1)} %collective-permute-done.27.refs_2_), channel_id=1, source_target_pairs={{0,16},{16,0},{1,17},{17,1},{2,18},{18,2},{3,19},{19,3},{4,20},{20... | collective-permute-start | bytes 1179656 | tf_op jit(solution)/shard_map/ppermute | solution.py:51
  203.7 3.6 %collective-permute-start.32 = (bf16[2,128,768]{2,1,0:T(8,128)(2,1)}, bf16[2,128,768]{2,1,0:T(8,128)(2,1)}, u32[]{:S(2)}, u32[]{:S(2)}) collective-permute-start(bf16[2,128,768]{2,1,0:T(8,128)(2,1)} %collective-permute-done.28.refs_3_), channel_id=1, source_target_pairs={{0,16},{16,0},{1,17},{17,1},{2,18},{18,2},{3,19},{19,3},{4,20},{20... | collective-permute-start | bytes 1179656 | tf_op jit(solution)/shard_map/ppermute | solution.py:51
  (16 other events, 84.7 us)

commit v3 on v2

v3 whole, which is shorter than its diff:
```python
import jax
import jax.numpy as jnp
import numpy as np
from jax import lax
from jax.experimental import pallas as pl
from jax.experimental.pallas import tpu as pltpu
from jax.sharding import Mesh, PartitionSpec as P

BS = 512
MOST = 96
TOK = 1024
D = 768
NSRC = 8
NBLK = 8
SLOTS = NSRC * MOST
EXTRA = 16
EXT = TOK + EXTRA
ROWS = (28, SLOTS, D)
SCORES = (40, BS, SLOTS)
LOW = -1e30
F32 = jnp.float32
BF16 = jnp.bfloat16

NAMES = ("v", "v'", "a", "b", "a'", "b'", "c", "c'")


def order(**came):
    return tuple(NAMES.index(came[n.replace("'", "_")]) for n in NAMES)


SWAPPED = order(v="v'", v_="v", a="a'", a_="a", b="b'", b_="b", c="c'", c_="c")
FROM_D = order(a="v", b_="v'", c="a", v_="a'", v="b", c_="b'", b="c", a_="c'")
FROM_E = order(b="v", a_="v'", v="a", c_="a'", c="b", v_="b'", a="c", b_="c'")
FROM_F = order(c="v", c_="v'", b="a", b_="a'", a="b", a_="b'", v="c", v_="c'")


def turn(a, axis, sign):
    axes = ("z", "core") if axis == "z" else ("core", axis)
    at = (lambda core, i: i * 2 + core) if axis == "z" else (lambda core, i: core * 4 + i)
    pairs = []
    for core in range(2):
        for i in range(4):
            pairs.append((at(core, i), at(core, (i + (sign if core == 0 else -sign)) % 4)))
    return lax.ppermute(a, axes, pairs)


def far(a, axis):
    return lax.ppermute(a, axis, [(i, (i + 2) % 4) for i in range(4)])


def swap(a):
    return lax.ppermute(a, "core", [(0, 1), (1, 0)])


def params(mib):
    return pltpu.CompilerParams(vmem_limit_bytes=mib * 1024 * 1024)


def cost(flops, nbytes, trans=0):
    return pl.CostEstimate(flops=int(flops), bytes_accessed=int(nbytes), transcendentals=int(trans))


def earlier():
    up = lax.broadcasted_iota(jnp.int32, (TOK, TOK), 0) < lax.broadcasted_iota(jnp.int32, (TOK, TOK), 1)
    return jnp.where(up, 1.0, 0.0).astype(BF16)


def ranks(tail, blk, up):
    tail = tail.astype(F32)
    hit = None
    for pick in range(4):
        named = jnp.concatenate([tail[2 * pick : 2 * pick + 1, 0:512], tail[2 * pick + 1 : 2 * pick + 2, 0:512]], axis=1)
        m = named == blk
        hit = m if hit is None else hit | m
    hit = jnp.where(hit, 1.0, 0.0)
    hits = jnp.concatenate([hit, jnp.zeros((8, TOK), F32)], axis=0).astype(BF16)
    before = jnp.dot(hits, up, preferred_element_type=F32)[0:NBLK]
    return jnp.where(hit > 0, before, -1.0)


def gathered(rank, vectors):
    slot = lax.broadcasted_iota(jnp.int32, (MOST, TOK), 0).astype(F32)
    hot = [jnp.where(slot == rank[b : b + 1, :], 1.0, 0.0).astype(BF16) for b in range(NBLK)]
    hot = jnp.concatenate(hot, axis=0)
    rows = jnp.dot(hot, vectors, preferred_element_type=F32).astype(BF16)
    return rows.reshape(NBLK, MOST, D)


def index_kernel(*refs):
    rank_refs, idx_ref = refs[:-1], refs[-1]
    sources = [(ref, k) for ref in rank_refs for k in range(ref.shape[0])]
    row = lax.broadcasted_iota(jnp.int32, (8, TOK), 0)
    v = lax.broadcasted_iota(jnp.int32, (8, TOK), 1)
    place = jnp.where(row == 0, v >> 3, jnp.where(row == 1, v & 7, jnp.where(row == 2, 1, 0)))
    place = place.astype(F32).astype(BF16)
    lane = lax.broadcasted_iota(jnp.int32, (1, SLOTS), 1)
    base = jnp.zeros((1, SLOTS), F32)
    for s in range(1, NSRC):
        base = base + jnp.where(lane >= s * MOST, float(TOK), 0.0)
    slot = lax.broadcasted_iota(jnp.int32, (MOST, TOK), 0).astype(F32)
    for b in range(NBLK):
        hot = [jnp.where(slot == ref[k, b : b + 1, :], 1.0, 0.0).astype(BF16) for ref, k in sources]
        hot = jnp.concatenate(hot, axis=0)
        found = lax.dot_general(place, hot, (((1,), (1,)), ((), ())), preferred_element_type=F32)
        where = found[0:1] * 8.0 + found[1:2] + base
        idx_ref[b : b + 1, :] = jnp.where(found[2:3] > 0, where, -1.0).astype(jnp.int32)


def indices(*rank):
    return pl.pallas_call(
        index_kernel,
        out_shape=jax.ShapeDtypeStruct((NBLK, SLOTS), jnp.int32),
        compiler_params=params(12),
        cost_estimate=cost(4e9, 1e6),
        name="indices",
    )(*rank)


def dispatch_kernel(n, *refs):
    sources, blk_ref, (rank_ref, out_ref, buf, sems, up) = refs[:n], refs[n], refs[-5:]
    i = pl.program_id(0)

    def copy(k):
        return pltpu.make_async_copy(sources[k], buf.at[k % 2], sems.at[k % 2])

    @pl.when(i == 0)
    def _():
        copy(0).start()
        up[...] = earlier()

    for k in range(n):
        @pl.when(i == k)
        def _(k=k):
            if k + 1 < n:
                copy(k + 1).start()
            copy(k).wait()

    rank = ranks(buf[i % 2, TOK:EXT, :], blk_ref[:, 0:1], up[...])
    rank_ref[0] = rank
    out_ref[...] = gathered(rank, buf[i % 2, 0:TOK, :])


def dispatch(first, sources, blk, rows):
    n = len(sources)
    anywhere = pl.BlockSpec(memory_space=pl.ANY)
    in_specs = [anywhere] * n + [pl.BlockSpec((NBLK, 128), lambda i: (0, 0))]
    args = [*sources, blk]
    alias = {}
    if rows is not None:
        in_specs.append(pl.BlockSpec(memory_space=pltpu.HBM))
        args.append(rows)
        alias = {n + 1: 1}

    def kern(*refs):
        dispatch_kernel(n, *refs)

    return pl.pallas_call(
        kern,
        grid=(n,),
        in_specs=in_specs,
        out_specs=(
            pl.BlockSpec((1, NBLK, TOK), lambda i: (i, 0, 0)),
            pl.BlockSpec((NBLK, MOST, D), lambda i: (0, first + i, 0)),
        ),
        out_shape=(
            jax.ShapeDtypeStruct((n, NBLK, TOK), F32),
            jax.ShapeDtypeStruct(ROWS, BF16),
        ),
        scratch_shapes=[
            pltpu.VMEM((2, EXT, D), BF16),
            pltpu.SemaphoreType.DMA((2,)),
            pltpu.VMEM((TOK, TOK), BF16),
        ],
        input_output_aliases=alias,
        compiler_params=params(20),
        cost_estimate=cost(2 * n * NBLK * MOST * TOK * D, n * 3e6),
        name=f"dispatch{first}",
    )(*args)


def half_norm(cent):
    wide = cent.astype(F32)
    return 0.5 * jnp.sum(wide * wide, axis=1, keepdims=True)


def score_chunk(cent, norm, rows):
    raw = lax.dot_general(cent, rows, (((1,), (1,)), ((), ())), preferred_element_type=F32)
    score = raw - norm
    peak = jnp.max(score, axis=0, keepdims=True)
    e = jnp.exp(score - peak)
    return e.astype(BF16), peak, peak + jnp.log(jnp.sum(e, axis=0, keepdims=True))


def middle_kernel(
    s0, s1, blk_ref, c0, c1, c2, rows_in,
    rows_out, rank_ref, e_out, peak_ref, lse_ref,
    vbuf, x03, x45, cb, eb, vsem, csem, xsem, osem, esem,
):
    sources = [pltpu.make_async_copy(s, vbuf.at[k], vsem.at[k]) for k, s in enumerate((s0, s1))]
    cents = [pltpu.make_async_copy(c, cb.at[k], csem.at[k]) for k, c in enumerate((c0, c1, c2))]
    first = pltpu.make_async_copy(rows_in.at[pl.ds(0, 6), pl.ds(0, 384), :], x03, xsem)
    for copy in sources:
        copy.start()
    up = earlier()
    for k in range(2):
        sources[k].wait()
        for copy in (first, cents[0]) if k == 0 else cents[1:]:
            copy.start()
        rank = ranks(vbuf[k, TOK:EXT, :], blk_ref[:, 0:1], up)
        rank_ref[k] = rank
        x45[:, k * MOST : (k + 1) * MOST, :] = gathered(rank, vbuf[k, 0:TOK, :])
    back = pltpu.make_async_copy(x45, rows_out.at[pl.ds(0, NBLK), pl.ds(384, 192), :], osem)
    back.start()
    first.wait()
    for q in range(3):
        cents[q].wait()
        for i in range(2):
            b = 2 * q + i
            cent = cb[q, i * BS : (i + 1) * BS, :]
            norm = half_norm(cent)
            chunks = (x03[b, 0:256, :], jnp.concatenate([x03[b, 256:384, :], x45[b, 0:128, :]], axis=0))
            for k, rows in enumerate(chunks):
                e, peak, lse = score_chunk(cent, norm, rows)
                eb[b, :, k * 256 : (k + 1) * 256] = e
                peak_ref[b : b + 1, k * 256 : (k + 1) * 256] = peak
                lse_ref[b : b + 1, k * 256 : (k + 1) * 256] = lse
            pltpu.make_async_copy(eb.at[b], e_out.at[b, :, pl.ds(0, 512)], esem.at[b]).start()
    back.wait()
    for b in range(6):
        pltpu.make_async_copy(eb.at[b], e_out.at[b, :, pl.ds(0, 512)], esem.at[b]).wait()


def middle(sources, blk, cents, rows):
    anywhere, hbm = pl.BlockSpec(memory_space=pl.ANY), pl.BlockSpec(memory_space=pltpu.HBM)
    vmem = pl.BlockSpec(memory_space=pltpu.VMEM)
    return pl.pallas_call(
        middle_kernel,
        in_specs=[anywhere] * 2 + [vmem] + [anywhere] * 3 + [hbm],
        out_specs=(hbm, vmem, hbm, vmem, vmem),
        out_shape=(
            jax.ShapeDtypeStruct(ROWS, BF16),
            jax.ShapeDtypeStruct((2, NBLK, TOK), F32),
            jax.ShapeDtypeStruct(SCORES, BF16),
            jax.ShapeDtypeStruct((NBLK, 512), F32),
            jax.ShapeDtypeStruct((NBLK, 512), F32),
        ),
        scratch_shapes=[
            pltpu.VMEM((2, EXT, D), BF16),
            pltpu.VMEM((6, 384, D), BF16),
            pltpu.VMEM((NBLK, 192, D), BF16),
            pltpu.VMEM((3, 1024, D), BF16),
            pltpu.VMEM((6, BS, 512), BF16),
            pltpu.SemaphoreType.DMA((2,)),
            pltpu.SemaphoreType.DMA((3,)),
            pltpu.SemaphoreType.DMA,
            pltpu.SemaphoreType.DMA,
            pltpu.SemaphoreType.DMA((6,)),
        ],
        input_output_aliases={6: 0},
        compiler_params=params(32),
        cost_estimate=cost(4 * NBLK * MOST * TOK * D, 20e6, 6 * BS * 512),
        name="middle",
    )(*sources, blk, *cents, rows)


def late_kernel(
    source0, source1, blk_ref, c0, c1, c2, c3, rank0, rank1, rank2, peak0, lse0, rows_in, e_in,
    rows_out, e_out, rank_ref, peak_ref, stat_ref,
    vbuf, xa, xb, x67, cb, ea, eb, lse_scr, vsem, csem, xsem, osem, esem,
):
    load0 = pltpu.make_async_copy(source0, vbuf.at[0], vsem.at[0])
    load1 = pltpu.make_async_copy(source1, vbuf.at[1], vsem.at[1])
    near = pltpu.make_async_copy(rows_in.at[pl.ds(0, 6), pl.ds(512, 64), :], xa, xsem.at[0])
    far_rows = pltpu.make_async_copy(rows_in.at[pl.ds(6, 2), pl.ds(0, 576), :], xb, xsem.at[1])
    cents = [pltpu.make_async_copy(c, cb.at[k], csem.at[k]) for k, c in enumerate((c0, c1, c2, c3))]
    load0.start()
    load1.start()
    peak_ref[:, 0:512] = peak0[...]
    lse_scr[:, 0:512] = lse0[...]
    up = earlier()
    load0.wait()
    for copy in (near, cents[0], cents[1]):
        copy.start()
    rank = ranks(vbuf[0, TOK:EXT, :], blk_ref[:, 0:1], up)
    rank_ref[0] = rank
    x67[:, 0:MOST, :] = gathered(rank, vbuf[0, 0:TOK, :])
    load1.wait()
    for copy in (cents[2], cents[3], far_rows):
        copy.start()
    rank = ranks(vbuf[1, TOK:EXT, :], blk_ref[:, 0:1], up)
    rank_ref[1] = rank
    x67[:, MOST : 2 * MOST, :] = gathered(rank, vbuf[1, 0:TOK, :])
    back = pltpu.make_async_copy(x67, rows_out.at[pl.ds(0, NBLK), pl.ds(576, 2 * MOST), :], osem)
    back.start()
    near.wait()

    @pl.loop(0, 3)
    def _(q):
        pltpu.make_async_copy(c0, cb.at[q], csem.at[q]).wait()
        for i in range(2):
            b = 2 * q + i
            cent = cb[q, i * BS : (i + 1) * BS, :]
            e, peak, lse = score_chunk(cent, half_norm(cent), jnp.concatenate([xa[b], x67[b]], axis=0))
            ea[b] = e
            peak_ref[pl.ds(b, 1), 512:768] = peak
            lse_scr[pl.ds(b, 1), 512:768] = lse
            pltpu.make_async_copy(ea.at[b], e_out.at[b, :, pl.ds(512, 256)], esem.at[b]).start()

    cents[3].wait()
    far_rows.wait()
    for i in range(2):
        b = 6 + i
        cent = cb[3, i * BS : (i + 1) * BS, :]
        norm = half_norm(cent)
        chunks = (xb[i, 0:256, :], xb[i, 256:512, :], jnp.concatenate([xb[i, 512:576, :], x67[b]], axis=0))
        for k, rows in enumerate(chunks):
            e, peak, lse = score_chunk(cent, norm, rows)
            eb[i, :, k * 256 : (k + 1) * 256] = e
            peak_ref[b : b + 1, k * 256 : (k + 1) * 256] = peak
            lse_scr[b : b + 1, k * 256 : (k + 1) * 256] = lse
        pltpu.make_async_copy(eb.at[i], e_out.at[b], esem.at[b]).start()

    sources = [(ref, k) for ref in (rank0, rank1, rank2, rank_ref) for k in range(ref.shape[0])]
    for s, (ref, k) in enumerate(sources):
        k0, k1 = s * MOST // 128, (s * MOST + MOST - 1) // 128
        for j in range(TOK // 128):
            r = ref[k, :, j * 128 : (j + 1) * 128].astype(jnp.int32)
            at = r + s * MOST
            low = at & 127
            got = jnp.take_along_axis(lse_scr[:, k0 * 128 : (k0 + 1) * 128], low, axis=1, mode="promise_in_bounds")
            if k1 > k0:
                other = jnp.take_along_axis(
                    lse_scr[:, k1 * 128 : (k1 + 1) * 128], low, axis=1, mode="promise_in_bounds"
                )
                got = jnp.where((at >> 7) == k0, got, other)
            got = jnp.where(r >= 0, got, LOW)
            m = jnp.max(got, axis=0, keepdims=True)
            t = jnp.sum(jnp.exp(got - m), axis=0, keepdims=True)
            stat_ref[s : s + 1, j * 128 : (j + 1) * 128] = m + jnp.log(t)

    back.wait()
    for b in range(6):
        pltpu.make_async_copy(ea.at[b], e_out.at[b, :, pl.ds(512, 256)], esem.at[b]).wait()
    for i in range(2):
        pltpu.make_async_copy(eb.at[i], e_out.at[6 + i], esem.at[6 + i]).wait()


def late_scores(sources, blk, cents, ranked, peak0, lse0, rows, e):
    anywhere, hbm = pl.BlockSpec(memory_space=pl.ANY), pl.BlockSpec(memory_space=pltpu.HBM)
    vmem = pl.BlockSpec(memory_space=pltpu.VMEM)
    return pl.pallas_call(
        late_kernel,
        in_specs=[anywhere] * 2 + [vmem] + [anywhere] * 4 + [vmem] * 5 + [hbm] * 2,
        out_specs=(hbm, hbm, vmem, vmem, vmem),
        out_shape=(
            jax.ShapeDtypeStruct(ROWS, BF16),
            jax.ShapeDtypeStruct(SCORES, BF16),
            jax.ShapeDtypeStruct((2, NBLK, TOK), F32),
            jax.ShapeDtypeStruct((NBLK, SLOTS), F32),
            jax.ShapeDtypeStruct((NSRC, TOK), F32),
        ),
        scratch_shapes=[
            pltpu.VMEM((2, EXT, D), BF16),
            pltpu.VMEM((6, 64, D), BF16),
            pltpu.VMEM((2, 576, D), BF16),
            pltpu.VMEM((NBLK, 2 * MOST, D), BF16),
            pltpu.VMEM((4, 1024, D), BF16),
            pltpu.VMEM((6, BS, 256), BF16),
            pltpu.VMEM((2, BS, SLOTS), BF16),
            pltpu.VMEM((NBLK, SLOTS), F32),
            pltpu.SemaphoreType.DMA((2,)),
            pltpu.SemaphoreType.DMA((4,)),
            pltpu.SemaphoreType.DMA((2,)),
            pltpu.SemaphoreType.DMA,
            pltpu.SemaphoreType.DMA((8,)),
        ],
        input_output_aliases={12: 0, 13: 1},
        compiler_params=params(34),
        cost_estimate=cost(2 * 6 * BS * SLOTS * D, 20e6, 4 * BS * SLOTS),
        name="late_scores",
    )(*sources, blk, *cents, *ranked, peak0, lse0, rows, e)


def factor_kernel(stat_refs, idx_ref, peak_ref, f_scr):
    own, from_d, from_e, from_f = stat_refs
    tables = []
    for s in range(NSRC):
        parts = [own[s : s + 1, :]]
        for ref, order in ((from_d, FROM_D), (from_e, FROM_E), (from_f, FROM_F)):
            parts.append(ref[order[s] : order[s] + 1, :])
        m = jnp.maximum(jnp.maximum(parts[0], parts[1]), jnp.maximum(parts[2], parts[3]))
        t = jnp.exp(parts[0] - m)
        for k in range(1, 4):
            t = t + jnp.exp(parts[k] - m)
        tables.append(m + jnp.log(t))
    for k in range(SLOTS // 128):
        at = idx_ref[:, k * 128 : (k + 1) * 128]
        low = at & 127
        high = at >> 7
        lse = jnp.zeros((NBLK, 128), F32)
        for s in range(k * 128 // MOST, (k * 128 + 127) // MOST + 1):
            for j in range(TOK // 128):
                table = jnp.broadcast_to(tables[s][:, j * 128 : (j + 1) * 128], (NBLK, 128))
                got = jnp.take_along_axis(table, low, axis=1, mode="promise_in_bounds")
                lse = jnp.where(high == s * (TOK // 128) + j, got, lse)
        f = jnp.exp(peak_ref[:, k * 128 : (k + 1) * 128] - lse)
        f_scr[:, k * 128 : (k + 1) * 128] = jnp.where(at >= 0, f, 0.0)


def sums_owner(i):
    t = i % 4
    return jnp.where(t == 0, 3, jnp.where(t == 3, 0, t))


def sums_kernel(where_ref, s0, s1, s2, s3, idx_any, peak_any, e_any, rows_any, *refs):
    outs, (f_scr, hbuf, gbuf, gcount, gtile, stats, idx_ref, peak_ref, e_buf, rows_buf, hsem, gsem, tsem, ssem, esem, rsem) = refs[:8], refs[8:]
    i = pl.program_id(0)
    q, slot = sums_owner(i), i % 2

    def send_h(k, slot=slot):
        return pltpu.make_async_copy(hbuf.at[slot], outs[k], hsem.at[slot])

    def send_g(k, slot=slot):
        start = pl.multiple_of(q * 128, 128)
        return pltpu.make_async_copy(gbuf.at[slot, k], outs[4 + k].at[pl.ds(start, 128), :], gsem.at[slot, k])

    def send_tile(k):
        return pltpu.make_async_copy(gtile.at[k], outs[4 + k].at[pl.ds(BS, EXTRA), :], tsem.at[k])

    def load_block(k):
        b = 2 * sums_owner(k) + k // 4
        pltpu.make_async_copy(e_any.at[b], e_buf.at[k], esem.at[k]).start()
        pltpu.make_async_copy(rows_any.at[b], rows_buf.at[k], rsem.at[k]).start()

    @pl.when(i == 0)
    def _():
        loads = [pltpu.make_async_copy(s, stats.at[k], ssem.at[k]) for k, s in enumerate((s0, s1, s2, s3))]
        loads.append(pltpu.make_async_copy(idx_any, idx_ref, ssem.at[4]))
        loads.append(pltpu.make_async_copy(peak_any, peak_ref, ssem.at[5]))
        for load in loads:
            load.start()
        for k in range(2):
            load_block(k)
        for load in loads:
            load.wait()
        factor_kernel([stats.at[k] for k in range(4)], idx_ref, peak_ref, f_scr)
        gcount[...] = jnp.zeros_like(gcount)

    @pl.when(i < 6)
    def _():
        load_block(i + 2)

    f = f_scr[pl.ds(2 * q + i // 4, 1), :]
    pltpu.make_async_copy(e_any.at[0], e_buf.at[i], esem.at[i]).wait()
    pltpu.make_async_copy(rows_any.at[0], rows_buf.at[i], rsem.at[i]).wait()
    totals, counts = [], []
    for m in range(4):
        w = e_buf[i, m * 128 : (m + 1) * 128, :].astype(F32) * f
        count = jnp.sum(w, axis=1, keepdims=True)
        counts.append(jnp.transpose(jnp.broadcast_to(count, (128, 128)))[0:EXTRA])
        totals.append(jnp.dot(w.astype(BF16), rows_buf[i], preferred_element_type=F32).astype(BF16))

    @pl.when((i == 2) | (i == 3))
    def _():
        send_h(0).wait()

    @pl.when((i == 6) | (i == 7))
    def _():
        for k in range(4):
            send_g(k).wait()

    @pl.when(i < 4)
    def _():
        for m in range(4):
            hbuf[slot, m * 128 : (m + 1) * 128, :] = totals[m]
        tile = jnp.concatenate([*counts, jnp.zeros((EXTRA, D - BS), F32)], axis=1)
        hbuf[slot, BS : BS + EXTRA, :] = tile.astype(BF16)
        for k in range(4):
            @pl.when(q == k)
            def _(k=k):
                send_h(k).start()

    @pl.when(i >= 4)
    def _():
        for m in range(4):
            at = sum(jnp.where(where_ref[4 + k] == m, k, 0) for k in range(1, 4))
            gbuf[slot, at] = totals[m]
            gcount[at, pl.ds(q, 1), :] = counts[m][0:1]
        for k in range(4):
            send_g(k).start()

    @pl.when(i == 7)
    def _():
        for k in range(4):
            tile = jnp.concatenate([gcount[k], jnp.zeros((8, 128), F32)], axis=0)
            tile = jnp.concatenate([tile, jnp.zeros((EXTRA, D - 128), F32)], axis=1)
            gtile[k] = tile.astype(BF16)
            send_tile(k).start()
        for other in range(2):
            send_h(0, other).wait()
            for k in range(4):
                send_g(k, other).wait()
        for k in range(4):
            send_tile(k).wait()


def sums(where, stats, idx, peak, e, rows):
    shape = (BS + EXTRA, D)
    out = pl.pallas_call(
        sums_kernel,
        grid=(8,),
        in_specs=[pl.BlockSpec(memory_space=pltpu.SMEM)]
        + [pl.BlockSpec(memory_space=pl.ANY)] * 6
        + [pl.BlockSpec(memory_space=pltpu.HBM)] * 2,
        out_specs=tuple([pl.BlockSpec(memory_space=pl.ANY)] * 8),
        out_shape=tuple([jax.ShapeDtypeStruct(shape, BF16)] * 8),
        scratch_shapes=[
            pltpu.VMEM((NBLK, SLOTS), F32),
            pltpu.VMEM((2, *shape), BF16),
            pltpu.VMEM((2, 4, 128, D), BF16),
            pltpu.VMEM((4, 8, 128), F32),
            pltpu.VMEM((4, EXTRA, D), BF16),
            pltpu.VMEM((4, NSRC, TOK), F32),
            pltpu.VMEM((NBLK, SLOTS), jnp.int32),
            pltpu.VMEM((NBLK, SLOTS), F32),
            pltpu.VMEM((NBLK, BS, SLOTS), BF16),
            pltpu.VMEM((NBLK, SLOTS, D), BF16),
            pltpu.SemaphoreType.DMA((2,)),
            pltpu.SemaphoreType.DMA((2, 4)),
            pltpu.SemaphoreType.DMA((4,)),
            pltpu.SemaphoreType.DMA((6,)),
            pltpu.SemaphoreType.DMA((8,)),
            pltpu.SemaphoreType.DMA((8,)),
        ],
        compiler_params=params(54),
        cost_estimate=cost(2 * 8 * BS * SLOTS * D, 24e6),
        name="sums",
    )(where, *stats, idx, peak, e, rows)
    return out[:4], out[4:]


def fetched(refs, buf, sem):
    copies = [pltpu.make_async_copy(ref, buf.at[k], sem.at[k]) for k, ref in enumerate(refs)]
    for copy in copies:
        copy.start()
    for copy in copies:
        copy.wait()
    return [buf.at[k] for k in range(len(refs))]


def parted_kernel(where_ref, *refs):
    outs, (acc, buf, sem) = refs[6:14], refs[14:]
    h0, h1, h2, g0, g1, g2 = fetched(refs[:6], buf, sem)

    def tile(counts):
        counts = jnp.broadcast_to(counts, (EXTRA, 128))
        return jnp.concatenate([counts, jnp.zeros((EXTRA, D - 128), F32)], axis=1).astype(BF16)

    acc[...] = h0[...].astype(F32) + h1[...].astype(F32) + h2[...].astype(F32)
    counts = acc[BS : BS + 8, 0:BS]
    for k in range(4):
        part = where_ref[4 + k]
        outs[k][0:128, :] = acc[pl.ds(pl.multiple_of(part * 128, 128), 128), :].astype(BF16)
        picked = counts[:, 0:128]
        for m in range(1, 4):
            picked = jnp.where(part == m, counts[:, m * 128 : (m + 1) * 128], picked)
        outs[k][128:, :] = tile(picked[0:1])
    counts = g0[BS:, 0:128].astype(F32) + g1[BS:, 0:128].astype(F32) + g2[BS:, 0:128].astype(F32)
    for k in range(4):
        rows = slice(k * 128, (k + 1) * 128)
        total = g0[rows, :].astype(F32) + g1[rows, :].astype(F32) + g2[rows, :].astype(F32)
        outs[4 + k][0:128, :] = total.astype(BF16)
        outs[4 + k][128:, :] = tile(counts[k : k + 1])


def parted(where, h, g):
    vmem = pl.BlockSpec(memory_space=pltpu.VMEM)
    out = pl.pallas_call(
        parted_kernel,
        in_specs=[pl.BlockSpec(memory_space=pltpu.SMEM)] + [pl.BlockSpec(memory_space=pl.ANY)] * 6,
        out_specs=(vmem,) * 8,
        out_shape=(jax.ShapeDtypeStruct((128 + EXTRA, D), BF16),) * 8,
        scratch_shapes=[
            pltpu.VMEM((BS + EXTRA, D), F32),
            pltpu.VMEM((6, BS + EXTRA, D), BF16),
            pltpu.SemaphoreType.DMA((6,)),
        ],
        compiler_params=params(16),
        cost_estimate=cost(1e6, 8e6),
        name="parted",
    )(where, *h, *g)
    return out[:4], out[4:]


def final_kernel(*refs):
    mine_ref, out_ref, buf, sem = refs[8:]
    h0, h1, h2, h3, g0, g1, g2, g3 = fetched(refs[:8], buf, sem)
    for i, refs in enumerate(((h0, h1, h2, h3), (g0, g1, g2, g3))):
        total = (refs[0][...].astype(F32) + refs[1][...].astype(F32)) + (refs[2][...].astype(F32) + refs[3][...].astype(F32))
        column = jnp.transpose(jnp.broadcast_to(total[128:129, 0:128], (128, 128)))[:, 0:1]
        out_ref[i] = ((total[0:128] + mine_ref[i].astype(F32)) / (column + 1.0)).astype(BF16)


def final(h, g, mine):
    return pl.pallas_call(
        final_kernel,
        in_specs=[pl.BlockSpec(memory_space=pl.ANY)] * 8 + [pl.BlockSpec(memory_space=pltpu.VMEM)],
        out_specs=pl.BlockSpec(memory_space=pltpu.VMEM),
        out_shape=jax.ShapeDtypeStruct((2, 128, D), BF16),
        scratch_shapes=[pltpu.VMEM((8, 128 + EXTRA, D), BF16), pltpu.SemaphoreType.DMA((8,))],
        compiler_params=params(8),
        cost_estimate=cost(1e6, 2e6),
        name="final",
    )(*h, *g, mine)


def place_kernel(where_ref, *refs):
    parts, (out_ref, buf, in_sem, out_sem) = refs[:8], refs[8:]
    loads = [pltpu.make_async_copy(part, buf.at[k], in_sem.at[k]) for k, part in enumerate(parts)]
    copies = []
    for side in range(2):
        for k in range(4):
            for i in range(2):
                block = where_ref[8 + side] * 2 + i
                quarter = where_ref[4 * side + k]
                copies.append(
                    pltpu.make_async_copy(
                        buf.at[side * 4 + k, i], out_ref.at[block, quarter], out_sem.at[len(copies)]
                    )
                )
    for load in loads:
        load.start()
    for k, load in enumerate(loads):
        load.wait()
        copies[2 * k].start()
        copies[2 * k + 1].start()
    for copy in copies:
        copy.wait()


def place(where, parts):
    return pl.pallas_call(
        place_kernel,
        in_specs=[pl.BlockSpec(memory_space=pltpu.SMEM)] + [pl.BlockSpec(memory_space=pl.ANY)] * 8,
        out_specs=pl.BlockSpec(memory_space=pl.ANY),
        out_shape=jax.ShapeDtypeStruct((4, 4, 128, D), BF16),
        scratch_shapes=[
            pltpu.VMEM((8, 2, 128, D), BF16),
            pltpu.SemaphoreType.DMA((8,)),
            pltpu.SemaphoreType.DMA((16,)),
        ],
        compiler_params=params(8),
        cost_estimate=cost(0, 6e6),
        name="place",
    )(where, *parts)


def tie(a, *after):
    return pl.pallas_call(
        lambda *refs: None,
        in_specs=[pl.BlockSpec(memory_space=pl.ANY)] * (1 + len(after)),
        out_specs=pl.BlockSpec(memory_space=pl.ANY),
        out_shape=jax.ShapeDtypeStruct(a.shape, a.dtype),
        input_output_aliases={0: 0},
        compiler_params=params(8),
        cost_estimate=cost(0, 0),
        name="tie",
    )(a, *after)


def add(*terms):
    total = terms[0].astype(F32)
    for t in terms[1:]:
        total = total + t.astype(F32)
    return total


def ring_terms(own, d, e, f, axis):
    r1 = turn(f, axis, 1)
    r2 = turn(d, axis, -1)
    r3 = turn(add(e, r1).astype(BF16), axis, 1)
    return own, r2, r3


def direct_terms(own, d, e, f, axis):
    return own, turn(d, axis, -1), turn(e, axis, 1), far(f, axis)


def body(vectors, centroids, candidates):
    core, x, y, z = (lax.axis_index(a) for a in ("core", "x", "y", "z"))
    step = 1 - 2 * core

    def around(i):
        return jnp.stack([i, (i - step) % 4, (i + step) % 4, (i + 2) % 4]).astype(jnp.int32)

    xs, zs = around(x), around(z)
    other_zs = jnp.stack([zs[0], zs[2], zs[1], zs[3]])

    where = jnp.concatenate([xs, zs])
    tail = jnp.pad(candidates.T.reshape(8, 512).astype(BF16), ((0, EXTRA - 8), (0, D - 512)))
    v = jnp.concatenate([vectors, tail])
    a, b = turn(v, "y", 1), turn(v, "y", -1)
    c0 = lax.dynamic_slice_in_dim(centroids, core * 1024, 1024, 0)
    c1, c2 = turn(c0, "x", 1), turn(c0, "x", -1)
    mine = lax.dynamic_slice_in_dim(c0.reshape(2, BS, D), z * 128, 128, 1)
    blk = ((y * 4 + xs) * 4 + 2 * core)[:, None] + jnp.arange(2, dtype=jnp.int32)[None, :]
    blk = jnp.broadcast_to(blk.reshape(NBLK, 1), (NBLK, 128)).astype(F32)

    rank0, rows = dispatch(0, (v, swap(v)), blk, None)
    a = tie(a, rank0, b, c1, c2)
    c = turn(a, "y", 1)
    c3 = turn(c1, "x", 1)
    rank1, rows = dispatch(2, (a, b), blk, rows)
    rows, rank2, e, peak0, lse0 = middle((swap(a), swap(b)), blk, (c0, c1, c2), rows)
    c = tie(c, lse0, c3)
    ranked = (rank0, rank1, rank2)
    rows, e, rank3, peak, stat = late_scores((c, swap(c)), blk, (c0, c1, c2, c3), ranked, peak0, lse0, rows, e)
    idx = indices(*ranked, rank3)

    theirs = swap(stat)
    theirs = jnp.concatenate([theirs[s : s + 1] for s in SWAPPED])
    m = jnp.maximum(stat, theirs)
    merged = m + jnp.log(jnp.exp(stat - m) + jnp.exp(theirs - m))
    stats = (merged, turn(merged, "y", 1), turn(merged, "y", -1), far(merged, "y"))

    h, g = sums(where, stats, idx, peak, e, rows)
    h, g = ring_terms(*h, "x"), ring_terms(*g, "z")
    h, g = parted(where, h, g)
    h, g = direct_terms(*h, "z"), direct_terms(*g, "x")
    fresh = final(h, g, mine)

    others = [turn(fresh, "z", 1), turn(fresh, "z", -1), far(fresh, "z")]
    parts = [fresh, *others] + [swap(p) for p in (fresh, *others)]
    places = jnp.concatenate([zs, other_zs, jnp.stack([core, 1 - core])]).astype(jnp.int32)
    return place(places, parts).reshape(2048, D)


def solution(mesh):
    fine = Mesh(np.asarray(mesh.devices).reshape(4, 2, 4, 4), ("z", "core", "y", "x"))
    return jax.shard_map(
        body,
        mesh=fine,
        in_specs=(P(("z", "core", "y", "x"), None), P(("y", "x"), None), P(("z", "core", "y", "x"), None)),
        out_specs=P(("y", "x"), None),
        check_vma=False,
    )
```

time: 214 us -> 190 us (0.89); the launches traced: 211 us -> 190 us
  Pallas kernels: 81 us -> 56.9 us
  waiting for transfers between devices: 53.6 us -> 62.6 us
  local copies, waits for them, and re-layouts: 9.83 us -> 5.1 us
    pallas_call x4 -> x2, Pallas kernels: 24.8 us -> 12 us  [dispatch(): pl.pallas_call(kern, grid=(n,), in_specs=in_specs, out_specs=(pl.BlockSpe...]
    pallas_call x3, Pallas kernels: 30.2 us -> 24.1 us  [the longest x1 11 us: late_scores(): pl.pallas_call(late_kernel, in_specs=[anywhere] * 2 + [vmem] + [anywhere]...]
    ppermute x9, waiting for transfers between devices: 1.4 us -> 5.65 us  [swap(): return lax.ppermute(a, 'core', [(0, 1), (1, 0)])]
    ppermute x20, waiting for transfers between devices: 50.3 us -> 53.6 us  [turn(): return lax.ppermute(a, axes, pairs)]
    unnamed x30 -> x24, local copies, waits for them, and re-layouts: 4.61 us -> 1.84 us
  transfers between devices with their start and end apart: 33 -> 33, of which waited for: 10 -> 16; matrix products, arithmetic and copies ran while one was open for 3% -> 3% of each run, Pallas kernels for 19% -> 14%
where the time goes in v3:
time: 190 us
  waiting for transfers between devices  62.6 us (33%)
  starting transfers between devices  59.5 us (31%)
  Pallas kernels  56.9 us (30%)
  other arithmetic  5.35 us (3%)
  local copies, waits for them, and re-layouts  5.1 us (3%)
    ppermute x20, waiting for transfers between devices, turn(): return lax.ppermute(a, axes, pairs)  53.6 us
    ppermute x20, starting transfers between devices, turn(): return lax.ppermute(a, axes, pairs)  32.7 us
    ppermute x9, starting transfers between devices, swap(): return lax.ppermute(a, 'core', [(0, 1), (1, 0)])  22.2 us
    pallas_call x2, Pallas kernels, dispatch(): pl.pallas_call(kern, grid=(n,), in_specs=in_specs, out_specs=(pl.BlockSpe...  12 us
    pallas_call x1, Pallas kernels, sums(): pl.pallas_call(sums_kernel, grid=(8,), in_specs=[pl.BlockSpec(memory_spac...  11.5 us
    pallas_call x1, Pallas kernels, late_scores(): pl.pallas_call(late_kernel, in_specs=[anywhere] * 2 + [vmem] + [anywhere]...  11 us
    pallas_call x1, Pallas kernels, middle(): pl.pallas_call(middle_kernel, in_specs=[anywhere] * 2 + [vmem] + [anywher...  10.4 us
    ppermute x9, waiting for transfers between devices, swap(): return lax.ppermute(a, 'core', [(0, 1), (1, 0)])  5.65 us
  transfers between devices with their start and end apart: 33, of which 16 were waited for; matrix products, arithmetic and copies ran while one was open for 3% of the time, Pallas kernels for 14%

profile of v3, /device:TPU:1, one launch (start us, length us, event | category | flops | bytes accessed | tf_op | source)
XLA Modules:
  0.0 189.9 jit_solution(11447309025732485690)
XLA Ops:
  0.9 2.7 %fusion.1.refs_0_ = bf16[1040,768]{1,0:T(8,128)(2,1)} fusion(bf16[8,512]{1,0:T(8,128)(2,1)S(1)} %convert_element_type.36, bf16[1024,768]{1,0:T(8,128)(2,1)} %param.3), kind=kLoop, calls=%fused_computation.4 | loop fusion | flops 4792320 | bytes 3178496 | tf_op jit(solution)/shard_map/concatenate | solution.py:701
  5.0 2.8 %collective-permute-start = (bf16[1040,768]{1,0:T(8,128)(2,1)}, bf16[1040,768]{1,0:T(8,128)(2,1)}, u32[]{:S(2)}, u32[]{:S(2)}) collective-permute-start(bf16[1040,768]{1,0:T(8,128)(2,1)} %fusion.1.refs_0_), channel_id=1, source_target_pairs={{0,4},{4,8},{8,12},{12,0},{16,28},{20,16},{24,20},{28,24},{1,5},{5... | collective-permute-start | bytes 4792328 | tf_op jit(solution)/shard_map/ppermute | solution.py:44
  9.1 2.5 %collective-permute-start.3 = (bf16[1024,768]{1,0:T(8,128)(2,1)}, bf16[1024,768]{1,0:T(8,128)(2,1)S(1)}, u32[]{:S(2)}, u32[]{:S(2)}) collective-permute-start(bf16[1024,768]{1,0:T(8,128)(2,1)} %constant_dynamic-slice_fusion.1.c0), channel_id=1, source_target_pairs={{0,1},{1,2},{2,3},{3,0},{16,19},{17,16},{18,17},{19,18},{4,5},{5,6... | collective-permute-start | bytes 4718600 | tf_op jit(solution)/shard_map/ppermute | solution.py:44
  11.9 6.0 %dispatch0.1 = (f32[2,8,1024]{2,1,0:T(8,128)S(1)}, bf16[28,768,768]{2,1,0:T(8,128)(2,1)}) custom-call(bf16[1040,768]{1,0:T(8,128)(2,1)} %fusion.1.refs_0_, bf16[1040,768]{1,0:T(8,128)(2,1)} %collective-permute-done.1.refs_1_, f32[8,128]{1,0:T(8,128)S(1)} %broadcast_in_dim.2.refs_2_.blk_ref), custom_call_target="tpu_custom_call" | custom-call | flops 2415919104 | bytes 6000000 | tf_op jit(solution)/shard_map/dispatch0/pallas_call | solution.py:157
  17.9 26.8 %collective-permute-done.3.refs_3_.c1 = bf16[1024,768]{1,0:T(8,128)(2,1)S(1)} collective-permute-done((bf16[1024,768]{1,0:T(8,128)(2,1)}, bf16[1024,768]{1,0:T(8,128)(2,1)S(1)}, u32[]{:S(2)}, u32[]{:S(2)}) %collective-permute-start.3) | collective-permute-done | bytes 1572896 | tf_op jit(solution)/shard_map/ppermute | solution.py:44
  44.7 2.8 %collective-permute-done.4.refs_4_.c2 = bf16[1024,768]{1,0:T(8,128)(2,1)S(1)} collective-permute-done((bf16[1024,768]{1,0:T(8,128)(2,1)}, bf16[1024,768]{1,0:T(8,128)(2,1)S(1)}, u32[]{:S(2)}, u32[]{:S(2)}) %collective-permute-start.4) | collective-permute-done | bytes 1572896 | tf_op jit(solution)/shard_map/ppermute | solution.py:44
  48.2 1.6 collective-permute-start.5
  49.8 2.9 %collective-permute-start.8 = (bf16[1024,768]{1,0:T(8,128)(2,1)S(1)}, bf16[1024,768]{1,0:T(8,128)(2,1)S(1)}, u32[]{:S(2)}, u32[]{:S(2)}) collective-permute-start(bf16[1024,768]{1,0:T(8,128)(2,1)S(1)} %collective-permute-done.3.refs_3_.c1), channel_id=1, source_target_pairs={{0,1},{1,2},{2,3},{3,0},{16,19},{17,16},{18,17},{19,18},{4,5},{5,6... | collective-permute-start | bytes 4718600 | tf_op jit(solution)/shard_map/ppermute | solution.py:44
  52.7 6.0 %dispatch2.1 = (f32[2,8,1024]{2,1,0:T(8,128)S(1)}, bf16[28,768,768]{2,1,0:T(8,128)(2,1)}) custom-call(bf16[1040,768]{1,0:T(8,128)(2,1)} %tie.2.refs_0_, bf16[1040,768]{1,0:T(8,128)(2,1)} %collective-permute-done.2.refs_2_.refs_1_, f32[8,128]{1,0:T(8,128)S(1)} %broadcast_in_dim.2.refs_2_.blk_ref, ...), custom_call_target="tpu_custom_call", output_to_operand_aliasing={{1}: (3, {})} | custom-call | flops 2415919104 | bytes 6000000 | tf_op jit(solution)/shard_map/dispatch2/pallas_call | solution.py:157
  58.8 10.4 %middle.1 = (bf16[28,768,768]{2,1,0:T(8,128)(2,1)}, f32[2,8,1024]{2,1,0:T(8,128)S(1)}, bf16[40,512,768]{2,1,0:T(8,128)(2,1)}, f32[8,512]{1,0:T(8,128)S(1)}, f32[8,512]{1,0:T(8,128)S(1)}) custom-call(bf16[1040,768]{1,0:T(8,128)(2,1)S(1)} %collective-permute-done.6.s0, ...), custom_call_target="tpu_custom_call", output_to_operand_aliasing={{0}: (6, {})} | custom-call | flops 2415919104 | bytes 20000000 | tf_op jit(solution)/shard_map/middle/pallas_call | solution.py:236
  70.4 3.1 %collective-permute-done.9.source1 = bf16[1040,768]{1,0:T(8,128)(2,1)S(1)} collective-permute-done((bf16[1040,768]{1,0:T(8,128)(2,1)S(1)}, bf16[1040,768]{1,0:T(8,128)(2,1)S(1)}, u32[]{:S(2)}, u32[]{:S(2)}) %collective-permute-start.9) | collective-permute-done | bytes 1597472 | tf_op jit(solution)/shard_map/ppermute | solution.py:52
  73.5 11.0 %late_scores.1 = (bf16[28,768,768]{2,1,0:T(8,128)(2,1)}, bf16[40,512,768]{2,1,0:T(8,128)(2,1)}, f32[2,8,1024]{2,1,0:T(8,128)S(1)}, f32[8,768]{1,0:T(8,128)S(1)}, f32[8,1024]{1,0:T(8,128)S(1)}) custom-call(bf16[1040,768]{1,0:T(8,128)(2,1)S(1)} %tie.3.source0, ...), custom_call_target="tpu_custom_call", output_to_operand_aliasing={{0}: (12, {}), {1}: (13, {})} | custom-call | flops 3623878656 | bytes 20000000 | tf_op jit(solution)/shard_map/late_scores/pallas_call | solution.py:351
  86.4 2.5 %collective-permute-start.11 = (f32[8,1024]{1,0:T(8,128)S(1)}, f32[8,1024]{1,0:T(8,128)S(1)}, u32[]{:S(2)}, u32[]{:S(2)}) collective-permute-start(f32[8,1024]{1,0:T(8,128)S(1)} %log_add_fusion.s0), channel_id=1, source_target_pairs={{0,4},{4,8},{8,12},{12,0},{16,28},{20,16},{24,20},{28,24},{1,5},{5... | collective-permute-start | bytes 98312 | tf_op jit(solution)/shard_map/ppermute | solution.py:44
  88.9 1.9 collective-permute-start.13
  90.8 3.4 %indices.1.idx_any = s32[8,768]{1,0:T(8,128)S(1)} custom-call(f32[2,8,1024]{2,1,0:T(8,128)S(1)} %get-tuple-element.35.refs_1_.rank0.refs_0_, f32[2,8,1024]{2,1,0:T(8,128)S(1)} %get-tuple-element.39.rank1.refs_1_, f32[2,8,1024]{2,1,0:T(8,128)S(1)} %get-tuple-element.40.rank2.refs_2_, f32[2,8,1024]{2,1,0:T(8,128)S(1)} %get-tuple-element.45.refs_3_), custom_call_target="tpu_custom_call" | custom-call | flops 4000000000 | bytes 1000000 | tf_op jit(solution)/shard_map/indices/pallas_call | solution.py:110
  95.5 11.5 %sums.1 = (bf16[528,768]{1,0:T(8,128)(2,1)}, bf16[528,768]{1,0:T(8,128)(2,1)}, bf16[528,768]{1,0:T(8,128)(2,1)}, bf16[528,768]{1,0:T(8,128)(2,1)}, bf16[528,768]...) custom-call(s32[8]{0:T(128)} %concatenate.20.where_ref, ...), custom_call_target="tpu_custom_call" | custom-call | flops 4831838208 | bytes 24000000 | tf_op jit(solution)/shard_map/sums/pallas_call | solution.py:509
  107.0 1.8 collective-permute-start.15
  108.8 3.8 %collective-permute-start.18 = (bf16[528,768]{1,0:T(8,128)(2,1)}, bf16[528,768]{1,0:T(8,128)(2,1)S(1)}, u32[]{:S(2)}, u32[]{:S(2)}) collective-permute-start(bf16[528,768]{1,0:T(8,128)(2,1)} %get-tuple-element.56), channel_id=1, source_target_pairs={{0,32},{32,64},{64,96},{96,0},{16,112},{48,16},{80,48},{112,80},{1... | collective-permute-start | bytes 2433032 | tf_op jit(solution)/shard_map/ppermute | solution.py:44
  112.6 11.1 %collective-permute-done.15 = bf16[528,768]{1,0:T(8,128)(2,1)S(1)} collective-permute-done((bf16[528,768]{1,0:T(8,128)(2,1)}, bf16[528,768]{1,0:T(8,128)(2,1)S(1)}, u32[]{:S(2)}, u32[]{:S(2)}) %collective-permute-start.15) | collective-permute-done | bytes 811040 | tf_op jit(solution)/shard_map/ppermute | solution.py:44
  125.1 1.9 collective-permute-start.16
  127.8 5.1 %collective-permute-start.19 = (bf16[528,768]{1,0:T(8,128)(2,1)S(1)}, bf16[528,768]{1,0:T(8,128)(2,1)S(1)}, u32[]{:S(2)}, u32[]{:S(2)}) collective-permute-start(bf16[528,768]{1,0:T(8,128)(2,1)S(1)} %add_convert_fusion), channel_id=1, source_target_pairs={{0,32},{32,64},{64,96},{96,0},{16,112},{48,16},{80,48},{112,80},{1... | collective-permute-start | bytes 2433032 | tf_op jit(solution)/shard_map/ppermute | solution.py:44
  132.9 3.6 %collective-permute-done.16.refs_2_ = bf16[528,768]{1,0:T(8,128)(2,1)S(1)} collective-permute-done((bf16[528,768]{1,0:T(8,128)(2,1)S(1)}, bf16[528,768]{1,0:T(8,128)(2,1)S(1)}, u32[]{:S(2)}, u32[]{:S(2)}) %collective-permute-start.16) | collective-permute-done | bytes 811040 | tf_op jit(solution)/shard_map/ppermute | solution.py:44
  136.5 5.6 %collective-permute-done.19.refs_5_ = bf16[528,768]{1,0:T(8,128)(2,1)S(1)} collective-permute-done((bf16[528,768]{1,0:T(8,128)(2,1)S(1)}, bf16[528,768]{1,0:T(8,128)(2,1)S(1)}, u32[]{:S(2)}, u32[]{:S(2)}) %collective-permute-start.19) | collective-permute-done | bytes 811040 | tf_op jit(solution)/shard_map/ppermute | solution.py:44
  142.1 2.3 %parted.1 = (bf16[144,768]{1,0:T(8,128)(2,1)S(1)}, bf16[144,768]{1,0:T(8,128)(2,1)S(1)}, bf16[144,768]{1,0:T(8,128)(2,1)S(1)}, bf16[144,768]{1,0:T(8,128)(2,1)S(...) custom-call(s32[8]{0:T(128)S(1)} %copy-done.6, ...), custom_call_target="tpu_custom_call" | custom-call | flops 1000000 | bytes 8000000 | tf_op jit(solution)/shard_map/parted/pallas_call | solution.py:578
  144.5 3.5 %collective-permute-start.21 = (bf16[144,768]{1,0:T(8,128)(2,1)S(1)}, bf16[144,768]{1,0:T(8,128)(2,1)S(1)}, u32[]{:S(2)}, u32[]{:S(2)}) collective-permute-start(bf16[144,768]{1,0:T(8,128)(2,1)S(1)} %get-tuple-element.59), channel_id=1, source_target_pairs={{0,32},{32,64},{64,96},{96,0},{16,112},{48,16},{80,48},{112,80},{1... | collective-permute-start | bytes 663560 | tf_op jit(solution)/shard_map/ppermute | solution.py:44
  149.0 2.7 %collective-permute-start.24 = (bf16[144,768]{1,0:T(8,128)(2,1)S(1)}, bf16[144,768]{1,0:T(8,128)(2,1)S(1)}, u32[]{:S(2)}, u32[]{:S(2)}) collective-permute-start(bf16[144,768]{1,0:T(8,128)(2,1)S(1)} %get-tuple-element.63), channel_id=1, source_target_pairs={{0,1},{1,2},{2,3},{3,0},{16,19},{17,16},{18,17},{19,18},{4,5},{5,6... | collective-permute-start | bytes 663560 | tf_op jit(solution)/shard_map/ppermute | solution.py:44
  152.8 2.0 %collective-permute-done.22.refs_3_ = bf16[144,768]{1,0:T(8,128)(2,1)S(1)} collective-permute-done((bf16[144,768]{1,0:T(8,128)(2,1)S(1)}, bf16[144,768]{1,0:T(8,128)(2,1)S(1)}, u32[]{:S(2)}, u32[]{:S(2)}) %collective-permute-start.22) | collective-permute-done | bytes 221216 | tf_op jit(solution)/shard_map/ppermute | solution.py:48
  155.0 1.9 %collective-permute-done.24.refs_6_ = bf16[144,768]{1,0:T(8,128)(2,1)S(1)} collective-permute-done((bf16[144,768]{1,0:T(8,128)(2,1)S(1)}, bf16[144,768]{1,0:T(8,128)(2,1)S(1)}, u32[]{:S(2)}, u32[]{:S(2)}) %collective-permute-start.24) | collective-permute-done | bytes 221216 | tf_op jit(solution)/shard_map/ppermute | solution.py:44
  158.3 2.7 %final.1.refs_0_ = bf16[2,128,768]{2,1,0:T(8,128)(2,1)S(1)} custom-call(bf16[144,768]{1,0:T(8,128)(2,1)S(1)} %get-tuple-element.57.refs_0_, bf16[144,768]{1,0:T(8,128)(2,1)S(1)} %collective-permute-done.20.refs_1_, bf16[144,768]{1,0:T(8,128)(2,1)S(1)} %collective-permute-done.21.refs_2_, bf16[144,768]{1,0:T(8,128)(2,1)S(1)} %collective-permute-done.22.refs_3_, ...), custom_call_target="tpu_custom_call" | custom-call | flops 1000000 | bytes 2000000 | tf_op jit(solution)/shard_map/final/pallas_call | solution.py:605
  164.1 9.0 %collective-permute-start.29 = (bf16[2,128,768]{2,1,0:T(8,128)(2,1)S(1)}, bf16[2,128,768]{2,1,0:T(8,128)(2,1)}, u32[]{:S(2)}, u32[]{:S(2)}) collective-permute-start(bf16[2,128,768]{2,1,0:T(8,128)(2,1)S(1)} %final.1.refs_0_), channel_id=1, source_target_pairs={{0,16},{16,0},{1,17},{17,1},{2,18},{18,2},{3,19},{19,3},{4,20},{20... | collective-permute-start | bytes 1179656 | tf_op jit(solution)/shard_map/ppermute | solution.py:52
  173.1 10.2 %collective-permute-start.30 = (bf16[2,128,768]{2,1,0:T(8,128)(2,1)}, bf16[2,128,768]{2,1,0:T(8,128)(2,1)}, u32[]{:S(2)}, u32[]{:S(2)}) collective-permute-start(bf16[2,128,768]{2,1,0:T(8,128)(2,1)} %collective-permute-done.26.refs_1_), channel_id=1, source_target_pairs={{0,16},{16,0},{1,17},{17,1},{2,18},{18,2},{3,19},{19,3},{4,20},{20... | collective-permute-start | bytes 1179656 | tf_op jit(solution)/shard_map/ppermute | solution.py:52
  186.1 3.6 %place.1 = bf16[4,4,128,768]{3,2,1,0:T(8,128)(2,1)} custom-call(s32[10]{0:T(128)S(1)} %concatenate.19.where_ref, bf16[2,128,768]{2,1,0:T(8,128)(2,1)S(1)} %final.1.refs_0_, bf16[2,128,768]{2,1,0:T(8,128)(2,1)} %collective-permute-done.26.refs_1_, bf16[2,128,768]{2,1,0:T(8,128)(2,1)} %collective-permute-done.27.refs_2_, ...), custom_call_target="tpu_custom_call" | custom-call | bytes 6000000 | tf_op jit(solution)/shard_map/place/pallas_call | solution.py:642
  (86 shorter events, 20.7 us)
Async XLA Ops:
  3.6 8.2 %collective-permute-start.1 = (bf16[1040,768]{1,0:T(8,128)(2,1)}, bf16[1040,768]{1,0:T(8,128)(2,1)}, u32[]{:S(2)}, u32[]{:S(2)}) collective-permute-start(bf16[1040,768]{1,0:T(8,128)(2,1)} %fusion.1.refs_0_), channel_id=1, source_target_pairs={{0,16},{16,0},{1,17},{17,1},{2,18},{18,2},{3,19},{19,3},{4,20},{20... | collective-permute-start | bytes 4792328 | tf_op jit(solution)/shard_map/ppermute | solution.py:52
  5.0 42.5 %collective-permute-start = (bf16[1040,768]{1,0:T(8,128)(2,1)}, bf16[1040,768]{1,0:T(8,128)(2,1)}, u32[]{:S(2)}, u32[]{:S(2)}) collective-permute-start(bf16[1040,768]{1,0:T(8,128)(2,1)} %fusion.1.refs_0_), channel_id=1, source_target_pairs={{0,4},{4,8},{8,12},{12,0},{16,28},{20,16},{24,20},{28,24},{1,5},{5... | collective-permute-start | bytes 4792328 | tf_op jit(solution)/shard_map/ppermute | solution.py:44
  7.9 39.7 %collective-permute-start.2 = (bf16[1040,768]{1,0:T(8,128)(2,1)}, bf16[1040,768]{1,0:T(8,128)(2,1)}, u32[]{:S(2)}, u32[]{:S(2)}) collective-permute-start(bf16[1040,768]{1,0:T(8,128)(2,1)} %fusion.1.refs_0_), channel_id=1, source_target_pairs={{0,12},{4,0},{8,4},{12,8},{16,20},{20,24},{24,28},{28,16},{1,13},{... | collective-permute-start | bytes 4792328 | tf_op jit(solution)/shard_map/ppermute | solution.py:44
  9.1 35.6 %collective-permute-start.3 = (bf16[1024,768]{1,0:T(8,128)(2,1)}, bf16[1024,768]{1,0:T(8,128)(2,1)S(1)}, u32[]{:S(2)}, u32[]{:S(2)}) collective-permute-start(bf16[1024,768]{1,0:T(8,128)(2,1)} %constant_dynamic-slice_fusion.1.c0), channel_id=1, source_target_pairs={{0,1},{1,2},{2,3},{3,0},{16,19},{17,16},{18,17},{19,18},{4,5},{5,6... | collective-permute-start | bytes 4718600 | tf_op jit(solution)/shard_map/ppermute | solution.py:44
  11.6 36.0 %collective-permute-start.4 = (bf16[1024,768]{1,0:T(8,128)(2,1)}, bf16[1024,768]{1,0:T(8,128)(2,1)S(1)}, u32[]{:S(2)}, u32[]{:S(2)}) collective-permute-start(bf16[1024,768]{1,0:T(8,128)(2,1)} %constant_dynamic-slice_fusion.1.c0), channel_id=1, source_target_pairs={{0,3},{1,0},{2,1},{3,2},{16,17},{17,18},{18,19},{19,16},{4,7},{5,4... | collective-permute-start | bytes 4718600 | tf_op jit(solution)/shard_map/ppermute | solution.py:44
  47.6 11.2 %collective-permute-start.6 = (bf16[1040,768]{1,0:T(8,128)(2,1)}, bf16[1040,768]{1,0:T(8,128)(2,1)S(1)}, u32[]{:S(2)}, u32[]{:S(2)}) collective-permute-start(bf16[1040,768]{1,0:T(8,128)(2,1)} %tie.2.refs_0_), channel_id=1, source_target_pairs={{0,16},{16,0},{1,17},{17,1},{2,18},{18,2},{3,19},{19,3},{4,20},{20... | collective-permute-start | bytes 4792328 | tf_op jit(solution)/shard_map/ppermute | solution.py:52
  47.7 11.1 %collective-permute-start.7 = (bf16[1040,768]{1,0:T(8,128)(2,1)}, bf16[1040,768]{1,0:T(8,128)(2,1)S(1)}, u32[]{:S(2)}, u32[]{:S(2)}) collective-permute-start(bf16[1040,768]{1,0:T(8,128)(2,1)} %collective-permute-done.2.refs_2_.refs_1_), channel_id=1, source_target_pairs={{0,16},{16,0},{1,17},{17,1},{2,18},{18,2},{3,19},{19,3},{4,20},{20... | collective-permute-start | bytes 4792328 | tf_op jit(solution)/shard_map/ppermute | solution.py:52
  48.2 21.9 %collective-permute-start.5 = (bf16[1040,768]{1,0:T(8,128)(2,1)}, bf16[1040,768]{1,0:T(8,128)(2,1)S(1)}, u32[]{:S(2)}, u32[]{:S(2)}) collective-permute-start(bf16[1040,768]{1,0:T(8,128)(2,1)} %tie.2.refs_0_), channel_id=1, source_target_pairs={{0,4},{4,8},{8,12},{12,0},{16,28},{20,16},{24,20},{28,24},{1,5},{5... | collective-permute-start | bytes 4792328 | tf_op jit(solution)/shard_map/ppermute | solution.py:44
  49.8 20.3 %collective-permute-start.8 = (bf16[1024,768]{1,0:T(8,128)(2,1)S(1)}, bf16[1024,768]{1,0:T(8,128)(2,1)S(1)}, u32[]{:S(2)}, u32[]{:S(2)}) collective-permute-start(bf16[1024,768]{1,0:T(8,128)(2,1)S(1)} %collective-permute-done.3.refs_3_.c1), channel_id=1, source_target_pairs={{0,1},{1,2},{2,3},{3,0},{16,19},{17,16},{18,17},{19,18},{4,5},{5,6... | collective-permute-start | bytes 4718600 | tf_op jit(solution)/shard_map/ppermute | solution.py:44
  70.1 3.4 %collective-permute-start.9 = (bf16[1040,768]{1,0:T(8,128)(2,1)S(1)}, bf16[1040,768]{1,0:T(8,128)(2,1)S(1)}, u32[]{:S(2)}, u32[]{:S(2)}) collective-permute-start(bf16[1040,768]{1,0:T(8,128)(2,1)S(1)} %tie.3.source0), channel_id=1, source_target_pairs={{0,16},{16,0},{1,17},{17,1},{2,18},{18,2},{3,19},{19,3},{4,20},{20... | collective-permute-start | bytes 4792328 | tf_op jit(solution)/shard_map/ppermute | solution.py:52
  86.4 8.4 %collective-permute-start.11 = (f32[8,1024]{1,0:T(8,128)S(1)}, f32[8,1024]{1,0:T(8,128)S(1)}, u32[]{:S(2)}, u32[]{:S(2)}) collective-permute-start(f32[8,1024]{1,0:T(8,128)S(1)} %log_add_fusion.s0), channel_id=1, source_target_pairs={{0,4},{4,8},{8,12},{12,0},{16,28},{20,16},{24,20},{28,24},{1,5},{5... | collective-permute-start | bytes 98312 | tf_op jit(solution)/shard_map/ppermute | solution.py:44
  88.9 5.9 %collective-permute-start.12 = (f32[8,1024]{1,0:T(8,128)S(1)}, f32[8,1024]{1,0:T(8,128)S(1)}, u32[]{:S(2)}, u32[]{:S(2)}) collective-permute-start(f32[8,1024]{1,0:T(8,128)S(1)} %log_add_fusion.s0), channel_id=1, source_target_pairs={{0,12},{4,0},{8,4},{12,8},{16,20},{20,24},{24,28},{28,16},{1,13},{... | collective-permute-start | bytes 98312 | tf_op jit(solution)/shard_map/ppermute | solution.py:44
  88.9 5.9 %collective-permute-start.13 = (f32[8,1024]{1,0:T(8,128)S(1)}, f32[8,1024]{1,0:T(8,128)S(1)}, u32[]{:S(2)}, u32[]{:S(2)}) collective-permute-start(f32[8,1024]{1,0:T(8,128)S(1)} %log_add_fusion.s0), channel_id=1, source_target_pairs={{0,8},{4,12},{8,0},{12,4},{1,9},{5,13},{9,1},{13,5},{2,10},{6,14},... | collective-permute-start | bytes 98312 | tf_op jit(solution)/shard_map/ppermute | solution.py:48
  107.0 16.7 %collective-permute-start.15 = (bf16[528,768]{1,0:T(8,128)(2,1)}, bf16[528,768]{1,0:T(8,128)(2,1)S(1)}, u32[]{:S(2)}, u32[]{:S(2)}) collective-permute-start(bf16[528,768]{1,0:T(8,128)(2,1)} %get-tuple-element.52), channel_id=1, source_target_pairs={{0,1},{1,2},{2,3},{3,0},{16,19},{17,16},{18,17},{19,18},{4,5},{5,6... | collective-permute-start | bytes 2433032 | tf_op jit(solution)/shard_map/ppermute | solution.py:44
  108.8 18.7 %collective-permute-start.18 = (bf16[528,768]{1,0:T(8,128)(2,1)}, bf16[528,768]{1,0:T(8,128)(2,1)S(1)}, u32[]{:S(2)}, u32[]{:S(2)}) collective-permute-start(bf16[528,768]{1,0:T(8,128)(2,1)} %get-tuple-element.56), channel_id=1, source_target_pairs={{0,32},{32,64},{64,96},{96,0},{16,112},{48,16},{80,48},{112,80},{1... | collective-permute-start | bytes 2433032 | tf_op jit(solution)/shard_map/ppermute | solution.py:44
  112.6 20.3 %collective-permute-start.14 = (bf16[528,768]{1,0:T(8,128)(2,1)}, bf16[528,768]{1,0:T(8,128)(2,1)S(1)}, u32[]{:S(2)}, u32[]{:S(2)}) collective-permute-start(bf16[528,768]{1,0:T(8,128)(2,1)} %get-tuple-element.50), channel_id=1, source_target_pairs={{0,3},{1,0},{2,1},{3,2},{16,17},{17,18},{18,19},{19,16},{4,7},{5,4... | collective-permute-start | bytes 2433032 | tf_op jit(solution)/shard_map/ppermute | solution.py:44
  112.6 20.3 %collective-permute-start.17 = (bf16[528,768]{1,0:T(8,128)(2,1)}, bf16[528,768]{1,0:T(8,128)(2,1)S(1)}, u32[]{:S(2)}, u32[]{:S(2)}) collective-permute-start(bf16[528,768]{1,0:T(8,128)(2,1)} %get-tuple-element.54), channel_id=1, source_target_pairs={{0,96},{32,0},{64,32},{96,64},{16,48},{48,80},{80,112},{112,16},{1... | collective-permute-start | bytes 2433032 | tf_op jit(solution)/shard_map/ppermute | solution.py:44
  125.1 11.5 %collective-permute-start.16 = (bf16[528,768]{1,0:T(8,128)(2,1)S(1)}, bf16[528,768]{1,0:T(8,128)(2,1)S(1)}, u32[]{:S(2)}, u32[]{:S(2)}) collective-permute-start(bf16[528,768]{1,0:T(8,128)(2,1)S(1)} %add_convert_fusion.1), channel_id=1, source_target_pairs={{0,1},{1,2},{2,3},{3,0},{16,19},{17,16},{18,17},{19,18},{4,5},{5,6... | collective-permute-start | bytes 2433032 | tf_op jit(solution)/shard_map/ppermute | solution.py:44
  127.8 14.3 %collective-permute-start.19 = (bf16[528,768]{1,0:T(8,128)(2,1)S(1)}, bf16[528,768]{1,0:T(8,128)(2,1)S(1)}, u32[]{:S(2)}, u32[]{:S(2)}) collective-permute-start(bf16[528,768]{1,0:T(8,128)(2,1)S(1)} %add_convert_fusion), channel_id=1, source_target_pairs={{0,32},{32,64},{64,96},{96,0},{16,112},{48,16},{80,48},{112,80},{1... | collective-permute-start | bytes 2433032 | tf_op jit(solution)/shard_map/ppermute | solution.py:44
  144.4 7.4 %collective-permute-start.20 = (bf16[144,768]{1,0:T(8,128)(2,1)S(1)}, bf16[144,768]{1,0:T(8,128)(2,1)S(1)}, u32[]{:S(2)}, u32[]{:S(2)}) collective-permute-start(bf16[144,768]{1,0:T(8,128)(2,1)S(1)} %get-tuple-element.58), channel_id=1, source_target_pairs={{0,96},{32,0},{64,32},{96,64},{16,48},{48,80},{80,112},{112,16},{1... | collective-permute-start | bytes 663560 | tf_op jit(solution)/shard_map/ppermute | solution.py:44
  144.5 8.3 %collective-permute-start.21 = (bf16[144,768]{1,0:T(8,128)(2,1)S(1)}, bf16[144,768]{1,0:T(8,128)(2,1)S(1)}, u32[]{:S(2)}, u32[]{:S(2)}) collective-permute-start(bf16[144,768]{1,0:T(8,128)(2,1)S(1)} %get-tuple-element.59), channel_id=1, source_target_pairs={{0,32},{32,64},{64,96},{96,0},{16,112},{48,16},{80,48},{112,80},{1... | collective-permute-start | bytes 663560 | tf_op jit(solution)/shard_map/ppermute | solution.py:44
  147.9 6.9 %collective-permute-start.22 = (bf16[144,768]{1,0:T(8,128)(2,1)S(1)}, bf16[144,768]{1,0:T(8,128)(2,1)S(1)}, u32[]{:S(2)}, u32[]{:S(2)}) collective-permute-start(bf16[144,768]{1,0:T(8,128)(2,1)S(1)} %get-tuple-element.60), channel_id=1, source_target_pairs={{0,64},{32,96},{64,0},{96,32},{1,65},{33,97},{65,1},{97,33},{2,66}... | collective-permute-start | bytes 663560 | tf_op jit(solution)/shard_map/ppermute | solution.py:48
  149.0 6.0 %collective-permute-start.23 = (bf16[144,768]{1,0:T(8,128)(2,1)S(1)}, bf16[144,768]{1,0:T(8,128)(2,1)S(1)}, u32[]{:S(2)}, u32[]{:S(2)}) collective-permute-start(bf16[144,768]{1,0:T(8,128)(2,1)S(1)} %get-tuple-element.62), channel_id=1, source_target_pairs={{0,3},{1,0},{2,1},{3,2},{16,17},{17,18},{18,19},{19,16},{4,7},{5,4... | collective-permute-start | bytes 663560 | tf_op jit(solution)/shard_map/ppermute | solution.py:44
  149.0 7.9 %collective-permute-start.24 = (bf16[144,768]{1,0:T(8,128)(2,1)S(1)}, bf16[144,768]{1,0:T(8,128)(2,1)S(1)}, u32[]{:S(2)}, u32[]{:S(2)}) collective-permute-start(bf16[144,768]{1,0:T(8,128)(2,1)S(1)} %get-tuple-element.63), channel_id=1, source_target_pairs={{0,1},{1,2},{2,3},{3,0},{16,19},{17,16},{18,17},{19,18},{4,5},{5,6... | collective-permute-start | bytes 663560 | tf_op jit(solution)/shard_map/ppermute | solution.py:44
  151.7 6.6 %collective-permute-start.25 = (bf16[144,768]{1,0:T(8,128)(2,1)S(1)}, bf16[144,768]{1,0:T(8,128)(2,1)S(1)}, u32[]{:S(2)}, u32[]{:S(2)}) collective-permute-start(bf16[144,768]{1,0:T(8,128)(2,1)S(1)} %get-tuple-element.64), channel_id=1, source_target_pairs={{0,2},{1,3},{2,0},{3,1},{4,6},{5,7},{6,4},{7,5},{8,10},{9,11},{10,... | collective-permute-start | bytes 663560 | tf_op jit(solution)/shard_map/ppermute | solution.py:48
  161.0 12.1 %collective-permute-start.26 = (bf16[2,128,768]{2,1,0:T(8,128)(2,1)S(1)}, bf16[2,128,768]{2,1,0:T(8,128)(2,1)}, u32[]{:S(2)}, u32[]{:S(2)}) collective-permute-start(bf16[2,128,768]{2,1,0:T(8,128)(2,1)S(1)} %final.1.refs_0_), channel_id=1, source_target_pairs={{0,32},{32,64},{64,96},{96,0},{16,112},{48,16},{80,48},{112,80},{1... | collective-permute-start | bytes 1179656 | tf_op jit(solution)/shard_map/ppermute | solution.py:44
  161.7 21.6 %collective-permute-start.27 = (bf16[2,128,768]{2,1,0:T(8,128)(2,1)S(1)}, bf16[2,128,768]{2,1,0:T(8,128)(2,1)}, u32[]{:S(2)}, u32[]{:S(2)}) collective-permute-start(bf16[2,128,768]{2,1,0:T(8,128)(2,1)S(1)} %final.1.refs_0_), channel_id=1, source_target_pairs={{0,96},{32,0},{64,32},{96,64},{16,48},{48,80},{80,112},{112,16},{1... | collective-permute-start | bytes 1179656 | tf_op jit(solution)/shard_map/ppermute | solution.py:44
  162.5 20.7 %collective-permute-start.28 = (bf16[2,128,768]{2,1,0:T(8,128)(2,1)S(1)}, bf16[2,128,768]{2,1,0:T(8,128)(2,1)}, u32[]{:S(2)}, u32[]{:S(2)}) collective-permute-start(bf16[2,128,768]{2,1,0:T(8,128)(2,1)S(1)} %final.1.refs_0_), channel_id=1, source_target_pairs={{0,64},{32,96},{64,0},{96,32},{1,65},{33,97},{65,1},{97,33},{2,66}... | collective-permute-start | bytes 1179656 | tf_op jit(solution)/shard_map/ppermute | solution.py:48
  164.1 19.8 %collective-permute-start.29 = (bf16[2,128,768]{2,1,0:T(8,128)(2,1)S(1)}, bf16[2,128,768]{2,1,0:T(8,128)(2,1)}, u32[]{:S(2)}, u32[]{:S(2)}) collective-permute-start(bf16[2,128,768]{2,1,0:T(8,128)(2,1)S(1)} %final.1.refs_0_), channel_id=1, source_target_pairs={{0,16},{16,0},{1,17},{17,1},{2,18},{18,2},{3,19},{19,3},{4,20},{20... | collective-permute-start | bytes 1179656 | tf_op jit(solution)/shard_map/ppermute | solution.py:52
  173.1 11.9 %collective-permute-start.30 = (bf16[2,128,768]{2,1,0:T(8,128)(2,1)}, bf16[2,128,768]{2,1,0:T(8,128)(2,1)}, u32[]{:S(2)}, u32[]{:S(2)}) collective-permute-start(bf16[2,128,768]{2,1,0:T(8,128)(2,1)} %collective-permute-done.26.refs_1_), channel_id=1, source_target_pairs={{0,16},{16,0},{1,17},{17,1},{2,18},{18,2},{3,19},{19,3},{4,20},{20... | collective-permute-start | bytes 1179656 | tf_op jit(solution)/shard_map/ppermute | solution.py:52
  183.3 2.3 %collective-permute-start.31 = (bf16[2,128,768]{2,1,0:T(8,128)(2,1)}, bf16[2,128,768]{2,1,0:T(8,128)(2,1)}, u32[]{:S(2)}, u32[]{:S(2)}) collective-permute-start(bf16[2,128,768]{2,1,0:T(8,128)(2,1)} %collective-permute-done.27.refs_2_), channel_id=1, source_target_pairs={{0,16},{16,0},{1,17},{17,1},{2,18},{18,2},{3,19},{19,3},{4,20},{20... | collective-permute-start | bytes 1179656 | tf_op jit(solution)/shard_map/ppermute | solution.py:52
  183.3 2.8 %collective-permute-start.32 = (bf16[2,128,768]{2,1,0:T(8,128)(2,1)}, bf16[2,128,768]{2,1,0:T(8,128)(2,1)}, u32[]{:S(2)}, u32[]{:S(2)}) collective-permute-start(bf16[2,128,768]{2,1,0:T(8,128)(2,1)} %collective-permute-done.28.refs_3_), channel_id=1, source_target_pairs={{0,16},{16,0},{1,17},{17,1},{2,18},{18,2},{3,19},{19,3},{4,20},{20... | collective-permute-start | bytes 1179656 | tf_op jit(solution)/shard_map/ppermute | solution.py:52
  (13 other events, 97.5 us)

commit v4 on v3

--- a/solution.py
+++ b/solution.py
@@ -65,6 +65,45 @@
     return jnp.where(up, 1.0, 0.0).astype(BF16)
 
 
+def pack_kernel(vectors, cand_ref, out, buf, in_sem, out_sem):
+    loads, stores = [], []
+    for k in range(4):
+        rows = pl.ds(k * 256, 256)
+        loads.append(pltpu.make_async_copy(vectors.at[rows, :], buf.at[rows, :], in_sem.at[k]))
+        stores.append(pltpu.make_async_copy(buf.at[rows, :], out.at[rows, :], out_sem.at[k]))
+        loads[k].start()
+    cand = cand_ref[...].astype(F32)
+    halves = [cand[pick : pick + 1, h * 512 : (h + 1) * 512] for pick in range(4) for h in range(2)]
+    tail = jnp.concatenate([*halves, jnp.zeros((EXTRA - 8, 512), F32)], axis=0)
+    tail = jnp.concatenate([tail, jnp.zeros((EXTRA, D - 512), F32)], axis=1)
+    buf[TOK:EXT, :] = tail.astype(BF16)
+    end = pltpu.make_async_copy(buf.at[pl.ds(TOK, EXTRA), :], out.at[pl.ds(TOK, EXTRA), :], out_sem.at[4])
+    end.start()
+    for load, store in zip(loads, stores):
+        load.wait()
+        store.start()
+    for store in (*stores, end):
+        store.wait()
+
+
+def pack(vectors, cand):
+    anywhere = pl.BlockSpec(memory_space=pl.ANY)
+    return pl.pallas_call(
+        pack_kernel,
+        in_specs=[anywhere, pl.BlockSpec(memory_space=pltpu.VMEM)],
+        out_specs=anywhere,
+        out_shape=jax.ShapeDtypeStruct((EXT, D), BF16),
+        scratch_shapes=[
+            pltpu.VMEM((EXT, D), BF16),
+            pltpu.SemaphoreType.DMA((4,)),
+            pltpu.SemaphoreType.DMA((5,)),
+        ],
+        compiler_params=params(60),
+        cost_estimate=cost(0, 3e6),
+        name="pack",
+    )(vectors, cand)
+
+
 def ranks(tail, blk, up):
     tail = tail.astype(F32)
     hit = None
@@ -86,34 +125,42 @@
     return rows.reshape(NBLK, MOST, D)
 
 
-def index_kernel(*refs):
+def index_kernel(pieces, *refs):
     rank_refs, idx_ref = refs[:-1], refs[-1]
     sources = [(ref, k) for ref in rank_refs for k in range(ref.shape[0])]
     row = lax.broadcasted_iota(jnp.int32, (8, TOK), 0)
     v = lax.broadcasted_iota(jnp.int32, (8, TOK), 1)
     place = jnp.where(row == 0, v >> 3, jnp.where(row == 1, v & 7, jnp.where(row == 2, 1, 0)))
     place = place.astype(F32).astype(BF16)
-    lane = lax.broadcasted_iota(jnp.int32, (1, SLOTS), 1)
-    base = jnp.zeros((1, SLOTS), F32)
-    for s in range(1, NSRC):
-        base = base + jnp.where(lane >= s * MOST, float(TOK), 0.0)
-    slot = lax.broadcasted_iota(jnp.int32, (MOST, TOK), 0).astype(F32)
+    lane = lax.broadcasted_iota(jnp.int32, (1, idx_ref.shape[1]), 1)
+    base, end = jnp.zeros(lane.shape, F32), 0
+    for s, _, lo, hi in pieces:
+        base = jnp.where(lane >= end, float(s * TOK), base)
+        end += hi - lo
     for b in range(NBLK):
-        hot = [jnp.where(slot == ref[k, b : b + 1, :], 1.0, 0.0).astype(BF16) for ref, k in sources]
+        hot = []
+        for _, at, lo, hi in pieces:
+            ref, k = sources[at]
+            slot = (lax.broadcasted_iota(jnp.int32, (hi - lo, TOK), 0) + lo).astype(F32)
+            hot.append(jnp.where(slot == ref[k, b : b + 1, :], 1.0, 0.0).astype(BF16))
         hot = jnp.concatenate(hot, axis=0)
         found = lax.dot_general(place, hot, (((1,), (1,)), ((), ())), preferred_element_type=F32)
         where = found[0:1] * 8.0 + found[1:2] + base
         idx_ref[b : b + 1, :] = jnp.where(found[2:3] > 0, where, -1.0).astype(jnp.int32)
 
 
-def indices(*rank):
-    return pl.pallas_call(
-        index_kernel,
-        out_shape=jax.ShapeDtypeStruct((NBLK, SLOTS), jnp.int32),
+def indices(ranked, pieces):
+    def kern(*refs):
+        index_kernel(pieces, *refs)
+
+    width = sum(hi - lo for _, _, lo, hi in pieces)
+    return pl.pallas_call(
+        kern,
+        out_shape=jax.ShapeDtypeStruct((NBLK, width), jnp.int32),
         compiler_params=params(12),
         cost_estimate=cost(4e9, 1e6),
         name="indices",
-    )(*rank)
+    )(*ranked)
 
 
 def dispatch_kernel(n, *refs):
@@ -172,7 +219,7 @@
             pltpu.VMEM((TOK, TOK), BF16),
         ],
         input_output_aliases=alias,
-        compiler_params=params(20),
+        compiler_params=params(34),
         cost_estimate=cost(2 * n * NBLK * MOST * TOK * D, n * 3e6),
         name=f"dispatch{first}",
     )(*args)
@@ -257,40 +304,32 @@
             pltpu.SemaphoreType.DMA((6,)),
         ],
         input_output_aliases={6: 0},
-        compiler_params=params(32),
+        compiler_params=params(34),
         cost_estimate=cost(4 * NBLK * MOST * TOK * D, 20e6, 6 * BS * 512),
         name="middle",
     )(*sources, blk, *cents, rows)
 
 
 def late_kernel(
-    source0, source1, blk_ref, c0, c1, c2, c3, rank0, rank1, rank2, peak0, lse0, rows_in, e_in,
+    source, blk_ref, c0, c1, c2, c3, rank0, rank1, rank2, rank3, peak0, lse0, rows_in, e_in,
     rows_out, e_out, rank_ref, peak_ref, stat_ref,
-    vbuf, xa, xb, x67, cb, ea, eb, lse_scr, vsem, csem, xsem, osem, esem,
+    vbuf, xa, xb, x7, cb, ea, eb, lse_scr, vsem, csem, xsem, osem, esem,
 ):
-    load0 = pltpu.make_async_copy(source0, vbuf.at[0], vsem.at[0])
-    load1 = pltpu.make_async_copy(source1, vbuf.at[1], vsem.at[1])
-    near = pltpu.make_async_copy(rows_in.at[pl.ds(0, 6), pl.ds(512, 64), :], xa, xsem.at[0])
-    far_rows = pltpu.make_async_copy(rows_in.at[pl.ds(6, 2), pl.ds(0, 576), :], xb, xsem.at[1])
+    load = pltpu.make_async_copy(source, vbuf, vsem)
+    near = pltpu.make_async_copy(rows_in.at[pl.ds(0, 6), pl.ds(512, 160), :], xa, xsem.at[0])
+    far_rows = pltpu.make_async_copy(rows_in.at[pl.ds(6, 2), pl.ds(0, 672), :], xb, xsem.at[1])
     cents = [pltpu.make_async_copy(c, cb.at[k], csem.at[k]) for k, c in enumerate((c0, c1, c2, c3))]
-    load0.start()
-    load1.start()
+    load.start()
     peak_ref[:, 0:512] = peak0[...]
     lse_scr[:, 0:512] = lse0[...]
     up = earlier()
-    load0.wait()
-    for copy in (near, cents[0], cents[1]):
+    load.wait()
+    for copy in (near, *cents, far_rows):
         copy.start()
-    rank = ranks(vbuf[0, TOK:EXT, :], blk_ref[:, 0:1], up)
+    rank = ranks(vbuf[TOK:EXT, :], blk_ref[:, 0:1], up)
     rank_ref[0] = rank
-    x67[:, 0:MOST, :] = gathered(rank, vbuf[0, 0:TOK, :])
-    load1.wait()
-    for copy in (cents[2], cents[3], far_rows):
-        copy.start()
-    rank = ranks(vbuf[1, TOK:EXT, :], blk_ref[:, 0:1], up)
-    rank_ref[1] = rank
-    x67[:, MOST : 2 * MOST, :] = gathered(rank, vbuf[1, 0:TOK, :])
-    back = pltpu.make_async_copy(x67, rows_out.at[pl.ds(0, NBLK), pl.ds(576, 2 * MOST), :], osem)
+    x7[...] = gathered(rank, vbuf[0:TOK, :])
+    back = pltpu.make_async_copy(x7, rows_out.at[pl.ds(0, NBLK), pl.ds(672, MOST), :], osem)
     back.start()
     near.wait()
 
@@ -300,7 +339,7 @@
         for i in range(2):
             b = 2 * q + i
             cent = cb[q, i * BS : (i + 1) * BS, :]
-            e, peak, lse = score_chunk(cent, half_norm(cent), jnp.concatenate([xa[b], x67[b]], axis=0))
+            e, peak, lse = score_chunk(cent, half_norm(cent), jnp.concatenate([xa[b], x7[b]], axis=0))
             ea[b] = e
             peak_ref[pl.ds(b, 1), 512:768] = peak
             lse_scr[pl.ds(b, 1), 512:768] = lse
@@ -312,7 +351,7 @@
         b = 6 + i
         cent = cb[3, i * BS : (i + 1) * BS, :]
         norm = half_norm(cent)
-        chunks = (xb[i, 0:256, :], xb[i, 256:512, :], jnp.concatenate([xb[i, 512:576, :], x67[b]], axis=0))
+        chunks = (xb[i, 0:256, :], xb[i, 256:512, :], jnp.concatenate([xb[i, 512:672, :], x7[b]], axis=0))
         for k, rows in enumerate(chunks):
             e, peak, lse = score_chunk(cent, norm, rows)
             eb[i, :, k * 256 : (k + 1) * 256] = e
@@ -320,7 +359,7 @@
             lse_scr[b : b + 1, k * 256 : (k + 1) * 256] = lse
         pltpu.make_async_copy(eb.at[i], e_out.at[b], esem.at[b]).start()
 
-    sources = [(ref, k) for ref in (rank0, rank1, rank2, rank_ref) for k in range(ref.shape[0])]
+    sources = [(ref, k) for ref in (rank0, rank1, rank2, rank3, rank_ref) for k in range(ref.shape[0])]
     for s, (ref, k) in enumerate(sources):
         k0, k1 = s * MOST // 128, (s * MOST + MOST - 1) // 128
         for j in range(TOK // 128):
@@ -345,30 +384,30 @@
         pltpu.make_async_copy(eb.at[i], e_out.at[6 + i], esem.at[6 + i]).wait()
 
 
-def late_scores(sources, blk, cents, ranked, peak0, lse0, rows, e):
+def late_scores(source, blk, cents, ranked, peak0, lse0, rows, e):
     anywhere, hbm = pl.BlockSpec(memory_space=pl.ANY), pl.BlockSpec(memory_space=pltpu.HBM)
     vmem = pl.BlockSpec(memory_space=pltpu.VMEM)
     return pl.pallas_call(
         late_kernel,
-        in_specs=[anywhere] * 2 + [vmem] + [anywhere] * 4 + [vmem] * 5 + [hbm] * 2,
+        in_specs=[anywhere, vmem] + [anywhere] * 4 + [vmem] * 6 + [hbm] * 2,
         out_specs=(hbm, hbm, vmem, vmem, vmem),
         out_shape=(
             jax.ShapeDtypeStruct(ROWS, BF16),
             jax.ShapeDtypeStruct(SCORES, BF16),
-            jax.ShapeDtypeStruct((2, NBLK, TOK), F32),
+            jax.ShapeDtypeStruct((1, NBLK, TOK), F32),
             jax.ShapeDtypeStruct((NBLK, SLOTS), F32),
             jax.ShapeDtypeStruct((NSRC, TOK), F32),
         ),
         scratch_shapes=[
-            pltpu.VMEM((2, EXT, D), BF16),
-            pltpu.VMEM((6, 64, D), BF16),
-            pltpu.VMEM((2, 576, D), BF16),
-            pltpu.VMEM((NBLK, 2 * MOST, D), BF16),
+            pltpu.VMEM((EXT, D), BF16),
+            pltpu.VMEM((6, 160, D), BF16),
+            pltpu.VMEM((2, 672, D), BF16),
+            pltpu.VMEM((NBLK, MOST, D), BF16),
             pltpu.VMEM((4, 1024, D), BF16),
             pltpu.VMEM((6, BS, 256), BF16),
             pltpu.VMEM((2, BS, SLOTS), BF16),
             pltpu.VMEM((NBLK, SLOTS), F32),
-            pltpu.SemaphoreType.DMA((2,)),
+            pltpu.SemaphoreType.DMA,
             pltpu.SemaphoreType.DMA((4,)),
             pltpu.SemaphoreType.DMA((2,)),
             pltpu.SemaphoreType.DMA,
@@ -378,7 +417,7 @@
         compiler_params=params(34),
         cost_estimate=cost(2 * 6 * BS * SLOTS * D, 20e6, 4 * BS * SLOTS),
         name="late_scores",
-    )(*sources, blk, *cents, *ranked, peak0, lse0, rows, e)
+    )(source, blk, *cents, *ranked, peak0, lse0, rows, e)
 
 
 def factor_kernel(stat_refs, idx_ref, peak_ref, f_scr):
@@ -407,50 +446,59 @@
         f_scr[:, k * 128 : (k + 1) * 128] = jnp.where(at >= 0, f, 0.0)
 
 
-def sums_owner(i):
-    t = i % 4
-    return jnp.where(t == 0, 3, jnp.where(t == 3, 0, t))
-
-
-def sums_kernel(where_ref, s0, s1, s2, s3, idx_any, peak_any, e_any, rows_any, *refs):
-    outs, (f_scr, hbuf, gbuf, gcount, gtile, stats, idx_ref, peak_ref, e_buf, rows_buf, hsem, gsem, tsem, ssem, esem, rsem) = refs[:8], refs[8:]
+def load_factors(s0, s1, s2, s3, idx0, idx1, peak_any, factor_out, f_scr, stats, idx_ref, peak_ref, sem):
+    loads = [pltpu.make_async_copy(s, stats.at[k], sem.at[k]) for k, s in enumerate((s0, s1, s2, s3))]
+    loads.append(pltpu.make_async_copy(idx0, idx_ref.at[:, pl.ds(0, 512)], sem.at[4]))
+    loads.append(pltpu.make_async_copy(idx1, idx_ref.at[:, pl.ds(512, 256)], sem.at[5]))
+    loads.append(pltpu.make_async_copy(peak_any, peak_ref, sem.at[6]))
+    for load in loads:
+        load.start()
+    for load in loads:
+        load.wait()
+    factor_kernel([stats.at[k] for k in range(4)], idx_ref, peak_ref, f_scr)
+    factor_out[...] = f_scr[...]
+
+
+def sums_kernel(part, owners, n_in, *refs):
+    ins, refs = refs[:n_in], refs[n_in:]
+    e_any, rows_any = ins[-2:]
+    n = len(owners)
     i = pl.program_id(0)
-    q, slot = sums_owner(i), i % 2
-
-    def send_h(k, slot=slot):
-        return pltpu.make_async_copy(hbuf.at[slot], outs[k], hsem.at[slot])
-
-    def send_g(k, slot=slot):
-        start = pl.multiple_of(q * 128, 128)
-        return pltpu.make_async_copy(gbuf.at[slot, k], outs[4 + k].at[pl.ds(start, 128), :], gsem.at[slot, k])
-
-    def send_tile(k):
-        return pltpu.make_async_copy(gtile.at[k], outs[4 + k].at[pl.ds(BS, EXTRA), :], tsem.at[k])
+    slot = i % 2
+
+    def owner(k):
+        return sum(jnp.where(k == step, q, 0) for step, q in enumerate(owners))
+
+    q = owner(i)
+    if part == 1:
+        outs, factor_out, f_scr, refs = refs[:4], refs[4], refs[5], refs[6:]
+        (e_buf, rows_buf, esem, rsem), refs = refs[:4], refs[4:]
+    else:
+        outs, refs = refs[:n], refs[n:]
+        (f_scr, e_buf, rows_buf, fsem, esem, rsem), refs = refs[:6], refs[6:]
 
     def load_block(k):
-        b = 2 * sums_owner(k) + k // 4
+        b = 2 * owner(k) + part
         pltpu.make_async_copy(e_any.at[b], e_buf.at[k], esem.at[k]).start()
         pltpu.make_async_copy(rows_any.at[b], rows_buf.at[k], rsem.at[k]).start()
 
     @pl.when(i == 0)
     def _():
-        loads = [pltpu.make_async_copy(s, stats.at[k], ssem.at[k]) for k, s in enumerate((s0, s1, s2, s3))]
-        loads.append(pltpu.make_async_copy(idx_any, idx_ref, ssem.at[4]))
-        loads.append(pltpu.make_async_copy(peak_any, peak_ref, ssem.at[5]))
-        for load in loads:
+        for k in range(min(2, n)):
+            load_block(k)
+        if part == 1:
+            load_factors(*ins[1:8], factor_out, f_scr, *refs[:4])
+        else:
+            load = pltpu.make_async_copy(ins[0], f_scr, fsem)
             load.start()
-        for k in range(2):
-            load_block(k)
-        for load in loads:
             load.wait()
-        factor_kernel([stats.at[k] for k in range(4)], idx_ref, peak_ref, f_scr)
-        gcount[...] = jnp.zeros_like(gcount)
-
-    @pl.when(i < 6)
-    def _():
-        load_block(i + 2)
-
-    f = f_scr[pl.ds(2 * q + i // 4, 1), :]
+
+    if n > 2:
+        @pl.when(i < n - 2)
+        def _():
+            load_block(i + 2)
+
+    f = f_scr[pl.ds(2 * q + part, 1), :]
     pltpu.make_async_copy(e_any.at[0], e_buf.at[i], esem.at[i]).wait()
     pltpu.make_async_copy(rows_any.at[0], rows_buf.at[i], rsem.at[i]).wait()
     totals, counts = [], []
@@ -459,37 +507,53 @@
         count = jnp.sum(w, axis=1, keepdims=True)
         counts.append(jnp.transpose(jnp.broadcast_to(count, (128, 128)))[0:EXTRA])
         totals.append(jnp.dot(w.astype(BF16), rows_buf[i], preferred_element_type=F32).astype(BF16))
-
-    @pl.when((i == 2) | (i == 3))
+    if part == 0:
+        owner_first(i, n, totals, counts, outs, *refs)
+    else:
+        part_first(i, q, slot, ins[0], totals, counts, outs, *refs[4:])
+
+
+def owner_first(i, n, totals, counts, outs, buf, sem):
+    for m in range(4):
+        buf[i, m * 128 : (m + 1) * 128, :] = totals[m]
+    tile = jnp.concatenate([*counts, jnp.zeros((EXTRA, D - BS), F32)], axis=1)
+    buf[i, BS : BS + EXTRA, :] = tile.astype(BF16)
+    for k in range(n):
+        @pl.when(i == k)
+        def _(k=k):
+            pltpu.make_async_copy(buf.at[k], outs[k], sem.at[k]).start()
+
+    @pl.when(i == n - 1)
     def _():
-        send_h(0).wait()
-
-    @pl.when((i == 6) | (i == 7))
+        for k in range(n):
+            pltpu.make_async_copy(buf.at[k], outs[k], sem.at[k]).wait()
+
+
+def part_first(i, q, slot, where_ref, totals, counts, outs, buf, gcount, gtile, sem, tsem):
+    def send(k, slot=slot):
+        start = pl.multiple_of(q * 128, 128)
+        return pltpu.make_async_copy(buf.at[slot, k], outs[k].at[pl.ds(start, 128), :], sem.at[slot, k])
+
+    def send_tile(k):
+        return pltpu.make_async_copy(gtile.at[k], outs[k].at[pl.ds(BS, EXTRA), :], tsem.at[k])
+
+    @pl.when(i == 0)
+    def _():
+        gcount[...] = jnp.zeros_like(gcount)
+
+    @pl.when(i >= 2)
     def _():
         for k in range(4):
-            send_g(k).wait()
-
-    @pl.when(i < 4)
-    def _():
-        for m in range(4):
-            hbuf[slot, m * 128 : (m + 1) * 128, :] = totals[m]
-        tile = jnp.concatenate([*counts, jnp.zeros((EXTRA, D - BS), F32)], axis=1)
-        hbuf[slot, BS : BS + EXTRA, :] = tile.astype(BF16)
-        for k in range(4):
-            @pl.when(q == k)
-            def _(k=k):
-                send_h(k).start()
-
-    @pl.when(i >= 4)
-    def _():
-        for m in range(4):
-            at = sum(jnp.where(where_ref[4 + k] == m, k, 0) for k in range(1, 4))
-            gbuf[slot, at] = totals[m]
-            gcount[at, pl.ds(q, 1), :] = counts[m][0:1]
-        for k in range(4):
-            send_g(k).start()
-
-    @pl.when(i == 7)
+            send(k).wait()
+
+    for m in range(4):
+        at = sum(jnp.where(where_ref[4 + k] == m, k, 0) for k in range(1, 4))
+        buf[slot, at] = totals[m]
+        gcount[at, pl.ds(q, 1), :] = counts[m][0:1]
+    for k in range(4):
+        send(k).start()
+
+    @pl.when(i == 3)
     def _():
         for k in range(4):
             tile = jnp.concatenate([gcount[k], jnp.zeros((8, 128), F32)], axis=0)
@@ -497,46 +561,79 @@
             gtile[k] = tile.astype(BF16)
             send_tile(k).start()
         for other in range(2):
-            send_h(0, other).wait()
             for k in range(4):
-                send_g(k, other).wait()
+                send(k, other).wait()
         for k in range(4):
             send_tile(k).wait()
 
 
-def sums(where, stats, idx, peak, e, rows):
-    shape = (BS + EXTRA, D)
-    out = pl.pallas_call(
-        sums_kernel,
-        grid=(8,),
-        in_specs=[pl.BlockSpec(memory_space=pltpu.SMEM)]
-        + [pl.BlockSpec(memory_space=pl.ANY)] * 6
-        + [pl.BlockSpec(memory_space=pltpu.HBM)] * 2,
-        out_specs=tuple([pl.BlockSpec(memory_space=pl.ANY)] * 8),
-        out_shape=tuple([jax.ShapeDtypeStruct(shape, BF16)] * 8),
-        scratch_shapes=[
-            pltpu.VMEM((NBLK, SLOTS), F32),
-            pltpu.VMEM((2, *shape), BF16),
-            pltpu.VMEM((2, 4, 128, D), BF16),
-            pltpu.VMEM((4, 8, 128), F32),
-            pltpu.VMEM((4, EXTRA, D), BF16),
-            pltpu.VMEM((4, NSRC, TOK), F32),
-            pltpu.VMEM((NBLK, SLOTS), jnp.int32),
-            pltpu.VMEM((NBLK, SLOTS), F32),
-            pltpu.VMEM((NBLK, BS, SLOTS), BF16),
-            pltpu.VMEM((NBLK, SLOTS, D), BF16),
-            pltpu.SemaphoreType.DMA((2,)),
-            pltpu.SemaphoreType.DMA((2, 4)),
-            pltpu.SemaphoreType.DMA((4,)),
-            pltpu.SemaphoreType.DMA((6,)),
-            pltpu.SemaphoreType.DMA((8,)),
-            pltpu.SemaphoreType.DMA((8,)),
-        ],
+SUMS_SHAPE = (BS + EXTRA, D)
+
+
+def sums_call(part, owners, small, big, out_shape, out_specs, own):
+    n = len(owners)
+
+    def kern(*refs):
+        sums_kernel(part, owners, len(small) + len(big), *refs)
+
+    specs = [pl.BlockSpec(memory_space=pl.ANY)] * len(small)
+    if part == 1:
+        specs[0] = pl.BlockSpec(memory_space=pltpu.SMEM)
+    factor = [pltpu.VMEM((NBLK, SLOTS), F32)]
+    return pl.pallas_call(
+        kern,
+        grid=(n,),
+        in_specs=specs + [pl.BlockSpec(memory_space=pltpu.HBM)] * len(big),
+        out_specs=out_specs,
+        out_shape=out_shape,
+        scratch_shapes=factor
+        + [pltpu.VMEM((n, BS, SLOTS), BF16), pltpu.VMEM((n, SLOTS, D), BF16)]
+        + ([pltpu.SemaphoreType.DMA] if part == 0 else [])
+        + [pltpu.SemaphoreType.DMA((n,)), pltpu.SemaphoreType.DMA((n,))]
+        + own,
         compiler_params=params(54),
-        cost_estimate=cost(2 * 8 * BS * SLOTS * D, 24e6),
-        name="sums",
-    )(where, *stats, idx, peak, e, rows)
-    return out[:4], out[4:]
+        cost_estimate=cost(2 * n * BS * SLOTS * D, n * 3e6),
+        name=f"sums{part}",
+    )(*small, *big)
+
+
+def part_sums(where, stats, idx, peak, e, rows):
+    anywhere = pl.BlockSpec(memory_space=pl.ANY)
+    own = [
+        pltpu.VMEM((4, NSRC, TOK), F32),
+        pltpu.VMEM((NBLK, SLOTS), jnp.int32),
+        pltpu.VMEM((NBLK, SLOTS), F32),
+        pltpu.SemaphoreType.DMA((7,)),
+        pltpu.VMEM((2, 4, 128, D), BF16),
+        pltpu.VMEM((4, 8, 128), F32),
+        pltpu.VMEM((4, EXTRA, D), BF16),
+        pltpu.SemaphoreType.DMA((2, 4)),
+        pltpu.SemaphoreType.DMA((4,)),
+    ]
+    *out, factor = sums_call(
+        1,
+        (3, 1, 2, 0),
+        (where, *stats, *idx, peak),
+        (e, rows),
+        (jax.ShapeDtypeStruct(SUMS_SHAPE, BF16),) * 4 + (jax.ShapeDtypeStruct((NBLK, SLOTS), F32),),
+        (anywhere,) * 4 + (pl.BlockSpec((NBLK, SLOTS), lambda i: (0, 0)),),
+        own,
+    )
+    return out, factor
+
+
+def owner_sums(owners, factor, after, e, rows):
+    n = len(owners)
+    own = [pltpu.VMEM((n, *SUMS_SHAPE), BF16), pltpu.SemaphoreType.DMA((n,))]
+    return sums_call(
+        0,
+        owners,
+        (factor, after),
+        (e, rows),
+        (jax.ShapeDtypeStruct(SUMS_SHAPE, BF16),) * n,
+        (pl.BlockSpec(memory_space=pl.ANY),) * n,
+        own,
+    )
 
 
 def fetched(refs, buf, sem):
@@ -548,14 +645,14 @@
     return [buf.at[k] for k in range(len(refs))]
 
 
-def parted_kernel(where_ref, *refs):
-    outs, (acc, buf, sem) = refs[6:14], refs[14:]
-    h0, h1, h2, g0, g1, g2 = fetched(refs[:6], buf, sem)
-
-    def tile(counts):
-        counts = jnp.broadcast_to(counts, (EXTRA, 128))
-        return jnp.concatenate([counts, jnp.zeros((EXTRA, D - 128), F32)], axis=1).astype(BF16)
-
+def count_tile(counts):
+    counts = jnp.broadcast_to(counts, (EXTRA, 128))
+    return jnp.concatenate([counts, jnp.zeros((EXTRA, D - 128), F32)], axis=1).astype(BF16)
+
+
+def owner_parts_kernel(where_ref, *refs):
+    outs, (acc, buf, sem) = refs[3:7], refs[7:]
+    h0, h1, h2 = fetched(refs[:3], buf, sem)
     acc[...] = h0[...].astype(F32) + h1[...].astype(F32) + h2[...].astype(F32)
     counts = acc[BS : BS + 8, 0:BS]
     for k in range(4):
@@ -564,32 +661,36 @@
         picked = counts[:, 0:128]
         for m in range(1, 4):
             picked = jnp.where(part == m, counts[:, m * 128 : (m + 1) * 128], picked)
-        outs[k][128:, :] = tile(picked[0:1])
+        outs[k][128:, :] = count_tile(picked[0:1])
+
+
+def part_owners_kernel(where_ref, *refs):
+    outs, (_, buf, sem) = refs[3:7], refs[7:]
+    g0, g1, g2 = fetched(refs[:3], buf, sem)
     counts = g0[BS:, 0:128].astype(F32) + g1[BS:, 0:128].astype(F32) + g2[BS:, 0:128].astype(F32)
     for k in range(4):
         rows = slice(k * 128, (k + 1) * 128)
         total = g0[rows, :].astype(F32) + g1[rows, :].astype(F32) + g2[rows, :].astype(F32)
-        outs[4 + k][0:128, :] = total.astype(BF16)
-        outs[4 + k][128:, :] = tile(counts[k : k + 1])
-
-
-def parted(where, h, g):
+        outs[k][0:128, :] = total.astype(BF16)
+        outs[k][128:, :] = count_tile(counts[k : k + 1])
+
+
+def parted(part, where, terms):
     vmem = pl.BlockSpec(memory_space=pltpu.VMEM)
-    out = pl.pallas_call(
-        parted_kernel,
-        in_specs=[pl.BlockSpec(memory_space=pltpu.SMEM)] + [pl.BlockSpec(memory_space=pl.ANY)] * 6,
-        out_specs=(vmem,) * 8,
-        out_shape=(jax.ShapeDtypeStruct((128 + EXTRA, D), BF16),) * 8,
+    return pl.pallas_call(
+        owner_parts_kernel if part == 0 else part_owners_kernel,
+        in_specs=[pl.BlockSpec(memory_space=pltpu.SMEM)] + [pl.BlockSpec(memory_space=pl.ANY)] * 3,
+        out_specs=(vmem,) * 4,
+        out_shape=(jax.ShapeDtypeStruct((128 + EXTRA, D), BF16),) * 4,
         scratch_shapes=[
             pltpu.VMEM((BS + EXTRA, D), F32),
-            pltpu.VMEM((6, BS + EXTRA, D), BF16),
-            pltpu.SemaphoreType.DMA((6,)),
+            pltpu.VMEM((3, BS + EXTRA, D), BF16),
+            pltpu.SemaphoreType.DMA((3,)),
         ],
-        compiler_params=params(16),
-        cost_estimate=cost(1e6, 8e6),
-        name="parted",
-    )(where, *h, *g)
-    return out[:4], out[4:]
+        compiler_params=params(12),
+        cost_estimate=cost(1e6, 4e6),
+        name=f"parted{part}",
+    )(where, *terms)
 
 
 def final_kernel(*refs):
@@ -675,11 +776,12 @@
     return total
 
 
-def ring_terms(own, d, e, f, axis):
+def ring_terms(own, d, e, f, axis, after=None):
     r1 = turn(f, axis, 1)
-    r2 = turn(d, axis, -1)
-    r3 = turn(add(e, r1).astype(BF16), axis, 1)
-    return own, r2, r3
+    r2 = turn(d if after is None else tie(d, after), axis, -1)
+    e = add(e, r1).astype(BF16)
+    r3 = turn(e, axis, 1)
+    return (own, r2, r3), e
 
 
 def direct_terms(own, d, e, f, axis):
@@ -697,8 +799,7 @@
     other_zs = jnp.stack([zs[0], zs[2], zs[1], zs[3]])
 
     where = jnp.concatenate([xs, zs])
-    tail = jnp.pad(candidates.T.reshape(8, 512).astype(BF16), ((0, EXTRA - 8), (0, D - 512)))
-    v = jnp.concatenate([vectors, tail])
+    v = pack(vectors, candidates.T)
     a, b = turn(v, "y", 1), turn(v, "y", -1)
     c0 = lax.dynamic_slice_in_dim(centroids, core * 1024, 1024, 0)
     c1, c2 = turn(c0, "x", 1), turn(c0, "x", -1)
@@ -712,10 +813,14 @@
     c3 = turn(c1, "x", 1)
     rank1, rows = dispatch(2, (a, b), blk, rows)
     rows, rank2, e, peak0, lse0 = middle((swap(a), swap(b)), blk, (c0, c1, c2), rows)
-    c = tie(c, lse0, c3)
     ranked = (rank0, rank1, rank2)
-    rows, e, rank3, peak, stat = late_scores((c, swap(c)), blk, (c0, c1, c2, c3), ranked, peak0, lse0, rows, e)
-    idx = indices(*ranked, rank3)
+    idx0 = indices(ranked, [(s, s, 0, MOST) for s in range(5)] + [(5, 5, 0, 32)])
+    c = tie(c, idx0, c3)
+    rank3, rows = dispatch(6, (c,), blk, rows)
+    rows, e, rank4, peak, stat = late_scores(
+        swap(c), blk, (c0, c1, c2, c3), (*ranked, rank3), peak0, lse0, rows, e
+    )
+    idx = (idx0, indices((rank2, rank3, rank4), [(5, 1, 32, MOST), (6, 2, 0, MOST), (7, 3, 0, MOST)]))
 
     theirs = swap(stat)
     theirs = jnp.concatenate([theirs[s : s + 1] for s in SWAPPED])
@@ -723,10 +828,13 @@
     merged = m + jnp.log(jnp.exp(stat - m) + jnp.exp(theirs - m))
     stats = (merged, turn(merged, "y", 1), turn(merged, "y", -1), far(merged, "y"))
 
-    h, g = sums(where, stats, idx, peak, e, rows)
-    h, g = ring_terms(*h, "x"), ring_terms(*g, "z")
-    h, g = parted(where, h, g)
-    h, g = direct_terms(*h, "z"), direct_terms(*g, "x")
+    g, factor = part_sums(where, stats, idx, peak, e, rows)
+    (h3,) = owner_sums((3,), factor, factor, e, rows)
+    h1, h2, h0 = owner_sums((1, 2, 0), factor, h3, e, rows)
+    g, _ = ring_terms(*g, "z", h0)
+    h, _ = ring_terms(h0, h1, h2, h3, "x")
+    h = direct_terms(*parted(0, where, h), "z")
+    g = direct_terms(*parted(1, where, g), "x")
     fresh = final(h, g, mine)
 
     others = [turn(fresh, "z", 1), turn(fresh, "z", -1), far(fresh, "z")]

time: 190 us -> 189 us (level)
  Pallas kernels: 56.9 us -> 65.9 us
  waiting for transfers between devices: 62.6 us -> 55.7 us
  local copies, waits for them, and re-layouts: 5.1 us -> 10.3 us
  other arithmetic: 5.35 us -> 0.64 us
  starting transfers between devices: 59.5 us -> 55.1 us
    pallas_call x4 -> x9, Pallas kernels: 28.1 us -> 35.4 us  [the longest x3 17.4 us: sums_call(): pl.pallas_call(kern, grid=(n,), in_specs=specs + [pl.BlockSpec(memory_spa...]
    unnamed x24 -> x40, local copies, waits for them, and re-layouts: 1.84 us -> 7.01 us
    ppermute x20, waiting for transfers between devices: 53.6 us -> 48.6 us  [turn(): return lax.ppermute(a, axes, pairs)]
    ppermute x20, starting transfers between devices: 32.7 us -> 28.9 us  [turn(): return lax.ppermute(a, axes, pairs)]
    ppermute x9, waiting for transfers between devices: 5.65 us -> 2.57 us  [swap(): return lax.ppermute(a, 'core', [(0, 1), (1, 0)])]
    concatenate x1 -> x0, other arithmetic: 2.73 us -> none  [body(): v = jnp.concatenate([vectors, tail])]
    convert_element_type x3 -> x2, other arithmetic: 2.43 us -> 0.45 us  [ring_terms(): e = add(e, r1).astype(BF16)]
    pallas_call x2 -> x3, Pallas kernels: 12 us -> 13.8 us  [dispatch(): pl.pallas_call(kern, grid=(n,), in_specs=in_specs, out_specs=(pl.BlockSpe...]
  transfers between devices with their start and end apart: 33 -> 33, of which waited for: 16 -> 12; matrix products, arithmetic and copies ran while one was open for 3% -> 2% of each run, Pallas kernels for 14% -> 19%
where the time goes in v4:
time: 189 us; the launch traced here: 188 us
  Pallas kernels  65.9 us (35%)
  waiting for transfers between devices  55.7 us (29%)
  starting transfers between devices  55.1 us (29%)
  local copies, waits for them, and re-layouts  10.3 us (5%)
    ppermute x20, waiting for transfers between devices, turn(): return lax.ppermute(a, axes, pairs)  48.6 us
    ppermute x20, starting transfers between devices, turn(): return lax.ppermute(a, axes, pairs)  28.9 us
    ppermute x9, starting transfers between devices, swap(): return lax.ppermute(a, 'core', [(0, 1), (1, 0)])  20.8 us
    pallas_call x3, Pallas kernels, sums_call(): pl.pallas_call(kern, grid=(n,), in_specs=specs + [pl.BlockSpec(memory_spa...  17.4 us
    pallas_call x3, Pallas kernels, dispatch(): pl.pallas_call(kern, grid=(n,), in_specs=in_specs, out_specs=(pl.BlockSpe...  13.8 us
    pallas_call x1, Pallas kernels, middle(): pl.pallas_call(middle_kernel, in_specs=[anywhere] * 2 + [vmem] + [anywher...  10.5 us
    pallas_call x1, Pallas kernels, late_scores(): pl.pallas_call(late_kernel, in_specs=[anywhere, vmem] + [anywhere] * 4 +...  8.08 us
    unnamed x40, local copies, waits for them, and re-layouts  7.01 us
  transfers between devices with their start and end apart: 33, of which 12 were waited for; matrix products, arithmetic and copies ran while one was open for 2% of the time, Pallas kernels for 19%

profile of v4, /device:TPU:1, one launch (start us, length us, event | category | flops | bytes accessed | tf_op | source)
XLA Modules:
  0.0 188.2 jit_solution(8106893200804554592)
XLA Ops:
  0.0 3.2 %pack.1.refs_0_ = bf16[1040,768]{1,0:T(8,128)(2,1)} custom-call(bf16[1024,768]{1,0:T(8,128)(2,1)} %vectors.1, s32[4,1024]{1,0:T(4,128)} %bitcast.13), custom_call_target="tpu_custom_call" | custom-call | bytes 3000000 | tf_op jit(solution)/shard_map/pack/pallas_call | solution.py:91
  4.7 2.8 %collective-permute-start = (bf16[1040,768]{1,0:T(8,128)(2,1)}, bf16[1040,768]{1,0:T(8,128)(2,1)}, u32[]{:S(2)}, u32[]{:S(2)}) collective-permute-start(bf16[1040,768]{1,0:T(8,128)(2,1)} %pack.1.refs_0_), channel_id=1, source_target_pairs={{0,4},{4,8},{8,12},{12,0},{16,28},{20,16},{24,20},{28,24},{1,5},{5... | collective-permute-start | bytes 4792328 | tf_op jit(solution)/shard_map/ppermute | solution.py:44
  8.8 2.5 %collective-permute-start.3 = (bf16[1024,768]{1,0:T(8,128)(2,1)}, bf16[1024,768]{1,0:T(8,128)(2,1)S(1)}, u32[]{:S(2)}, u32[]{:S(2)}) collective-permute-start(bf16[1024,768]{1,0:T(8,128)(2,1)} %constant_dynamic-slice_fusion.1.c0), channel_id=1, source_target_pairs={{0,1},{1,2},{2,3},{3,0},{16,19},{17,16},{18,17},{19,18},{4,5},{5,6... | collective-permute-start | bytes 4718600 | tf_op jit(solution)/shard_map/ppermute | solution.py:44
  13.0 4.9 %dispatch0.1 = (f32[2,8,1024]{2,1,0:T(8,128)S(1)}, bf16[28,768,768]{2,1,0:T(8,128)(2,1)}) custom-call(bf16[1040,768]{1,0:T(8,128)(2,1)S(1)} %copy-done.4, bf16[1040,768]{1,0:T(8,128)(2,1)} %collective-permute-done.1.refs_1_, f32[8,128]{1,0:T(8,128)S(1)} %broadcast_in_dim.2.refs_2_.blk_ref.refs_1_), custom_call_target="tpu_custom_call" | custom-call | flops 2415919104 | bytes 6000000 | tf_op jit(solution)/shard_map/dispatch0/pallas_call | solution.py:204
  18.0 26.4 %collective-permute-done.3.refs_3_.c1 = bf16[1024,768]{1,0:T(8,128)(2,1)S(1)} collective-permute-done((bf16[1024,768]{1,0:T(8,128)(2,1)}, bf16[1024,768]{1,0:T(8,128)(2,1)S(1)}, u32[]{:S(2)}, u32[]{:S(2)}) %collective-permute-start.3) | collective-permute-done | bytes 1572896 | tf_op jit(solution)/shard_map/ppermute | solution.py:44
  44.3 3.0 %collective-permute-done.4.refs_4_.c2 = bf16[1024,768]{1,0:T(8,128)(2,1)S(1)} collective-permute-done((bf16[1024,768]{1,0:T(8,128)(2,1)}, bf16[1024,768]{1,0:T(8,128)(2,1)S(1)}, u32[]{:S(2)}, u32[]{:S(2)}) %collective-permute-start.4) | collective-permute-done | bytes 1572896 | tf_op jit(solution)/shard_map/ppermute | solution.py:44
  49.5 2.9 %collective-permute-start.8 = (bf16[1024,768]{1,0:T(8,128)(2,1)S(1)}, bf16[1024,768]{1,0:T(8,128)(2,1)S(1)}, u32[]{:S(2)}, u32[]{:S(2)}) collective-permute-start(bf16[1024,768]{1,0:T(8,128)(2,1)S(1)} %collective-permute-done.3.refs_3_.c1), channel_id=1, source_target_pairs={{0,1},{1,2},{2,3},{3,0},{16,19},{17,16},{18,17},{19,18},{4,5},{5,6... | collective-permute-start | bytes 4718600 | tf_op jit(solution)/shard_map/ppermute | solution.py:44
  52.4 6.0 %dispatch2.1 = (f32[2,8,1024]{2,1,0:T(8,128)S(1)}, bf16[28,768,768]{2,1,0:T(8,128)(2,1)}) custom-call(bf16[1040,768]{1,0:T(8,128)(2,1)} %tie.3.refs_0_, bf16[1040,768]{1,0:T(8,128)(2,1)} %collective-permute-done.2.refs_2_.refs_1_, f32[8,128]{1,0:T(8,128)S(1)} %broadcast_in_dim.2.refs_2_.blk_ref.refs_1_, ...), custom_call_target="tpu_custom_call", output_to_operand_aliasing={{1}: (3, {})} | custom-call | flops 2415919104 | bytes 6000000 | tf_op jit(solution)/shard_map/dispatch2/pallas_call | solution.py:204
  58.4 10.5 %middle.1 = (bf16[28,768,768]{2,1,0:T(8,128)(2,1)}, f32[2,8,1024]{2,1,0:T(8,128)S(1)}, bf16[40,512,768]{2,1,0:T(8,128)(2,1)}, f32[8,512]{1,0:T(8,128)S(1)}, f32[8,512]{1,0:T(8,128)S(1)}) custom-call(bf16[1040,768]{1,0:T(8,128)(2,1)S(1)} %collective-permute-done.6.s0, ...), custom_call_target="tpu_custom_call", output_to_operand_aliasing={{0}: (6, {})} | custom-call | flops 2415919104 | bytes 20000000 | tf_op jit(solution)/shard_map/middle/pallas_call | solution.py:283
  68.9 2.3 %indices.2.refs_1_.refs_5_ = s32[8,512]{1,0:T(8,128)S(1)} custom-call(f32[2,8,1024]{2,1,0:T(8,128)S(1)} %get-tuple-element.37.refs_1_.refs_0_.rank0, f32[2,8,1024]{2,1,0:T(8,128)S(1)} %get-tuple-element.39.refs_1_.rank1, f32[2,8,1024]{2,1,0:T(8,128)S(1)} %get-tuple-element.41.refs_2_.rank2.refs_0_), custom_call_target="tpu_custom_call" | custom-call | flops 4000000000 | bytes 1000000 | tf_op jit(solution)/shard_map/indices/pallas_call | solution.py:157
  71.8 2.9 %dispatch6.1 = (f32[1,8,1024]{2,1,0:T(8,128)S(1)}, bf16[28,768,768]{2,1,0:T(8,128)(2,1)}) custom-call(bf16[1040,768]{1,0:T(8,128)(2,1)S(1)} %tie.4.refs_0_, f32[8,128]{1,0:T(8,128)S(1)} %broadcast_in_dim.2.refs_2_.blk_ref.refs_1_, bf16[28,768,768]{2,1,0:T(8,128)(2,1)} %get-tuple-element.42.refs_2_), custom_call_target="tpu_custom_call", output_to_operand_aliasing={{1}: (2, {})} | custom-call | flops 1207959552 | bytes 3000000 | tf_op jit(solution)/shard_map/dispatch6/pallas_call | solution.py:204
  75.2 8.1 %late_scores.1 = (bf16[28,768,768]{2,1,0:T(8,128)(2,1)}, bf16[40,512,768]{2,1,0:T(8,128)(2,1)}, f32[1,8,1024]{2,1,0:T(8,128)S(1)}, f32[8,768]{1,0:T(8,128)S(1)}, f32[8,1024]{1,0:T(8,128)S(1)}) custom-call(bf16[1040,768]{1,0:T(8,128)(2,1)S(1)} %collective-permute-done.9.source, ...), custom_call_target="tpu_custom_call", output_to_operand_aliasing={{0}: (12, {}), {1}: (13, {})} | custom-call | flops 3623878656 | bytes 20000000 | tf_op jit(solution)/shard_map/late_scores/pallas_call | solution.py:390
  91.7 8.6 %sums1.1 = (bf16[528,768]{1,0:T(8,128)(2,1)}, bf16[528,768]{1,0:T(8,128)(2,1)}, bf16[528,768]{1,0:T(8,128)(2,1)}, bf16[528,768]{1,0:T(8,128)(2,1)}, f32[8,768]{1,0:T(8,128)}) custom-call(s32[8]{0:T(128)} %concatenate.17.refs_0_.where_ref, f32[8,1024]{1,0:T(8,128)} %copy-done.15, f32[8,1024]{1,0:T(8,128)} %copy-done.16, f32[8,1024]{1,0:T(8,128)} %copy-done.17, ...), custom_call_target="tpu_custom_call" | custom-call | flops 2415919104 | bytes 12000000 | tf_op jit(solution)/shard_map/sums1/pallas_call | solution.py:583
  100.3 3.3 %sums0.2.refs_1_ = bf16[528,768]{1,0:T(8,128)(2,1)} custom-call(f32[8,768]{1,0:T(8,128)} %get-tuple-element.53.refs_0_.refs_1_, f32[8,768]{1,0:T(8,128)} %get-tuple-element.53.refs_0_.refs_1_, bf16[40,512,768]{2,1,0:T(8,128)(2,1)} %get-tuple-element.51.refs_8_.refs_2_, bf16[28,768,768]{2,1,0:T(8,128)(2,1)} %get-tuple-element.52.refs_9_.refs_3_), custom_call_target="tpu_custom_call" | custom-call | flops 603979776 | bytes 3000000 | tf_op jit(solution)/shard_map/sums0/pallas_call | solution.py:583
  104.7 3.8 %collective-permute-start.21 = (bf16[528,768]{1,0:T(8,128)(2,1)S(1)}, bf16[528,768]{1,0:T(8,128)(2,1)S(1)}, u32[]{:S(2)}, u32[]{:S(2)}) collective-permute-start(bf16[528,768]{1,0:T(8,128)(2,1)S(1)} %copy-done.19), channel_id=1, source_target_pairs={{0,32},{32,64},{64,96},{96,0},{16,112},{48,16},{80,48},{112,80},{1... | collective-permute-start | bytes 2433032 | tf_op jit(solution)/shard_map/ppermute | solution.py:44
  108.5 5.5 %sums0.3 = (bf16[528,768]{1,0:T(8,128)(2,1)}, bf16[528,768]{1,0:T(8,128)(2,1)}, bf16[528,768]{1,0:T(8,128)(2,1)}) custom-call(f32[8,768]{1,0:T(8,128)} %get-tuple-element.53.refs_0_.refs_1_, bf16[528,768]{1,0:T(8,128)(2,1)} %sums0.2.refs_1_, bf16[40,512,768]{2,1,0:T(8,128)(2,1)} %get-tuple-element.51.refs_8_.refs_2_, ...), custom_call_target="tpu_custom_call" | custom-call | flops 1811939328 | bytes 9000000 | tf_op jit(solution)/shard_map/sums0/pallas_call | solution.py:583
  117.3 2.4 %collective-permute-start.16 = (bf16[528,768]{1,0:T(8,128)(2,1)S(1)}, bf16[528,768]{1,0:T(8,128)(2,1)S(1)}, u32[]{:S(2)}, u32[]{:S(2)}) collective-permute-start(bf16[528,768]{1,0:T(8,128)(2,1)S(1)} %add_convert_fusion.1), channel_id=1, source_target_pairs={{0,1},{1,2},{2,3},{3,0},{16,19},{17,16},{18,17},{19,18},{4,5},{5,6... | collective-permute-start | bytes 2433032 | tf_op jit(solution)/shard_map/ppermute | solution.py:44
  119.9 1.8 collective-permute-start.22
  121.6 9.1 %collective-permute-done.14.refs_1_ = bf16[528,768]{1,0:T(8,128)(2,1)S(1)} collective-permute-done((bf16[528,768]{1,0:T(8,128)(2,1)}, bf16[528,768]{1,0:T(8,128)(2,1)S(1)}, u32[]{:S(2)}, u32[]{:S(2)}) %collective-permute-start.14) | collective-permute-done | bytes 811040 | tf_op jit(solution)/shard_map/ppermute | solution.py:44
  130.8 5.3 %collective-permute-done.16.refs_2_ = bf16[528,768]{1,0:T(8,128)(2,1)S(1)} collective-permute-done((bf16[528,768]{1,0:T(8,128)(2,1)S(1)}, bf16[528,768]{1,0:T(8,128)(2,1)S(1)}, u32[]{:S(2)}, u32[]{:S(2)}) %collective-permute-start.16) | collective-permute-done | bytes 811040 | tf_op jit(solution)/shard_map/ppermute | solution.py:44
  138.6 1.7 collective-permute-start.18
  141.8 1.7 parted1.1
  143.6 3.5 %collective-permute-start.24 = (bf16[144,768]{1,0:T(8,128)(2,1)}, bf16[144,768]{1,0:T(8,128)(2,1)S(1)}, u32[]{:S(2)}, u32[]{:S(2)}) collective-permute-start(bf16[144,768]{1,0:T(8,128)(2,1)} %get-tuple-element.67), channel_id=1, source_target_pairs={{0,1},{1,2},{2,3},{3,0},{16,19},{17,16},{18,17},{19,18},{4,5},{5,6... | collective-permute-start | bytes 663560 | tf_op jit(solution)/shard_map/ppermute | solution.py:44
  150.9 2.4 %collective-permute-done.24.refs_6_ = bf16[144,768]{1,0:T(8,128)(2,1)S(1)} collective-permute-done((bf16[144,768]{1,0:T(8,128)(2,1)}, bf16[144,768]{1,0:T(8,128)(2,1)S(1)}, u32[]{:S(2)}, u32[]{:S(2)}) %collective-permute-start.24) | collective-permute-done | bytes 221216 | tf_op jit(solution)/shard_map/ppermute | solution.py:44
  153.3 3.7 %collective-permute-done.25.refs_7_ = bf16[144,768]{1,0:T(8,128)(2,1)S(1)} collective-permute-done((bf16[144,768]{1,0:T(8,128)(2,1)S(1)}, bf16[144,768]{1,0:T(8,128)(2,1)S(1)}, u32[]{:S(2)}, u32[]{:S(2)}) %collective-permute-start.25) | collective-permute-done | bytes 221216 | tf_op jit(solution)/shard_map/ppermute | solution.py:48
  158.0 2.7 %final.1.refs_0_ = bf16[2,128,768]{2,1,0:T(8,128)(2,1)S(1)} custom-call(bf16[144,768]{1,0:T(8,128)(2,1)S(1)} %copy-done.8, bf16[144,768]{1,0:T(8,128)(2,1)S(1)} %collective-permute-done.17.refs_1_, bf16[144,768]{1,0:T(8,128)(2,1)S(1)} %collective-permute-done.18.refs_2_, bf16[144,768]{1,0:T(8,128)(2,1)S(1)} %collective-permute-done.19.refs_3_, ...), custom_call_target="tpu_custom_call" | custom-call | flops 1000000 | bytes 2000000 | tf_op jit(solution)/shard_map/final/pallas_call | solution.py:706
  162.2 2.0 %collective-permute-start.28 = (bf16[2,128,768]{2,1,0:T(8,128)(2,1)S(1)}, bf16[2,128,768]{2,1,0:T(8,128)(2,1)}, u32[]{:S(2)}, u32[]{:S(2)}) collective-permute-start(bf16[2,128,768]{2,1,0:T(8,128)(2,1)S(1)} %final.1.refs_0_), channel_id=1, source_target_pairs={{0,64},{32,96},{64,0},{96,32},{1,65},{33,97},{65,1},{97,33},{2,66}... | collective-permute-start | bytes 1179656 | tf_op jit(solution)/shard_map/ppermute | solution.py:48
  164.1 3.7 %collective-permute-start.29 = (bf16[2,128,768]{2,1,0:T(8,128)(2,1)S(1)}, bf16[2,128,768]{2,1,0:T(8,128)(2,1)}, u32[]{:S(2)}, u32[]{:S(2)}) collective-permute-start(bf16[2,128,768]{2,1,0:T(8,128)(2,1)S(1)} %final.1.refs_0_), channel_id=1, source_target_pairs={{0,16},{16,0},{1,17},{17,1},{2,18},{18,2},{3,19},{19,3},{4,20},{20... | collective-permute-start | bytes 1179656 | tf_op jit(solution)/shard_map/ppermute | solution.py:52
  167.9 8.0 %collective-permute-start.30 = (bf16[2,128,768]{2,1,0:T(8,128)(2,1)}, bf16[2,128,768]{2,1,0:T(8,128)(2,1)}, u32[]{:S(2)}, u32[]{:S(2)}) collective-permute-start(bf16[2,128,768]{2,1,0:T(8,128)(2,1)} %collective-permute-done.26.refs_1_), channel_id=1, source_target_pairs={{0,16},{16,0},{1,17},{17,1},{2,18},{18,2},{3,19},{19,3},{4,20},{20... | collective-permute-start | bytes 1179656 | tf_op jit(solution)/shard_map/ppermute | solution.py:52
  175.9 4.5 %collective-permute-start.31 = (bf16[2,128,768]{2,1,0:T(8,128)(2,1)}, bf16[2,128,768]{2,1,0:T(8,128)(2,1)}, u32[]{:S(2)}, u32[]{:S(2)}) collective-permute-start(bf16[2,128,768]{2,1,0:T(8,128)(2,1)} %collective-permute-done.27.refs_2_), channel_id=1, source_target_pairs={{0,16},{16,0},{1,17},{17,1},{2,18},{18,2},{3,19},{19,3},{4,20},{20... | collective-permute-start | bytes 1179656 | tf_op jit(solution)/shard_map/ppermute | solution.py:52
  180.5 2.3 %collective-permute-start.32 = (bf16[2,128,768]{2,1,0:T(8,128)(2,1)}, bf16[2,128,768]{2,1,0:T(8,128)(2,1)}, u32[]{:S(2)}, u32[]{:S(2)}) collective-permute-start(bf16[2,128,768]{2,1,0:T(8,128)(2,1)} %collective-permute-done.28.refs_3_), channel_id=1, source_target_pairs={{0,16},{16,0},{1,17},{17,1},{2,18},{18,2},{3,19},{19,3},{4,20},{20... | collective-permute-start | bytes 1179656 | tf_op jit(solution)/shard_map/ppermute | solution.py:52
  184.4 3.6 %place.1 = bf16[4,4,128,768]{3,2,1,0:T(8,128)(2,1)} custom-call(s32[10]{0:T(128)S(1)} %concatenate.16.where_ref, bf16[2,128,768]{2,1,0:T(8,128)(2,1)S(1)} %final.1.refs_0_, bf16[2,128,768]{2,1,0:T(8,128)(2,1)} %collective-permute-done.26.refs_1_, bf16[2,128,768]{2,1,0:T(8,128)(2,1)} %collective-permute-done.27.refs_2_, ...), custom_call_target="tpu_custom_call" | custom-call | bytes 6000000 | tf_op jit(solution)/shard_map/place/pallas_call | solution.py:743
  (106 shorter events, 32.8 us)
Async XLA Ops:
  3.2 8.4 %collective-permute-start.1 = (bf16[1040,768]{1,0:T(8,128)(2,1)}, bf16[1040,768]{1,0:T(8,128)(2,1)}, u32[]{:S(2)}, u32[]{:S(2)}) collective-permute-start(bf16[1040,768]{1,0:T(8,128)(2,1)} %pack.1.refs_0_), channel_id=1, source_target_pairs={{0,16},{16,0},{1,17},{17,1},{2,18},{18,2},{3,19},{19,3},{4,20},{20... | collective-permute-start | bytes 4792328 | tf_op jit(solution)/shard_map/ppermute | solution.py:52
  4.7 42.6 %collective-permute-start = (bf16[1040,768]{1,0:T(8,128)(2,1)}, bf16[1040,768]{1,0:T(8,128)(2,1)}, u32[]{:S(2)}, u32[]{:S(2)}) collective-permute-start(bf16[1040,768]{1,0:T(8,128)(2,1)} %pack.1.refs_0_), channel_id=1, source_target_pairs={{0,4},{4,8},{8,12},{12,0},{16,28},{20,16},{24,20},{28,24},{1,5},{5... | collective-permute-start | bytes 4792328 | tf_op jit(solution)/shard_map/ppermute | solution.py:44
  7.5 39.8 %collective-permute-start.2 = (bf16[1040,768]{1,0:T(8,128)(2,1)}, bf16[1040,768]{1,0:T(8,128)(2,1)}, u32[]{:S(2)}, u32[]{:S(2)}) collective-permute-start(bf16[1040,768]{1,0:T(8,128)(2,1)} %pack.1.refs_0_), channel_id=1, source_target_pairs={{0,12},{4,0},{8,4},{12,8},{16,20},{20,24},{24,28},{28,16},{1,13},{... | collective-permute-start | bytes 4792328 | tf_op jit(solution)/shard_map/ppermute | solution.py:44
  8.8 35.5 %collective-permute-start.3 = (bf16[1024,768]{1,0:T(8,128)(2,1)}, bf16[1024,768]{1,0:T(8,128)(2,1)S(1)}, u32[]{:S(2)}, u32[]{:S(2)}) collective-permute-start(bf16[1024,768]{1,0:T(8,128)(2,1)} %constant_dynamic-slice_fusion.1.c0), channel_id=1, source_target_pairs={{0,1},{1,2},{2,3},{3,0},{16,19},{17,16},{18,17},{19,18},{4,5},{5,6... | collective-permute-start | bytes 4718600 | tf_op jit(solution)/shard_map/ppermute | solution.py:44
  11.3 36.0 %collective-permute-start.4 = (bf16[1024,768]{1,0:T(8,128)(2,1)}, bf16[1024,768]{1,0:T(8,128)(2,1)S(1)}, u32[]{:S(2)}, u32[]{:S(2)}) collective-permute-start(bf16[1024,768]{1,0:T(8,128)(2,1)} %constant_dynamic-slice_fusion.1.c0), channel_id=1, source_target_pairs={{0,3},{1,0},{2,1},{3,2},{16,17},{17,18},{18,19},{19,16},{4,7},{5,4... | collective-permute-start | bytes 4718600 | tf_op jit(solution)/shard_map/ppermute | solution.py:44
  47.3 11.1 %collective-permute-start.6 = (bf16[1040,768]{1,0:T(8,128)(2,1)}, bf16[1040,768]{1,0:T(8,128)(2,1)S(1)}, u32[]{:S(2)}, u32[]{:S(2)}) collective-permute-start(bf16[1040,768]{1,0:T(8,128)(2,1)} %tie.3.refs_0_), channel_id=1, source_target_pairs={{0,16},{16,0},{1,17},{17,1},{2,18},{18,2},{3,19},{19,3},{4,20},{20... | collective-permute-start | bytes 4792328 | tf_op jit(solution)/shard_map/ppermute | solution.py:52
  47.4 11.0 %collective-permute-start.7 = (bf16[1040,768]{1,0:T(8,128)(2,1)}, bf16[1040,768]{1,0:T(8,128)(2,1)S(1)}, u32[]{:S(2)}, u32[]{:S(2)}) collective-permute-start(bf16[1040,768]{1,0:T(8,128)(2,1)} %collective-permute-done.2.refs_2_.refs_1_), channel_id=1, source_target_pairs={{0,16},{16,0},{1,17},{17,1},{2,18},{18,2},{3,19},{19,3},{4,20},{20... | collective-permute-start | bytes 4792328 | tf_op jit(solution)/shard_map/ppermute | solution.py:52
  47.9 23.3 %collective-permute-start.5 = (bf16[1040,768]{1,0:T(8,128)(2,1)}, bf16[1040,768]{1,0:T(8,128)(2,1)S(1)}, u32[]{:S(2)}, u32[]{:S(2)}) collective-permute-start(bf16[1040,768]{1,0:T(8,128)(2,1)} %tie.3.refs_0_), channel_id=1, source_target_pairs={{0,4},{4,8},{8,12},{12,0},{16,28},{20,16},{24,20},{28,24},{1,5},{5... | collective-permute-start | bytes 4792328 | tf_op jit(solution)/shard_map/ppermute | solution.py:44
  49.5 21.7 %collective-permute-start.8 = (bf16[1024,768]{1,0:T(8,128)(2,1)S(1)}, bf16[1024,768]{1,0:T(8,128)(2,1)S(1)}, u32[]{:S(2)}, u32[]{:S(2)}) collective-permute-start(bf16[1024,768]{1,0:T(8,128)(2,1)S(1)} %collective-permute-done.3.refs_3_.c1), channel_id=1, source_target_pairs={{0,1},{1,2},{2,3},{3,0},{16,19},{17,16},{18,17},{19,18},{4,5},{5,6... | collective-permute-start | bytes 4718600 | tf_op jit(solution)/shard_map/ppermute | solution.py:44
  71.8 3.4 %collective-permute-start.9 = (bf16[1040,768]{1,0:T(8,128)(2,1)S(1)}, bf16[1040,768]{1,0:T(8,128)(2,1)S(1)}, u32[]{:S(2)}, u32[]{:S(2)}) collective-permute-start(bf16[1040,768]{1,0:T(8,128)(2,1)S(1)} %tie.4.refs_0_), channel_id=1, source_target_pairs={{0,16},{16,0},{1,17},{17,1},{2,18},{18,2},{3,19},{19,3},{4,20},{20... | collective-permute-start | bytes 4792328 | tf_op jit(solution)/shard_map/ppermute | solution.py:52
  85.3 4.2 %collective-permute-start.11 = (f32[8,1024]{1,0:T(8,128)S(1)}, f32[8,1024]{1,0:T(8,128)S(1)}, u32[]{:S(2)}, u32[]{:S(2)}) collective-permute-start(f32[8,1024]{1,0:T(8,128)S(1)} %log_add_fusion.refs_1_), channel_id=1, source_target_pairs={{0,4},{4,8},{8,12},{12,0},{16,28},{20,16},{24,20},{28,24},{1,5},{5... | collective-permute-start | bytes 98312 | tf_op jit(solution)/shard_map/ppermute | solution.py:44
  85.8 4.5 %collective-permute-start.12 = (f32[8,1024]{1,0:T(8,128)S(1)}, f32[8,1024]{1,0:T(8,128)S(1)}, u32[]{:S(2)}, u32[]{:S(2)}) collective-permute-start(f32[8,1024]{1,0:T(8,128)S(1)} %log_add_fusion.refs_1_), channel_id=1, source_target_pairs={{0,12},{4,0},{8,4},{12,8},{16,20},{20,24},{24,28},{28,16},{1,13},{... | collective-permute-start | bytes 98312 | tf_op jit(solution)/shard_map/ppermute | solution.py:44
  86.8 4.3 %collective-permute-start.13 = (f32[8,1024]{1,0:T(8,128)S(1)}, f32[8,1024]{1,0:T(8,128)S(1)}, u32[]{:S(2)}, u32[]{:S(2)}) collective-permute-start(f32[8,1024]{1,0:T(8,128)S(1)} %log_add_fusion.refs_1_), channel_id=1, source_target_pairs={{0,8},{4,12},{8,0},{12,4},{1,9},{5,13},{9,1},{13,5},{2,10},{6,14},... | collective-permute-start | bytes 98312 | tf_op jit(solution)/shard_map/ppermute | solution.py:48
  103.6 12.3 %collective-permute-start.15 = (bf16[528,768]{1,0:T(8,128)(2,1)}, bf16[528,768]{1,0:T(8,128)(2,1)S(1)}, u32[]{:S(2)}, u32[]{:S(2)}) collective-permute-start(bf16[528,768]{1,0:T(8,128)(2,1)} %sums0.2.refs_1_), channel_id=1, source_target_pairs={{0,1},{1,2},{2,3},{3,0},{16,19},{17,16},{18,17},{19,18},{4,5},{5,6... | collective-permute-start | bytes 2433032 | tf_op jit(solution)/shard_map/ppermute | solution.py:44
  104.7 14.9 %collective-permute-start.21 = (bf16[528,768]{1,0:T(8,128)(2,1)S(1)}, bf16[528,768]{1,0:T(8,128)(2,1)S(1)}, u32[]{:S(2)}, u32[]{:S(2)}) collective-permute-start(bf16[528,768]{1,0:T(8,128)(2,1)S(1)} %copy-done.19), channel_id=1, source_target_pairs={{0,32},{32,64},{64,96},{96,0},{16,112},{48,16},{80,48},{112,80},{1... | collective-permute-start | bytes 2433032 | tf_op jit(solution)/shard_map/ppermute | solution.py:44
  114.0 16.7 %collective-permute-start.14 = (bf16[528,768]{1,0:T(8,128)(2,1)}, bf16[528,768]{1,0:T(8,128)(2,1)S(1)}, u32[]{:S(2)}, u32[]{:S(2)}) collective-permute-start(bf16[528,768]{1,0:T(8,128)(2,1)} %get-tuple-element.55), channel_id=1, source_target_pairs={{0,3},{1,0},{2,1},{3,2},{16,17},{17,18},{18,19},{19,16},{4,7},{5,4... | collective-permute-start | bytes 2433032 | tf_op jit(solution)/shard_map/ppermute | solution.py:44
  115.9 25.9 %collective-permute-start.20 = (bf16[528,768]{1,0:T(8,128)(2,1)S(1)}, bf16[528,768]{1,0:T(8,128)(2,1)S(1)}, u32[]{:S(2)}, u32[]{:S(2)}) collective-permute-start(bf16[528,768]{1,0:T(8,128)(2,1)S(1)} %tie.5), channel_id=1, source_target_pairs={{0,96},{32,0},{64,32},{96,64},{16,48},{48,80},{80,112},{112,16},{1... | collective-permute-start | bytes 2433032 | tf_op jit(solution)/shard_map/ppermute | solution.py:44
  117.3 18.8 %collective-permute-start.16 = (bf16[528,768]{1,0:T(8,128)(2,1)S(1)}, bf16[528,768]{1,0:T(8,128)(2,1)S(1)}, u32[]{:S(2)}, u32[]{:S(2)}) collective-permute-start(bf16[528,768]{1,0:T(8,128)(2,1)S(1)} %add_convert_fusion.1), channel_id=1, source_target_pairs={{0,1},{1,2},{2,3},{3,0},{16,19},{17,16},{18,17},{19,18},{4,5},{5,6... | collective-permute-start | bytes 2433032 | tf_op jit(solution)/shard_map/ppermute | solution.py:44
  119.9 21.9 %collective-permute-start.22 = (bf16[528,768]{1,0:T(8,128)(2,1)S(1)}, bf16[528,768]{1,0:T(8,128)(2,1)S(1)}, u32[]{:S(2)}, u32[]{:S(2)}) collective-permute-start(bf16[528,768]{1,0:T(8,128)(2,1)S(1)} %add_convert_fusion), channel_id=1, source_target_pairs={{0,32},{32,64},{64,96},{96,0},{16,112},{48,16},{80,48},{112,80},{1... | collective-permute-start | bytes 2433032 | tf_op jit(solution)/shard_map/ppermute | solution.py:44
  137.5 9.6 %collective-permute-start.17 = (bf16[144,768]{1,0:T(8,128)(2,1)S(1)}, bf16[144,768]{1,0:T(8,128)(2,1)S(1)}, u32[]{:S(2)}, u32[]{:S(2)}) collective-permute-start(bf16[144,768]{1,0:T(8,128)(2,1)S(1)} %get-tuple-element.58), channel_id=1, source_target_pairs={{0,96},{32,0},{64,32},{96,64},{16,48},{48,80},{80,112},{112,16},{1... | collective-permute-start | bytes 663560 | tf_op jit(solution)/shard_map/ppermute | solution.py:44
  138.6 10.7 %collective-permute-start.18 = (bf16[144,768]{1,0:T(8,128)(2,1)S(1)}, bf16[144,768]{1,0:T(8,128)(2,1)S(1)}, u32[]{:S(2)}, u32[]{:S(2)}) collective-permute-start(bf16[144,768]{1,0:T(8,128)(2,1)S(1)} %get-tuple-element.59), channel_id=1, source_target_pairs={{0,32},{32,64},{64,96},{96,0},{16,112},{48,16},{80,48},{112,80},{1... | collective-permute-start | bytes 663560 | tf_op jit(solution)/shard_map/ppermute | solution.py:44
  140.3 9.0 %collective-permute-start.19 = (bf16[144,768]{1,0:T(8,128)(2,1)S(1)}, bf16[144,768]{1,0:T(8,128)(2,1)S(1)}, u32[]{:S(2)}, u32[]{:S(2)}) collective-permute-start(bf16[144,768]{1,0:T(8,128)(2,1)S(1)} %get-tuple-element.60), channel_id=1, source_target_pairs={{0,64},{32,96},{64,0},{96,32},{1,65},{33,97},{65,1},{97,33},{2,66}... | collective-permute-start | bytes 663560 | tf_op jit(solution)/shard_map/ppermute | solution.py:48
  143.6 7.3 %collective-permute-start.23 = (bf16[144,768]{1,0:T(8,128)(2,1)}, bf16[144,768]{1,0:T(8,128)(2,1)S(1)}, u32[]{:S(2)}, u32[]{:S(2)}) collective-permute-start(bf16[144,768]{1,0:T(8,128)(2,1)} %get-tuple-element.66), channel_id=1, source_target_pairs={{0,3},{1,0},{2,1},{3,2},{16,17},{17,18},{18,19},{19,16},{4,7},{5,4... | collective-permute-start | bytes 663560 | tf_op jit(solution)/shard_map/ppermute | solution.py:44
  143.6 9.6 %collective-permute-start.24 = (bf16[144,768]{1,0:T(8,128)(2,1)}, bf16[144,768]{1,0:T(8,128)(2,1)S(1)}, u32[]{:S(2)}, u32[]{:S(2)}) collective-permute-start(bf16[144,768]{1,0:T(8,128)(2,1)} %get-tuple-element.67), channel_id=1, source_target_pairs={{0,1},{1,2},{2,3},{3,0},{16,19},{17,16},{18,17},{19,18},{4,5},{5,6... | collective-permute-start | bytes 663560 | tf_op jit(solution)/shard_map/ppermute | solution.py:44
  147.1 9.9 %collective-permute-start.25 = (bf16[144,768]{1,0:T(8,128)(2,1)S(1)}, bf16[144,768]{1,0:T(8,128)(2,1)S(1)}, u32[]{:S(2)}, u32[]{:S(2)}) collective-permute-start(bf16[144,768]{1,0:T(8,128)(2,1)S(1)} %get-tuple-element.68), channel_id=1, source_target_pairs={{0,2},{1,3},{2,0},{3,1},{4,6},{5,7},{6,4},{7,5},{8,10},{9,11},{10,... | collective-permute-start | bytes 663560 | tf_op jit(solution)/shard_map/ppermute | solution.py:48
  160.6 7.3 %collective-permute-start.26 = (bf16[2,128,768]{2,1,0:T(8,128)(2,1)S(1)}, bf16[2,128,768]{2,1,0:T(8,128)(2,1)}, u32[]{:S(2)}, u32[]{:S(2)}) collective-permute-start(bf16[2,128,768]{2,1,0:T(8,128)(2,1)S(1)} %final.1.refs_0_), channel_id=1, source_target_pairs={{0,32},{32,64},{64,96},{96,0},{16,112},{48,16},{80,48},{112,80},{1... | collective-permute-start | bytes 1179656 | tf_op jit(solution)/shard_map/ppermute | solution.py:44
  161.1 14.8 %collective-permute-start.27 = (bf16[2,128,768]{2,1,0:T(8,128)(2,1)S(1)}, bf16[2,128,768]{2,1,0:T(8,128)(2,1)}, u32[]{:S(2)}, u32[]{:S(2)}) collective-permute-start(bf16[2,128,768]{2,1,0:T(8,128)(2,1)S(1)} %final.1.refs_0_), channel_id=1, source_target_pairs={{0,96},{32,0},{64,32},{96,64},{16,48},{48,80},{80,112},{112,16},{1... | collective-permute-start | bytes 1179656 | tf_op jit(solution)/shard_map/ppermute | solution.py:44
  162.2 18.3 %collective-permute-start.28 = (bf16[2,128,768]{2,1,0:T(8,128)(2,1)S(1)}, bf16[2,128,768]{2,1,0:T(8,128)(2,1)}, u32[]{:S(2)}, u32[]{:S(2)}) collective-permute-start(bf16[2,128,768]{2,1,0:T(8,128)(2,1)S(1)} %final.1.refs_0_), channel_id=1, source_target_pairs={{0,64},{32,96},{64,0},{96,32},{1,65},{33,97},{65,1},{97,33},{2,66}... | collective-permute-start | bytes 1179656 | tf_op jit(solution)/shard_map/ppermute | solution.py:48
  164.1 18.7 %collective-permute-start.29 = (bf16[2,128,768]{2,1,0:T(8,128)(2,1)S(1)}, bf16[2,128,768]{2,1,0:T(8,128)(2,1)}, u32[]{:S(2)}, u32[]{:S(2)}) collective-permute-start(bf16[2,128,768]{2,1,0:T(8,128)(2,1)S(1)} %final.1.refs_0_), channel_id=1, source_target_pairs={{0,16},{16,0},{1,17},{17,1},{2,18},{18,2},{3,19},{19,3},{4,20},{20... | collective-permute-start | bytes 1179656 | tf_op jit(solution)/shard_map/ppermute | solution.py:52
  167.9 14.9 %collective-permute-start.30 = (bf16[2,128,768]{2,1,0:T(8,128)(2,1)}, bf16[2,128,768]{2,1,0:T(8,128)(2,1)}, u32[]{:S(2)}, u32[]{:S(2)}) collective-permute-start(bf16[2,128,768]{2,1,0:T(8,128)(2,1)} %collective-permute-done.26.refs_1_), channel_id=1, source_target_pairs={{0,16},{16,0},{1,17},{17,1},{2,18},{18,2},{3,19},{19,3},{4,20},{20... | collective-permute-start | bytes 1179656 | tf_op jit(solution)/shard_map/ppermute | solution.py:52
  175.9 6.9 %collective-permute-start.31 = (bf16[2,128,768]{2,1,0:T(8,128)(2,1)}, bf16[2,128,768]{2,1,0:T(8,128)(2,1)}, u32[]{:S(2)}, u32[]{:S(2)}) collective-permute-start(bf16[2,128,768]{2,1,0:T(8,128)(2,1)} %collective-permute-done.27.refs_2_), channel_id=1, source_target_pairs={{0,16},{16,0},{1,17},{17,1},{2,18},{18,2},{3,19},{19,3},{4,20},{20... | collective-permute-start | bytes 1179656 | tf_op jit(solution)/shard_map/ppermute | solution.py:52
  180.5 4.0 %collective-permute-start.32 = (bf16[2,128,768]{2,1,0:T(8,128)(2,1)}, bf16[2,128,768]{2,1,0:T(8,128)(2,1)}, u32[]{:S(2)}, u32[]{:S(2)}) collective-permute-start(bf16[2,128,768]{2,1,0:T(8,128)(2,1)} %collective-permute-done.28.refs_3_), channel_id=1, source_target_pairs={{0,16},{16,0},{1,17},{17,1},{2,18},{18,2},{3,19},{19,3},{4,20},{20... | collective-permute-start | bytes 1179656 | tf_op jit(solution)/shard_map/ppermute | solution.py:52
  (21 other events, 116.6 us)

commit v5 on v4

--- a/solution.py
+++ b/solution.py
@@ -459,46 +459,48 @@
     factor_out[...] = f_scr[...]
 
 
-def sums_kernel(part, owners, n_in, *refs):
+def sums_kernel(steps, n_in, *refs):
     ins, refs = refs[:n_in], refs[n_in:]
     e_any, rows_any = ins[-2:]
-    n = len(owners)
+    n = len(steps)
+    first_call = steps[0][1] == 1
     i = pl.program_id(0)
     slot = i % 2
 
-    def owner(k):
-        return sum(jnp.where(k == step, q, 0) for step, q in enumerate(owners))
-
-    q = owner(i)
-    if part == 1:
-        outs, factor_out, f_scr, refs = refs[:4], refs[4], refs[5], refs[6:]
+    def at_step(k, column):
+        return sum(jnp.where(k == step, entry[column], 0) for step, entry in enumerate(steps))
+
+    def block(k):
+        return 2 * at_step(k, 0) + at_step(k, 1)
+
+    if first_call:
+        outs, factor_out, f_scr, refs = refs[:5], refs[5], refs[6], refs[7:]
         (e_buf, rows_buf, esem, rsem), refs = refs[:4], refs[4:]
     else:
         outs, refs = refs[:n], refs[n:]
         (f_scr, e_buf, rows_buf, fsem, esem, rsem), refs = refs[:6], refs[6:]
 
     def load_block(k):
-        b = 2 * owner(k) + part
+        b = block(k)
         pltpu.make_async_copy(e_any.at[b], e_buf.at[k], esem.at[k]).start()
         pltpu.make_async_copy(rows_any.at[b], rows_buf.at[k], rsem.at[k]).start()
 
     @pl.when(i == 0)
     def _():
-        for k in range(min(2, n)):
+        for k in range(2):
             load_block(k)
-        if part == 1:
+        if first_call:
             load_factors(*ins[1:8], factor_out, f_scr, *refs[:4])
         else:
             load = pltpu.make_async_copy(ins[0], f_scr, fsem)
             load.start()
             load.wait()
 
-    if n > 2:
-        @pl.when(i < n - 2)
-        def _():
-            load_block(i + 2)
-
-    f = f_scr[pl.ds(2 * q + part, 1), :]
+    @pl.when(i < n - 2)
+    def _():
+        load_block(i + 2)
+
+    f = f_scr[pl.ds(block(i), 1), :]
     pltpu.make_async_copy(e_any.at[0], e_buf.at[i], esem.at[i]).wait()
     pltpu.make_async_copy(rows_any.at[0], rows_buf.at[i], rsem.at[i]).wait()
     totals, counts = [], []
@@ -507,10 +509,14 @@
         count = jnp.sum(w, axis=1, keepdims=True)
         counts.append(jnp.transpose(jnp.broadcast_to(count, (128, 128)))[0:EXTRA])
         totals.append(jnp.dot(w.astype(BF16), rows_buf[i], preferred_element_type=F32).astype(BF16))
-    if part == 0:
+    if first_call:
+        part_first(i, at_step(i, 0), slot, ins[0], totals, counts, outs[:4], *refs[4:9])
+
+        @pl.when(i == 4)
+        def _():
+            owner_first(0, 1, totals, counts, outs[4:], *refs[9:])
+    else:
         owner_first(i, n, totals, counts, outs, *refs)
-    else:
-        part_first(i, q, slot, ins[0], totals, counts, outs, *refs[4:])
 
 
 def owner_first(i, n, totals, counts, outs, buf, sem):
@@ -541,17 +547,19 @@
     def _():
         gcount[...] = jnp.zeros_like(gcount)
 
-    @pl.when(i >= 2)
+    @pl.when((i == 2) | (i == 3))
     def _():
         for k in range(4):
             send(k).wait()
 
-    for m in range(4):
-        at = sum(jnp.where(where_ref[4 + k] == m, k, 0) for k in range(1, 4))
-        buf[slot, at] = totals[m]
-        gcount[at, pl.ds(q, 1), :] = counts[m][0:1]
-    for k in range(4):
-        send(k).start()
+    @pl.when(i < 4)
+    def _():
+        for m in range(4):
+            at = sum(jnp.where(where_ref[4 + k] == m, k, 0) for k in range(1, 4))
+            buf[slot, at] = totals[m]
+            gcount[at, pl.ds(q, 1), :] = counts[m][0:1]
+        for k in range(4):
+            send(k).start()
 
     @pl.when(i == 3)
     def _():
@@ -560,6 +568,9 @@
             tile = jnp.concatenate([tile, jnp.zeros((EXTRA, D - 128), F32)], axis=1)
             gtile[k] = tile.astype(BF16)
             send_tile(k).start()
+
+    @pl.when(i == 4)
+    def _():
         for other in range(2):
             for k in range(4):
                 send(k, other).wait()
@@ -570,14 +581,15 @@
 SUMS_SHAPE = (BS + EXTRA, D)
 
 
-def sums_call(part, owners, small, big, out_shape, out_specs, own):
-    n = len(owners)
+def sums_call(steps, small, big, out_shape, out_specs, own):
+    n = len(steps)
+    first_call = steps[0][1] == 1
 
     def kern(*refs):
-        sums_kernel(part, owners, len(small) + len(big), *refs)
+        sums_kernel(steps, len(small) + len(big), *refs)
 
     specs = [pl.BlockSpec(memory_space=pl.ANY)] * len(small)
-    if part == 1:
+    if first_call:
         specs[0] = pl.BlockSpec(memory_space=pltpu.SMEM)
     factor = [pltpu.VMEM((NBLK, SLOTS), F32)]
     return pl.pallas_call(
@@ -588,16 +600,16 @@
         out_shape=out_shape,
         scratch_shapes=factor
         + [pltpu.VMEM((n, BS, SLOTS), BF16), pltpu.VMEM((n, SLOTS, D), BF16)]
-        + ([pltpu.SemaphoreType.DMA] if part == 0 else [])
+        + ([] if first_call else [pltpu.SemaphoreType.DMA])
         + [pltpu.SemaphoreType.DMA((n,)), pltpu.SemaphoreType.DMA((n,))]
         + own,
         compiler_params=params(54),
         cost_estimate=cost(2 * n * BS * SLOTS * D, n * 3e6),
-        name=f"sums{part}",
+        name=f"sums{n}",
     )(*small, *big)
 
 
-def part_sums(where, stats, idx, peak, e, rows):
+def first_sums(where, stats, idx, peak, e, rows):
     anywhere = pl.BlockSpec(memory_space=pl.ANY)
     own = [
         pltpu.VMEM((4, NSRC, TOK), F32),
@@ -609,26 +621,26 @@
         pltpu.VMEM((4, EXTRA, D), BF16),
         pltpu.SemaphoreType.DMA((2, 4)),
         pltpu.SemaphoreType.DMA((4,)),
+        pltpu.VMEM((1, *SUMS_SHAPE), BF16),
+        pltpu.SemaphoreType.DMA((1,)),
     ]
     *out, factor = sums_call(
-        1,
-        (3, 1, 2, 0),
+        ((3, 1), (1, 1), (2, 1), (0, 1), (3, 0)),
         (where, *stats, *idx, peak),
         (e, rows),
-        (jax.ShapeDtypeStruct(SUMS_SHAPE, BF16),) * 4 + (jax.ShapeDtypeStruct((NBLK, SLOTS), F32),),
-        (anywhere,) * 4 + (pl.BlockSpec((NBLK, SLOTS), lambda i: (0, 0)),),
+        (jax.ShapeDtypeStruct(SUMS_SHAPE, BF16),) * 5 + (jax.ShapeDtypeStruct((NBLK, SLOTS), F32),),
+        (anywhere,) * 5 + (pl.BlockSpec((NBLK, SLOTS), lambda i: (0, 0)),),
         own,
     )
-    return out, factor
-
-
-def owner_sums(owners, factor, after, e, rows):
+    return out[:4], out[4], factor
+
+
+def owner_sums(owners, factor, e, rows):
     n = len(owners)
     own = [pltpu.VMEM((n, *SUMS_SHAPE), BF16), pltpu.SemaphoreType.DMA((n,))]
     return sums_call(
-        0,
-        owners,
-        (factor, after),
+        tuple((q, 0) for q in owners),
+        (factor,),
         (e, rows),
         (jax.ShapeDtypeStruct(SUMS_SHAPE, BF16),) * n,
         (pl.BlockSpec(memory_space=pl.ANY),) * n,
@@ -828,9 +840,8 @@
     merged = m + jnp.log(jnp.exp(stat - m) + jnp.exp(theirs - m))
     stats = (merged, turn(merged, "y", 1), turn(merged, "y", -1), far(merged, "y"))
 
-    g, factor = part_sums(where, stats, idx, peak, e, rows)
-    (h3,) = owner_sums((3,), factor, factor, e, rows)
-    h1, h2, h0 = owner_sums((1, 2, 0), factor, h3, e, rows)
+    g, h3, factor = first_sums(where, stats, idx, peak, e, rows)
+    h1, h2, h0 = owner_sums((1, 2, 0), factor, e, rows)
     g, _ = ring_terms(*g, "z", h0)
     h, _ = ring_terms(h0, h1, h2, h3, "x")
     h = direct_terms(*parted(0, where, h), "z")

time: 189 us -> 187 us (0.989)
  Pallas kernels: 65.9 us -> 63.8 us
    pallas_call x3 -> x2, Pallas kernels: 17.4 us -> 15.3 us  [sums_call(): pl.pallas_call(kern, grid=(n,), in_specs=specs + [pl.BlockSpec(memory_spa...]
    unnamed x40 -> x38, local copies, waits for them, and re-layouts: 7.01 us -> 6.99 us
  transfers between devices with their start and end apart: 33 -> 33, of which waited for: 12 -> 15; matrix products, arithmetic and copies ran while one was open for 2% -> 2% of each run, Pallas kernels for 19% -> 20%
where the time goes in v5:
time: 187 us
  Pallas kernels  63.8 us (34%)
  waiting for transfers between devices  57.1 us (31%)
  starting transfers between devices  54.8 us (29%)
  local copies, waits for them, and re-layouts  10.2 us (5%)
    ppermute x20, waiting for transfers between devices, turn(): return lax.ppermute(a, axes, pairs)  49.1 us
    ppermute x20, starting transfers between devices, turn(): return lax.ppermute(a, axes, pairs)  28.8 us
    ppermute x9, starting transfers between devices, swap(): return lax.ppermute(a, 'core', [(0, 1), (1, 0)])  21.2 us
    pallas_call x2, Pallas kernels, sums_call(): pl.pallas_call(kern, grid=(n,), in_specs=specs + [pl.BlockSpec(memory_spa...  15.3 us
    pallas_call x3, Pallas kernels, dispatch(): pl.pallas_call(kern, grid=(n,), in_specs=in_specs, out_specs=(pl.BlockSpe...  13.8 us
    pallas_call x1, Pallas kernels, middle(): pl.pallas_call(middle_kernel, in_specs=[anywhere] * 2 + [vmem] + [anywher...  10.4 us
    pallas_call x1, Pallas kernels, late_scores(): pl.pallas_call(late_kernel, in_specs=[anywhere, vmem] + [anywhere] * 4 +...  8.09 us
    unnamed x38, local copies, waits for them, and re-layouts  6.99 us
  transfers between devices with their start and end apart: 33, of which 15 were waited for; matrix products, arithmetic and copies ran while one was open for 2% of the time, Pallas kernels for 20%

profile of v5, /device:TPU:1, one launch (start us, length us, event | category | flops | bytes accessed | tf_op | source)
XLA Modules:
  0.0 187.0 jit_solution(13881827735894230685)
XLA Ops:
  0.0 3.2 %pack.1.refs_0_ = bf16[1040,768]{1,0:T(8,128)(2,1)} custom-call(bf16[1024,768]{1,0:T(8,128)(2,1)} %vectors.1, s32[4,1024]{1,0:T(4,128)} %bitcast.13), custom_call_target="tpu_custom_call" | custom-call | bytes 3000000 | tf_op jit(solution)/shard_map/pack/pallas_call | solution.py:91
  3.2 1.5 collective-permute-start.1
  4.7 2.8 %collective-permute-start = (bf16[1040,768]{1,0:T(8,128)(2,1)}, bf16[1040,768]{1,0:T(8,128)(2,1)}, u32[]{:S(2)}, u32[]{:S(2)}) collective-permute-start(bf16[1040,768]{1,0:T(8,128)(2,1)} %pack.1.refs_0_), channel_id=1, source_target_pairs={{0,4},{4,8},{8,12},{12,0},{16,28},{20,16},{24,20},{28,24},{1,5},{5... | collective-permute-start | bytes 4792328 | tf_op jit(solution)/shard_map/ppermute | solution.py:44
  8.8 2.5 %collective-permute-start.3 = (bf16[1024,768]{1,0:T(8,128)(2,1)}, bf16[1024,768]{1,0:T(8,128)(2,1)S(1)}, u32[]{:S(2)}, u32[]{:S(2)}) collective-permute-start(bf16[1024,768]{1,0:T(8,128)(2,1)} %constant_dynamic-slice_fusion.1.c0), channel_id=1, source_target_pairs={{0,1},{1,2},{2,3},{3,0},{16,19},{17,16},{18,17},{19,18},{4,5},{5,6... | collective-permute-start | bytes 4718600 | tf_op jit(solution)/shard_map/ppermute | solution.py:44
  13.0 4.9 %dispatch0.1 = (f32[2,8,1024]{2,1,0:T(8,128)S(1)}, bf16[28,768,768]{2,1,0:T(8,128)(2,1)}) custom-call(bf16[1040,768]{1,0:T(8,128)(2,1)S(1)} %copy-done.4, bf16[1040,768]{1,0:T(8,128)(2,1)} %collective-permute-done.1.refs_1_, f32[8,128]{1,0:T(8,128)S(1)} %broadcast_in_dim.2.refs_2_.blk_ref.refs_1_), custom_call_target="tpu_custom_call" | custom-call | flops 2415919104 | bytes 6000000 | tf_op jit(solution)/shard_map/dispatch0/pallas_call | solution.py:204
  17.9 26.4 %collective-permute-done.3.refs_3_.c1 = bf16[1024,768]{1,0:T(8,128)(2,1)S(1)} collective-permute-done((bf16[1024,768]{1,0:T(8,128)(2,1)}, bf16[1024,768]{1,0:T(8,128)(2,1)S(1)}, u32[]{:S(2)}, u32[]{:S(2)}) %collective-permute-start.3) | collective-permute-done | bytes 1572896 | tf_op jit(solution)/shard_map/ppermute | solution.py:44
  44.3 3.0 %collective-permute-done.4.refs_4_.c2 = bf16[1024,768]{1,0:T(8,128)(2,1)S(1)} collective-permute-done((bf16[1024,768]{1,0:T(8,128)(2,1)}, bf16[1024,768]{1,0:T(8,128)(2,1)S(1)}, u32[]{:S(2)}, u32[]{:S(2)}) %collective-permute-start.4) | collective-permute-done | bytes 1572896 | tf_op jit(solution)/shard_map/ppermute | solution.py:44
  47.9 1.6 collective-permute-start.5
  49.5 2.9 %collective-permute-start.8 = (bf16[1024,768]{1,0:T(8,128)(2,1)S(1)}, bf16[1024,768]{1,0:T(8,128)(2,1)S(1)}, u32[]{:S(2)}, u32[]{:S(2)}) collective-permute-start(bf16[1024,768]{1,0:T(8,128)(2,1)S(1)} %collective-permute-done.3.refs_3_.c1), channel_id=1, source_target_pairs={{0,1},{1,2},{2,3},{3,0},{16,19},{17,16},{18,17},{19,18},{4,5},{5,6... | collective-permute-start | bytes 4718600 | tf_op jit(solution)/shard_map/ppermute | solution.py:44
  52.4 6.0 %dispatch2.1 = (f32[2,8,1024]{2,1,0:T(8,128)S(1)}, bf16[28,768,768]{2,1,0:T(8,128)(2,1)}) custom-call(bf16[1040,768]{1,0:T(8,128)(2,1)} %tie.3.refs_0_, bf16[1040,768]{1,0:T(8,128)(2,1)} %collective-permute-done.2.refs_2_.refs_1_, f32[8,128]{1,0:T(8,128)S(1)} %broadcast_in_dim.2.refs_2_.blk_ref.refs_1_, ...), custom_call_target="tpu_custom_call", output_to_operand_aliasing={{1}: (3, {})} | custom-call | flops 2415919104 | bytes 6000000 | tf_op jit(solution)/shard_map/dispatch2/pallas_call | solution.py:204
  58.4 10.4 %middle.1 = (bf16[28,768,768]{2,1,0:T(8,128)(2,1)}, f32[2,8,1024]{2,1,0:T(8,128)S(1)}, bf16[40,512,768]{2,1,0:T(8,128)(2,1)}, f32[8,512]{1,0:T(8,128)S(1)}, f32[8,512]{1,0:T(8,128)S(1)}) custom-call(bf16[1040,768]{1,0:T(8,128)(2,1)S(1)} %collective-permute-done.6.s0, ...), custom_call_target="tpu_custom_call", output_to_operand_aliasing={{0}: (6, {})} | custom-call | flops 2415919104 | bytes 20000000 | tf_op jit(solution)/shard_map/middle/pallas_call | solution.py:283
  68.9 2.3 %indices.2.refs_1_.refs_5_ = s32[8,512]{1,0:T(8,128)S(1)} custom-call(f32[2,8,1024]{2,1,0:T(8,128)S(1)} %get-tuple-element.38.refs_1_.refs_0_.rank0, f32[2,8,1024]{2,1,0:T(8,128)S(1)} %get-tuple-element.40.refs_1_.rank1, f32[2,8,1024]{2,1,0:T(8,128)S(1)} %get-tuple-element.42.refs_2_.rank2.refs_0_), custom_call_target="tpu_custom_call" | custom-call | flops 4000000000 | bytes 1000000 | tf_op jit(solution)/shard_map/indices/pallas_call | solution.py:157
  71.8 2.9 %dispatch6.1 = (f32[1,8,1024]{2,1,0:T(8,128)S(1)}, bf16[28,768,768]{2,1,0:T(8,128)(2,1)}) custom-call(bf16[1040,768]{1,0:T(8,128)(2,1)S(1)} %tie.4.refs_0_, f32[8,128]{1,0:T(8,128)S(1)} %broadcast_in_dim.2.refs_2_.blk_ref.refs_1_, bf16[28,768,768]{2,1,0:T(8,128)(2,1)} %get-tuple-element.43.refs_2_), custom_call_target="tpu_custom_call", output_to_operand_aliasing={{1}: (2, {})} | custom-call | flops 1207959552 | bytes 3000000 | tf_op jit(solution)/shard_map/dispatch6/pallas_call | solution.py:204
  75.2 8.1 %late_scores.1 = (bf16[28,768,768]{2,1,0:T(8,128)(2,1)}, bf16[40,512,768]{2,1,0:T(8,128)(2,1)}, f32[1,8,1024]{2,1,0:T(8,128)S(1)}, f32[8,768]{1,0:T(8,128)S(1)}, f32[8,1024]{1,0:T(8,128)S(1)}) custom-call(bf16[1040,768]{1,0:T(8,128)(2,1)S(1)} %collective-permute-done.9.source, ...), custom_call_target="tpu_custom_call", output_to_operand_aliasing={{0}: (12, {}), {1}: (13, {})} | custom-call | flops 3623878656 | bytes 20000000 | tf_op jit(solution)/shard_map/late_scores/pallas_call | solution.py:390
  91.6 9.7 %sums5.1 = (bf16[528,768]{1,0:T(8,128)(2,1)}, bf16[528,768]{1,0:T(8,128)(2,1)}, bf16[528,768]{1,0:T(8,128)(2,1)}, bf16[528,768]{1,0:T(8,128)(2,1)}, bf16[528,768]{1,0:T(8,128)(2,1)}, /*index=5*/f32[8,768]{1,0:T(8,128)}) custom-call(s32[8]{0:T(128)} %concatenate.17.refs_0_.where_ref, f32[8,1024]{1,0:T(8,128)} %copy-done.15, f32[8,1024]{1,0:T(8,128)} %copy-done.16, ...), custom_call_target="tpu_custom_call" | custom-call | flops 3019898880 | bytes 15000000 | tf_op jit(solution)/shard_map/sums5/pallas_call | solution.py:595
  102.5 3.8 %collective-permute-start.21 = (bf16[528,768]{1,0:T(8,128)(2,1)}, bf16[528,768]{1,0:T(8,128)(2,1)S(1)}, u32[]{:S(2)}, u32[]{:S(2)}) collective-permute-start(bf16[528,768]{1,0:T(8,128)(2,1)} %get-tuple-element.66), channel_id=1, source_target_pairs={{0,32},{32,64},{64,96},{96,0},{16,112},{48,16},{80,48},{112,80},{1... | collective-permute-start | bytes 2433032 | tf_op jit(solution)/shard_map/ppermute | solution.py:44
  106.2 5.6 %sums3.1 = (bf16[528,768]{1,0:T(8,128)(2,1)}, bf16[528,768]{1,0:T(8,128)(2,1)}, bf16[528,768]{1,0:T(8,128)(2,1)}) custom-call(f32[8,768]{1,0:T(8,128)} %get-tuple-element.54.refs_0_, bf16[40,512,768]{2,1,0:T(8,128)(2,1)} %get-tuple-element.52.refs_8_.refs_1_, bf16[28,768,768]{2,1,0:T(8,128)(2,1)} %get-tuple-element.53.refs_9_.refs_2_), custom_call_target="tpu_custom_call" | custom-call | flops 1811939328 | bytes 9000000 | tf_op jit(solution)/shard_map/sums3/pallas_call | solution.py:595
  114.9 2.3 %collective-permute-start.16 = (bf16[528,768]{1,0:T(8,128)(2,1)S(1)}, bf16[528,768]{1,0:T(8,128)(2,1)S(1)}, u32[]{:S(2)}, u32[]{:S(2)}) collective-permute-start(bf16[528,768]{1,0:T(8,128)(2,1)S(1)} %add_convert_fusion.1), channel_id=1, source_target_pairs={{0,1},{1,2},{2,3},{3,0},{16,19},{17,16},{18,17},{19,18},{4,5},{5,6... | collective-permute-start | bytes 2433032 | tf_op jit(solution)/shard_map/ppermute | solution.py:44
  117.4 1.9 %collective-permute-start.22 = (bf16[528,768]{1,0:T(8,128)(2,1)S(1)}, bf16[528,768]{1,0:T(8,128)(2,1)S(1)}, u32[]{:S(2)}, u32[]{:S(2)}) collective-permute-start(bf16[528,768]{1,0:T(8,128)(2,1)S(1)} %add_convert_fusion), channel_id=1, source_target_pairs={{0,32},{32,64},{64,96},{96,0},{16,112},{48,16},{80,48},{112,80},{1... | collective-permute-start | bytes 2433032 | tf_op jit(solution)/shard_map/ppermute | solution.py:44
  119.4 9.0 %collective-permute-done.14.refs_1_ = bf16[528,768]{1,0:T(8,128)(2,1)S(1)} collective-permute-done((bf16[528,768]{1,0:T(8,128)(2,1)}, bf16[528,768]{1,0:T(8,128)(2,1)S(1)}, u32[]{:S(2)}, u32[]{:S(2)}) %collective-permute-start.14) | collective-permute-done | bytes 811040 | tf_op jit(solution)/shard_map/ppermute | solution.py:44
  128.3 5.3 %collective-permute-done.16.refs_2_ = bf16[528,768]{1,0:T(8,128)(2,1)S(1)} collective-permute-done((bf16[528,768]{1,0:T(8,128)(2,1)S(1)}, bf16[528,768]{1,0:T(8,128)(2,1)S(1)}, u32[]{:S(2)}, u32[]{:S(2)}) %collective-permute-start.16) | collective-permute-done | bytes 811040 | tf_op jit(solution)/shard_map/ppermute | solution.py:44
  136.2 1.7 collective-permute-start.18
  137.9 1.9 %collective-permute-start.19 = (bf16[144,768]{1,0:T(8,128)(2,1)S(1)}, bf16[144,768]{1,0:T(8,128)(2,1)S(1)}, u32[]{:S(2)}, u32[]{:S(2)}) collective-permute-start(bf16[144,768]{1,0:T(8,128)(2,1)S(1)} %get-tuple-element.62), channel_id=1, source_target_pairs={{0,64},{32,96},{64,0},{96,32},{1,65},{33,97},{65,1},{97,33},{2,66}... | collective-permute-start | bytes 663560 | tf_op jit(solution)/shard_map/ppermute | solution.py:48
  139.8 1.7 parted1.1
  141.6 3.5 %collective-permute-start.24 = (bf16[144,768]{1,0:T(8,128)(2,1)}, bf16[144,768]{1,0:T(8,128)(2,1)S(1)}, u32[]{:S(2)}, u32[]{:S(2)}) collective-permute-start(bf16[144,768]{1,0:T(8,128)(2,1)} %get-tuple-element.69), channel_id=1, source_target_pairs={{0,1},{1,2},{2,3},{3,0},{16,19},{17,16},{18,17},{19,18},{4,5},{5,6... | collective-permute-start | bytes 663560 | tf_op jit(solution)/shard_map/ppermute | solution.py:44
  147.2 1.6 collective-permute-done.23.refs_5_
  148.8 2.4 %collective-permute-done.24.refs_6_ = bf16[144,768]{1,0:T(8,128)(2,1)S(1)} collective-permute-done((bf16[144,768]{1,0:T(8,128)(2,1)}, bf16[144,768]{1,0:T(8,128)(2,1)S(1)}, u32[]{:S(2)}, u32[]{:S(2)}) %collective-permute-start.24) | collective-permute-done | bytes 221216 | tf_op jit(solution)/shard_map/ppermute | solution.py:44
  151.2 3.9 %collective-permute-done.25.refs_7_ = bf16[144,768]{1,0:T(8,128)(2,1)S(1)} collective-permute-done((bf16[144,768]{1,0:T(8,128)(2,1)S(1)}, bf16[144,768]{1,0:T(8,128)(2,1)S(1)}, u32[]{:S(2)}, u32[]{:S(2)}) %collective-permute-start.25) | collective-permute-done | bytes 221216 | tf_op jit(solution)/shard_map/ppermute | solution.py:48
  156.1 2.7 %final.1.refs_0_ = bf16[2,128,768]{2,1,0:T(8,128)(2,1)S(1)} custom-call(bf16[144,768]{1,0:T(8,128)(2,1)S(1)} %copy-done.8, bf16[144,768]{1,0:T(8,128)(2,1)S(1)} %collective-permute-done.17.refs_1_, bf16[144,768]{1,0:T(8,128)(2,1)S(1)} %collective-permute-done.18.refs_2_, bf16[144,768]{1,0:T(8,128)(2,1)S(1)} %collective-permute-done.19.refs_3_, ...), custom_call_target="tpu_custom_call" | custom-call | flops 1000000 | bytes 2000000 | tf_op jit(solution)/shard_map/final/pallas_call | solution.py:718
  161.2 4.2 %collective-permute-start.29 = (bf16[2,128,768]{2,1,0:T(8,128)(2,1)S(1)}, bf16[2,128,768]{2,1,0:T(8,128)(2,1)}, u32[]{:S(2)}, u32[]{:S(2)}) collective-permute-start(bf16[2,128,768]{2,1,0:T(8,128)(2,1)S(1)} %final.1.refs_0_), channel_id=1, source_target_pairs={{0,16},{16,0},{1,17},{17,1},{2,18},{18,2},{3,19},{19,3},{4,20},{20... | collective-permute-start | bytes 1179656 | tf_op jit(solution)/shard_map/ppermute | solution.py:52
  166.1 14.3 %collective-permute-start.30 = (bf16[2,128,768]{2,1,0:T(8,128)(2,1)}, bf16[2,128,768]{2,1,0:T(8,128)(2,1)}, u32[]{:S(2)}, u32[]{:S(2)}) collective-permute-start(bf16[2,128,768]{2,1,0:T(8,128)(2,1)} %collective-permute-done.26.refs_1_), channel_id=1, source_target_pairs={{0,16},{16,0},{1,17},{17,1},{2,18},{18,2},{3,19},{19,3},{4,20},{20... | collective-permute-start | bytes 1179656 | tf_op jit(solution)/shard_map/ppermute | solution.py:52
  183.2 3.6 %place.1 = bf16[4,4,128,768]{3,2,1,0:T(8,128)(2,1)} custom-call(s32[10]{0:T(128)S(1)} %concatenate.16.where_ref, bf16[2,128,768]{2,1,0:T(8,128)(2,1)S(1)} %final.1.refs_0_, bf16[2,128,768]{2,1,0:T(8,128)(2,1)} %collective-permute-done.26.refs_1_, bf16[2,128,768]{2,1,0:T(8,128)(2,1)} %collective-permute-done.27.refs_2_, ...), custom_call_target="tpu_custom_call" | custom-call | bytes 6000000 | tf_op jit(solution)/shard_map/place/pallas_call | solution.py:755
  (103 shorter events, 29.0 us)
Async XLA Ops:
  3.2 8.3 %collective-permute-start.1 = (bf16[1040,768]{1,0:T(8,128)(2,1)}, bf16[1040,768]{1,0:T(8,128)(2,1)}, u32[]{:S(2)}, u32[]{:S(2)}) collective-permute-start(bf16[1040,768]{1,0:T(8,128)(2,1)} %pack.1.refs_0_), channel_id=1, source_target_pairs={{0,16},{16,0},{1,17},{17,1},{2,18},{18,2},{3,19},{19,3},{4,20},{20... | collective-permute-start | bytes 4792328 | tf_op jit(solution)/shard_map/ppermute | solution.py:52
  4.7 42.6 %collective-permute-start = (bf16[1040,768]{1,0:T(8,128)(2,1)}, bf16[1040,768]{1,0:T(8,128)(2,1)}, u32[]{:S(2)}, u32[]{:S(2)}) collective-permute-start(bf16[1040,768]{1,0:T(8,128)(2,1)} %pack.1.refs_0_), channel_id=1, source_target_pairs={{0,4},{4,8},{8,12},{12,0},{16,28},{20,16},{24,20},{28,24},{1,5},{5... | collective-permute-start | bytes 4792328 | tf_op jit(solution)/shard_map/ppermute | solution.py:44
  7.5 39.8 %collective-permute-start.2 = (bf16[1040,768]{1,0:T(8,128)(2,1)}, bf16[1040,768]{1,0:T(8,128)(2,1)}, u32[]{:S(2)}, u32[]{:S(2)}) collective-permute-start(bf16[1040,768]{1,0:T(8,128)(2,1)} %pack.1.refs_0_), channel_id=1, source_target_pairs={{0,12},{4,0},{8,4},{12,8},{16,20},{20,24},{24,28},{28,16},{1,13},{... | collective-permute-start | bytes 4792328 | tf_op jit(solution)/shard_map/ppermute | solution.py:44
  8.8 35.5 %collective-permute-start.3 = (bf16[1024,768]{1,0:T(8,128)(2,1)}, bf16[1024,768]{1,0:T(8,128)(2,1)S(1)}, u32[]{:S(2)}, u32[]{:S(2)}) collective-permute-start(bf16[1024,768]{1,0:T(8,128)(2,1)} %constant_dynamic-slice_fusion.1.c0), channel_id=1, source_target_pairs={{0,1},{1,2},{2,3},{3,0},{16,19},{17,16},{18,17},{19,18},{4,5},{5,6... | collective-permute-start | bytes 4718600 | tf_op jit(solution)/shard_map/ppermute | solution.py:44
  11.3 36.0 %collective-permute-start.4 = (bf16[1024,768]{1,0:T(8,128)(2,1)}, bf16[1024,768]{1,0:T(8,128)(2,1)S(1)}, u32[]{:S(2)}, u32[]{:S(2)}) collective-permute-start(bf16[1024,768]{1,0:T(8,128)(2,1)} %constant_dynamic-slice_fusion.1.c0), channel_id=1, source_target_pairs={{0,3},{1,0},{2,1},{3,2},{16,17},{17,18},{18,19},{19,16},{4,7},{5,4... | collective-permute-start | bytes 4718600 | tf_op jit(solution)/shard_map/ppermute | solution.py:44
  47.3 11.1 %collective-permute-start.6 = (bf16[1040,768]{1,0:T(8,128)(2,1)}, bf16[1040,768]{1,0:T(8,128)(2,1)S(1)}, u32[]{:S(2)}, u32[]{:S(2)}) collective-permute-start(bf16[1040,768]{1,0:T(8,128)(2,1)} %tie.3.refs_0_), channel_id=1, source_target_pairs={{0,16},{16,0},{1,17},{17,1},{2,18},{18,2},{3,19},{19,3},{4,20},{20... | collective-permute-start | bytes 4792328 | tf_op jit(solution)/shard_map/ppermute | solution.py:52
  47.4 11.0 %collective-permute-start.7 = (bf16[1040,768]{1,0:T(8,128)(2,1)}, bf16[1040,768]{1,0:T(8,128)(2,1)S(1)}, u32[]{:S(2)}, u32[]{:S(2)}) collective-permute-start(bf16[1040,768]{1,0:T(8,128)(2,1)} %collective-permute-done.2.refs_2_.refs_1_), channel_id=1, source_target_pairs={{0,16},{16,0},{1,17},{17,1},{2,18},{18,2},{3,19},{19,3},{4,20},{20... | collective-permute-start | bytes 4792328 | tf_op jit(solution)/shard_map/ppermute | solution.py:52
  47.9 23.3 %collective-permute-start.5 = (bf16[1040,768]{1,0:T(8,128)(2,1)}, bf16[1040,768]{1,0:T(8,128)(2,1)S(1)}, u32[]{:S(2)}, u32[]{:S(2)}) collective-permute-start(bf16[1040,768]{1,0:T(8,128)(2,1)} %tie.3.refs_0_), channel_id=1, source_target_pairs={{0,4},{4,8},{8,12},{12,0},{16,28},{20,16},{24,20},{28,24},{1,5},{5... | collective-permute-start | bytes 4792328 | tf_op jit(solution)/shard_map/ppermute | solution.py:44
  49.5 21.7 %collective-permute-start.8 = (bf16[1024,768]{1,0:T(8,128)(2,1)S(1)}, bf16[1024,768]{1,0:T(8,128)(2,1)S(1)}, u32[]{:S(2)}, u32[]{:S(2)}) collective-permute-start(bf16[1024,768]{1,0:T(8,128)(2,1)S(1)} %collective-permute-done.3.refs_3_.c1), channel_id=1, source_target_pairs={{0,1},{1,2},{2,3},{3,0},{16,19},{17,16},{18,17},{19,18},{4,5},{5,6... | collective-permute-start | bytes 4718600 | tf_op jit(solution)/shard_map/ppermute | solution.py:44
  71.8 3.4 %collective-permute-start.9 = (bf16[1040,768]{1,0:T(8,128)(2,1)S(1)}, bf16[1040,768]{1,0:T(8,128)(2,1)S(1)}, u32[]{:S(2)}, u32[]{:S(2)}) collective-permute-start(bf16[1040,768]{1,0:T(8,128)(2,1)S(1)} %tie.4.refs_0_), channel_id=1, source_target_pairs={{0,16},{16,0},{1,17},{17,1},{2,18},{18,2},{3,19},{19,3},{4,20},{20... | collective-permute-start | bytes 4792328 | tf_op jit(solution)/shard_map/ppermute | solution.py:52
  85.2 4.2 %collective-permute-start.11 = (f32[8,1024]{1,0:T(8,128)S(1)}, f32[8,1024]{1,0:T(8,128)S(1)}, u32[]{:S(2)}, u32[]{:S(2)}) collective-permute-start(f32[8,1024]{1,0:T(8,128)S(1)} %log_add_fusion.refs_1_), channel_id=1, source_target_pairs={{0,4},{4,8},{8,12},{12,0},{16,28},{20,16},{24,20},{28,24},{1,5},{5... | collective-permute-start | bytes 98312 | tf_op jit(solution)/shard_map/ppermute | solution.py:44
  85.8 4.5 %collective-permute-start.12 = (f32[8,1024]{1,0:T(8,128)S(1)}, f32[8,1024]{1,0:T(8,128)S(1)}, u32[]{:S(2)}, u32[]{:S(2)}) collective-permute-start(f32[8,1024]{1,0:T(8,128)S(1)} %log_add_fusion.refs_1_), channel_id=1, source_target_pairs={{0,12},{4,0},{8,4},{12,8},{16,20},{20,24},{24,28},{28,16},{1,13},{... | collective-permute-start | bytes 98312 | tf_op jit(solution)/shard_map/ppermute | solution.py:44
  86.8 4.3 %collective-permute-start.13 = (f32[8,1024]{1,0:T(8,128)S(1)}, f32[8,1024]{1,0:T(8,128)S(1)}, u32[]{:S(2)}, u32[]{:S(2)}) collective-permute-start(f32[8,1024]{1,0:T(8,128)S(1)} %log_add_fusion.refs_1_), channel_id=1, source_target_pairs={{0,8},{4,12},{8,0},{12,4},{1,9},{5,13},{9,1},{13,5},{2,10},{6,14},... | collective-permute-start | bytes 98312 | tf_op jit(solution)/shard_map/ppermute | solution.py:48
  101.3 12.2 %collective-permute-start.15 = (bf16[528,768]{1,0:T(8,128)(2,1)}, bf16[528,768]{1,0:T(8,128)(2,1)S(1)}, u32[]{:S(2)}, u32[]{:S(2)}) collective-permute-start(bf16[528,768]{1,0:T(8,128)(2,1)} %get-tuple-element.58), channel_id=1, source_target_pairs={{0,1},{1,2},{2,3},{3,0},{16,19},{17,16},{18,17},{19,18},{4,5},{5,6... | collective-permute-start | bytes 2433032 | tf_op jit(solution)/shard_map/ppermute | solution.py:44
  102.5 14.7 %collective-permute-start.21 = (bf16[528,768]{1,0:T(8,128)(2,1)}, bf16[528,768]{1,0:T(8,128)(2,1)S(1)}, u32[]{:S(2)}, u32[]{:S(2)}) collective-permute-start(bf16[528,768]{1,0:T(8,128)(2,1)} %get-tuple-element.66), channel_id=1, source_target_pairs={{0,32},{32,64},{64,96},{96,0},{16,112},{48,16},{80,48},{112,80},{1... | collective-permute-start | bytes 2433032 | tf_op jit(solution)/shard_map/ppermute | solution.py:44
  111.9 16.5 %collective-permute-start.14 = (bf16[528,768]{1,0:T(8,128)(2,1)}, bf16[528,768]{1,0:T(8,128)(2,1)S(1)}, u32[]{:S(2)}, u32[]{:S(2)}) collective-permute-start(bf16[528,768]{1,0:T(8,128)(2,1)} %get-tuple-element.56), channel_id=1, source_target_pairs={{0,3},{1,0},{2,1},{3,2},{16,17},{17,18},{18,19},{19,16},{4,7},{5,4... | collective-permute-start | bytes 2433032 | tf_op jit(solution)/shard_map/ppermute | solution.py:44
  113.5 26.3 %collective-permute-start.20 = (bf16[528,768]{1,0:T(8,128)(2,1)S(1)}, bf16[528,768]{1,0:T(8,128)(2,1)S(1)}, u32[]{:S(2)}, u32[]{:S(2)}) collective-permute-start(bf16[528,768]{1,0:T(8,128)(2,1)S(1)} %tie.5), channel_id=1, source_target_pairs={{0,96},{32,0},{64,32},{96,64},{16,48},{48,80},{80,112},{112,16},{1... | collective-permute-start | bytes 2433032 | tf_op jit(solution)/shard_map/ppermute | solution.py:44
  114.9 18.7 %collective-permute-start.16 = (bf16[528,768]{1,0:T(8,128)(2,1)S(1)}, bf16[528,768]{1,0:T(8,128)(2,1)S(1)}, u32[]{:S(2)}, u32[]{:S(2)}) collective-permute-start(bf16[528,768]{1,0:T(8,128)(2,1)S(1)} %add_convert_fusion.1), channel_id=1, source_target_pairs={{0,1},{1,2},{2,3},{3,0},{16,19},{17,16},{18,17},{19,18},{4,5},{5,6... | collective-permute-start | bytes 2433032 | tf_op jit(solution)/shard_map/ppermute | solution.py:44
  117.4 22.4 %collective-permute-start.22 = (bf16[528,768]{1,0:T(8,128)(2,1)S(1)}, bf16[528,768]{1,0:T(8,128)(2,1)S(1)}, u32[]{:S(2)}, u32[]{:S(2)}) collective-permute-start(bf16[528,768]{1,0:T(8,128)(2,1)S(1)} %add_convert_fusion), channel_id=1, source_target_pairs={{0,32},{32,64},{64,96},{96,0},{16,112},{48,16},{80,48},{112,80},{1... | collective-permute-start | bytes 2433032 | tf_op jit(solution)/shard_map/ppermute | solution.py:44
  135.1 10.0 %collective-permute-start.17 = (bf16[144,768]{1,0:T(8,128)(2,1)S(1)}, bf16[144,768]{1,0:T(8,128)(2,1)S(1)}, u32[]{:S(2)}, u32[]{:S(2)}) collective-permute-start(bf16[144,768]{1,0:T(8,128)(2,1)S(1)} %get-tuple-element.60), channel_id=1, source_target_pairs={{0,96},{32,0},{64,32},{96,64},{16,48},{48,80},{80,112},{112,16},{1... | collective-permute-start | bytes 663560 | tf_op jit(solution)/shard_map/ppermute | solution.py:44
  136.2 11.1 %collective-permute-start.18 = (bf16[144,768]{1,0:T(8,128)(2,1)S(1)}, bf16[144,768]{1,0:T(8,128)(2,1)S(1)}, u32[]{:S(2)}, u32[]{:S(2)}) collective-permute-start(bf16[144,768]{1,0:T(8,128)(2,1)S(1)} %get-tuple-element.61), channel_id=1, source_target_pairs={{0,32},{32,64},{64,96},{96,0},{16,112},{48,16},{80,48},{112,80},{1... | collective-permute-start | bytes 663560 | tf_op jit(solution)/shard_map/ppermute | solution.py:44
  137.9 9.4 %collective-permute-start.19 = (bf16[144,768]{1,0:T(8,128)(2,1)S(1)}, bf16[144,768]{1,0:T(8,128)(2,1)S(1)}, u32[]{:S(2)}, u32[]{:S(2)}) collective-permute-start(bf16[144,768]{1,0:T(8,128)(2,1)S(1)} %get-tuple-element.62), channel_id=1, source_target_pairs={{0,64},{32,96},{64,0},{96,32},{1,65},{33,97},{65,1},{97,33},{2,66}... | collective-permute-start | bytes 663560 | tf_op jit(solution)/shard_map/ppermute | solution.py:48
  141.5 7.3 %collective-permute-start.23 = (bf16[144,768]{1,0:T(8,128)(2,1)}, bf16[144,768]{1,0:T(8,128)(2,1)S(1)}, u32[]{:S(2)}, u32[]{:S(2)}) collective-permute-start(bf16[144,768]{1,0:T(8,128)(2,1)} %get-tuple-element.68), channel_id=1, source_target_pairs={{0,3},{1,0},{2,1},{3,2},{16,17},{17,18},{18,19},{19,16},{4,7},{5,4... | collective-permute-start | bytes 663560 | tf_op jit(solution)/shard_map/ppermute | solution.py:44
  141.6 9.6 %collective-permute-start.24 = (bf16[144,768]{1,0:T(8,128)(2,1)}, bf16[144,768]{1,0:T(8,128)(2,1)S(1)}, u32[]{:S(2)}, u32[]{:S(2)}) collective-permute-start(bf16[144,768]{1,0:T(8,128)(2,1)} %get-tuple-element.69), channel_id=1, source_target_pairs={{0,1},{1,2},{2,3},{3,0},{16,19},{17,16},{18,17},{19,18},{4,5},{5,6... | collective-permute-start | bytes 663560 | tf_op jit(solution)/shard_map/ppermute | solution.py:44
  145.1 10.1 %collective-permute-start.25 = (bf16[144,768]{1,0:T(8,128)(2,1)S(1)}, bf16[144,768]{1,0:T(8,128)(2,1)S(1)}, u32[]{:S(2)}, u32[]{:S(2)}) collective-permute-start(bf16[144,768]{1,0:T(8,128)(2,1)S(1)} %get-tuple-element.70), channel_id=1, source_target_pairs={{0,2},{1,3},{2,0},{3,1},{4,6},{5,7},{6,4},{7,5},{8,10},{9,11},{10,... | collective-permute-start | bytes 663560 | tf_op jit(solution)/shard_map/ppermute | solution.py:48
  158.8 7.4 %collective-permute-start.26 = (bf16[2,128,768]{2,1,0:T(8,128)(2,1)S(1)}, bf16[2,128,768]{2,1,0:T(8,128)(2,1)}, u32[]{:S(2)}, u32[]{:S(2)}) collective-permute-start(bf16[2,128,768]{2,1,0:T(8,128)(2,1)S(1)} %final.1.refs_0_), channel_id=1, source_target_pairs={{0,32},{32,64},{64,96},{96,0},{16,112},{48,16},{80,48},{112,80},{1... | collective-permute-start | bytes 1179656 | tf_op jit(solution)/shard_map/ppermute | solution.py:44
  159.1 21.3 %collective-permute-start.27 = (bf16[2,128,768]{2,1,0:T(8,128)(2,1)S(1)}, bf16[2,128,768]{2,1,0:T(8,128)(2,1)}, u32[]{:S(2)}, u32[]{:S(2)}) collective-permute-start(bf16[2,128,768]{2,1,0:T(8,128)(2,1)S(1)} %final.1.refs_0_), channel_id=1, source_target_pairs={{0,96},{32,0},{64,32},{96,64},{16,48},{48,80},{80,112},{112,16},{1... | collective-permute-start | bytes 1179656 | tf_op jit(solution)/shard_map/ppermute | solution.py:44
  160.3 20.1 %collective-permute-start.28 = (bf16[2,128,768]{2,1,0:T(8,128)(2,1)S(1)}, bf16[2,128,768]{2,1,0:T(8,128)(2,1)}, u32[]{:S(2)}, u32[]{:S(2)}) collective-permute-start(bf16[2,128,768]{2,1,0:T(8,128)(2,1)S(1)} %final.1.refs_0_), channel_id=1, source_target_pairs={{0,64},{32,96},{64,0},{96,32},{1,65},{33,97},{65,1},{97,33},{2,66}... | collective-permute-start | bytes 1179656 | tf_op jit(solution)/shard_map/ppermute | solution.py:48
  161.2 19.8 %collective-permute-start.29 = (bf16[2,128,768]{2,1,0:T(8,128)(2,1)S(1)}, bf16[2,128,768]{2,1,0:T(8,128)(2,1)}, u32[]{:S(2)}, u32[]{:S(2)}) collective-permute-start(bf16[2,128,768]{2,1,0:T(8,128)(2,1)S(1)} %final.1.refs_0_), channel_id=1, source_target_pairs={{0,16},{16,0},{1,17},{17,1},{2,18},{18,2},{3,19},{19,3},{4,20},{20... | collective-permute-start | bytes 1179656 | tf_op jit(solution)/shard_map/ppermute | solution.py:52
  166.1 16.0 %collective-permute-start.30 = (bf16[2,128,768]{2,1,0:T(8,128)(2,1)}, bf16[2,128,768]{2,1,0:T(8,128)(2,1)}, u32[]{:S(2)}, u32[]{:S(2)}) collective-permute-start(bf16[2,128,768]{2,1,0:T(8,128)(2,1)} %collective-permute-done.26.refs_1_), channel_id=1, source_target_pairs={{0,16},{16,0},{1,17},{17,1},{2,18},{18,2},{3,19},{19,3},{4,20},{20... | collective-permute-start | bytes 1179656 | tf_op jit(solution)/shard_map/ppermute | solution.py:52
  180.4 2.3 %collective-permute-start.31 = (bf16[2,128,768]{2,1,0:T(8,128)(2,1)}, bf16[2,128,768]{2,1,0:T(8,128)(2,1)}, u32[]{:S(2)}, u32[]{:S(2)}) collective-permute-start(bf16[2,128,768]{2,1,0:T(8,128)(2,1)} %collective-permute-done.27.refs_2_), channel_id=1, source_target_pairs={{0,16},{16,0},{1,17},{17,1},{2,18},{18,2},{3,19},{19,3},{4,20},{20... | collective-permute-start | bytes 1179656 | tf_op jit(solution)/shard_map/ppermute | solution.py:52
  180.4 2.8 %collective-permute-start.32 = (bf16[2,128,768]{2,1,0:T(8,128)(2,1)}, bf16[2,128,768]{2,1,0:T(8,128)(2,1)}, u32[]{:S(2)}, u32[]{:S(2)}) collective-permute-start(bf16[2,128,768]{2,1,0:T(8,128)(2,1)} %collective-permute-done.28.refs_3_), channel_id=1, source_target_pairs={{0,16},{16,0},{1,17},{17,1},{2,18},{18,2},{3,19},{19,3},{4,20},{20... | collective-permute-start | bytes 1179656 | tf_op jit(solution)/shard_map/ppermute | solution.py:52
  (20 other events, 109.5 us)

commit v6 on v5

--- a/solution.py
+++ b/solution.py
@@ -67,8 +67,8 @@
 
 def pack_kernel(vectors, cand_ref, out, buf, in_sem, out_sem):
     loads, stores = [], []
-    for k in range(4):
-        rows = pl.ds(k * 256, 256)
+    for k in range(2):
+        rows = pl.ds(k * 512, 512)
         loads.append(pltpu.make_async_copy(vectors.at[rows, :], buf.at[rows, :], in_sem.at[k]))
         stores.append(pltpu.make_async_copy(buf.at[rows, :], out.at[rows, :], out_sem.at[k]))
         loads[k].start()
@@ -842,8 +842,8 @@
 
     g, h3, factor = first_sums(where, stats, idx, peak, e, rows)
     h1, h2, h0 = owner_sums((1, 2, 0), factor, e, rows)
+    h, _ = ring_terms(h0, h1, h2, h3, "x", h2)
     g, _ = ring_terms(*g, "z", h0)
-    h, _ = ring_terms(h0, h1, h2, h3, "x")
     h = direct_terms(*parted(0, where, h), "z")
     g = direct_terms(*parted(1, where, g), "x")
     fresh = final(h, g, mine)

time: 187 us -> 186 us (level)
  transfers between devices with their start and end apart: 33 -> 33, of which waited for: 15 -> 12; matrix products, arithmetic and copies ran while one was open for 2% -> 2% of each run, Pallas kernels for 20% -> 20%
where the time goes in v6:
time: 186 us
  Pallas kernels  64.1 us (34%)
  starting transfers between devices  55.5 us (30%)
  waiting for transfers between devices  55.4 us (30%)
  local copies, waits for them, and re-layouts  9.85 us (5%)
    ppermute x20, waiting for transfers between devices, turn(): return lax.ppermute(a, axes, pairs)  47.6 us
    ppermute x20, starting transfers between devices, turn(): return lax.ppermute(a, axes, pairs)  28.4 us
    ppermute x9, starting transfers between devices, swap(): return lax.ppermute(a, 'core', [(0, 1), (1, 0)])  20.8 us
    pallas_call x2, Pallas kernels, sums_call(): pl.pallas_call(kern, grid=(n,), in_specs=specs + [pl.BlockSpec(memory_spa...  15.4 us
    pallas_call x3, Pallas kernels, dispatch(): pl.pallas_call(kern, grid=(n,), in_specs=in_specs, out_specs=(pl.BlockSpe...  13.8 us
    pallas_call x1, Pallas kernels, middle(): pl.pallas_call(middle_kernel, in_specs=[anywhere] * 2 + [vmem] + [anywher...  10.4 us
    pallas_call x1, Pallas kernels, late_scores(): pl.pallas_call(late_kernel, in_specs=[anywhere, vmem] + [anywhere] * 4 +...  8.09 us
    unnamed x38, local copies, waits for them, and re-layouts  6.6 us
  transfers between devices with their start and end apart: 33, of which 12 were waited for; matrix products, arithmetic and copies ran while one was open for 2% of the time, Pallas kernels for 20%

profile of v6, /device:TPU:1, one launch (start us, length us, event | category | flops | bytes accessed | tf_op | source)
XLA Modules:
  0.0 186.2 jit_solution(2881275874207024559)
XLA Ops:
  0.0 3.3 %pack.1.refs_0_ = bf16[1040,768]{1,0:T(8,128)(2,1)} custom-call(bf16[1024,768]{1,0:T(8,128)(2,1)} %vectors.1, s32[4,1024]{1,0:T(4,128)} %bitcast.13), custom_call_target="tpu_custom_call" | custom-call | bytes 3000000 | tf_op jit(solution)/shard_map/pack/pallas_call | solution.py:91
  4.8 2.8 %collective-permute-start = (bf16[1040,768]{1,0:T(8,128)(2,1)}, bf16[1040,768]{1,0:T(8,128)(2,1)}, u32[]{:S(2)}, u32[]{:S(2)}) collective-permute-start(bf16[1040,768]{1,0:T(8,128)(2,1)} %pack.1.refs_0_), channel_id=1, source_target_pairs={{0,4},{4,8},{8,12},{12,0},{16,28},{20,16},{24,20},{28,24},{1,5},{5... | collective-permute-start | bytes 4792328 | tf_op jit(solution)/shard_map/ppermute | solution.py:44
  8.9 2.5 %collective-permute-start.3 = (bf16[1024,768]{1,0:T(8,128)(2,1)}, bf16[1024,768]{1,0:T(8,128)(2,1)S(1)}, u32[]{:S(2)}, u32[]{:S(2)}) collective-permute-start(bf16[1024,768]{1,0:T(8,128)(2,1)} %constant_dynamic-slice_fusion.1.c0), channel_id=1, source_target_pairs={{0,1},{1,2},{2,3},{3,0},{16,19},{17,16},{18,17},{19,18},{4,5},{5,6... | collective-permute-start | bytes 4718600 | tf_op jit(solution)/shard_map/ppermute | solution.py:44
  13.2 4.9 %dispatch0.1 = (f32[2,8,1024]{2,1,0:T(8,128)S(1)}, bf16[28,768,768]{2,1,0:T(8,128)(2,1)}) custom-call(bf16[1040,768]{1,0:T(8,128)(2,1)S(1)} %copy-done.5, bf16[1040,768]{1,0:T(8,128)(2,1)} %collective-permute-done.1.refs_1_, f32[8,128]{1,0:T(8,128)S(1)} %broadcast_in_dim.2.refs_2_.blk_ref.refs_1_), custom_call_target="tpu_custom_call" | custom-call | flops 2415919104 | bytes 6000000 | tf_op jit(solution)/shard_map/dispatch0/pallas_call | solution.py:204
  18.1 26.4 %collective-permute-done.3.refs_3_.c1 = bf16[1024,768]{1,0:T(8,128)(2,1)S(1)} collective-permute-done((bf16[1024,768]{1,0:T(8,128)(2,1)}, bf16[1024,768]{1,0:T(8,128)(2,1)S(1)}, u32[]{:S(2)}, u32[]{:S(2)}) %collective-permute-start.3) | collective-permute-done | bytes 1572896 | tf_op jit(solution)/shard_map/ppermute | solution.py:44
  44.4 3.0 %collective-permute-done.4.refs_4_.c2 = bf16[1024,768]{1,0:T(8,128)(2,1)S(1)} collective-permute-done((bf16[1024,768]{1,0:T(8,128)(2,1)}, bf16[1024,768]{1,0:T(8,128)(2,1)S(1)}, u32[]{:S(2)}, u32[]{:S(2)}) %collective-permute-start.4) | collective-permute-done | bytes 1572896 | tf_op jit(solution)/shard_map/ppermute | solution.py:44
  48.0 1.6 collective-permute-start.5
  49.6 2.9 %collective-permute-start.8 = (bf16[1024,768]{1,0:T(8,128)(2,1)S(1)}, bf16[1024,768]{1,0:T(8,128)(2,1)S(1)}, u32[]{:S(2)}, u32[]{:S(2)}) collective-permute-start(bf16[1024,768]{1,0:T(8,128)(2,1)S(1)} %collective-permute-done.3.refs_3_.c1), channel_id=1, source_target_pairs={{0,1},{1,2},{2,3},{3,0},{16,19},{17,16},{18,17},{19,18},{4,5},{5,6... | collective-permute-start | bytes 4718600 | tf_op jit(solution)/shard_map/ppermute | solution.py:44
  52.5 6.0 %dispatch2.1 = (f32[2,8,1024]{2,1,0:T(8,128)S(1)}, bf16[28,768,768]{2,1,0:T(8,128)(2,1)}) custom-call(bf16[1040,768]{1,0:T(8,128)(2,1)} %tie.4.refs_0_, bf16[1040,768]{1,0:T(8,128)(2,1)} %collective-permute-done.2.refs_2_.refs_1_, f32[8,128]{1,0:T(8,128)S(1)} %broadcast_in_dim.2.refs_2_.blk_ref.refs_1_, ...), custom_call_target="tpu_custom_call", output_to_operand_aliasing={{1}: (3, {})} | custom-call | flops 2415919104 | bytes 6000000 | tf_op jit(solution)/shard_map/dispatch2/pallas_call | solution.py:204
  58.6 10.4 %middle.1 = (bf16[28,768,768]{2,1,0:T(8,128)(2,1)}, f32[2,8,1024]{2,1,0:T(8,128)S(1)}, bf16[40,512,768]{2,1,0:T(8,128)(2,1)}, f32[8,512]{1,0:T(8,128)S(1)}, f32[8,512]{1,0:T(8,128)S(1)}) custom-call(bf16[1040,768]{1,0:T(8,128)(2,1)S(1)} %collective-permute-done.6.s0, ...), custom_call_target="tpu_custom_call", output_to_operand_aliasing={{0}: (6, {})} | custom-call | flops 2415919104 | bytes 20000000 | tf_op jit(solution)/shard_map/middle/pallas_call | solution.py:283
  69.0 2.3 %indices.2.refs_1_.refs_5_ = s32[8,512]{1,0:T(8,128)S(1)} custom-call(f32[2,8,1024]{2,1,0:T(8,128)S(1)} %get-tuple-element.38.refs_1_.refs_0_.rank0, f32[2,8,1024]{2,1,0:T(8,128)S(1)} %get-tuple-element.40.refs_1_.rank1, f32[2,8,1024]{2,1,0:T(8,128)S(1)} %get-tuple-element.42.refs_2_.rank2.refs_0_), custom_call_target="tpu_custom_call" | custom-call | flops 4000000000 | bytes 1000000 | tf_op jit(solution)/shard_map/indices/pallas_call | solution.py:157
  71.9 2.9 %dispatch6.1 = (f32[1,8,1024]{2,1,0:T(8,128)S(1)}, bf16[28,768,768]{2,1,0:T(8,128)(2,1)}) custom-call(bf16[1040,768]{1,0:T(8,128)(2,1)S(1)} %tie.5.refs_0_, f32[8,128]{1,0:T(8,128)S(1)} %broadcast_in_dim.2.refs_2_.blk_ref.refs_1_, bf16[28,768,768]{2,1,0:T(8,128)(2,1)} %get-tuple-element.43.refs_2_), custom_call_target="tpu_custom_call", output_to_operand_aliasing={{1}: (2, {})} | custom-call | flops 1207959552 | bytes 3000000 | tf_op jit(solution)/shard_map/dispatch6/pallas_call | solution.py:204
  75.3 8.1 %late_scores.1 = (bf16[28,768,768]{2,1,0:T(8,128)(2,1)}, bf16[40,512,768]{2,1,0:T(8,128)(2,1)}, f32[1,8,1024]{2,1,0:T(8,128)S(1)}, f32[8,768]{1,0:T(8,128)S(1)}, f32[8,1024]{1,0:T(8,128)S(1)}) custom-call(bf16[1040,768]{1,0:T(8,128)(2,1)S(1)} %collective-permute-done.9.source, ...), custom_call_target="tpu_custom_call", output_to_operand_aliasing={{0}: (12, {}), {1}: (13, {})} | custom-call | flops 3623878656 | bytes 20000000 | tf_op jit(solution)/shard_map/late_scores/pallas_call | solution.py:390
  91.8 9.7 %sums5.1 = (bf16[528,768]{1,0:T(8,128)(2,1)}, bf16[528,768]{1,0:T(8,128)(2,1)}, bf16[528,768]{1,0:T(8,128)(2,1)}, bf16[528,768]{1,0:T(8,128)(2,1)}, bf16[528,768]{1,0:T(8,128)(2,1)}, /*index=5*/f32[8,768]{1,0:T(8,128)}) custom-call(s32[8]{0:T(128)} %concatenate.17.refs_0_.where_ref, f32[8,1024]{1,0:T(8,128)} %copy-done.15, f32[8,1024]{1,0:T(8,128)} %copy-done.16, ...), custom_call_target="tpu_custom_call" | custom-call | flops 3019898880 | bytes 15000000 | tf_op jit(solution)/shard_map/sums5/pallas_call | solution.py:595
  102.7 3.8 %collective-permute-start.21 = (bf16[528,768]{1,0:T(8,128)(2,1)}, bf16[528,768]{1,0:T(8,128)(2,1)S(1)}, u32[]{:S(2)}, u32[]{:S(2)}) collective-permute-start(bf16[528,768]{1,0:T(8,128)(2,1)} %get-tuple-element.66), channel_id=1, source_target_pairs={{0,32},{32,64},{64,96},{96,0},{16,112},{48,16},{80,48},{112,80},{1... | collective-permute-start | bytes 2433032 | tf_op jit(solution)/shard_map/ppermute | solution.py:44
  106.4 5.7 %sums3.1 = (bf16[528,768]{1,0:T(8,128)(2,1)}, bf16[528,768]{1,0:T(8,128)(2,1)}, bf16[528,768]{1,0:T(8,128)(2,1)}) custom-call(f32[8,768]{1,0:T(8,128)} %get-tuple-element.54.refs_0_, bf16[40,512,768]{2,1,0:T(8,128)(2,1)} %get-tuple-element.52.refs_8_.refs_1_, bf16[28,768,768]{2,1,0:T(8,128)(2,1)} %get-tuple-element.53.refs_9_.refs_2_), custom_call_target="tpu_custom_call" | custom-call | flops 1811939328 | bytes 9000000 | tf_op jit(solution)/shard_map/sums3/pallas_call | solution.py:595
  114.9 1.7 collective-permute-start.16
  116.9 2.7 %collective-permute-start.22 = (bf16[528,768]{1,0:T(8,128)(2,1)S(1)}, bf16[528,768]{1,0:T(8,128)(2,1)S(1)}, u32[]{:S(2)}, u32[]{:S(2)}) collective-permute-start(bf16[528,768]{1,0:T(8,128)(2,1)S(1)} %add_convert_fusion), channel_id=1, source_target_pairs={{0,32},{32,64},{64,96},{96,0},{16,112},{48,16},{80,48},{112,80},{1... | collective-permute-start | bytes 2433032 | tf_op jit(solution)/shard_map/ppermute | solution.py:44
  119.6 9.8 %collective-permute-done.14.refs_1_ = bf16[528,768]{1,0:T(8,128)(2,1)S(1)} collective-permute-done((bf16[528,768]{1,0:T(8,128)(2,1)}, bf16[528,768]{1,0:T(8,128)(2,1)S(1)}, u32[]{:S(2)}, u32[]{:S(2)}) %collective-permute-start.14) | collective-permute-done | bytes 811040 | tf_op jit(solution)/shard_map/ppermute | solution.py:44
  129.4 4.9 %collective-permute-done.16.refs_2_ = bf16[528,768]{1,0:T(8,128)(2,1)S(1)} collective-permute-done((bf16[528,768]{1,0:T(8,128)(2,1)S(1)}, bf16[528,768]{1,0:T(8,128)(2,1)S(1)}, u32[]{:S(2)}, u32[]{:S(2)}) %collective-permute-start.16) | collective-permute-done | bytes 811040 | tf_op jit(solution)/shard_map/ppermute | solution.py:44
  134.3 2.2 %parted0.1 = (bf16[144,768]{1,0:T(8,128)(2,1)S(1)}, bf16[144,768]{1,0:T(8,128)(2,1)S(1)}, bf16[144,768]{1,0:T(8,128)(2,1)}, bf16[144,768]{1,0:T(8,128)(2,1)S(1)}) custom-call(s32[8]{0:T(128)S(1)} %copy-done.12, bf16[528,768]{1,0:T(8,128)(2,1)S(1)} %copy-done.4, bf16[528,768]{1,0:T(8,128)(2,1)S(1)} %collective-permute-done.14.refs_1_, ...), custom_call_target="tpu_custom_call" | custom-call | flops 1000000 | bytes 4000000 | tf_op jit(solution)/shard_map/parted0/pallas_call | solution.py:692
  137.5 2.3 %collective-permute-start.18 = (bf16[144,768]{1,0:T(8,128)(2,1)}, bf16[144,768]{1,0:T(8,128)(2,1)S(1)}, u32[]{:S(2)}, u32[]{:S(2)}) collective-permute-start(bf16[144,768]{1,0:T(8,128)(2,1)} %get-tuple-element.61), channel_id=1, source_target_pairs={{0,32},{32,64},{64,96},{96,0},{16,112},{48,16},{80,48},{112,80},{1... | collective-permute-start | bytes 663560 | tf_op jit(solution)/shard_map/ppermute | solution.py:44
  142.5 3.1 %collective-permute-start.24 = (bf16[144,768]{1,0:T(8,128)(2,1)S(1)}, bf16[144,768]{1,0:T(8,128)(2,1)S(1)}, u32[]{:S(2)}, u32[]{:S(2)}) collective-permute-start(bf16[144,768]{1,0:T(8,128)(2,1)S(1)} %get-tuple-element.69), channel_id=1, source_target_pairs={{0,1},{1,2},{2,3},{3,0},{16,19},{17,16},{18,17},{19,18},{4,5},{5,6... | collective-permute-start | bytes 663560 | tf_op jit(solution)/shard_map/ppermute | solution.py:44
  150.5 4.4 %collective-permute-done.25.refs_7_ = bf16[144,768]{1,0:T(8,128)(2,1)S(1)} collective-permute-done((bf16[144,768]{1,0:T(8,128)(2,1)S(1)}, bf16[144,768]{1,0:T(8,128)(2,1)S(1)}, u32[]{:S(2)}, u32[]{:S(2)}) %collective-permute-start.25) | collective-permute-done | bytes 221216 | tf_op jit(solution)/shard_map/ppermute | solution.py:48
  154.9 2.7 %final.1.refs_0_ = bf16[2,128,768]{2,1,0:T(8,128)(2,1)S(1)} custom-call(bf16[144,768]{1,0:T(8,128)(2,1)S(1)} %copy-done.9, bf16[144,768]{1,0:T(8,128)(2,1)S(1)} %collective-permute-done.17.refs_1_, bf16[144,768]{1,0:T(8,128)(2,1)S(1)} %collective-permute-done.18.refs_2_, bf16[144,768]{1,0:T(8,128)(2,1)S(1)} %collective-permute-done.19.refs_3_, ...), custom_call_target="tpu_custom_call" | custom-call | flops 1000000 | bytes 2000000 | tf_op jit(solution)/shard_map/final/pallas_call | solution.py:718
  159.1 3.0 %collective-permute-start.28 = (bf16[2,128,768]{2,1,0:T(8,128)(2,1)S(1)}, bf16[2,128,768]{2,1,0:T(8,128)(2,1)}, u32[]{:S(2)}, u32[]{:S(2)}) collective-permute-start(bf16[2,128,768]{2,1,0:T(8,128)(2,1)S(1)} %final.1.refs_0_), channel_id=1, source_target_pairs={{0,64},{32,96},{64,0},{96,32},{1,65},{33,97},{65,1},{97,33},{2,66}... | collective-permute-start | bytes 1179656 | tf_op jit(solution)/shard_map/ppermute | solution.py:48
  162.1 4.4 %collective-permute-start.29 = (bf16[2,128,768]{2,1,0:T(8,128)(2,1)S(1)}, bf16[2,128,768]{2,1,0:T(8,128)(2,1)}, u32[]{:S(2)}, u32[]{:S(2)}) collective-permute-start(bf16[2,128,768]{2,1,0:T(8,128)(2,1)S(1)} %final.1.refs_0_), channel_id=1, source_target_pairs={{0,16},{16,0},{1,17},{17,1},{2,18},{18,2},{3,19},{19,3},{4,20},{20... | collective-permute-start | bytes 1179656 | tf_op jit(solution)/shard_map/ppermute | solution.py:52
  166.4 7.8 %collective-permute-start.30 = (bf16[2,128,768]{2,1,0:T(8,128)(2,1)}, bf16[2,128,768]{2,1,0:T(8,128)(2,1)}, u32[]{:S(2)}, u32[]{:S(2)}) collective-permute-start(bf16[2,128,768]{2,1,0:T(8,128)(2,1)} %collective-permute-done.26.refs_1_), channel_id=1, source_target_pairs={{0,16},{16,0},{1,17},{17,1},{2,18},{18,2},{3,19},{19,3},{4,20},{20... | collective-permute-start | bytes 1179656 | tf_op jit(solution)/shard_map/ppermute | solution.py:52
  174.2 2.9 %collective-permute-start.31 = (bf16[2,128,768]{2,1,0:T(8,128)(2,1)}, bf16[2,128,768]{2,1,0:T(8,128)(2,1)}, u32[]{:S(2)}, u32[]{:S(2)}) collective-permute-start(bf16[2,128,768]{2,1,0:T(8,128)(2,1)} %collective-permute-done.27.refs_2_), channel_id=1, source_target_pairs={{0,16},{16,0},{1,17},{17,1},{2,18},{18,2},{3,19},{19,3},{4,20},{20... | collective-permute-start | bytes 1179656 | tf_op jit(solution)/shard_map/ppermute | solution.py:52
  177.1 3.6 %collective-permute-start.32 = (bf16[2,128,768]{2,1,0:T(8,128)(2,1)}, bf16[2,128,768]{2,1,0:T(8,128)(2,1)}, u32[]{:S(2)}, u32[]{:S(2)}) collective-permute-start(bf16[2,128,768]{2,1,0:T(8,128)(2,1)} %collective-permute-done.28.refs_3_), channel_id=1, source_target_pairs={{0,16},{16,0},{1,17},{17,1},{2,18},{18,2},{3,19},{19,3},{4,20},{20... | collective-permute-start | bytes 1179656 | tf_op jit(solution)/shard_map/ppermute | solution.py:52
  180.8 1.6 collective-permute-done.32.refs_7_
  182.4 3.6 %place.1 = bf16[4,4,128,768]{3,2,1,0:T(8,128)(2,1)} custom-call(s32[10]{0:T(128)S(1)} %concatenate.16.where_ref, bf16[2,128,768]{2,1,0:T(8,128)(2,1)S(1)} %final.1.refs_0_, bf16[2,128,768]{2,1,0:T(8,128)(2,1)} %collective-permute-done.26.refs_1_, bf16[2,128,768]{2,1,0:T(8,128)(2,1)} %collective-permute-done.27.refs_2_, ...), custom_call_target="tpu_custom_call" | custom-call | bytes 6000000 | tf_op jit(solution)/shard_map/place/pallas_call | solution.py:755
  (104 shorter events, 28.8 us)
Async XLA Ops:
  3.3 8.3 %collective-permute-start.1 = (bf16[1040,768]{1,0:T(8,128)(2,1)}, bf16[1040,768]{1,0:T(8,128)(2,1)}, u32[]{:S(2)}, u32[]{:S(2)}) collective-permute-start(bf16[1040,768]{1,0:T(8,128)(2,1)} %pack.1.refs_0_), channel_id=1, source_target_pairs={{0,16},{16,0},{1,17},{17,1},{2,18},{18,2},{3,19},{19,3},{4,20},{20... | collective-permute-start | bytes 4792328 | tf_op jit(solution)/shard_map/ppermute | solution.py:52
  4.8 42.6 %collective-permute-start = (bf16[1040,768]{1,0:T(8,128)(2,1)}, bf16[1040,768]{1,0:T(8,128)(2,1)}, u32[]{:S(2)}, u32[]{:S(2)}) collective-permute-start(bf16[1040,768]{1,0:T(8,128)(2,1)} %pack.1.refs_0_), channel_id=1, source_target_pairs={{0,4},{4,8},{8,12},{12,0},{16,28},{20,16},{24,20},{28,24},{1,5},{5... | collective-permute-start | bytes 4792328 | tf_op jit(solution)/shard_map/ppermute | solution.py:44
  7.7 39.8 %collective-permute-start.2 = (bf16[1040,768]{1,0:T(8,128)(2,1)}, bf16[1040,768]{1,0:T(8,128)(2,1)}, u32[]{:S(2)}, u32[]{:S(2)}) collective-permute-start(bf16[1040,768]{1,0:T(8,128)(2,1)} %pack.1.refs_0_), channel_id=1, source_target_pairs={{0,12},{4,0},{8,4},{12,8},{16,20},{20,24},{24,28},{28,16},{1,13},{... | collective-permute-start | bytes 4792328 | tf_op jit(solution)/shard_map/ppermute | solution.py:44
  8.9 35.5 %collective-permute-start.3 = (bf16[1024,768]{1,0:T(8,128)(2,1)}, bf16[1024,768]{1,0:T(8,128)(2,1)S(1)}, u32[]{:S(2)}, u32[]{:S(2)}) collective-permute-start(bf16[1024,768]{1,0:T(8,128)(2,1)} %constant_dynamic-slice_fusion.1.c0), channel_id=1, source_target_pairs={{0,1},{1,2},{2,3},{3,0},{16,19},{17,16},{18,17},{19,18},{4,5},{5,6... | collective-permute-start | bytes 4718600 | tf_op jit(solution)/shard_map/ppermute | solution.py:44
  11.4 36.0 %collective-permute-start.4 = (bf16[1024,768]{1,0:T(8,128)(2,1)}, bf16[1024,768]{1,0:T(8,128)(2,1)S(1)}, u32[]{:S(2)}, u32[]{:S(2)}) collective-permute-start(bf16[1024,768]{1,0:T(8,128)(2,1)} %constant_dynamic-slice_fusion.1.c0), channel_id=1, source_target_pairs={{0,3},{1,0},{2,1},{3,2},{16,17},{17,18},{18,19},{19,16},{4,7},{5,4... | collective-permute-start | bytes 4718600 | tf_op jit(solution)/shard_map/ppermute | solution.py:44
  47.4 11.1 %collective-permute-start.6 = (bf16[1040,768]{1,0:T(8,128)(2,1)}, bf16[1040,768]{1,0:T(8,128)(2,1)S(1)}, u32[]{:S(2)}, u32[]{:S(2)}) collective-permute-start(bf16[1040,768]{1,0:T(8,128)(2,1)} %tie.4.refs_0_), channel_id=1, source_target_pairs={{0,16},{16,0},{1,17},{17,1},{2,18},{18,2},{3,19},{19,3},{4,20},{20... | collective-permute-start | bytes 4792328 | tf_op jit(solution)/shard_map/ppermute | solution.py:52
  47.5 11.0 %collective-permute-start.7 = (bf16[1040,768]{1,0:T(8,128)(2,1)}, bf16[1040,768]{1,0:T(8,128)(2,1)S(1)}, u32[]{:S(2)}, u32[]{:S(2)}) collective-permute-start(bf16[1040,768]{1,0:T(8,128)(2,1)} %collective-permute-done.2.refs_2_.refs_1_), channel_id=1, source_target_pairs={{0,16},{16,0},{1,17},{17,1},{2,18},{18,2},{3,19},{19,3},{4,20},{20... | collective-permute-start | bytes 4792328 | tf_op jit(solution)/shard_map/ppermute | solution.py:52
  48.0 23.3 %collective-permute-start.5 = (bf16[1040,768]{1,0:T(8,128)(2,1)}, bf16[1040,768]{1,0:T(8,128)(2,1)S(1)}, u32[]{:S(2)}, u32[]{:S(2)}) collective-permute-start(bf16[1040,768]{1,0:T(8,128)(2,1)} %tie.4.refs_0_), channel_id=1, source_target_pairs={{0,4},{4,8},{8,12},{12,0},{16,28},{20,16},{24,20},{28,24},{1,5},{5... | collective-permute-start | bytes 4792328 | tf_op jit(solution)/shard_map/ppermute | solution.py:44
  49.6 21.7 %collective-permute-start.8 = (bf16[1024,768]{1,0:T(8,128)(2,1)S(1)}, bf16[1024,768]{1,0:T(8,128)(2,1)S(1)}, u32[]{:S(2)}, u32[]{:S(2)}) collective-permute-start(bf16[1024,768]{1,0:T(8,128)(2,1)S(1)} %collective-permute-done.3.refs_3_.c1), channel_id=1, source_target_pairs={{0,1},{1,2},{2,3},{3,0},{16,19},{17,16},{18,17},{19,18},{4,5},{5,6... | collective-permute-start | bytes 4718600 | tf_op jit(solution)/shard_map/ppermute | solution.py:44
  71.9 3.4 %collective-permute-start.9 = (bf16[1040,768]{1,0:T(8,128)(2,1)S(1)}, bf16[1040,768]{1,0:T(8,128)(2,1)S(1)}, u32[]{:S(2)}, u32[]{:S(2)}) collective-permute-start(bf16[1040,768]{1,0:T(8,128)(2,1)S(1)} %tie.5.refs_0_), channel_id=1, source_target_pairs={{0,16},{16,0},{1,17},{17,1},{2,18},{18,2},{3,19},{19,3},{4,20},{20... | collective-permute-start | bytes 4792328 | tf_op jit(solution)/shard_map/ppermute | solution.py:52
  85.4 4.2 %collective-permute-start.11 = (f32[8,1024]{1,0:T(8,128)S(1)}, f32[8,1024]{1,0:T(8,128)S(1)}, u32[]{:S(2)}, u32[]{:S(2)}) collective-permute-start(f32[8,1024]{1,0:T(8,128)S(1)} %log_add_fusion.refs_1_), channel_id=1, source_target_pairs={{0,4},{4,8},{8,12},{12,0},{16,28},{20,16},{24,20},{28,24},{1,5},{5... | collective-permute-start | bytes 98312 | tf_op jit(solution)/shard_map/ppermute | solution.py:44
  85.9 4.5 %collective-permute-start.12 = (f32[8,1024]{1,0:T(8,128)S(1)}, f32[8,1024]{1,0:T(8,128)S(1)}, u32[]{:S(2)}, u32[]{:S(2)}) collective-permute-start(f32[8,1024]{1,0:T(8,128)S(1)} %log_add_fusion.refs_1_), channel_id=1, source_target_pairs={{0,12},{4,0},{8,4},{12,8},{16,20},{20,24},{24,28},{28,16},{1,13},{... | collective-permute-start | bytes 98312 | tf_op jit(solution)/shard_map/ppermute | solution.py:44
  86.9 4.3 %collective-permute-start.13 = (f32[8,1024]{1,0:T(8,128)S(1)}, f32[8,1024]{1,0:T(8,128)S(1)}, u32[]{:S(2)}, u32[]{:S(2)}) collective-permute-start(f32[8,1024]{1,0:T(8,128)S(1)} %log_add_fusion.refs_1_), channel_id=1, source_target_pairs={{0,8},{4,12},{8,0},{12,4},{1,9},{5,13},{9,1},{13,5},{2,10},{6,14},... | collective-permute-start | bytes 98312 | tf_op jit(solution)/shard_map/ppermute | solution.py:48
  101.5 12.9 %collective-permute-start.15 = (bf16[528,768]{1,0:T(8,128)(2,1)}, bf16[528,768]{1,0:T(8,128)(2,1)S(1)}, u32[]{:S(2)}, u32[]{:S(2)}) collective-permute-start(bf16[528,768]{1,0:T(8,128)(2,1)} %get-tuple-element.58), channel_id=1, source_target_pairs={{0,1},{1,2},{2,3},{3,0},{16,19},{17,16},{18,17},{19,18},{4,5},{5,6... | collective-permute-start | bytes 2433032 | tf_op jit(solution)/shard_map/ppermute | solution.py:44
  102.7 14.0 %collective-permute-start.21 = (bf16[528,768]{1,0:T(8,128)(2,1)}, bf16[528,768]{1,0:T(8,128)(2,1)S(1)}, u32[]{:S(2)}, u32[]{:S(2)}) collective-permute-start(bf16[528,768]{1,0:T(8,128)(2,1)} %get-tuple-element.66), channel_id=1, source_target_pairs={{0,32},{32,64},{64,96},{96,0},{16,112},{48,16},{80,48},{112,80},{1... | collective-permute-start | bytes 2433032 | tf_op jit(solution)/shard_map/ppermute | solution.py:44
  113.3 16.1 %collective-permute-start.14 = (bf16[528,768]{1,0:T(8,128)(2,1)}, bf16[528,768]{1,0:T(8,128)(2,1)S(1)}, u32[]{:S(2)}, u32[]{:S(2)}) collective-permute-start(bf16[528,768]{1,0:T(8,128)(2,1)} %tie.6), channel_id=1, source_target_pairs={{0,3},{1,0},{2,1},{3,2},{16,17},{17,18},{18,19},{19,16},{4,7},{5,4... | collective-permute-start | bytes 2433032 | tf_op jit(solution)/shard_map/ppermute | solution.py:44
  114.4 26.9 %collective-permute-start.20 = (bf16[528,768]{1,0:T(8,128)(2,1)S(1)}, bf16[528,768]{1,0:T(8,128)(2,1)S(1)}, u32[]{:S(2)}, u32[]{:S(2)}) collective-permute-start(bf16[528,768]{1,0:T(8,128)(2,1)S(1)} %tie.7), channel_id=1, source_target_pairs={{0,96},{32,0},{64,32},{96,64},{16,48},{48,80},{80,112},{112,16},{1... | collective-permute-start | bytes 2433032 | tf_op jit(solution)/shard_map/ppermute | solution.py:44
  114.9 19.4 %collective-permute-start.16 = (bf16[528,768]{1,0:T(8,128)(2,1)S(1)}, bf16[528,768]{1,0:T(8,128)(2,1)S(1)}, u32[]{:S(2)}, u32[]{:S(2)}) collective-permute-start(bf16[528,768]{1,0:T(8,128)(2,1)S(1)} %add_convert_fusion.1), channel_id=1, source_target_pairs={{0,1},{1,2},{2,3},{3,0},{16,19},{17,16},{18,17},{19,18},{4,5},{5,6... | collective-permute-start | bytes 2433032 | tf_op jit(solution)/shard_map/ppermute | solution.py:44
  116.9 24.4 %collective-permute-start.22 = (bf16[528,768]{1,0:T(8,128)(2,1)S(1)}, bf16[528,768]{1,0:T(8,128)(2,1)S(1)}, u32[]{:S(2)}, u32[]{:S(2)}) collective-permute-start(bf16[528,768]{1,0:T(8,128)(2,1)S(1)} %add_convert_fusion), channel_id=1, source_target_pairs={{0,32},{32,64},{64,96},{96,0},{16,112},{48,16},{80,48},{112,80},{1... | collective-permute-start | bytes 2433032 | tf_op jit(solution)/shard_map/ppermute | solution.py:44
  137.2 8.4 %collective-permute-start.17 = (bf16[144,768]{1,0:T(8,128)(2,1)S(1)}, bf16[144,768]{1,0:T(8,128)(2,1)S(1)}, u32[]{:S(2)}, u32[]{:S(2)}) collective-permute-start(bf16[144,768]{1,0:T(8,128)(2,1)S(1)} %get-tuple-element.60), channel_id=1, source_target_pairs={{0,96},{32,0},{64,32},{96,64},{16,48},{48,80},{80,112},{112,16},{1... | collective-permute-start | bytes 663560 | tf_op jit(solution)/shard_map/ppermute | solution.py:44
  137.5 10.2 %collective-permute-start.18 = (bf16[144,768]{1,0:T(8,128)(2,1)}, bf16[144,768]{1,0:T(8,128)(2,1)S(1)}, u32[]{:S(2)}, u32[]{:S(2)}) collective-permute-start(bf16[144,768]{1,0:T(8,128)(2,1)} %get-tuple-element.61), channel_id=1, source_target_pairs={{0,32},{32,64},{64,96},{96,0},{16,112},{48,16},{80,48},{112,80},{1... | collective-permute-start | bytes 663560 | tf_op jit(solution)/shard_map/ppermute | solution.py:44
  139.9 7.9 %collective-permute-start.19 = (bf16[144,768]{1,0:T(8,128)(2,1)S(1)}, bf16[144,768]{1,0:T(8,128)(2,1)S(1)}, u32[]{:S(2)}, u32[]{:S(2)}) collective-permute-start(bf16[144,768]{1,0:T(8,128)(2,1)S(1)} %get-tuple-element.62), channel_id=1, source_target_pairs={{0,64},{32,96},{64,0},{96,32},{1,65},{33,97},{65,1},{97,33},{2,66}... | collective-permute-start | bytes 663560 | tf_op jit(solution)/shard_map/ppermute | solution.py:48
  142.4 6.7 %collective-permute-start.23 = (bf16[144,768]{1,0:T(8,128)(2,1)S(1)}, bf16[144,768]{1,0:T(8,128)(2,1)S(1)}, u32[]{:S(2)}, u32[]{:S(2)}) collective-permute-start(bf16[144,768]{1,0:T(8,128)(2,1)S(1)} %get-tuple-element.68), channel_id=1, source_target_pairs={{0,3},{1,0},{2,1},{3,2},{16,17},{17,18},{18,19},{19,16},{4,7},{5,4... | collective-permute-start | bytes 663560 | tf_op jit(solution)/shard_map/ppermute | solution.py:44
  142.5 7.9 %collective-permute-start.24 = (bf16[144,768]{1,0:T(8,128)(2,1)S(1)}, bf16[144,768]{1,0:T(8,128)(2,1)S(1)}, u32[]{:S(2)}, u32[]{:S(2)}) collective-permute-start(bf16[144,768]{1,0:T(8,128)(2,1)S(1)} %get-tuple-element.69), channel_id=1, source_target_pairs={{0,1},{1,2},{2,3},{3,0},{16,19},{17,16},{18,17},{19,18},{4,5},{5,6... | collective-permute-start | bytes 663560 | tf_op jit(solution)/shard_map/ppermute | solution.py:44
  145.6 9.3 %collective-permute-start.25 = (bf16[144,768]{1,0:T(8,128)(2,1)S(1)}, bf16[144,768]{1,0:T(8,128)(2,1)S(1)}, u32[]{:S(2)}, u32[]{:S(2)}) collective-permute-start(bf16[144,768]{1,0:T(8,128)(2,1)S(1)} %get-tuple-element.70), channel_id=1, source_target_pairs={{0,2},{1,3},{2,0},{3,1},{4,6},{5,7},{6,4},{7,5},{8,10},{9,11},{10,... | collective-permute-start | bytes 663560 | tf_op jit(solution)/shard_map/ppermute | solution.py:48
  157.6 8.9 %collective-permute-start.26 = (bf16[2,128,768]{2,1,0:T(8,128)(2,1)S(1)}, bf16[2,128,768]{2,1,0:T(8,128)(2,1)}, u32[]{:S(2)}, u32[]{:S(2)}) collective-permute-start(bf16[2,128,768]{2,1,0:T(8,128)(2,1)S(1)} %final.1.refs_0_), channel_id=1, source_target_pairs={{0,32},{32,64},{64,96},{96,0},{16,112},{48,16},{80,48},{112,80},{1... | collective-permute-start | bytes 1179656 | tf_op jit(solution)/shard_map/ppermute | solution.py:44
  157.7 16.5 %collective-permute-start.27 = (bf16[2,128,768]{2,1,0:T(8,128)(2,1)S(1)}, bf16[2,128,768]{2,1,0:T(8,128)(2,1)}, u32[]{:S(2)}, u32[]{:S(2)}) collective-permute-start(bf16[2,128,768]{2,1,0:T(8,128)(2,1)S(1)} %final.1.refs_0_), channel_id=1, source_target_pairs={{0,96},{32,0},{64,32},{96,64},{16,48},{48,80},{80,112},{112,16},{1... | collective-permute-start | bytes 1179656 | tf_op jit(solution)/shard_map/ppermute | solution.py:44
  159.1 18.0 %collective-permute-start.28 = (bf16[2,128,768]{2,1,0:T(8,128)(2,1)S(1)}, bf16[2,128,768]{2,1,0:T(8,128)(2,1)}, u32[]{:S(2)}, u32[]{:S(2)}) collective-permute-start(bf16[2,128,768]{2,1,0:T(8,128)(2,1)S(1)} %final.1.refs_0_), channel_id=1, source_target_pairs={{0,64},{32,96},{64,0},{96,32},{1,65},{33,97},{65,1},{97,33},{2,66}... | collective-permute-start | bytes 1179656 | tf_op jit(solution)/shard_map/ppermute | solution.py:48
  162.1 18.7 %collective-permute-start.29 = (bf16[2,128,768]{2,1,0:T(8,128)(2,1)S(1)}, bf16[2,128,768]{2,1,0:T(8,128)(2,1)}, u32[]{:S(2)}, u32[]{:S(2)}) collective-permute-start(bf16[2,128,768]{2,1,0:T(8,128)(2,1)S(1)} %final.1.refs_0_), channel_id=1, source_target_pairs={{0,16},{16,0},{1,17},{17,1},{2,18},{18,2},{3,19},{19,3},{4,20},{20... | collective-permute-start | bytes 1179656 | tf_op jit(solution)/shard_map/ppermute | solution.py:52
  166.4 14.3 %collective-permute-start.30 = (bf16[2,128,768]{2,1,0:T(8,128)(2,1)}, bf16[2,128,768]{2,1,0:T(8,128)(2,1)}, u32[]{:S(2)}, u32[]{:S(2)}) collective-permute-start(bf16[2,128,768]{2,1,0:T(8,128)(2,1)} %collective-permute-done.26.refs_1_), channel_id=1, source_target_pairs={{0,16},{16,0},{1,17},{17,1},{2,18},{18,2},{3,19},{19,3},{4,20},{20... | collective-permute-start | bytes 1179656 | tf_op jit(solution)/shard_map/ppermute | solution.py:52
  174.2 6.6 %collective-permute-start.31 = (bf16[2,128,768]{2,1,0:T(8,128)(2,1)}, bf16[2,128,768]{2,1,0:T(8,128)(2,1)}, u32[]{:S(2)}, u32[]{:S(2)}) collective-permute-start(bf16[2,128,768]{2,1,0:T(8,128)(2,1)} %collective-permute-done.27.refs_2_), channel_id=1, source_target_pairs={{0,16},{16,0},{1,17},{17,1},{2,18},{18,2},{3,19},{19,3},{4,20},{20... | collective-permute-start | bytes 1179656 | tf_op jit(solution)/shard_map/ppermute | solution.py:52
  177.1 5.3 %collective-permute-start.32 = (bf16[2,128,768]{2,1,0:T(8,128)(2,1)}, bf16[2,128,768]{2,1,0:T(8,128)(2,1)}, u32[]{:S(2)}, u32[]{:S(2)}) collective-permute-start(bf16[2,128,768]{2,1,0:T(8,128)(2,1)} %collective-permute-done.28.refs_3_), channel_id=1, source_target_pairs={{0,16},{16,0},{1,17},{17,1},{2,18},{18,2},{3,19},{19,3},{4,20},{20... | collective-permute-start | bytes 1179656 | tf_op jit(solution)/shard_map/ppermute | solution.py:52
  (20 other events, 95.2 us)

commit v7 on v6

--- a/solution.py
+++ b/solution.py
@@ -446,15 +446,17 @@
         f_scr[:, k * 128 : (k + 1) * 128] = jnp.where(at >= 0, f, 0.0)
 
 
-def load_factors(s0, s1, s2, s3, idx0, idx1, peak_any, factor_out, f_scr, stats, idx_ref, peak_ref, sem):
+def load_factors(s0, s1, s2, s3, idx0, idx1, peak_any, factor_out, f_scr, stats, idx_ref, peak_ref, sem, load_block):
     loads = [pltpu.make_async_copy(s, stats.at[k], sem.at[k]) for k, s in enumerate((s0, s1, s2, s3))]
     loads.append(pltpu.make_async_copy(idx0, idx_ref.at[:, pl.ds(0, 512)], sem.at[4]))
     loads.append(pltpu.make_async_copy(idx1, idx_ref.at[:, pl.ds(512, 256)], sem.at[5]))
     loads.append(pltpu.make_async_copy(peak_any, peak_ref, sem.at[6]))
     for load in loads:
         load.start()
+    load_block(0)
     for load in loads:
         load.wait()
+    load_block(1)
     factor_kernel([stats.at[k] for k in range(4)], idx_ref, peak_ref, f_scr)
     factor_out[...] = f_scr[...]
 
@@ -487,11 +489,11 @@
 
     @pl.when(i == 0)
     def _():
-        for k in range(2):
-            load_block(k)
         if first_call:
-            load_factors(*ins[1:8], factor_out, f_scr, *refs[:4])
+            load_factors(*ins[1:8], factor_out, f_scr, *refs[:4], load_block)
         else:
+            for k in range(2):
+                load_block(k)
             load = pltpu.make_async_copy(ins[0], f_scr, fsem)
             load.start()
             load.wait()

time: 186 us -> 186 us (level)
  no operation moved by 1% of the time
where the time goes in v7:
time: 186 us
  Pallas kernels  63.5 us (34%)
  starting transfers between devices  55.5 us (30%)
  waiting for transfers between devices  55.4 us (30%)
  local copies, waits for them, and re-layouts  9.85 us (5%)
    ppermute x20, waiting for transfers between devices, turn(): return lax.ppermute(a, axes, pairs)  47.6 us
    ppermute x20, starting transfers between devices, turn(): return lax.ppermute(a, axes, pairs)  28.4 us
    ppermute x9, starting transfers between devices, swap(): return lax.ppermute(a, 'core', [(0, 1), (1, 0)])  20.8 us
    pallas_call x2, Pallas kernels, sums_call(): pl.pallas_call(kern, grid=(n,), in_specs=specs + [pl.BlockSpec(memory_spa...  14.8 us
    pallas_call x3, Pallas kernels, dispatch(): pl.pallas_call(kern, grid=(n,), in_specs=in_specs, out_specs=(pl.BlockSpe...  13.8 us
    pallas_call x1, Pallas kernels, middle(): pl.pallas_call(middle_kernel, in_specs=[anywhere] * 2 + [vmem] + [anywher...  10.4 us
    pallas_call x1, Pallas kernels, late_scores(): pl.pallas_call(late_kernel, in_specs=[anywhere, vmem] + [anywhere] * 4 +...  8.09 us
    unnamed x38, local copies, waits for them, and re-layouts  6.61 us
  transfers between devices with their start and end apart: 33, of which 12 were waited for; matrix products, arithmetic and copies ran while one was open for 2% of the time, Pallas kernels for 20%

profile of v7, /device:TPU:1, one launch (start us, length us, event | category | flops | bytes accessed | tf_op | source)
XLA Modules:
  0.0 185.5 jit_solution(1743572902646984798)
XLA Ops:
  0.0 3.3 %pack.1.refs_0_ = bf16[1040,768]{1,0:T(8,128)(2,1)} custom-call(bf16[1024,768]{1,0:T(8,128)(2,1)} %vectors.1, s32[4,1024]{1,0:T(4,128)} %bitcast.13), custom_call_target="tpu_custom_call" | custom-call | bytes 3000000 | tf_op jit(solution)/shard_map/pack/pallas_call | solution.py:91
  4.8 2.8 %collective-permute-start = (bf16[1040,768]{1,0:T(8,128)(2,1)}, bf16[1040,768]{1,0:T(8,128)(2,1)}, u32[]{:S(2)}, u32[]{:S(2)}) collective-permute-start(bf16[1040,768]{1,0:T(8,128)(2,1)} %pack.1.refs_0_), channel_id=1, source_target_pairs={{0,4},{4,8},{8,12},{12,0},{16,28},{20,16},{24,20},{28,24},{1,5},{5... | collective-permute-start | bytes 4792328 | tf_op jit(solution)/shard_map/ppermute | solution.py:44
  8.9 2.5 %collective-permute-start.3 = (bf16[1024,768]{1,0:T(8,128)(2,1)}, bf16[1024,768]{1,0:T(8,128)(2,1)S(1)}, u32[]{:S(2)}, u32[]{:S(2)}) collective-permute-start(bf16[1024,768]{1,0:T(8,128)(2,1)} %constant_dynamic-slice_fusion.1.c0), channel_id=1, source_target_pairs={{0,1},{1,2},{2,3},{3,0},{16,19},{17,16},{18,17},{19,18},{4,5},{5,6... | collective-permute-start | bytes 4718600 | tf_op jit(solution)/shard_map/ppermute | solution.py:44
  13.2 4.9 %dispatch0.1 = (f32[2,8,1024]{2,1,0:T(8,128)S(1)}, bf16[28,768,768]{2,1,0:T(8,128)(2,1)}) custom-call(bf16[1040,768]{1,0:T(8,128)(2,1)S(1)} %copy-done.5, bf16[1040,768]{1,0:T(8,128)(2,1)} %collective-permute-done.1.refs_1_, f32[8,128]{1,0:T(8,128)S(1)} %broadcast_in_dim.2.refs_2_.blk_ref.refs_1_), custom_call_target="tpu_custom_call" | custom-call | flops 2415919104 | bytes 6000000 | tf_op jit(solution)/shard_map/dispatch0/pallas_call | solution.py:204
  18.1 26.4 %collective-permute-done.3.refs_3_.c1 = bf16[1024,768]{1,0:T(8,128)(2,1)S(1)} collective-permute-done((bf16[1024,768]{1,0:T(8,128)(2,1)}, bf16[1024,768]{1,0:T(8,128)(2,1)S(1)}, u32[]{:S(2)}, u32[]{:S(2)}) %collective-permute-start.3) | collective-permute-done | bytes 1572896 | tf_op jit(solution)/shard_map/ppermute | solution.py:44
  44.4 3.0 %collective-permute-done.4.refs_4_.c2 = bf16[1024,768]{1,0:T(8,128)(2,1)S(1)} collective-permute-done((bf16[1024,768]{1,0:T(8,128)(2,1)}, bf16[1024,768]{1,0:T(8,128)(2,1)S(1)}, u32[]{:S(2)}, u32[]{:S(2)}) %collective-permute-start.4) | collective-permute-done | bytes 1572896 | tf_op jit(solution)/shard_map/ppermute | solution.py:44
  48.0 1.6 collective-permute-start.5
  49.6 2.9 %collective-permute-start.8 = (bf16[1024,768]{1,0:T(8,128)(2,1)S(1)}, bf16[1024,768]{1,0:T(8,128)(2,1)S(1)}, u32[]{:S(2)}, u32[]{:S(2)}) collective-permute-start(bf16[1024,768]{1,0:T(8,128)(2,1)S(1)} %collective-permute-done.3.refs_3_.c1), channel_id=1, source_target_pairs={{0,1},{1,2},{2,3},{3,0},{16,19},{17,16},{18,17},{19,18},{4,5},{5,6... | collective-permute-start | bytes 4718600 | tf_op jit(solution)/shard_map/ppermute | solution.py:44
  52.5 6.0 %dispatch2.1 = (f32[2,8,1024]{2,1,0:T(8,128)S(1)}, bf16[28,768,768]{2,1,0:T(8,128)(2,1)}) custom-call(bf16[1040,768]{1,0:T(8,128)(2,1)} %tie.4.refs_0_, bf16[1040,768]{1,0:T(8,128)(2,1)} %collective-permute-done.2.refs_2_.refs_1_, f32[8,128]{1,0:T(8,128)S(1)} %broadcast_in_dim.2.refs_2_.blk_ref.refs_1_, ...), custom_call_target="tpu_custom_call", output_to_operand_aliasing={{1}: (3, {})} | custom-call | flops 2415919104 | bytes 6000000 | tf_op jit(solution)/shard_map/dispatch2/pallas_call | solution.py:204
  58.6 10.4 %middle.1 = (bf16[28,768,768]{2,1,0:T(8,128)(2,1)}, f32[2,8,1024]{2,1,0:T(8,128)S(1)}, bf16[40,512,768]{2,1,0:T(8,128)(2,1)}, f32[8,512]{1,0:T(8,128)S(1)}, f32[8,512]{1,0:T(8,128)S(1)}) custom-call(bf16[1040,768]{1,0:T(8,128)(2,1)S(1)} %collective-permute-done.6.s0, ...), custom_call_target="tpu_custom_call", output_to_operand_aliasing={{0}: (6, {})} | custom-call | flops 2415919104 | bytes 20000000 | tf_op jit(solution)/shard_map/middle/pallas_call | solution.py:283
  69.0 2.3 %indices.2.refs_1_.refs_5_ = s32[8,512]{1,0:T(8,128)S(1)} custom-call(f32[2,8,1024]{2,1,0:T(8,128)S(1)} %get-tuple-element.38.refs_1_.refs_0_.rank0, f32[2,8,1024]{2,1,0:T(8,128)S(1)} %get-tuple-element.40.refs_1_.rank1, f32[2,8,1024]{2,1,0:T(8,128)S(1)} %get-tuple-element.42.refs_2_.rank2.refs_0_), custom_call_target="tpu_custom_call" | custom-call | flops 4000000000 | bytes 1000000 | tf_op jit(solution)/shard_map/indices/pallas_call | solution.py:157
  71.9 2.9 %dispatch6.1 = (f32[1,8,1024]{2,1,0:T(8,128)S(1)}, bf16[28,768,768]{2,1,0:T(8,128)(2,1)}) custom-call(bf16[1040,768]{1,0:T(8,128)(2,1)S(1)} %tie.5.refs_0_, f32[8,128]{1,0:T(8,128)S(1)} %broadcast_in_dim.2.refs_2_.blk_ref.refs_1_, bf16[28,768,768]{2,1,0:T(8,128)(2,1)} %get-tuple-element.43.refs_2_), custom_call_target="tpu_custom_call", output_to_operand_aliasing={{1}: (2, {})} | custom-call | flops 1207959552 | bytes 3000000 | tf_op jit(solution)/shard_map/dispatch6/pallas_call | solution.py:204
  75.3 8.1 %late_scores.1 = (bf16[28,768,768]{2,1,0:T(8,128)(2,1)}, bf16[40,512,768]{2,1,0:T(8,128)(2,1)}, f32[1,8,1024]{2,1,0:T(8,128)S(1)}, f32[8,768]{1,0:T(8,128)S(1)}, f32[8,1024]{1,0:T(8,128)S(1)}) custom-call(bf16[1040,768]{1,0:T(8,128)(2,1)S(1)} %collective-permute-done.9.source, ...), custom_call_target="tpu_custom_call", output_to_operand_aliasing={{0}: (12, {}), {1}: (13, {})} | custom-call | flops 3623878656 | bytes 20000000 | tf_op jit(solution)/shard_map/late_scores/pallas_call | solution.py:390
  91.8 9.1 %sums5.1 = (bf16[528,768]{1,0:T(8,128)(2,1)}, bf16[528,768]{1,0:T(8,128)(2,1)}, bf16[528,768]{1,0:T(8,128)(2,1)}, bf16[528,768]{1,0:T(8,128)(2,1)}, bf16[528,768]{1,0:T(8,128)(2,1)}, /*index=5*/f32[8,768]{1,0:T(8,128)}) custom-call(s32[8]{0:T(128)} %concatenate.17.refs_0_.where_ref, f32[8,1024]{1,0:T(8,128)} %copy-done.15, f32[8,1024]{1,0:T(8,128)} %copy-done.16, ...), custom_call_target="tpu_custom_call" | custom-call | flops 3019898880 | bytes 15000000 | tf_op jit(solution)/shard_map/sums5/pallas_call | solution.py:597
  102.1 3.8 %collective-permute-start.21 = (bf16[528,768]{1,0:T(8,128)(2,1)}, bf16[528,768]{1,0:T(8,128)(2,1)S(1)}, u32[]{:S(2)}, u32[]{:S(2)}) collective-permute-start(bf16[528,768]{1,0:T(8,128)(2,1)} %get-tuple-element.66), channel_id=1, source_target_pairs={{0,32},{32,64},{64,96},{96,0},{16,112},{48,16},{80,48},{112,80},{1... | collective-permute-start | bytes 2433032 | tf_op jit(solution)/shard_map/ppermute | solution.py:44
  105.8 5.7 %sums3.1 = (bf16[528,768]{1,0:T(8,128)(2,1)}, bf16[528,768]{1,0:T(8,128)(2,1)}, bf16[528,768]{1,0:T(8,128)(2,1)}) custom-call(f32[8,768]{1,0:T(8,128)} %get-tuple-element.54.refs_0_, bf16[40,512,768]{2,1,0:T(8,128)(2,1)} %get-tuple-element.52.refs_8_.refs_1_, bf16[28,768,768]{2,1,0:T(8,128)(2,1)} %get-tuple-element.53.refs_9_.refs_2_), custom_call_target="tpu_custom_call" | custom-call | flops 1811939328 | bytes 9000000 | tf_op jit(solution)/shard_map/sums3/pallas_call | solution.py:597
  114.3 1.7 collective-permute-start.16
  116.3 2.7 %collective-permute-start.22 = (bf16[528,768]{1,0:T(8,128)(2,1)S(1)}, bf16[528,768]{1,0:T(8,128)(2,1)S(1)}, u32[]{:S(2)}, u32[]{:S(2)}) collective-permute-start(bf16[528,768]{1,0:T(8,128)(2,1)S(1)} %add_convert_fusion), channel_id=1, source_target_pairs={{0,32},{32,64},{64,96},{96,0},{16,112},{48,16},{80,48},{112,80},{1... | collective-permute-start | bytes 2433032 | tf_op jit(solution)/shard_map/ppermute | solution.py:44
  119.0 9.8 %collective-permute-done.14.refs_1_ = bf16[528,768]{1,0:T(8,128)(2,1)S(1)} collective-permute-done((bf16[528,768]{1,0:T(8,128)(2,1)}, bf16[528,768]{1,0:T(8,128)(2,1)S(1)}, u32[]{:S(2)}, u32[]{:S(2)}) %collective-permute-start.14) | collective-permute-done | bytes 811040 | tf_op jit(solution)/shard_map/ppermute | solution.py:44
  128.8 4.9 %collective-permute-done.16.refs_2_ = bf16[528,768]{1,0:T(8,128)(2,1)S(1)} collective-permute-done((bf16[528,768]{1,0:T(8,128)(2,1)S(1)}, bf16[528,768]{1,0:T(8,128)(2,1)S(1)}, u32[]{:S(2)}, u32[]{:S(2)}) %collective-permute-start.16) | collective-permute-done | bytes 811040 | tf_op jit(solution)/shard_map/ppermute | solution.py:44
  133.7 2.2 %parted0.1 = (bf16[144,768]{1,0:T(8,128)(2,1)S(1)}, bf16[144,768]{1,0:T(8,128)(2,1)S(1)}, bf16[144,768]{1,0:T(8,128)(2,1)}, bf16[144,768]{1,0:T(8,128)(2,1)S(1)}) custom-call(s32[8]{0:T(128)S(1)} %copy-done.12, bf16[528,768]{1,0:T(8,128)(2,1)S(1)} %copy-done.4, bf16[528,768]{1,0:T(8,128)(2,1)S(1)} %collective-permute-done.14.refs_1_, ...), custom_call_target="tpu_custom_call" | custom-call | flops 1000000 | bytes 4000000 | tf_op jit(solution)/shard_map/parted0/pallas_call | solution.py:694
  136.9 2.3 %collective-permute-start.18 = (bf16[144,768]{1,0:T(8,128)(2,1)}, bf16[144,768]{1,0:T(8,128)(2,1)S(1)}, u32[]{:S(2)}, u32[]{:S(2)}) collective-permute-start(bf16[144,768]{1,0:T(8,128)(2,1)} %get-tuple-element.61), channel_id=1, source_target_pairs={{0,32},{32,64},{64,96},{96,0},{16,112},{48,16},{80,48},{112,80},{1... | collective-permute-start | bytes 663560 | tf_op jit(solution)/shard_map/ppermute | solution.py:44
  141.9 3.1 %collective-permute-start.24 = (bf16[144,768]{1,0:T(8,128)(2,1)S(1)}, bf16[144,768]{1,0:T(8,128)(2,1)S(1)}, u32[]{:S(2)}, u32[]{:S(2)}) collective-permute-start(bf16[144,768]{1,0:T(8,128)(2,1)S(1)} %get-tuple-element.69), channel_id=1, source_target_pairs={{0,1},{1,2},{2,3},{3,0},{16,19},{17,16},{18,17},{19,18},{4,5},{5,6... | collective-permute-start | bytes 663560 | tf_op jit(solution)/shard_map/ppermute | solution.py:44
  149.9 4.4 %collective-permute-done.25.refs_7_ = bf16[144,768]{1,0:T(8,128)(2,1)S(1)} collective-permute-done((bf16[144,768]{1,0:T(8,128)(2,1)S(1)}, bf16[144,768]{1,0:T(8,128)(2,1)S(1)}, u32[]{:S(2)}, u32[]{:S(2)}) %collective-permute-start.25) | collective-permute-done | bytes 221216 | tf_op jit(solution)/shard_map/ppermute | solution.py:48
  154.3 2.7 %final.1.refs_0_ = bf16[2,128,768]{2,1,0:T(8,128)(2,1)S(1)} custom-call(bf16[144,768]{1,0:T(8,128)(2,1)S(1)} %copy-done.9, bf16[144,768]{1,0:T(8,128)(2,1)S(1)} %collective-permute-done.17.refs_1_, bf16[144,768]{1,0:T(8,128)(2,1)S(1)} %collective-permute-done.18.refs_2_, bf16[144,768]{1,0:T(8,128)(2,1)S(1)} %collective-permute-done.19.refs_3_, ...), custom_call_target="tpu_custom_call" | custom-call | flops 1000000 | bytes 2000000 | tf_op jit(solution)/shard_map/final/pallas_call | solution.py:720
  158.5 3.0 %collective-permute-start.28 = (bf16[2,128,768]{2,1,0:T(8,128)(2,1)S(1)}, bf16[2,128,768]{2,1,0:T(8,128)(2,1)}, u32[]{:S(2)}, u32[]{:S(2)}) collective-permute-start(bf16[2,128,768]{2,1,0:T(8,128)(2,1)S(1)} %final.1.refs_0_), channel_id=1, source_target_pairs={{0,64},{32,96},{64,0},{96,32},{1,65},{33,97},{65,1},{97,33},{2,66}... | collective-permute-start | bytes 1179656 | tf_op jit(solution)/shard_map/ppermute | solution.py:48
  161.5 4.4 %collective-permute-start.29 = (bf16[2,128,768]{2,1,0:T(8,128)(2,1)S(1)}, bf16[2,128,768]{2,1,0:T(8,128)(2,1)}, u32[]{:S(2)}, u32[]{:S(2)}) collective-permute-start(bf16[2,128,768]{2,1,0:T(8,128)(2,1)S(1)} %final.1.refs_0_), channel_id=1, source_target_pairs={{0,16},{16,0},{1,17},{17,1},{2,18},{18,2},{3,19},{19,3},{4,20},{20... | collective-permute-start | bytes 1179656 | tf_op jit(solution)/shard_map/ppermute | solution.py:52
  165.8 7.8 %collective-permute-start.30 = (bf16[2,128,768]{2,1,0:T(8,128)(2,1)}, bf16[2,128,768]{2,1,0:T(8,128)(2,1)}, u32[]{:S(2)}, u32[]{:S(2)}) collective-permute-start(bf16[2,128,768]{2,1,0:T(8,128)(2,1)} %collective-permute-done.26.refs_1_), channel_id=1, source_target_pairs={{0,16},{16,0},{1,17},{17,1},{2,18},{18,2},{3,19},{19,3},{4,20},{20... | collective-permute-start | bytes 1179656 | tf_op jit(solution)/shard_map/ppermute | solution.py:52
  173.6 2.9 %collective-permute-start.31 = (bf16[2,128,768]{2,1,0:T(8,128)(2,1)}, bf16[2,128,768]{2,1,0:T(8,128)(2,1)}, u32[]{:S(2)}, u32[]{:S(2)}) collective-permute-start(bf16[2,128,768]{2,1,0:T(8,128)(2,1)} %collective-permute-done.27.refs_2_), channel_id=1, source_target_pairs={{0,16},{16,0},{1,17},{17,1},{2,18},{18,2},{3,19},{19,3},{4,20},{20... | collective-permute-start | bytes 1179656 | tf_op jit(solution)/shard_map/ppermute | solution.py:52
  176.5 3.6 %collective-permute-start.32 = (bf16[2,128,768]{2,1,0:T(8,128)(2,1)}, bf16[2,128,768]{2,1,0:T(8,128)(2,1)}, u32[]{:S(2)}, u32[]{:S(2)}) collective-permute-start(bf16[2,128,768]{2,1,0:T(8,128)(2,1)} %collective-permute-done.28.refs_3_), channel_id=1, source_target_pairs={{0,16},{16,0},{1,17},{17,1},{2,18},{18,2},{3,19},{19,3},{4,20},{20... | collective-permute-start | bytes 1179656 | tf_op jit(solution)/shard_map/ppermute | solution.py:52
  180.2 1.6 collective-permute-done.32.refs_7_
  181.7 3.6 %place.1 = bf16[4,4,128,768]{3,2,1,0:T(8,128)(2,1)} custom-call(s32[10]{0:T(128)S(1)} %concatenate.16.where_ref, bf16[2,128,768]{2,1,0:T(8,128)(2,1)S(1)} %final.1.refs_0_, bf16[2,128,768]{2,1,0:T(8,128)(2,1)} %collective-permute-done.26.refs_1_, bf16[2,128,768]{2,1,0:T(8,128)(2,1)} %collective-permute-done.27.refs_2_, ...), custom_call_target="tpu_custom_call" | custom-call | bytes 6000000 | tf_op jit(solution)/shard_map/place/pallas_call | solution.py:757
  (104 shorter events, 28.8 us)
Async XLA Ops:
  3.3 8.3 %collective-permute-start.1 = (bf16[1040,768]{1,0:T(8,128)(2,1)}, bf16[1040,768]{1,0:T(8,128)(2,1)}, u32[]{:S(2)}, u32[]{:S(2)}) collective-permute-start(bf16[1040,768]{1,0:T(8,128)(2,1)} %pack.1.refs_0_), channel_id=1, source_target_pairs={{0,16},{16,0},{1,17},{17,1},{2,18},{18,2},{3,19},{19,3},{4,20},{20... | collective-permute-start | bytes 4792328 | tf_op jit(solution)/shard_map/ppermute | solution.py:52
  4.8 42.6 %collective-permute-start = (bf16[1040,768]{1,0:T(8,128)(2,1)}, bf16[1040,768]{1,0:T(8,128)(2,1)}, u32[]{:S(2)}, u32[]{:S(2)}) collective-permute-start(bf16[1040,768]{1,0:T(8,128)(2,1)} %pack.1.refs_0_), channel_id=1, source_target_pairs={{0,4},{4,8},{8,12},{12,0},{16,28},{20,16},{24,20},{28,24},{1,5},{5... | collective-permute-start | bytes 4792328 | tf_op jit(solution)/shard_map/ppermute | solution.py:44
  7.7 39.8 %collective-permute-start.2 = (bf16[1040,768]{1,0:T(8,128)(2,1)}, bf16[1040,768]{1,0:T(8,128)(2,1)}, u32[]{:S(2)}, u32[]{:S(2)}) collective-permute-start(bf16[1040,768]{1,0:T(8,128)(2,1)} %pack.1.refs_0_), channel_id=1, source_target_pairs={{0,12},{4,0},{8,4},{12,8},{16,20},{20,24},{24,28},{28,16},{1,13},{... | collective-permute-start | bytes 4792328 | tf_op jit(solution)/shard_map/ppermute | solution.py:44
  8.9 35.5 %collective-permute-start.3 = (bf16[1024,768]{1,0:T(8,128)(2,1)}, bf16[1024,768]{1,0:T(8,128)(2,1)S(1)}, u32[]{:S(2)}, u32[]{:S(2)}) collective-permute-start(bf16[1024,768]{1,0:T(8,128)(2,1)} %constant_dynamic-slice_fusion.1.c0), channel_id=1, source_target_pairs={{0,1},{1,2},{2,3},{3,0},{16,19},{17,16},{18,17},{19,18},{4,5},{5,6... | collective-permute-start | bytes 4718600 | tf_op jit(solution)/shard_map/ppermute | solution.py:44
  11.4 36.0 %collective-permute-start.4 = (bf16[1024,768]{1,0:T(8,128)(2,1)}, bf16[1024,768]{1,0:T(8,128)(2,1)S(1)}, u32[]{:S(2)}, u32[]{:S(2)}) collective-permute-start(bf16[1024,768]{1,0:T(8,128)(2,1)} %constant_dynamic-slice_fusion.1.c0), channel_id=1, source_target_pairs={{0,3},{1,0},{2,1},{3,2},{16,17},{17,18},{18,19},{19,16},{4,7},{5,4... | collective-permute-start | bytes 4718600 | tf_op jit(solution)/shard_map/ppermute | solution.py:44
  47.4 11.1 %collective-permute-start.6 = (bf16[1040,768]{1,0:T(8,128)(2,1)}, bf16[1040,768]{1,0:T(8,128)(2,1)S(1)}, u32[]{:S(2)}, u32[]{:S(2)}) collective-permute-start(bf16[1040,768]{1,0:T(8,128)(2,1)} %tie.4.refs_0_), channel_id=1, source_target_pairs={{0,16},{16,0},{1,17},{17,1},{2,18},{18,2},{3,19},{19,3},{4,20},{20... | collective-permute-start | bytes 4792328 | tf_op jit(solution)/shard_map/ppermute | solution.py:52
  47.5 11.0 %collective-permute-start.7 = (bf16[1040,768]{1,0:T(8,128)(2,1)}, bf16[1040,768]{1,0:T(8,128)(2,1)S(1)}, u32[]{:S(2)}, u32[]{:S(2)}) collective-permute-start(bf16[1040,768]{1,0:T(8,128)(2,1)} %collective-permute-done.2.refs_2_.refs_1_), channel_id=1, source_target_pairs={{0,16},{16,0},{1,17},{17,1},{2,18},{18,2},{3,19},{19,3},{4,20},{20... | collective-permute-start | bytes 4792328 | tf_op jit(solution)/shard_map/ppermute | solution.py:52
  48.0 23.3 %collective-permute-start.5 = (bf16[1040,768]{1,0:T(8,128)(2,1)}, bf16[1040,768]{1,0:T(8,128)(2,1)S(1)}, u32[]{:S(2)}, u32[]{:S(2)}) collective-permute-start(bf16[1040,768]{1,0:T(8,128)(2,1)} %tie.4.refs_0_), channel_id=1, source_target_pairs={{0,4},{4,8},{8,12},{12,0},{16,28},{20,16},{24,20},{28,24},{1,5},{5... | collective-permute-start | bytes 4792328 | tf_op jit(solution)/shard_map/ppermute | solution.py:44
  49.6 21.7 %collective-permute-start.8 = (bf16[1024,768]{1,0:T(8,128)(2,1)S(1)}, bf16[1024,768]{1,0:T(8,128)(2,1)S(1)}, u32[]{:S(2)}, u32[]{:S(2)}) collective-permute-start(bf16[1024,768]{1,0:T(8,128)(2,1)S(1)} %collective-permute-done.3.refs_3_.c1), channel_id=1, source_target_pairs={{0,1},{1,2},{2,3},{3,0},{16,19},{17,16},{18,17},{19,18},{4,5},{5,6... | collective-permute-start | bytes 4718600 | tf_op jit(solution)/shard_map/ppermute | solution.py:44
  71.9 3.4 %collective-permute-start.9 = (bf16[1040,768]{1,0:T(8,128)(2,1)S(1)}, bf16[1040,768]{1,0:T(8,128)(2,1)S(1)}, u32[]{:S(2)}, u32[]{:S(2)}) collective-permute-start(bf16[1040,768]{1,0:T(8,128)(2,1)S(1)} %tie.5.refs_0_), channel_id=1, source_target_pairs={{0,16},{16,0},{1,17},{17,1},{2,18},{18,2},{3,19},{19,3},{4,20},{20... | collective-permute-start | bytes 4792328 | tf_op jit(solution)/shard_map/ppermute | solution.py:52
  85.4 4.2 %collective-permute-start.11 = (f32[8,1024]{1,0:T(8,128)S(1)}, f32[8,1024]{1,0:T(8,128)S(1)}, u32[]{:S(2)}, u32[]{:S(2)}) collective-permute-start(f32[8,1024]{1,0:T(8,128)S(1)} %log_add_fusion.refs_1_), channel_id=1, source_target_pairs={{0,4},{4,8},{8,12},{12,0},{16,28},{20,16},{24,20},{28,24},{1,5},{5... | collective-permute-start | bytes 98312 | tf_op jit(solution)/shard_map/ppermute | solution.py:44
  85.9 4.5 %collective-permute-start.12 = (f32[8,1024]{1,0:T(8,128)S(1)}, f32[8,1024]{1,0:T(8,128)S(1)}, u32[]{:S(2)}, u32[]{:S(2)}) collective-permute-start(f32[8,1024]{1,0:T(8,128)S(1)} %log_add_fusion.refs_1_), channel_id=1, source_target_pairs={{0,12},{4,0},{8,4},{12,8},{16,20},{20,24},{24,28},{28,16},{1,13},{... | collective-permute-start | bytes 98312 | tf_op jit(solution)/shard_map/ppermute | solution.py:44
  86.9 4.3 %collective-permute-start.13 = (f32[8,1024]{1,0:T(8,128)S(1)}, f32[8,1024]{1,0:T(8,128)S(1)}, u32[]{:S(2)}, u32[]{:S(2)}) collective-permute-start(f32[8,1024]{1,0:T(8,128)S(1)} %log_add_fusion.refs_1_), channel_id=1, source_target_pairs={{0,8},{4,12},{8,0},{12,4},{1,9},{5,13},{9,1},{13,5},{2,10},{6,14},... | collective-permute-start | bytes 98312 | tf_op jit(solution)/shard_map/ppermute | solution.py:48
  100.9 12.9 %collective-permute-start.15 = (bf16[528,768]{1,0:T(8,128)(2,1)}, bf16[528,768]{1,0:T(8,128)(2,1)S(1)}, u32[]{:S(2)}, u32[]{:S(2)}) collective-permute-start(bf16[528,768]{1,0:T(8,128)(2,1)} %get-tuple-element.58), channel_id=1, source_target_pairs={{0,1},{1,2},{2,3},{3,0},{16,19},{17,16},{18,17},{19,18},{4,5},{5,6... | collective-permute-start | bytes 2433032 | tf_op jit(solution)/shard_map/ppermute | solution.py:44
  102.1 14.0 %collective-permute-start.21 = (bf16[528,768]{1,0:T(8,128)(2,1)}, bf16[528,768]{1,0:T(8,128)(2,1)S(1)}, u32[]{:S(2)}, u32[]{:S(2)}) collective-permute-start(bf16[528,768]{1,0:T(8,128)(2,1)} %get-tuple-element.66), channel_id=1, source_target_pairs={{0,32},{32,64},{64,96},{96,0},{16,112},{48,16},{80,48},{112,80},{1... | collective-permute-start | bytes 2433032 | tf_op jit(solution)/shard_map/ppermute | solution.py:44
  112.7 16.1 %collective-permute-start.14 = (bf16[528,768]{1,0:T(8,128)(2,1)}, bf16[528,768]{1,0:T(8,128)(2,1)S(1)}, u32[]{:S(2)}, u32[]{:S(2)}) collective-permute-start(bf16[528,768]{1,0:T(8,128)(2,1)} %tie.6), channel_id=1, source_target_pairs={{0,3},{1,0},{2,1},{3,2},{16,17},{17,18},{18,19},{19,16},{4,7},{5,4... | collective-permute-start | bytes 2433032 | tf_op jit(solution)/shard_map/ppermute | solution.py:44
  113.8 26.9 %collective-permute-start.20 = (bf16[528,768]{1,0:T(8,128)(2,1)S(1)}, bf16[528,768]{1,0:T(8,128)(2,1)S(1)}, u32[]{:S(2)}, u32[]{:S(2)}) collective-permute-start(bf16[528,768]{1,0:T(8,128)(2,1)S(1)} %tie.7), channel_id=1, source_target_pairs={{0,96},{32,0},{64,32},{96,64},{16,48},{48,80},{80,112},{112,16},{1... | collective-permute-start | bytes 2433032 | tf_op jit(solution)/shard_map/ppermute | solution.py:44
  114.3 19.4 %collective-permute-start.16 = (bf16[528,768]{1,0:T(8,128)(2,1)S(1)}, bf16[528,768]{1,0:T(8,128)(2,1)S(1)}, u32[]{:S(2)}, u32[]{:S(2)}) collective-permute-start(bf16[528,768]{1,0:T(8,128)(2,1)S(1)} %add_convert_fusion.1), channel_id=1, source_target_pairs={{0,1},{1,2},{2,3},{3,0},{16,19},{17,16},{18,17},{19,18},{4,5},{5,6... | collective-permute-start | bytes 2433032 | tf_op jit(solution)/shard_map/ppermute | solution.py:44
  116.3 24.4 %collective-permute-start.22 = (bf16[528,768]{1,0:T(8,128)(2,1)S(1)}, bf16[528,768]{1,0:T(8,128)(2,1)S(1)}, u32[]{:S(2)}, u32[]{:S(2)}) collective-permute-start(bf16[528,768]{1,0:T(8,128)(2,1)S(1)} %add_convert_fusion), channel_id=1, source_target_pairs={{0,32},{32,64},{64,96},{96,0},{16,112},{48,16},{80,48},{112,80},{1... | collective-permute-start | bytes 2433032 | tf_op jit(solution)/shard_map/ppermute | solution.py:44
  136.6 8.4 %collective-permute-start.17 = (bf16[144,768]{1,0:T(8,128)(2,1)S(1)}, bf16[144,768]{1,0:T(8,128)(2,1)S(1)}, u32[]{:S(2)}, u32[]{:S(2)}) collective-permute-start(bf16[144,768]{1,0:T(8,128)(2,1)S(1)} %get-tuple-element.60), channel_id=1, source_target_pairs={{0,96},{32,0},{64,32},{96,64},{16,48},{48,80},{80,112},{112,16},{1... | collective-permute-start | bytes 663560 | tf_op jit(solution)/shard_map/ppermute | solution.py:44
  136.9 10.2 %collective-permute-start.18 = (bf16[144,768]{1,0:T(8,128)(2,1)}, bf16[144,768]{1,0:T(8,128)(2,1)S(1)}, u32[]{:S(2)}, u32[]{:S(2)}) collective-permute-start(bf16[144,768]{1,0:T(8,128)(2,1)} %get-tuple-element.61), channel_id=1, source_target_pairs={{0,32},{32,64},{64,96},{96,0},{16,112},{48,16},{80,48},{112,80},{1... | collective-permute-start | bytes 663560 | tf_op jit(solution)/shard_map/ppermute | solution.py:44
  139.3 7.9 %collective-permute-start.19 = (bf16[144,768]{1,0:T(8,128)(2,1)S(1)}, bf16[144,768]{1,0:T(8,128)(2,1)S(1)}, u32[]{:S(2)}, u32[]{:S(2)}) collective-permute-start(bf16[144,768]{1,0:T(8,128)(2,1)S(1)} %get-tuple-element.62), channel_id=1, source_target_pairs={{0,64},{32,96},{64,0},{96,32},{1,65},{33,97},{65,1},{97,33},{2,66}... | collective-permute-start | bytes 663560 | tf_op jit(solution)/shard_map/ppermute | solution.py:48
  141.8 6.7 %collective-permute-start.23 = (bf16[144,768]{1,0:T(8,128)(2,1)S(1)}, bf16[144,768]{1,0:T(8,128)(2,1)S(1)}, u32[]{:S(2)}, u32[]{:S(2)}) collective-permute-start(bf16[144,768]{1,0:T(8,128)(2,1)S(1)} %get-tuple-element.68), channel_id=1, source_target_pairs={{0,3},{1,0},{2,1},{3,2},{16,17},{17,18},{18,19},{19,16},{4,7},{5,4... | collective-permute-start | bytes 663560 | tf_op jit(solution)/shard_map/ppermute | solution.py:44
  141.9 7.9 %collective-permute-start.24 = (bf16[144,768]{1,0:T(8,128)(2,1)S(1)}, bf16[144,768]{1,0:T(8,128)(2,1)S(1)}, u32[]{:S(2)}, u32[]{:S(2)}) collective-permute-start(bf16[144,768]{1,0:T(8,128)(2,1)S(1)} %get-tuple-element.69), channel_id=1, source_target_pairs={{0,1},{1,2},{2,3},{3,0},{16,19},{17,16},{18,17},{19,18},{4,5},{5,6... | collective-permute-start | bytes 663560 | tf_op jit(solution)/shard_map/ppermute | solution.py:44
  145.0 9.3 %collective-permute-start.25 = (bf16[144,768]{1,0:T(8,128)(2,1)S(1)}, bf16[144,768]{1,0:T(8,128)(2,1)S(1)}, u32[]{:S(2)}, u32[]{:S(2)}) collective-permute-start(bf16[144,768]{1,0:T(8,128)(2,1)S(1)} %get-tuple-element.70), channel_id=1, source_target_pairs={{0,2},{1,3},{2,0},{3,1},{4,6},{5,7},{6,4},{7,5},{8,10},{9,11},{10,... | collective-permute-start | bytes 663560 | tf_op jit(solution)/shard_map/ppermute | solution.py:48
  157.0 8.9 %collective-permute-start.26 = (bf16[2,128,768]{2,1,0:T(8,128)(2,1)S(1)}, bf16[2,128,768]{2,1,0:T(8,128)(2,1)}, u32[]{:S(2)}, u32[]{:S(2)}) collective-permute-start(bf16[2,128,768]{2,1,0:T(8,128)(2,1)S(1)} %final.1.refs_0_), channel_id=1, source_target_pairs={{0,32},{32,64},{64,96},{96,0},{16,112},{48,16},{80,48},{112,80},{1... | collective-permute-start | bytes 1179656 | tf_op jit(solution)/shard_map/ppermute | solution.py:44
  157.1 16.5 %collective-permute-start.27 = (bf16[2,128,768]{2,1,0:T(8,128)(2,1)S(1)}, bf16[2,128,768]{2,1,0:T(8,128)(2,1)}, u32[]{:S(2)}, u32[]{:S(2)}) collective-permute-start(bf16[2,128,768]{2,1,0:T(8,128)(2,1)S(1)} %final.1.refs_0_), channel_id=1, source_target_pairs={{0,96},{32,0},{64,32},{96,64},{16,48},{48,80},{80,112},{112,16},{1... | collective-permute-start | bytes 1179656 | tf_op jit(solution)/shard_map/ppermute | solution.py:44
  158.5 18.0 %collective-permute-start.28 = (bf16[2,128,768]{2,1,0:T(8,128)(2,1)S(1)}, bf16[2,128,768]{2,1,0:T(8,128)(2,1)}, u32[]{:S(2)}, u32[]{:S(2)}) collective-permute-start(bf16[2,128,768]{2,1,0:T(8,128)(2,1)S(1)} %final.1.refs_0_), channel_id=1, source_target_pairs={{0,64},{32,96},{64,0},{96,32},{1,65},{33,97},{65,1},{97,33},{2,66}... | collective-permute-start | bytes 1179656 | tf_op jit(solution)/shard_map/ppermute | solution.py:48
  161.5 18.7 %collective-permute-start.29 = (bf16[2,128,768]{2,1,0:T(8,128)(2,1)S(1)}, bf16[2,128,768]{2,1,0:T(8,128)(2,1)}, u32[]{:S(2)}, u32[]{:S(2)}) collective-permute-start(bf16[2,128,768]{2,1,0:T(8,128)(2,1)S(1)} %final.1.refs_0_), channel_id=1, source_target_pairs={{0,16},{16,0},{1,17},{17,1},{2,18},{18,2},{3,19},{19,3},{4,20},{20... | collective-permute-start | bytes 1179656 | tf_op jit(solution)/shard_map/ppermute | solution.py:52
  165.8 14.3 %collective-permute-start.30 = (bf16[2,128,768]{2,1,0:T(8,128)(2,1)}, bf16[2,128,768]{2,1,0:T(8,128)(2,1)}, u32[]{:S(2)}, u32[]{:S(2)}) collective-permute-start(bf16[2,128,768]{2,1,0:T(8,128)(2,1)} %collective-permute-done.26.refs_1_), channel_id=1, source_target_pairs={{0,16},{16,0},{1,17},{17,1},{2,18},{18,2},{3,19},{19,3},{4,20},{20... | collective-permute-start | bytes 1179656 | tf_op jit(solution)/shard_map/ppermute | solution.py:52
  173.6 6.5 %collective-permute-start.31 = (bf16[2,128,768]{2,1,0:T(8,128)(2,1)}, bf16[2,128,768]{2,1,0:T(8,128)(2,1)}, u32[]{:S(2)}, u32[]{:S(2)}) collective-permute-start(bf16[2,128,768]{2,1,0:T(8,128)(2,1)} %collective-permute-done.27.refs_2_), channel_id=1, source_target_pairs={{0,16},{16,0},{1,17},{17,1},{2,18},{18,2},{3,19},{19,3},{4,20},{20... | collective-permute-start | bytes 1179656 | tf_op jit(solution)/shard_map/ppermute | solution.py:52
  176.5 5.2 %collective-permute-start.32 = (bf16[2,128,768]{2,1,0:T(8,128)(2,1)}, bf16[2,128,768]{2,1,0:T(8,128)(2,1)}, u32[]{:S(2)}, u32[]{:S(2)}) collective-permute-start(bf16[2,128,768]{2,1,0:T(8,128)(2,1)} %collective-permute-done.28.refs_3_), channel_id=1, source_target_pairs={{0,16},{16,0},{1,17},{17,1},{2,18},{18,2},{3,19},{19,3},{4,20},{20... | collective-permute-start | bytes 1179656 | tf_op jit(solution)/shard_map/ppermute | solution.py:52
  (20 other events, 95.2 us)
